TPU v7x, 32 devices: a whole 2x2x4 slice. The times are simulated.
32 devices in a mesh: dp: 8 (over y, x, core), blk: 4 (over z).
Axes of the slice: x: 2, y: 2, z: 4, core: 2. Of those that a mesh axis runs over, the one named last changes fastest.
Arguments:
- tokens: bfloat16 [8192, 2048], P(('dp', 'blk')), may hold values from -6 to 6
- cotangent: bfloat16 [8192, 2048], P(('dp', 'blk')), may hold values from -6 to 6
- lengths: int32 [3, 4], replicated, may hold values from 0 to 4096, as said below
- branch_weight: bfloat16 [2048, 2560], P('dp', 'blk'), may hold values from -0.125 to 0.125
- mixer_weight: bfloat16 [2048, 2560], P('dp', 'blk'), may hold values from -0.125 to 0.125
- branch_bias: bfloat16 [2560], P('blk'), may hold values from -3 to 3
- mixer_bias: bfloat16 [2560], P('blk'), may hold values from -3 to 3
- conv_taps: bfloat16 [2560, 4], P('blk'), may hold values from -3 to 3
- conv_bias: bfloat16 [2560], P('blk'), may hold values from -2 to 2
- decay_weight: bfloat16 [2560, 160], P('blk'), may hold values from -0.5 to 0.5
- input_weight: bfloat16 [2560, 160], P('blk'), may hold values from -0.5 to 0.5
- decay_bias: bfloat16 [2560], P('blk'), may hold values from -4 to 4
- input_bias: bfloat16 [2560], P('blk'), may hold values from -4 to 4
- decay_param: bfloat16 [2560], P('blk'), may hold values from 4 to 11
- output_weight: bfloat16 [2560, 2048], P('blk', 'dp'), may hold values from -0.25 to 0.25
- first_gain: bfloat16 [2048], replicated, may hold values from 0.099609375 to 1.8984375
- second_gain: bfloat16 [2048], replicated, may hold values from 0.099609375 to 1.8984375
- gate_weight: bfloat16 [2048, 6144], P(None, ('dp', 'blk')), may hold values from -0.125 to 0.125
- up_weight: bfloat16 [2048, 6144], P(None, ('dp', 'blk')), may hold values from -0.125 to 0.125
- down_weight: bfloat16 [6144, 2048], P(('dp', 'blk')), may hold values from -0.15625 to 0.15625
Outputs:
- output: bfloat16 [8192, 2048], P(('dp', 'blk'))
- token_grad: bfloat16 [8192, 2048], P(('dp', 'blk'))
- branch_weight_grad: float32 [2048, 2560], P('dp', 'blk')
- mixer_weight_grad: float32 [2048, 2560], P('dp', 'blk')
- branch_bias_grad: float32 [2560], P('blk')
- mixer_bias_grad: float32 [2560], P('blk')
- conv_taps_grad: float32 [2560, 4], P('blk')
- conv_bias_grad: float32 [2560], P('blk')
- decay_weight_grad: float32 [2560, 160], P('blk')
- input_weight_grad: float32 [2560, 160], P('blk')
- decay_bias_grad: float32 [2560], P('blk')
- input_bias_grad: float32 [2560], P('blk')
- decay_param_grad: float32 [2560], P('blk')
- output_weight_grad: float32 [2560, 2048], P('blk', 'dp')
- first_gain_grad: float32 [2048], replicated
- second_gain_grad: float32 [2048], replicated
- gate_weight_grad: float32 [2048, 6144], P(None, ('dp', 'blk'))
- up_weight_grad: float32 [2048, 6144], P(None, ('dp', 'blk'))
- down_weight_grad: float32 [6144, 2048], P(('dp', 'blk'))
Inputs may be any that keep to these rules, and one draw needn't show every extreme that they name: Row b holds the lengths of the 4 sequence slots of bucket b in packing order, a slot may be empty; they sum to at most the bucket's size (4096, or 2048 for the first and the last bucket) and the rest of the bucket is padding at its end.
All inputs are finite; a program needn't handle non-finite values.
Results may differ from a plain program's by a relative error of at most 0.02.
Values may be sent and summed in bfloat16 or wider, within the bound.
No kernel may reach another device: no remote copies, remote signals or barrier semaphores. Data moves between devices by JAX's collectives and lax.ppermute only.
A program may use at most 384 MiB of HBM per device.

v0:
```python
from functools import partial

import jax
import jax.numpy as jnp
from jax import lax
from jax.sharding import PartitionSpec as P

BUCKET_DP = 4


EPS = 1e-06
DECAY = 8.0


def shifted_2(x, axis, by):
    count = lax.axis_size(axis)
    pairs = [(i, i + by) for i in range(count) if 0 <= i + by < count]
    return lax.ppermute(x, axis, pairs)


def entering_2(part, axis, combine, identity, reverse):
    count = lax.axis_size(axis)
    place = lax.axis_index(axis)
    ahead = count - 1 - place if reverse else place
    gathered = jax.tree.map(lambda a: lax.all_gather(a, axis), part)
    state = jax.tree.map(lambda a, e: jnp.zeros_like(a) + jnp.asarray(e, a.dtype), part, identity)

    def one(hop, state):
        source = count - 1 - hop if reverse else hop
        return combine(
            state, jax.tree.map(lambda a: lax.dynamic_index_in_dim(a, source, 0, False), gathered)
        )

    return lax.fori_loop(0, ahead, one, state)


def affine(earlier, later):
    return (earlier[0] * later[0], later[0] * earlier[1] + later[1])


def normed(values, gain_vec):
    return values * lax.rsqrt(jnp.mean(values * values, axis=-1, keepdims=True) + EPS) * gain_vec


def coefficients(pre_decay, pre_input, conv_float, param_chan, carries, restart, filled):
    gate_decay = jax.nn.sigmoid(pre_decay)
    log_decay = -DECAY * gate_decay * jax.nn.softplus(-param_chan)
    square_root = jnp.sqrt(-jnp.expm1(2.0 * log_decay))
    factor = jnp.where(restart, 1.0, square_root)
    return (jnp.exp(log_decay) * carries, filled * factor * jax.nn.sigmoid(pre_input) * conv_float)


def plain(former, latter):
    return jnp.dot(former, latter, preferred_element_type=jnp.float32)


def trailing(former, latter):
    return lax.dot_general(
        former, latter, (((1,), (1,)), ((), ())), preferred_element_type=jnp.float32
    )


def leading(former, latter):
    return lax.dot_general(
        former, latter, (((0,), (0,)), ((), ())), preferred_element_type=jnp.float32
    )


def segment_place(bucket_row, positions):
    first_end = bucket_row[0]
    second_end = first_end + bucket_row[1]
    third_end = second_end + bucket_row[2]
    final_end = third_end + bucket_row[3]
    begins = jnp.zeros_like(positions)
    for border in (first_end, second_end, third_end):
        begins = jnp.where(positions >= border, border, begins)
    return (positions - begins, (positions >= 0) & (positions < final_end))


def body(
    tokens,
    cotangent,
    lengths,
    branch_weight,
    mixer_weight,
    branch_bias,
    mixer_bias,
    conv_taps,
    conv_bias,
    decay_weight,
    input_weight,
    decay_bias,
    input_bias,
    decay_param,
    output_weight,
    first_gain,
    second_gain,
    gate_weight,
    up_weight,
    down_weight,
):
    f32 = jnp.float32
    branch_own, mixer_own, output_own = (
        lax.all_gather(branch_weight, "dp", axis=0, tiled=True),
        lax.all_gather(mixer_weight, "dp", axis=0, tiled=True),
        lax.all_gather(output_weight, "dp", axis=1, tiled=True),
    )
    inputs = tokens.astype(f32)
    norm_one, norm_back_one = jax.vjp(normed, inputs, first_gain.astype(f32))
    low_one = norm_one.astype(jnp.bfloat16)
    low_rows = lax.all_gather(low_one, "blk", axis=0, tiled=True)
    branch_pre = plain(low_rows, branch_own) + branch_bias.astype(f32)
    branch_act, gelu_back_one = jax.vjp(jax.nn.gelu, branch_pre)
    channels = (plain(low_rows, mixer_own) + mixer_bias.astype(f32)).astype(jnp.bfloat16)
    rows_dp, width = channels.shape
    taps_own = conv_taps.astype(f32)
    span = taps_own.shape[1]
    block_width = decay_weight.shape[1]
    heads = width // block_width
    dp_place = lax.axis_index("dp")
    shifted = dp_place + BUCKET_DP // 2
    bucket_index = shifted // BUCKET_DP
    anchor = jnp.where(bucket_index == 0, BUCKET_DP // 2 * rows_dp, 0)
    bucket_row = lax.dynamic_slice_in_dim(lengths, bucket_index, 1, 0)[0]
    positions = shifted % BUCKET_DP * rows_dp - anchor + jnp.arange(rows_dp, dtype=jnp.int32)
    seg_pos, filled = segment_place(bucket_row, positions)
    rim = shifted_2(channels[rows_dp - (span - 1) :], "dp", 1)
    extended = jnp.concatenate([rim, channels], axis=0).astype(f32)
    masks = [(seg_pos >= lag).astype(f32)[:, None] for lag in range(span)]
    conv_out = conv_bias.astype(f32) + jnp.zeros((rows_dp, width), f32)
    for lag in range(span):
        offset = span - 1 - lag
        conv_out = conv_out + taps_own[:, lag] * masks[lag] * extended[offset : offset + rows_dp]
    conv_low = conv_out.astype(jnp.bfloat16)
    blocks_low = conv_low.reshape(rows_dp, heads, block_width)
    decay_own = decay_weight.reshape(heads, block_width, block_width)
    input_own = input_weight.reshape(heads, block_width, block_width)
    pre_decay = jnp.einsum(
        "thc,hcd->thd", blocks_low, decay_own, preferred_element_type=f32
    ).reshape(rows_dp, width) + decay_bias.astype(f32)
    pre_input = jnp.einsum(
        "thc,hcd->thd", blocks_low, input_own, preferred_element_type=f32
    ).reshape(rows_dp, width) + input_bias.astype(f32)
    restart = (seg_pos == 0)[:, None]
    carries = ((seg_pos != 0) & filled).astype(f32)[:, None]
    filled_col = filled.astype(f32)[:, None]
    local_coeffs = partial(coefficients, carries=carries, restart=restart, filled=filled_col)
    (decays, drives), coeff_back = jax.vjp(
        local_coeffs, pre_decay, pre_input, conv_low.astype(f32), decay_param.astype(f32)
    )
    decay_cum, state_local = lax.associative_scan(affine, (decays, drives))
    unit_pair = (jnp.ones((width,), f32), jnp.zeros((width,), f32))
    entering = entering_2((decay_cum[-1], state_local[-1]), "dp", affine, unit_pair, False)[1]
    states = state_local + decay_cum * entering
    state_float = states.astype(jnp.bfloat16).astype(f32)
    mixed_low = (branch_act * state_float).astype(jnp.bfloat16)
    resid = inputs + lax.psum_scatter(
        plain(mixed_low, output_own), "blk", scatter_dimension=0, tiled=True
    )
    norm_two, norm_back_two = jax.vjp(normed, resid, second_gain.astype(f32))
    low_two = norm_two.astype(jnp.bfloat16)
    feed_rows, feed_grad = (low_two, cotangent)
    gate_use, up_use, down_use = (
        lax.all_gather(gate_weight, ("dp", "blk"), axis=1, tiled=True),
        lax.all_gather(up_weight, ("dp", "blk"), axis=1, tiled=True),
        lax.all_gather(down_weight, ("dp", "blk"), axis=0, tiled=True),
    )
    gate_pre = plain(feed_rows, gate_use)
    up_pre = plain(feed_rows, up_use)
    gate_act, gelu_back_two = jax.vjp(jax.nn.gelu, gate_pre)
    hidden = (gate_act * up_pre).astype(jnp.bfloat16)
    feed_part = plain(hidden, down_use)
    output = (resid + feed_part).astype(jnp.bfloat16)
    hidden_grad = trailing(feed_grad, down_use)
    gate_grad = gelu_back_two(hidden_grad * up_pre)[0].astype(jnp.bfloat16)
    up_grad = (hidden_grad * gate_act).astype(jnp.bfloat16)
    norm_part = trailing(gate_grad, gate_use) + trailing(up_grad, up_use)
    gate_sum, up_sum, down_sum = (
        lax.psum_scatter(
            leading(feed_rows, gate_grad), ("dp", "blk"), scatter_dimension=1, tiled=True
        ),
        lax.psum_scatter(
            leading(feed_rows, up_grad), ("dp", "blk"), scatter_dimension=1, tiled=True
        ),
        lax.psum_scatter(
            leading(hidden, feed_grad), ("dp", "blk"), scatter_dimension=0, tiled=True
        ),
    )
    resid_norm, second_term = norm_back_two(norm_part)
    resid_grad = cotangent.astype(f32) + resid_norm
    resid_low = resid_grad.astype(jnp.bfloat16)
    resid_rows = lax.all_gather(resid_low, "blk", axis=0, tiled=True)
    output_term = leading(mixed_low, resid_rows)
    mixed_grad = trailing(resid_rows, output_own)
    state_grad = (mixed_grad * branch_act).astype(jnp.bfloat16).astype(f32)
    branch_grad_low = gelu_back_one(mixed_grad * state_float)[0].astype(jnp.bfloat16)
    next_decay = jnp.concatenate([decays[1:], jnp.ones((1, width), f32)], axis=0)
    reach, adjoint_local = lax.associative_scan(affine, (next_decay, state_grad), reverse=True)
    leaving = entering_2(
        (decays[0] * reach[0], decays[0] * adjoint_local[0]), "dp", affine, unit_pair, True
    )[1]
    adjoint = adjoint_local + reach * leaving
    previous = jnp.concatenate([entering[None, :], states[:-1]], axis=0)
    decay_pre_grad, input_pre_grad, direct_grad, param_term = coeff_back(
        (adjoint * previous, adjoint)
    )
    decay_low = decay_pre_grad.astype(jnp.bfloat16)
    input_low = input_pre_grad.astype(jnp.bfloat16)
    decay_blocks = decay_low.reshape(rows_dp, heads, block_width)
    input_blocks = input_low.reshape(rows_dp, heads, block_width)
    conv_grad = direct_grad + (
        jnp.einsum("thd,hcd->thc", decay_blocks, decay_own, preferred_element_type=f32)
        + jnp.einsum("thd,hcd->thc", input_blocks, input_own, preferred_element_type=f32)
    ).reshape(rows_dp, width)
    decay_term = jnp.einsum(
        "thc,thd->hcd", blocks_low, decay_blocks, preferred_element_type=f32
    ).reshape(width, block_width)
    input_term = jnp.einsum(
        "thc,thd->hcd", blocks_low, input_blocks, preferred_element_type=f32
    ).reshape(width, block_width)
    decay_bias_term = jnp.sum(decay_low.astype(f32), axis=0)
    input_bias_term = jnp.sum(input_low.astype(f32), axis=0)
    conv_bias_term = jnp.sum(conv_grad, axis=0)
    ext_grad = jnp.zeros((rows_dp + span - 1, width), f32)
    tap_terms = []
    for lag in range(span):
        offset = span - 1 - lag
        weighted = masks[lag] * conv_grad
        tap_terms.append(jnp.sum(weighted * extended[offset : offset + rows_dp], axis=0))
        ext_grad = ext_grad.at[offset : offset + rows_dp].add(taps_own[:, lag] * weighted)
    taps_term = jnp.stack(tap_terms, axis=1)
    returned = shifted_2(ext_grad[: span - 1], "dp", -1)
    channel_grad = ext_grad[span - 1 :].at[rows_dp - (span - 1) :].add(returned)
    mixer_grad_low = channel_grad.astype(jnp.bfloat16)
    branch_term = leading(low_rows, branch_grad_low)
    mixer_term = leading(low_rows, mixer_grad_low)
    branch_bias_term = jnp.sum(branch_grad_low.astype(f32), axis=0)
    mixer_bias_term = jnp.sum(mixer_grad_low.astype(f32), axis=0)
    low_grad = lax.psum_scatter(
        trailing(branch_grad_low, branch_own) + trailing(mixer_grad_low, mixer_own),
        "blk",
        scatter_dimension=0,
        tiled=True,
    )
    input_norm, first_term = norm_back_one(low_grad)
    token_grad = (resid_grad + input_norm).astype(jnp.bfloat16)
    branch_sum, mixer_sum, output_sum = (
        lax.psum_scatter(branch_term, "dp", scatter_dimension=0, tiled=True),
        lax.psum_scatter(mixer_term, "dp", scatter_dimension=0, tiled=True),
        lax.psum_scatter(output_term, "dp", scatter_dimension=1, tiled=True),
    )
    (
        branch_bias_sum,
        mixer_bias_sum,
        taps_sum,
        conv_bias_sum,
        decay_sum,
        input_sum,
        decay_bias_sum,
        input_bias_sum,
        param_sum,
    ) = lax.psum(
        (
            branch_bias_term,
            mixer_bias_term,
            taps_term,
            conv_bias_term,
            decay_term,
            input_term,
            decay_bias_term,
            input_bias_term,
            param_term,
        ),
        "dp",
    )
    first_sum, second_sum = lax.psum((first_term, second_term), ("dp", "blk"))
    return (
        output,
        token_grad,
        branch_sum,
        mixer_sum,
        branch_bias_sum,
        mixer_bias_sum,
        taps_sum,
        conv_bias_sum,
        decay_sum,
        input_sum,
        decay_bias_sum,
        input_bias_sum,
        param_sum,
        output_sum,
        first_sum,
        second_sum,
        gate_sum,
        up_sum,
        down_sum,
    )


def solution(mesh):
    return jax.shard_map(
        body,
        mesh=mesh,
        in_specs=(
            P(("dp", "blk"), None),
            P(("dp", "blk"), None),
            P(),
            P("dp", "blk"),
            P("dp", "blk"),
            P("blk"),
            P("blk"),
            P("blk", None),
            P("blk"),
            P("blk", None),
            P("blk", None),
            P("blk"),
            P("blk"),
            P("blk"),
            P("blk", "dp"),
            P(),
            P(),
            P(None, ("dp", "blk")),
            P(None, ("dp", "blk")),
            P(("dp", "blk"), None),
        ),
        out_specs=(
            P(("dp", "blk"), None),
            P(("dp", "blk"), None),
            P("dp", "blk"),
            P("dp", "blk"),
            P("blk"),
            P("blk"),
            P("blk", None),
            P("blk"),
            P("blk", None),
            P("blk", None),
            P("blk"),
            P("blk"),
            P("blk"),
            P("blk", "dp"),
            P(),
            P(),
            P(None, ("dp", "blk")),
            P(None, ("dp", "blk")),
            P(("dp", "blk"), None),
        ),
        check_vma=False,
    )
```

profile of v0, /device:TPU:3, one launch (start us, length us, event | category | flops | bytes accessed | tf_op | source)
XLA Modules:
  0.0 3202.2 jit_solution(4857193150937181027)
XLA Ops:
  21.6 20.9 all-gather.17.cloned.1.call-done
  42.6 82.5 %all-gather.13.cloned.1.call-done = bf16[1024,2048]{1,0:T(8,128)(2,1)} async-done(((bf16[256,2048]{1,0:T(8,128)(2,1)}), bf16[1024,2048]{1,0:T(8,128)(2,1)}) %all-gather.13.cloned.1.call-update) | async-done | bytes 4194320 | tf_op jit(solution)/shard_map/all_gather | solution.py:111
  125.1 6.4 add_convert_fusion.1
  158.1 7.9 convert_multiply_fusion.7
  166.0 7.1 slice.787
  173.2 7.0 slice.788
  304.2 7.0 slice.858
  348.0 5.2 pad.275
  353.2 5.3 pad.276
  359.2 9.7 all-gather.1
  369.1 5.2 pad.295
  374.3 5.3 pad.296
  380.3 8.8 all-gather
  389.4 12.4 fusion.7
  401.7 7.9 fusion.94
  411.5 179.2 %reduce-scatter.9.cloned.1.call-done = f32[256,2048]{1,0:T(8,128)} async-done(((f32[1024,2048]{1,0:T(8,128)}), f32[256,2048]{1,0:T(8,128)}) %reduce-scatter.9.cloned.1.call-update) | async-done | bytes 2097168 | tf_op jit(solution)/shard_map/reduce_scatter | solution.py:157
  593.0 91.2 %all-gather.21.cloned.1.call-done = bf16[2048,6144]{0,1:T(8,128)(2,1)} async-done(((bf16[2048,192]{0,1:T(8,128)(2,1)}), bf16[2048,6144]{0,1:T(8,128)(2,1)}) %all-gather.21.cloned.1.call-update) | async-done | bytes 25165840 | tf_op jit(solution)/shard_map/all_gather | solution.py:164
  684.2 14.5 fusion.95
  698.7 140.7 %all-gather.23.cloned.1.call-done = bf16[2048,6144]{0,1:T(8,128)(2,1)} async-done(((bf16[2048,192]{0,1:T(8,128)(2,1)}), bf16[2048,6144]{0,1:T(8,128)(2,1)}) %all-gather.23.cloned.1.call-update) | async-done | bytes 25165840 | tf_op jit(solution)/shard_map/all_gather | solution.py:165
  839.4 13.6 fusion.96
  853.0 141.6 %all-gather.25.cloned.1.call-done = bf16[6144,2048]{1,0:T(8,128)(2,1)} async-done(((bf16[192,2048]{1,0:T(8,128)(2,1)}), bf16[6144,2048]{1,0:T(8,128)(2,1)}) %all-gather.25.cloned.1.call-update) | async-done | bytes 25165840 | tf_op jit(solution)/shard_map/all_gather | solution.py:166
  994.6 20.8 multiply_convert_fusion
  1015.4 13.2 fusion.97
  1028.6 12.8 multiply_reduce_fusion.5
  1059.9 10.8 slice.885
  1070.8 6.5 slice.892
  1077.3 6.7 slice.883
  1084.1 39.1 %all-gather.27.cloned.1.call-done = bf16[1024,2048]{1,0:T(8,128)(2,1)} async-done(((bf16[256,2048]{1,0:T(8,128)(2,1)}), bf16[1024,2048]{1,0:T(8,128)(2,1)}) %all-gather.27.cloned.1.call-update) | async-done | bytes 4194320 | tf_op jit(solution)/shard_map/all_gather | solution.py:192
  1123.2 11.2 convert_reduce_fusion.3
  1142.9 10.7 slice.887
  1153.6 10.7 slice.889
  1259.9 6.1 slice.960
  1266.7 6.8 slice.961
  1291.8 4.9 pad.314
  1304.5 5.2 pad.336
  1316.6 9.4 pad.315
  1326.0 9.2 pad.335
  1342.1 9.5 all-gather.3
  1351.6 8.0 all-gather.2
  1360.0 20.7 rev.9
  1380.8 20.9 rev.8
  1401.9 9.5 multiply_reduce_fusion
  1412.1 7.4 convert_reduce_fusion
  1435.4 7.8 multiply_reduce_fusion.4
  1448.5 7.6 scatter-add.19
  1460.0 7.5 scatter-add.20
  1473.5 6.1 fusion.98
  1480.1 9.2 convolution_add_fusion
  1495.5 7.4 fusion.102
  1504.2 8.0 fusion.99
  1513.5 8.1 fusion.109
  1522.8 21.5 fusion.103
  1544.4 22.2 fusion.104
  1567.8 21.4 fusion.105
  1590.9 13.5 fusion.22
  1604.9 23.4 all-reduce.84
  1634.5 41.1 %all-reduce.83 = (f32[2048]{0:T(1024)}, f32[2048]{0:T(1024)}) all-reduce(f32[2048]{0:T(1024)S(1)} %get-tuple-element.215, f32[2048]{0:T(1024)S(1)} %copy-done.144), channel_id=1, replica_groups=mesh['dp'=8,'blk'=4] {'dp','blk'}, use_global_device_ids=true, to_apply=%region_33.34 | all-reduce | flops 4096 | bytes 32768 | tf_op jit(solution)/shard_map/psum | solution.py:276
  1680.3 10.7 all-reduce.88.cloned.1.call-done
  1691.1 61.6 %reduce-scatter.17.cloned.1.call-done = f32[640,256]{1,0:T(8,128)} async-done(((f32[640,2048]{1,0:T(8,128)}), f32[640,256]{1,0:T(8,128)}) %reduce-scatter.17.cloned.1.call-update) | async-done | bytes 655376 | tf_op jit(solution)/shard_map/reduce_scatter | solution.py:250
  1752.7 60.8 %reduce-scatter.13.cloned.1.call-done = f32[256,640]{1,0:T(8,128)} async-done(((f32[2048,640]{1,0:T(8,128)}), f32[256,640]{1,0:T(8,128)}) %reduce-scatter.13.cloned.1.call-update) | async-done | bytes 655376 | tf_op jit(solution)/shard_map/reduce_scatter | solution.py:248
  1813.5 60.6 %reduce-scatter.15.cloned.1.call-done = f32[256,640]{1,0:T(8,128)} async-done(((f32[2048,640]{1,0:T(8,128)}), f32[256,640]{1,0:T(8,128)}) %reduce-scatter.15.cloned.1.call-update) | async-done | bytes 655376 | tf_op jit(solution)/shard_map/reduce_scatter | solution.py:249
  1874.0 439.8 %reduce-scatter.19.cloned.1.call-done = f32[2048,192]{0,1:T(8,128)} async-done(((f32[2048,6144]{0,1:T(8,128)}), f32[2048,192]{0,1:T(8,128)}) %reduce-scatter.19.cloned.1.call-update) | async-done | bytes 1572880 | tf_op jit(solution)/shard_map/reduce_scatter | solution.py:179
  2313.8 438.8 %reduce-scatter.21.cloned.1.call-done = f32[2048,192]{0,1:T(8,128)} async-done(((f32[2048,6144]{0,1:T(8,128)}), f32[2048,192]{0,1:T(8,128)}) %reduce-scatter.21.cloned.1.call-update) | async-done | bytes 1572880 | tf_op jit(solution)/shard_map/reduce_scatter | solution.py:182
  2752.6 438.5 %reduce-scatter.23.cloned.1.call-done = f32[192,2048]{1,0:T(8,128)} async-done(((f32[6144,2048]{1,0:T(8,128)}), f32[192,2048]{1,0:T(8,128)}) %reduce-scatter.23.cloned.1.call-update) | async-done | bytes 1572880 | tf_op jit(solution)/shard_map/reduce_scatter | solution.py:185
  (758 shorter events, 425.8 us)
Async XLA Ops:
  8.1 34.5 %all-gather.17.cloned.1.call-start = ((), (), s32[]{:S(2)}) async-start(), calls=%async_computation.10 | async-start | bytes 2949120 | tf_op jit(solution)/shard_map/all_gather | solution.py:105
  8.8 116.3 %all-gather.13.cloned.1.call-start = ((), (), s32[]{:S(2)}) async-start(), calls=%async_computation.8 | async-start | bytes 5242880 | tf_op jit(solution)/shard_map/all_gather | solution.py:111
  14.7 374.6 %all-gather.15.cloned.1.call-start = ((), (), s32[]{:S(2)}) async-start(), calls=%async_computation.9 | async-start | bytes 2949120 | tf_op jit(solution)/shard_map/all_gather | solution.py:104
  15.5 386.3 %all-gather.19.cloned.1.call-start = ((), (), s32[]{:S(2)}) async-start(), calls=%async_computation.11 | async-start | bytes 2949120 | tf_op jit(solution)/shard_map/all_gather | solution.py:106
  16.1 574.7 %reduce-scatter.9.cloned.1.call-start = ((), (), s32[]{:S(2)}) async-start(), calls=%async_computation.12 | async-start | bytes 10485760 | tf_op jit(solution)/shard_map/reduce_scatter | solution.py:157
  19.4 138.6 %copy-start.60 = (f32[1024]{0:T(1024)}, f32[1024]{0:T(1024)S(1)}, u32[]{:S(2)}) copy-start(f32[1024]{0:T(1024)S(1)} %get-tuple-element.377) | copy-start | bytes 12292
  19.4 138.6 %copy-start.62 = (f32[1024]{0:T(1024)}, f32[1024]{0:T(1024)S(1)}, u32[]{:S(2)}) copy-start(f32[1024]{0:T(1024)S(1)} %get-tuple-element.378) | copy-start | bytes 12292
  20.1 137.9 %copy-start.64 = (f32[1024]{0:T(1024)}, f32[1024]{0:T(1024)S(1)}, u32[]{:S(2)}) copy-start(f32[1024]{0:T(1024)S(1)} %get-tuple-element.379) | copy-start | bytes 12292
  20.1 137.9 %copy-start.66 = (f32[1024]{0:T(1024)}, f32[1024]{0:T(1024)S(1)}, u32[]{:S(2)}) copy-start(f32[1024]{0:T(1024)S(1)} %get-tuple-element.380) | copy-start | bytes 12292
  20.2 137.8 %copy-start.70 = (f32[640]{0:T(1024)}, f32[640]{0:T(1024)S(1)}, u32[]{:S(2)}) copy-start(f32[640]{0:T(1024)S(1)} %get-tuple-element.219) | copy-start | bytes 7684
  20.2 137.8 %copy-start.72 = (f32[640]{0:T(1024)}, f32[640]{0:T(1024)S(1)}, u32[]{:S(2)}) copy-start(f32[640]{0:T(1024)S(1)} %get-tuple-element.220) | copy-start | bytes 7684
  20.2 137.8 %copy-start.74 = (f32[640]{0:T(1024)}, f32[640]{0:T(1024)S(1)}, u32[]{:S(2)}) copy-start(f32[640]{0:T(1024)S(1)} %get-tuple-element.221) | copy-start | bytes 7684
  20.2 137.8 %copy-start.76 = (f32[640]{0:T(1024)}, f32[640]{0:T(1024)S(1)}, u32[]{:S(2)}) copy-start(f32[640]{0:T(1024)S(1)} %get-tuple-element.218) | copy-start | bytes 7684
  21.5 136.5 %copy-start.95 = (f32[1024]{0:T(1024)}, f32[1024]{0:T(1024)S(1)}, u32[]{:S(2)}) copy-start(f32[1024]{0:T(1024)S(1)} %get-tuple-element.375) | copy-start | bytes 12292
  21.5 136.5 %copy-start.97 = (pred[1024]{0:T(1024)(128)(4,1)}, pred[1024]{0:T(1024)(128)(4,1)S(1)}, u32[]{:S(2)}) copy-start(pred[1024]{0:T(1024)(128)(4,1)S(1)} %get-tuple-element.376) | copy-start | bytes 3076
  21.6 136.5 %copy-start.82 = (f32[640]{0:T(1024)}, f32[640]{0:T(1024)S(1)}, u32[]{:S(2)}) copy-start(f32[640]{0:T(1024)S(1)} %broadcast_multiply_fusion) | copy-start | bytes 7684
  21.6 114.8 %copy-start.150 = (bf16[640]{0:T(1024)(128)(2,1)S(1)}, bf16[640]{0:T(1024)(128)(2,1)}, u32[]{:S(2)}) copy-start(bf16[640]{0:T(1024)(128)(2,1)} %param.42) | copy-start | bytes 3844
  21.6 114.8 %copy-start.58 = (bf16[640,160]{0,1:T(8,128)(2,1)S(1)}, bf16[640,160]{0,1:T(8,128)(2,1)}, u32[]{:S(2)}) copy-start(bf16[640,160]{0,1:T(8,128)(2,1)} %param.43) | copy-start | bytes 614404
  21.6 115.0 %copy-start.59 = (bf16[640,160]{0,1:T(8,128)(2,1)S(1)}, bf16[640,160]{0,1:T(8,128)(2,1)}, u32[]{:S(2)}) copy-start(bf16[640,160]{0,1:T(8,128)(2,1)} %param.44) | copy-start | bytes 614404
  21.6 115.1 %copy-start.151 = (bf16[640]{0:T(1024)(128)(2,1)S(1)}, bf16[640]{0:T(1024)(128)(2,1)}, u32[]{:S(2)}) copy-start(bf16[640]{0:T(1024)(128)(2,1)} %param.45) | copy-start | bytes 3844
  21.6 115.2 %copy-start.152 = (bf16[640]{0:T(1024)(128)(2,1)S(1)}, bf16[640]{0:T(1024)(128)(2,1)}, u32[]{:S(2)}) copy-start(bf16[640]{0:T(1024)(128)(2,1)} %param.46) | copy-start | bytes 3844
  21.6 115.2 %copy-start.153 = (bf16[640]{0:T(1024)(128)(2,1)S(1)}, bf16[640]{0:T(1024)(128)(2,1)}, u32[]{:S(2)}) copy-start(bf16[640]{0:T(1024)(128)(2,1)} %param.39) | copy-start | bytes 3844
  132.6 4.9 collective-permute-start
  136.3 21.7 copy-start.84
  136.4 21.7 copy-start.90
  136.8 21.3 copy-start.86
  136.8 21.3 copy-start.88
  409.7 181.1 %copy-start.13 = (bf16[256,2048]{1,0:T(8,128)(2,1)S(1)}, bf16[256,2048]{1,0:T(8,128)(2,1)}, u32[]{:S(2)}) copy-start(bf16[256,2048]{1,0:T(8,128)(2,1)} %param.34) | copy-start | bytes 3145732
  409.7 274.5 %all-gather.21.cloned.1.call-start = ((), (), s32[]{:S(2)}) async-start(), calls=%async_computation.13 | async-start | bytes 25952256 | tf_op jit(solution)/shard_map/all_gather | solution.py:164
  410.3 429.1 %all-gather.23.cloned.1.call-start = ((), (), s32[]{:S(2)}) async-start(), calls=%async_computation.14 | async-start | bytes 25952256 | tf_op jit(solution)/shard_map/all_gather | solution.py:165
  410.9 583.7 %all-gather.25.cloned.1.call-start = ((), (), s32[]{:S(2)}) async-start(), calls=%async_computation.15 | async-start | bytes 25952256 | tf_op jit(solution)/shard_map/all_gather | solution.py:166
  411.4 711.8 %all-gather.27.cloned.1.call-start = ((), (), s32[]{:S(2)}) async-start(), calls=%async_computation.16 | async-start | bytes 5242880 | tf_op jit(solution)/shard_map/all_gather | solution.py:192
  411.5 629.9 %copy-start.80 = (f32[2048]{0:T(1024)}, f32[2048]{0:T(1024)S(1)}, u32[]{:S(2)}) copy-start(f32[2048]{0:T(1024)S(1)} %convert_element_type.173) | copy-start | bytes 24580
  592.7 448.6 %copy-start.8 = (f32[256,2048]{1,0:T(8,128)}, f32[256,2048]{1,0:T(8,128)S(1)}, u32[]{:S(2)}) copy-start(f32[256,2048]{1,0:T(8,128)S(1)} %get-tuple-element.266) | copy-start | bytes 6291460
  592.8 448.6 %copy-start.102 = (f32[256]{0:T(256)}, f32[256]{0:T(256)S(1)}, u32[]{:S(2)}) copy-start(f32[256]{0:T(256)S(1)} %fusion.72) | copy-start | bytes 3076
  593.0 91.2 %copy-start.24 = (bf16[256,2048]{1,0:T(8,128)(2,1)}, bf16[256,2048]{1,0:T(8,128)(2,1)S(1)}, u32[]{:S(2)}) copy-start(bf16[256,2048]{1,0:T(8,128)(2,1)S(1)} %multiply_convert_fusion.3) | copy-start | bytes 3145732
  698.7 295.9 %copy-start.22 = (bf16[256,2048]{1,0:T(8,128)(2,1)S(1)}, bf16[256,2048]{1,0:T(8,128)(2,1)}, u32[]{:S(2)}) copy-start(bf16[256,2048]{1,0:T(8,128)(2,1)} %param.35) | copy-start | bytes 3145732
  1044.5 587.7 %reduce-scatter.11.cloned.1.call-start = ((), (), s32[]{:S(2)}) async-start(), calls=%async_computation.17 | async-start | bytes 10485760 | tf_op jit(solution)/shard_map/reduce_scatter | solution.py:239
  1380.7 21.1 copy-start.67
  1380.7 21.1 copy-start.71
  1380.7 21.1 copy-start.73
  1380.7 21.1 copy-start.75
  1380.7 21.1 copy-start.77
  1380.7 21.1 copy-start.83
  1380.8 21.1 copy-start.85
  1380.8 21.1 copy-start.87
  1380.8 21.1 copy-start.89
  1471.3 8.6 collective-permute-start.1
  1489.3 201.8 %all-reduce.88.cloned.1.call-start = ((), (), s32[]{:S(2)}) async-start(), calls=%async_computation.24 | async-start | bytes 1638400 | tf_op jit(solution)/shard_map/psum | solution.py:262
  1495.4 257.3 %reduce-scatter.17.cloned.1.call-start = ((), (), s32[]{:S(2)}) async-start(), calls=%async_computation.20 | async-start | bytes 5898240 | tf_op jit(solution)/shard_map/reduce_scatter | solution.py:250
  1502.9 310.6 %reduce-scatter.13.cloned.1.call-start = ((), (), s32[]{:S(2)}) async-start(), calls=%async_computation.18 | async-start | bytes 5898240 | tf_op jit(solution)/shard_map/reduce_scatter | solution.py:248
  1512.2 361.8 %reduce-scatter.15.cloned.1.call-start = ((), (), s32[]{:S(2)}) async-start(), calls=%async_computation.19 | async-start | bytes 5898240 | tf_op jit(solution)/shard_map/reduce_scatter | solution.py:249
  1521.6 792.2 %reduce-scatter.19.cloned.1.call-start = ((), (), s32[]{:S(2)}) async-start(), calls=%async_computation.21 | async-start | bytes 51904512 | tf_op jit(solution)/shard_map/reduce_scatter | solution.py:179
  1544.4 1208.2 %reduce-scatter.21.cloned.1.call-start = ((), (), s32[]{:S(2)}) async-start(), calls=%async_computation.22 | async-start | bytes 51904512 | tf_op jit(solution)/shard_map/reduce_scatter | solution.py:182
  1566.6 1624.5 %reduce-scatter.23.cloned.1.call-start = ((), (), s32[]{:S(2)}) async-start(), calls=%async_computation.23 | async-start | bytes 51904512 | tf_op jit(solution)/shard_map/reduce_scatter | solution.py:185
  1590.9 41.3 %copy-start.14 = (bf16[256,2048]{1,0:T(8,128)(2,1)S(1)}, bf16[256,2048]{1,0:T(8,128)(2,1)}, u32[]{:S(2)}) copy-start(bf16[256,2048]{1,0:T(8,128)(2,1)} %param.34) | copy-start | bytes 3145732
  1590.9 41.3 %copy-start.79 = (f32[2048]{0:T(1024)S(1)}, f32[2048]{0:T(1024)}, u32[]{:S(2)}) copy-start(f32[2048]{0:T(1024)} %copy-done.78) | copy-start | bytes 24580
  1590.9 41.3 %copy-start.101 = (f32[256]{0:T(256)S(1)}, f32[256]{0:T(256)}, u32[]{:S(2)}) copy-start(f32[256]{0:T(256)} %copy-done.100) | copy-start | bytes 3076
  1604.5 30.0 copy-start.144
  1604.5 71.1 %copy-start.141 = (f32[256]{0:T(256)S(1)}, f32[256]{0:T(256)}, u32[]{:S(2)}) copy-start(f32[256]{0:T(256)} %copy-done.140) | copy-start | bytes 3076
  1604.5 71.1 %copy-start.81 = (f32[2048]{0:T(1024)S(1)}, f32[2048]{0:T(1024)}, u32[]{:S(2)}) copy-start(f32[2048]{0:T(1024)} %copy-done.80) | copy-start | bytes 24580
  1604.5 71.1 %copy-start.103 = (f32[256]{0:T(256)S(1)}, f32[256]{0:T(256)}, u32[]{:S(2)}) copy-start(f32[256]{0:T(256)} %copy-done.102) | copy-start | bytes 3076
  1604.5 71.1 %copy-start.139 = (f32[256]{0:T(256)S(1)}, f32[256]{0:T(256)}, u32[]{:S(2)}) copy-start(f32[256]{0:T(256)} %copy-done.138) | copy-start | bytes 3076
  1675.6 1519.0 %copy-start.1 = (s32[3,4]{1,0:T(4,128)S(1)}, s32[3,4]{1,0:T(4,128)}, u32[]{:S(2)}) copy-start(s32[3,4]{1,0:T(4,128)} %param.36) | copy-start | bytes 148
  (114 other events, 923.2 us)
Sparse Core Ops, SparseCore 0:
  10.8 31.7 all-gather.16
  44.7 80.3 all-gather.12
  127.0 29.0 all-gather.14
  157.8 30.4 all-gather.18
  409.8 180.9 reduce-scatter.8
  1044.6 78.5 all-gather.26
  1489.4 142.6 reduce-scatter.10
  1636.0 55.0 all-reduce.87
  1695.0 57.6 reduce-scatter.16
  1756.9 56.5 reduce-scatter.12
  1817.4 56.5 reduce-scatter.14
  1882.0 431.7 reduce-scatter.18
  2321.9 430.6 reduce-scatter.20
  2760.6 430.5 reduce-scatter.22
Sparse Core Ops, SparseCore 1:
  413.1 271.1 all-gather.20
  687.0 152.4 all-gather.22
  842.2 152.4 all-gather.24
where the time goes:
time: 3220 us; the launch traced here: 3200 us
  waiting for transfers between devices  2210 us (69%)
  local copies, waits for them, and re-layouts  466 us (14%)
  matrix products  247 us (8%)
  other arithmetic  146 us (5%)
  blocking collectives  101 us (3%)
    reduce_scatter x1, waiting for transfers between devices, body(): lax.psum_scatter(leading(feed_rows, gate_grad), ('dp', 'blk'), scatter_di...  440 us
    reduce_scatter x1, waiting for transfers between devices, body(): lax.psum_scatter(leading(feed_rows, up_grad), ('dp', 'blk'), scatter_dime...  439 us
    reduce_scatter x1, waiting for transfers between devices, body(): lax.psum_scatter(leading(hidden, feed_grad), ('dp', 'blk'), scatter_dimen...  439 us
    reduce_scatter x1, waiting for transfers between devices, body(): lax.psum_scatter(plain(mixed_low, output_own), 'blk', scatter_dimension=0...  179 us
    slice x73, local copies, waits for them, and re-layouts, body(): lax.associative_scan(affine, (next_decay, state_grad), reverse=True)  158 us
    all_gather x1, waiting for transfers between devices, body(): lax.all_gather(down_weight, ('dp', 'blk'), axis=0, tiled=True)  142 us
    all_gather x1, waiting for transfers between devices, body(): lax.all_gather(up_weight, ('dp', 'blk'), axis=1, tiled=True)  141 us
    slice x68, local copies, waits for them, and re-layouts, body(): decay_cum, state_local = lax.associative_scan(affine, (decays, drives))  127 us
  transfers between devices with their start and end apart: 19, of which 15 were waited for; matrix products, arithmetic and copies ran while one was open for 14% of the time, Pallas kernels for 0%

commit v1 on v0

v1 whole, which is shorter than its diff:
```python
from functools import partial

import jax
import jax.numpy as jnp
from jax import lax
from jax.experimental import pallas as pl
from jax.experimental.pallas import tpu as pltpu
from jax.sharding import PartitionSpec as P

BUCKET_DP = 4
EPS = 1e-06
DECAY = 8.0
TAPS = 4
QUARTERS = 4
TILE = 16
AXES = ("dp", "blk")
f32 = jnp.float32
bf16 = jnp.bfloat16
VMEM_BYTES = 40 * 2**20

BRANCH_BIAS, MIXER_BIAS, TAP_ROW, CONV_BIAS, DECAY_BIAS, INPUT_BIAS, PARAM = 0, 1, 2, 6, 7, 8, 9
SLOPE = 10


def plain(former, latter):
    return jnp.dot(former, latter, preferred_element_type=f32)


def trailing(former, latter):
    return lax.dot_general(former, latter, (((1,), (1,)), ((), ())), preferred_element_type=f32)


def leading(former, latter):
    return lax.dot_general(former, latter, (((0,), (0,)), ((), ())), preferred_element_type=f32)


class Places:
    def __init__(self, dp, blk):
        assert blk == QUARTERS and dp % (2 * QUARTERS) == 0
        self.n = dp * blk
        self.high = dp // (2 * QUARTERS)

    @staticmethod
    def split(i):
        return i // 32, i // 8 % 4, i // 4 % 2, i % 4

    @staticmethod
    def join(h, p, c, z):
        return ((h * 4 + p) * 2 + c) * 4 + z

    def send(self, x, route):
        pairs = []
        for i in range(self.n):
            to = route(*self.split(i))
            if to is not None:
                pairs.append((i, self.join(*to)))
        return jax.tree.map(lambda a: lax.ppermute(a, AXES, pairs), x)

    def one(self, x):
        return self.send(x, lambda h, p, c, z: (h, p ^ (1 + c), c, z))

    def two(self, x):
        return self.send(x, lambda h, p, c, z: (h, p ^ (2 - c), c, z))

    def flip_p(self, x, bit):
        return self.send(x, lambda h, p, c, z: (h, p ^ bit, c, z))

    def flip_z(self, x, bit):
        return self.send(x, lambda h, p, c, z: (h, p, c, z ^ bit))

    def core(self, x):
        return self.send(x, lambda h, p, c, z: (h, p, 1 - c, z))

    def along_z(self, x, by=1):
        return self.send(x, lambda h, p, c, z: (h, p, c, (z + by) % 4))

    def along_h(self, x):
        return self.send(x, lambda h, p, c, z: ((h + 1) % self.high, p, c, z))

    def turn(self, x):
        return self.send(x, lambda h, p, c, z: (h, z, c, p))

    def next_rows(self, x):
        def route(*at):
            i = self.join(*at) + 1
            return self.split(i) if i < self.n else None

        return self.send(x, route)

    def back_rows(self, x):
        def route(h, p, c, z):
            i = (c * 4 + z + 7) % 8
            return h, p, i // 4, i % 4

        return self.send(x, route)

    def back_high(self, x):
        return self.send(x, lambda h, p, c, z: (h - 1, p, c, z) if h else None)

    def gather_rows(self, x):
        first = self.one(x)
        second = self.two(x)
        return x, first, second, self.two(first)

    def scatter_rows(self, parts):
        far = self.two(parts[3]().astype(bf16))
        side = self.two(parts[2]().astype(bf16))
        near = self.one((parts[1]() + far.astype(f32)).astype(bf16))
        return parts[0]() + side.astype(f32) + near.astype(f32)

    def gather_high(self, x):
        held = [x]
        for _ in range(self.high - 1):
            held.append(self.along_h(held[-1]))
        return jnp.concatenate(held, axis=0) if len(held) > 1 else x

    def gather_column(self, x):
        x = self.gather_high(x)
        held = [x]
        for _ in range(3):
            held.append(self.along_z(held[-1]))
        return held, [self.core(a) for a in held]

    def scatter_high(self, x):
        if self.high == 1:
            return x
        rows = x.shape[0] // self.high
        piece = [x[k * rows : (k + 1) * rows] for k in range(self.high)]
        total = piece[1]
        for k in range(1, self.high):
            total = self.along_h(total.astype(bf16)).astype(f32) + piece[(k + 1) % self.high]
        return total

    def scatter_column(self, own, other):
        came = self.core(other)
        total = own(1).astype(f32) + came[1].astype(f32)
        for k in (2, 3, 0):
            total = (
                self.along_z(total.astype(bf16)).astype(f32)
                + own(k).astype(f32)
                + came[k].astype(f32)
            )
        return total

    def sum_plane(self, x):
        x = x + self.core(x)
        x = x + self.flip_p(x, 1)
        return x + self.flip_p(x, 2)

    def sum_all(self, x):
        x = self.sum_plane(x)
        x = x + self.flip_z(x, 1)
        x = x + self.flip_z(x, 2)
        total = x
        for _ in range(self.high - 1):
            x = self.along_h(x)
            total = total + x
        return total

    def sum_high(self, x):
        total = x
        for _ in range(self.high - 1):
            x = self.along_h(x)
            total = total + x
        return total


def swapped(offset):
    return (offset & 1) * 2 + offset // 2


def place_rows(info, chunk, first, shape):
    spot = info[chunk, 0] + first + lax.broadcasted_iota(jnp.int32, shape, 0)
    begin = jnp.zeros(shape, jnp.int32)
    for border in (1, 2, 3):
        begin = jnp.where(spot >= info[chunk, border], info[chunk, border], begin)
    return spot - begin, (spot >= 0) & (spot < info[chunk, 4])


def less_one(y):
    series = 1.0 + y * (1.0 / 6.0)
    for k in (5.0, 4.0, 3.0, 2.0):
        series = 1.0 + y * (1.0 / k) * series
    return jnp.where(y > -0.25, -y * series, 1.0 - jnp.exp(y))


def sigmoid(v):
    return 1.0 / (1.0 + jnp.exp(-v))


def scan_rows(a, b, back):
    rows = lax.broadcasted_iota(jnp.int32, a.shape, 0)
    count = a.shape[0]
    step = 1
    while step < count:
        by = count - step if back else step
        keep = rows < count - step if back else rows >= step
        b = jnp.where(keep, a * pltpu.roll(b, by, 0) + b, b)
        a = jnp.where(keep, a * pltpu.roll(a, by, 0), a)
        step *= 2
    return a, b


def forward_kernel(info, chan, rim, vec, dense, low, dec, state, reach, ext, pre):
    chunk = pl.program_id(0)
    rows, width = chan.shape[1:]
    ext[:TILE] = rim[0].astype(f32)
    ext[TILE:] = chan[0].astype(f32)

    def conv(t, _):
        base = pl.multiple_of(t * TILE, TILE)
        near = ext[pl.ds(base, 2 * TILE), :]
        seg, _filled = place_rows(info, chunk, base, (TILE, width))
        total = jnp.broadcast_to(vec[CONV_BIAS : CONV_BIAS + 1, :], (TILE, width))
        for lag in range(TAPS):
            moved = near[TILE - lag : 2 * TILE - lag]
            tap = vec[TAP_ROW + lag : TAP_ROW + lag + 1, :]
            total = total + jnp.where(seg >= lag, tap * moved, 0.0)
        low[0, pl.ds(base, TILE), :] = total.astype(bf16)
        return 0

    lax.fori_loop(0, rows // TILE, conv, 0)
    pre[...] = trailing(low[0], dense[...])

    def tile(t, held):
        base = pl.multiple_of(t * TILE, TILE)
        span = pl.ds(base, TILE)
        seg, filled = place_rows(info, chunk, base, (TILE, width))
        open_decay = sigmoid(pre[span, :width] + vec[DECAY_BIAS : DECAY_BIAS + 1, :])
        open_input = sigmoid(pre[span, width:] + vec[INPUT_BIAS : INPUT_BIAS + 1, :])
        log_decay = open_decay * vec[SLOPE : SLOPE + 1, :]
        decay = jnp.where((seg != 0) & filled, jnp.exp(log_decay), 0.0)
        factor = jnp.where(seg == 0, 1.0, jnp.sqrt(less_one(2.0 * log_decay)))
        drive = jnp.where(filled, factor * open_input * low[0, span, :].astype(f32), 0.0)
        dec[0, span, :] = decay
        entered, passed = held
        for half in range(TILE // 8):
            part = slice(half * 8, half * 8 + 8)
            a, b = scan_rows(decay[part], drive[part], False)
            b = b + a * entered
            a = a * passed
            at = pl.ds(pl.multiple_of(base + half * 8, 8), 8)
            state[0, at, :] = b
            reach[0, at, :] = a
            entered, passed = b[7:8], a[7:8]
        return entered, passed

    lax.fori_loop(
        0, rows // TILE, tile, (jnp.zeros((1, width), f32), jnp.ones((1, width), f32))
    )


def reverse_kernel(dec, grad, moved, reach):
    rows, width = dec.shape[1:]

    def tile(t, held):
        base = pl.multiple_of(rows - TILE - t * TILE, TILE)
        span = pl.ds(base, TILE)
        decay = dec[0, span, :]
        drive = decay * grad[0, span, :].astype(f32)
        entered, passed = held
        for half in reversed(range(TILE // 8)):
            part = slice(half * 8, half * 8 + 8)
            a, b = scan_rows(decay[part], drive[part], True)
            b = b + a * entered
            a = a * passed
            at = pl.ds(pl.multiple_of(base + half * 8, 8), 8)
            moved[0, at, :] = b
            reach[0, at, :] = a
            entered, passed = b[0:1], a[0:1]
        return entered, passed

    lax.fori_loop(
        0, rows // TILE, tile, (jnp.zeros((1, width), f32), jnp.ones((1, width), f32))
    )


def chain_kernel(back, spot, parts, own, total, every):
    p, c, z = spot[0], spot[1], spot[2]
    factor = jnp.ones((1, own.shape[-1]), f32)
    term = jnp.zeros((1, own.shape[-1]), f32)
    count = 8 * QUARTERS
    for i in reversed(range(count)) if back else range(count):
        j, cc, zz = i // 8, i // 4 % 2, i % 4
        every[i, 0:1, :] = factor
        every[i, 1:2, :] = term
        offset = j ^ p
        slot = swapped(offset) if cc else offset
        pair = parts[(z - zz + 4) % 4, c ^ cc, slot]
        term = pair[0:1] * term + pair[1:2]
        factor = pair[0:1] * factor
    total[0:1, :] = factor
    total[1:2, :] = term
    for r in range(QUARTERS):
        j = p ^ jnp.where(c == 0, r, (r & 1) * 2 + r // 2)
        own[r] = every[(j * 2 + c) * 4 + z]


def backward_kernel(
    info, chan, rim, vec, dense, low, state, reach, enter, grad, moved, span_back, leave,
    gates, chan_grad, rim_grad, sums,
    ext, pre, past, later, conv_grad,
):
    chunk = pl.program_id(0)
    rows, width = chan.shape[1:]
    ext[:TILE] = rim[0].astype(f32)
    ext[TILE:] = chan[0].astype(f32)
    pre[...] = trailing(low[0], dense[...])
    past[0:TILE] = jnp.broadcast_to(enter[0], (TILE, width))
    later[rows : rows + TILE] = jnp.broadcast_to(leave[0], (TILE, width))
    conv_grad[:TILE] = jnp.zeros((TILE, width), f32)
    conv_grad[rows + TILE :] = jnp.zeros((TILE, width), f32)

    @pl.when(chunk == 0)
    def _():
        sums[...] = jnp.zeros_like(sums)

    def fill(t, _):
        base = pl.multiple_of(t * TILE, TILE)
        span = pl.ds(base, TILE)
        past[pl.ds(pl.multiple_of(base + TILE, TILE), TILE), :] = (
            state[0, span, :] + reach[0, span, :] * enter[0]
        )
        later[span, :] = moved[0, span, :] + span_back[0, span, :] * leave[0]
        return 0

    lax.fori_loop(0, rows // TILE, fill, 0)

    def add(row, value):
        sums[row : row + 1, :] += jnp.sum(value, axis=0, keepdims=True)

    def tile(t, _):
        base = pl.multiple_of(t * TILE, TILE)
        span = pl.ds(base, TILE)
        seg, filled = place_rows(info, chunk, base, (TILE, width))
        restart = seg == 0
        before = past[pl.ds(base, 2 * TILE), :][TILE - 1 : 2 * TILE - 1]
        adjoint = grad[0, span, :].astype(f32) + later[pl.ds(base, 2 * TILE), :][1 : TILE + 1]
        open_decay = sigmoid(pre[span, :width] + vec[DECAY_BIAS : DECAY_BIAS + 1, :])
        open_input = sigmoid(pre[span, width:] + vec[INPUT_BIAS : INPUT_BIAS + 1, :])
        slope = vec[SLOPE : SLOPE + 1, :]
        log_decay = open_decay * slope
        decay = jnp.exp(log_decay)
        square = less_one(2.0 * log_decay)
        value = low[0, span, :].astype(f32)
        root = lax.rsqrt(square)
        factor = jnp.where(restart, 1.0, square * root)
        factor = jnp.where(square == 0.0, jnp.where(restart, 1.0, 0.0), factor)
        opened = jnp.where(filled, open_input * adjoint, 0.0)
        direct = factor * opened
        input_grad = direct * value * (1.0 - open_input)
        log_grad = jnp.where(restart | ~filled, 0.0, adjoint * before * decay) - jnp.where(
            restart, 0.0, opened * value * decay * decay * root
        )
        decay_grad = log_grad * slope * open_decay * (1.0 - open_decay)
        decay_low = decay_grad.astype(bf16)
        input_low = input_grad.astype(bf16)
        gates[0, span, :width] = decay_low
        gates[0, span, width:] = input_low
        conv_grad[pl.ds(pl.multiple_of(base + TILE, TILE), TILE), :] = direct
        add(0, decay_low.astype(f32))
        add(1, input_low.astype(f32))
        add(2, log_grad * open_decay)
        return 0

    lax.fori_loop(0, rows // TILE, tile, 0)
    conv_grad[TILE : rows + TILE] += plain(gates[0], dense[...])

    def taps(t, _):
        base = pl.multiple_of(t * TILE, TILE)
        near = conv_grad[pl.ds(base, 2 * TILE), :]
        back = jnp.zeros((TILE, width), f32)
        for lag in range(TAPS):
            seg, _filled = place_rows(info, chunk, base - TILE + lag, (TILE, width))
            tap = vec[TAP_ROW + lag : TAP_ROW + lag + 1, :]
            back = back + jnp.where(seg >= lag, tap * near[lag : TILE + lag], 0.0)

        @pl.when(t == 0)
        def _():
            rim_grad[0] = back[TILE - 8 :]

        @pl.when(t > 0)
        def _():
            at = pl.multiple_of(base - TILE, TILE)
            chan_grad[0, pl.ds(at, TILE), :] = back
            around = ext[pl.ds(at, 2 * TILE), :]
            seg, _filled = place_rows(info, chunk, at, (TILE, width))
            own = near[:TILE]
            add(3, own)
            for lag in range(TAPS):
                moved_in = around[TILE - lag : 2 * TILE - lag]
                add(4 + lag, jnp.where(seg >= lag, own * moved_in, 0.0))

        return 0

    lax.fori_loop(0, rows // TILE + 1, taps, 0)


def per_chunk(array):
    shape = array.shape
    return pl.BlockSpec((1, *shape[1:]), lambda i: (i,) + (0,) * (len(shape) - 1))


def whole(array):
    return pl.BlockSpec(array.shape, lambda i: (0,) * len(array.shape))


def in_smem():
    return pl.BlockSpec(memory_space=pltpu.SMEM)


def params():
    return pltpu.CompilerParams(vmem_limit_bytes=VMEM_BYTES)


def run_forward(info, chan, rim, vec, dense):
    count, rows, width = chan.shape
    shape = jax.ShapeDtypeStruct
    outs = [shape(chan.shape, bf16)] + [shape(chan.shape, f32)] * 3
    return pl.pallas_call(
        forward_kernel,
        grid=(count,),
        out_shape=outs,
        in_specs=[in_smem(), per_chunk(chan), per_chunk(rim), whole(vec), whole(dense)],
        out_specs=[per_chunk(o) for o in outs],
        scratch_shapes=[
            pltpu.VMEM((rows + TILE, width), f32),
            pltpu.VMEM((rows, 2 * width), f32),
        ],
        compiler_params=params(),
        cost_estimate=pl.CostEstimate(
            flops=4 * count * rows * width * width,
            bytes_accessed=count * rows * width * 16,
            transcendentals=count * rows * width * 5,
        ),
    )(info, chan, rim, vec, dense)


def run_reverse(dec, grad):
    count, rows, width = dec.shape
    outs = [jax.ShapeDtypeStruct(dec.shape, f32)] * 2
    return pl.pallas_call(
        reverse_kernel,
        grid=(count,),
        out_shape=outs,
        in_specs=[per_chunk(dec), per_chunk(grad)],
        out_specs=[per_chunk(o) for o in outs],
        compiler_params=params(),
        cost_estimate=pl.CostEstimate(
            flops=20 * count * rows * width,
            bytes_accessed=count * rows * width * 14,
            transcendentals=0,
        ),
    )(dec, grad)


def run_chain(spot, parts, back):
    width = parts.shape[-1]
    vmem = pl.BlockSpec(memory_space=pltpu.VMEM)
    return pl.pallas_call(
        partial(chain_kernel, back),
        out_shape=[
            jax.ShapeDtypeStruct((QUARTERS, 2, width), f32),
            jax.ShapeDtypeStruct((2, width), f32),
        ],
        in_specs=[in_smem(), vmem],
        out_specs=[vmem, vmem],
        scratch_shapes=[pltpu.VMEM((8 * QUARTERS, 2, width), f32)],
        compiler_params=params(),
    )(spot, parts)


def run_backward(info, chan, rim, vec, dense, low, state, reach, enter, grad, moved, span, leave):
    count, rows, width = chan.shape
    shape = jax.ShapeDtypeStruct
    outs = [
        shape((count, rows, 2 * width), bf16),
        shape((count, rows, width), f32),
        shape((count, 8, width), f32),
        shape((8, width), f32),
    ]
    cut = [chan, rim, vec, dense, low, state, reach, enter, grad, moved, span, leave]
    specs = [whole(a) if a is vec or a is dense else per_chunk(a) for a in cut]
    return pl.pallas_call(
        backward_kernel,
        grid=(count,),
        out_shape=outs,
        in_specs=[in_smem(), *specs],
        out_specs=[per_chunk(o) for o in outs[:3]] + [whole(outs[3])],
        scratch_shapes=[
            pltpu.VMEM((rows + TILE, width), f32),
            pltpu.VMEM((rows, 2 * width), f32),
            pltpu.VMEM((rows + TILE, width), f32),
            pltpu.VMEM((rows + TILE, width), f32),
            pltpu.VMEM((rows + 2 * TILE, width), f32),
        ],
        compiler_params=params(),
        cost_estimate=pl.CostEstimate(
            flops=8 * count * rows * width * width,
            bytes_accessed=count * rows * width * 32,
            transcendentals=count * rows * width * 6,
        ),
    )(info, *cut)


def laid_kernel(rows, at, *refs):
    count = len(refs) - 2
    pieces, out, sems = refs[:count], refs[count], refs[count + 1]
    each = pieces[0].shape[0] // rows
    copies = []
    for i, piece in enumerate(pieces):
        for k in range(each):
            n = i * each + k
            to = pl.ds(pl.multiple_of(at[n] * rows, rows), rows)
            copies.append(
                pltpu.make_async_copy(piece.at[pl.ds(k * rows, rows)], out.at[to], sems.at[n])
            )
    for copy in copies:
        copy.start()
    for copy in copies:
        copy.wait()


def lay(pieces, at, rows):
    count = at.shape[0]
    width = pieces[0].shape[1]
    anywhere = pl.BlockSpec(memory_space=pl.ANY)
    return pl.pallas_call(
        partial(laid_kernel, rows),
        out_shape=jax.ShapeDtypeStruct((count * rows, width), pieces[0].dtype),
        in_specs=[in_smem(), *[anywhere for _ in pieces]],
        out_specs=anywhere,
        scratch_shapes=[pltpu.SemaphoreType.DMA((count,))],
    )(at, *pieces)


def normed(values):
    rs = lax.rsqrt(jnp.mean(values * values, axis=-1, keepdims=True) + EPS)
    return rs, values * rs


def norm_back(rs, xs, gain, grad):
    scaled = gain * grad
    return rs * (scaled - xs * jnp.mean(xs * scaled, axis=-1, keepdims=True))


def body(
    places,
    tokens,
    cotangent,
    lengths,
    branch_weight,
    mixer_weight,
    branch_bias,
    mixer_bias,
    conv_taps,
    conv_bias,
    decay_weight,
    input_weight,
    decay_bias,
    input_bias,
    decay_param,
    output_weight,
    first_gain,
    second_gain,
    gate_weight,
    up_weight,
    down_weight,
):
    rows, features = tokens.shape
    slab, width = mixer_weight.shape
    block_width = decay_weight.shape[1]
    heads = width // block_width
    high = places.high
    dp_at, z = lax.axis_index("dp"), lax.axis_index("blk")
    h, p, c = dp_at // 8, dp_at // 2 % 4, dp_at % 2
    spot = jnp.stack([p, c, z]).astype(jnp.int32)

    straight = jnp.arange(QUARTERS, dtype=jnp.int32)
    order = p ^ jnp.where(c == 0, straight, (straight & 1) * 2 + straight // 2)
    chunk = ((h * 4 + order) * 2 + c) * 4 + z
    bucket_rows = BUCKET_DP * QUARTERS * rows
    start = chunk * rows
    bucket = (start + bucket_rows // 2) // bucket_rows
    begin = jnp.maximum(0, bucket * bucket_rows - bucket_rows // 2)
    ends = jnp.cumsum(jnp.take(lengths, bucket, axis=0), axis=1)
    info = jnp.concatenate([(start - begin)[:, None], ends], axis=1).astype(jnp.int32)

    inputs = tokens.astype(f32)
    gain_one, gain_two = first_gain.astype(f32), second_gain.astype(f32)
    rs_one, xs_one = normed(inputs)
    low_one = (xs_one * gain_one).astype(bf16)
    rim_rows = places.next_rows(low_one[rows - TILE :])

    def quarter(piece):
        own, other = places.gather_column(places.turn(piece))
        back = jnp.arange(high, dtype=jnp.int32)
        at = []
        for core in (c, 1 - c):
            for k in range(4):
                at.append((((h - back + high) % high) * 4 + (z - k + 4) % 4) * 2 + core)
        return lay([*own, *other], jnp.concatenate(at), slab)

    packed = jnp.concatenate(
        [
            jnp.stack([branch_bias, mixer_bias]),
            conv_taps.T,
            jnp.stack([conv_bias, decay_bias, input_bias, decay_param]),
            jnp.zeros((6, width), bf16),
        ],
        axis=0,
    )
    gate_flat = jnp.concatenate([decay_weight.T, input_weight.T], axis=0)
    mixer_own = quarter(mixer_weight)
    vectors = places.turn(packed).astype(f32)
    low_rows = jnp.stack(places.gather_rows(low_one)).reshape(QUARTERS * rows, features)
    rim_low = jnp.stack(places.gather_rows(rim_rows)).reshape(QUARTERS * TILE, features)
    gate_turned = places.turn(gate_flat)
    branch_own = quarter(branch_weight)
    output_own = quarter(output_weight.T)

    param = vectors[PARAM]
    vec = jnp.concatenate(
        [vectors[:SLOPE], -DECAY * jax.nn.softplus(-param)[None], vectors[SLOPE + 1 :]], axis=0
    )
    block_of = jnp.arange(width, dtype=jnp.int32) // block_width
    same = block_of[:, None] == block_of[None, :]
    dense = jnp.concatenate(
        [
            jnp.where(same, jnp.tile(gate_turned[:block_width], (heads, 1)), 0),
            jnp.where(same, jnp.tile(gate_turned[block_width:], (heads, 1)), 0),
        ],
        axis=0,
    ).astype(bf16)

    gate_col = places.gather_column(gate_weight.T)
    up_col = places.gather_column(up_weight.T)
    down_col = places.gather_column(down_weight)
    gate_use, up_use, down_use = (
        jnp.concatenate([*own, *other], axis=0) for own, other in (gate_col, up_col, down_col)
    )
    feed_grad = jnp.stack(places.gather_rows(cotangent)).reshape(QUARTERS * rows, features)

    channels = (plain(low_rows, mixer_own) + vec[MIXER_BIAS]).astype(bf16)
    rim = (plain(rim_low, mixer_own) + vec[MIXER_BIAS]).astype(bf16)
    channels = channels.reshape(QUARTERS, rows, width)
    rim = rim.reshape(QUARTERS, TILE, width)
    conv_low, decays, state_local, reach = run_forward(info, channels, rim, vec, dense)
    branch_pre = plain(low_rows, branch_own) + vec[BRANCH_BIAS]

    def entering(parts, back):
        pair = jnp.stack([parts, places.core(parts)])
        every = jnp.stack([pair] + [places.along_z(pair, k) for k in (1, 2, 3)])
        own, total = run_chain(spot, every, back)
        if high == 1:
            return own[:, 1:2]
        held = [total]
        for _ in range(high - 1):
            held.append(places.along_h(held[-1]))
        state = jnp.zeros((1, width), f32)
        for hop in range(high - 1):
            source = high - 1 - hop if back else hop
            far = (h - source + high) % high
            picked = lax.dynamic_index_in_dim(jnp.stack(held), far, 0, False)
            ahead = source > h if back else source < h
            state = jnp.where(ahead, picked[0:1] * state + picked[1:2], state)
        return own[:, 1:2] + own[:, 0:1] * state[None]

    enter = entering(jnp.stack([reach[:, -1], state_local[:, -1]], axis=1), False)
    branch_act, gelu_back_one = jax.vjp(jax.nn.gelu, branch_pre)
    state_low = (state_local + reach * enter).astype(bf16).reshape(QUARTERS * rows, width)
    mixed_low = (branch_act * state_low.astype(f32)).astype(bf16)

    def rows_of(array, k):
        return array[k * rows : (k + 1) * rows]

    resid = inputs + places.scatter_rows(
        [lambda k=k: trailing(rows_of(mixed_low, k), output_own) for k in range(QUARTERS)]
    )

    rs_two, xs_two = normed(resid)
    low_two = (xs_two * gain_two).astype(bf16)
    feed_rows = jnp.stack(places.gather_rows(low_two)).reshape(QUARTERS * rows, features)
    gate_pre = trailing(feed_rows, gate_use)
    up_pre = trailing(feed_rows, up_use)
    gate_act, gelu_back_two = jax.vjp(jax.nn.gelu, gate_pre)
    hidden = (gate_act * up_pre).astype(bf16)
    hidden_grad = trailing(feed_grad, down_use)
    gate_grad = gelu_back_two(hidden_grad * up_pre)[0].astype(bf16)
    up_grad = (hidden_grad * gate_act).astype(bf16)
    norm_grad = places.scatter_rows(
        [
            lambda k=k: plain(rows_of(gate_grad, k), gate_use) + plain(rows_of(up_grad, k), up_use)
            for k in range(QUARTERS)
        ]
    )

    def column_sum(term):
        term = term.astype(bf16).reshape(2, 4, -1, features)
        return places.scatter_high(places.scatter_column(lambda k: term[0, k], term[1]))

    down_sum = column_sum(leading(hidden, feed_grad))
    gate_sum = column_sum(leading(gate_grad, feed_rows)).T
    up_sum = column_sum(leading(up_grad, feed_rows)).T
    second_term = jnp.sum(norm_grad * xs_two, axis=0)
    resid_grad = cotangent.astype(f32) + norm_back(rs_two, xs_two, gain_two, norm_grad)

    resid_rows = jnp.stack(places.gather_rows(resid_grad.astype(bf16)))
    resid_rows = resid_rows.reshape(QUARTERS * rows, features)
    mixed_grad = plain(resid_rows, output_own)
    state_grad = (mixed_grad * branch_act).astype(bf16).reshape(QUARTERS, rows, width)
    branch_grad = gelu_back_one(mixed_grad * state_low.astype(f32))[0].astype(bf16)
    moved, span_back = run_reverse(decays, state_grad)
    leave = entering(jnp.stack([span_back[:, 0], moved[:, 0]], axis=1), True)
    gates, chan_grad, rim_grad, sums = run_backward(
        info, channels, rim, vec, dense, conv_low, state_local, reach, enter, state_grad, moved,
        span_back, leave,
    )

    came = places.back_rows(rim_grad)
    last = (c == 1) & (z == 3)
    wanted = order + jnp.where(last, 1, 0)
    from_core = jnp.where(z == 3, 1 - c, c)
    offset = (wanted % 4) ^ p
    slot = jnp.where(from_core == 0, offset, (offset & 1) * 2 + offset // 2)
    pick = (slot[:, None] == straight[None, :]).astype(f32)
    here = jnp.where(wanted < 4, 1.0, 0.0)[:, None]

    def picked(select, array):
        return jnp.sum(select[:, :, None, None] * array[None], axis=1)

    returned = picked(pick * here, came)
    if high > 1:
        returned = returned + picked(pick * (1.0 - here), places.back_high(came))
    chan_grad = chan_grad + jnp.pad(returned, ((0, 0), (rows - 8, 0), (0, 0)))
    mixer_grad = chan_grad.astype(bf16).reshape(QUARTERS * rows, width)

    branch_term = leading(low_rows, branch_grad)
    mixer_term = leading(low_rows, mixer_grad)
    output_term = leading(resid_rows, mixed_low)

    def quarter_sum(term):
        term = term.astype(bf16).reshape(high, 4, 2, slab, width)
        own = lax.dynamic_index_in_dim(term, c, 2, False)
        other = lax.dynamic_index_in_dim(term, 1 - c, 2, False)

        def by(array, k):
            return lax.dynamic_index_in_dim(array, (z - k + 4) % 4, 1, False)

        came_over = places.core(other)
        total = by(own, 1).astype(f32) + by(came_over, 1).astype(f32)
        for k in (2, 3, 0):
            total = (
                places.along_z(total.astype(bf16)).astype(f32)
                + by(own, k).astype(f32)
                + by(came_over, k).astype(f32)
            )
        if high > 1:
            back = (h - jnp.arange(high)) % high
            total = places.scatter_high(
                jnp.take(total, back, axis=0).reshape(high * slab, width)
            )
        return places.turn(total.astype(bf16).reshape(slab, width)).astype(f32)

    output_sum = quarter_sum(output_term).T
    branch_sum = quarter_sum(branch_term)
    mixer_sum = quarter_sum(mixer_term)

    low_grad = places.scatter_rows(
        [
            lambda k=k: trailing(rows_of(branch_grad, k), branch_own)
            + trailing(rows_of(mixer_grad, k), mixer_own)
            for k in range(QUARTERS)
        ]
    )
    token_grad = (resid_grad + norm_back(rs_one, xs_one, gain_one, low_grad)).astype(bf16)

    first_term = (
        jnp.sum(branch_term * branch_own.astype(f32), axis=1)
        + jnp.sum(mixer_term * mixer_own.astype(f32), axis=1)
    ) / gain_one
    gain_sums = places.sum_all(jnp.stack([first_term, second_term]))

    crossed = leading(gates.reshape(QUARTERS * rows, 2 * width), conv_low.reshape(-1, width))
    picked_blocks = block_of[None, :] == jnp.arange(heads)[:, None]
    gate_terms = jnp.sum(
        jnp.where(picked_blocks[None, :, None, :], crossed.reshape(2, heads, block_width, width), 0),
        axis=1,
    ).astype(bf16)
    vector_terms = jnp.concatenate(
        [
            sums,
            jnp.sum(branch_grad.astype(f32), axis=0)[None],
            jnp.sum(mixer_grad.astype(f32), axis=0)[None],
            jnp.zeros((6, width), f32),
        ],
        axis=0,
    )
    slope_back = DECAY * jax.nn.sigmoid(-param)
    vector_terms = vector_terms.at[2].multiply(slope_back)
    gate_total = places.sum_high(
        places.sum_plane(places.turn(gate_terms.reshape(2 * block_width, width)))
    ).astype(f32)
    vector_total = places.sum_high(places.sum_plane(places.turn(vector_terms)))
    return (
        (resid + feed_part(places, hidden, down_use, rows)).astype(bf16),
        token_grad,
        branch_sum,
        mixer_sum,
        vector_total[8],
        vector_total[9],
        vector_total[4:8].T,
        vector_total[3],
        gate_total[:block_width].T,
        gate_total[block_width:].T,
        vector_total[0],
        vector_total[1],
        vector_total[2],
        output_sum,
        gain_sums[0],
        gain_sums[1],
        gate_sum,
        up_sum,
        down_sum,
    )


def feed_part(places, hidden, down_use, rows):
    return places.scatter_rows(
        [
            lambda k=k: plain(hidden[k * rows : (k + 1) * rows], down_use)
            for k in range(QUARTERS)
        ]
    )


def solution(mesh):
    places = Places(mesh.shape["dp"], mesh.shape["blk"])
    return jax.shard_map(
        partial(body, places),
        mesh=mesh,
        in_specs=(
            P(("dp", "blk"), None),
            P(("dp", "blk"), None),
            P(),
            P("dp", "blk"),
            P("dp", "blk"),
            P("blk"),
            P("blk"),
            P("blk", None),
            P("blk"),
            P("blk", None),
            P("blk", None),
            P("blk"),
            P("blk"),
            P("blk"),
            P("blk", "dp"),
            P(),
            P(),
            P(None, ("dp", "blk")),
            P(None, ("dp", "blk")),
            P(("dp", "blk"), None),
        ),
        out_specs=(
            P(("dp", "blk"), None),
            P(("dp", "blk"), None),
            P("dp", "blk"),
            P("dp", "blk"),
            P("blk"),
            P("blk"),
            P("blk", None),
            P("blk"),
            P("blk", None),
            P("blk", None),
            P("blk"),
            P("blk"),
            P("blk"),
            P("blk", "dp"),
            P(),
            P(),
            P(None, ("dp", "blk")),
            P(None, ("dp", "blk")),
            P(("dp", "blk"), None),
        ),
        check_vma=False,
    )
```

time: 3220 us -> 1240 us (0.39)
  waiting for transfers between devices: 2210 us -> 422 us
  local copies, waits for them, and re-layouts: 466 us -> 88.7 us
  Pallas kernels: 0 us -> 290 us
  starting transfers between devices: 6.88 us -> 193 us
  blocking collectives: 101 us -> 0 us
  other arithmetic: 146 us -> 61.1 us
  matrix products: 247 us -> 172 us
    reduce_scatter x8 -> x0, waiting for transfers between devices: 1680 us -> none  [the longest x1 440 us: body(): lax.psum_scatter(leading(feed_rows, gate_grad), ('dp', 'blk'), scatter_di...]
    all_gather x8 -> x0, waiting for transfers between devices: 516 us -> none  [the longest x1 142 us: body(): lax.all_gather(down_weight, ('dp', 'blk'), axis=0, tiled=True)]
    ppermute x2 -> x124, waiting for transfers between devices: 0.01 us -> 422 us  [send(): return jax.tree.map(lambda a: lax.ppermute(a, AXES, pairs), x)]
    pallas_call x0 -> x8, Pallas kernels: none -> 290 us  [the longest x3 244 us: lay(): pl.pallas_call(partial(laid_kernel, rows), out_shape=jax.ShapeDtypeStruct...]
    slice x147 -> x15, local copies, waits for them, and re-layouts: 287 us -> 8.67 us  [the longest x3 6.27 us: column_sum(): term[1]]
    ppermute x2 -> x124, starting transfers between devices: 5.8 us -> 193 us  [send(): return jax.tree.map(lambda a: lax.ppermute(a, AXES, pairs), x)]
    pad x72 -> x0, local copies, waits for them, and re-layouts: 78.9 us -> none  [the longest x36 43.3 us: body(): lax.associative_scan(affine, (next_decay, state_grad), reverse=True)]
    psum x2 -> x0, blocking collectives: 64.5 us -> none  [the longest x1 41.1 us: body(): first_sum, second_sum = lax.psum((first_term, second_term), ('dp', 'blk'))]
  transfers between devices with their start and end apart: 19 -> 124, of which waited for: 15 -> 42; matrix products, arithmetic and copies ran while one was open for 14% -> 19% of each run, Pallas kernels for 0% -> 24%
where the time goes in v1:
time: 1240 us; the launch traced here: 1230 us
  waiting for transfers between devices  422 us (34%)
  Pallas kernels  290 us (23%)
  starting transfers between devices  193 us (16%)
  matrix products  172 us (14%)
  local copies, waits for them, and re-layouts  88.7 us (7%)
  other arithmetic  61.1 us (5%)
    ppermute x124, waiting for transfers between devices, send(): return jax.tree.map(lambda a: lax.ppermute(a, AXES, pairs), x)  422 us
    pallas_call x3, Pallas kernels, lay(): pl.pallas_call(partial(laid_kernel, rows), out_shape=jax.ShapeDtypeStruct...  244 us
    ppermute x124, starting transfers between devices, send(): return jax.tree.map(lambda a: lax.ppermute(a, AXES, pairs), x)  193 us
    dot_general x16, matrix products, plain(): return jnp.dot(former, latter, preferred_element_type=f32)  69.8 us
    unnamed x301, local copies, waits for them, and re-layouts  59 us
    dot_general x15, matrix products, trailing(): lax.dot_general(former, latter, (((1,), (1,)), ((), ())), preferred_eleme...  56.8 us
    dot_general x7, matrix products, leading(): lax.dot_general(former, latter, (((0,), (0,)), ((), ())), preferred_eleme...  44.9 us
    pallas_call x1, Pallas kernels, run_backward(): pl.pallas_call(backward_kernel, grid=(count,), out_shape=outs, in_specs=[...  25.9 us
  transfers between devices with their start and end apart: 124, of which 42 were waited for; matrix products, arithmetic and copies ran while one was open for 19% of the time, Pallas kernels for 24%

profile of v1, /device:TPU:3, one launch (start us, length us, event | category | flops | bytes accessed | tf_op | source)
XLA Modules:
  0.0 1230.5 jit_solution(2514185813808546640)
XLA Ops:
  19.4 5.3 collective-permute-start.24
  33.2 5.5 collective-permute-start.21
  41.4 33.7 %collective-permute-done.11 = bf16[16,640]{1,0:T(8,128)(2,1)S(1)} collective-permute-done((bf16[16,640]{1,0:T(8,128)(2,1)S(1)}, bf16[16,640]{1,0:T(8,128)(2,1)S(1)}, u32[]{:S(2)}, u32[]{:S(2)}) %collective-permute-start.11) | collective-permute-done | bytes 20512 | tf_op jit(solution)/shard_map/ppermute | solution.py:57
  77.2 17.3 %collective-permute-done.22 = bf16[16,2048]{1,0:T(8,128)(2,1)S(1)} collective-permute-done((bf16[16,2048]{1,0:T(8,128)(2,1)}, bf16[16,2048]{1,0:T(8,128)(2,1)S(1)}, u32[]{:S(2)}, u32[]{:S(2)}) %collective-permute-start.22) | collective-permute-done | bytes 65568 | tf_op jit(solution)/shard_map/ppermute | solution.py:57
  94.6 6.6 collective-permute-done.23
  105.6 25.3 %collective-permute-start.7 = (bf16[256,640]{1,0:T(8,128)(2,1)}, bf16[256,640]{1,0:T(8,128)(2,1)S(1)}, u32[]{:S(2)}, u32[]{:S(2)}) collective-permute-start(bf16[256,640]{1,0:T(8,128)(2,1)} %collective-permute-done.3.refs_0_), channel_id=1, source_target_pairs={{0,4},{1,5},{2,6},{3,7},{4,0},{5,1},{6,2},{7,3},{8,12},{9,13},{10,... | collective-permute-start | bytes 983048 | tf_op jit(solution)/shard_map/ppermute | solution.py:57
  132.4 10.2 collective-permute-done.30.refs_1_
  143.8 16.7 %collective-permute-start.17 = (bf16[256,640]{1,0:T(8,128)(2,1)S(1)}, bf16[256,640]{1,0:T(8,128)(2,1)S(1)}, u32[]{:S(2)}, u32[]{:S(2)}) collective-permute-start(bf16[256,640]{1,0:T(8,128)(2,1)S(1)} %collective-permute-done.13.refs_1_), channel_id=1, source_target_pairs={{0,4},{1,5},{2,6},{3,7},{4,0},{5,1},{6,2},{7,3},{8,12},{9,13},{10,... | collective-permute-start | bytes 983048 | tf_op jit(solution)/shard_map/ppermute | solution.py:57
  162.3 21.0 %collective-permute-done.14.refs_2_ = bf16[256,640]{1,0:T(8,128)(2,1)S(1)} collective-permute-done((bf16[256,640]{1,0:T(8,128)(2,1)S(1)}, bf16[256,640]{1,0:T(8,128)(2,1)S(1)}, u32[]{:S(2)}, u32[]{:S(2)}) %collective-permute-start.14) | collective-permute-done | bytes 327712 | tf_op jit(solution)/shard_map/ppermute | solution.py:57
  184.8 16.7 %collective-permute-start.18 = (bf16[256,640]{1,0:T(8,128)(2,1)S(1)}, bf16[256,640]{1,0:T(8,128)(2,1)S(1)}, u32[]{:S(2)}, u32[]{:S(2)}) collective-permute-start(bf16[256,640]{1,0:T(8,128)(2,1)S(1)} %collective-permute-done.14.refs_2_), channel_id=1, source_target_pairs={{0,4},{1,5},{2,6},{3,7},{4,0},{5,1},{6,2},{7,3},{8,12},{9,13},{10,... | collective-permute-start | bytes 983048 | tf_op jit(solution)/shard_map/ppermute | solution.py:57
  202.5 4.8 collective-permute-done.15.refs_3_
  208.3 16.6 %collective-permute-start.19 = (bf16[256,640]{1,0:T(8,128)(2,1)S(1)}, bf16[256,640]{1,0:T(8,128)(2,1)S(1)}, u32[]{:S(2)}, u32[]{:S(2)}) collective-permute-start(bf16[256,640]{1,0:T(8,128)(2,1)S(1)} %collective-permute-done.15.refs_3_), channel_id=1, source_target_pairs={{0,4},{1,5},{2,6},{3,7},{4,0},{5,1},{6,2},{7,3},{8,12},{9,13},{10,... | collective-permute-start | bytes 983048 | tf_op jit(solution)/shard_map/ppermute | solution.py:57
  233.6 81.2 %shard_map.340 = bf16[2048,640]{1,0:T(8,128)(2,1)} custom-call(s32[8]{0:T(128)} %concatenate.34.at, bf16[256,640]{1,0:T(8,128)(2,1)} %collective-permute-done.12.refs_0_, bf16[256,640]{1,0:T(8,128)(2,1)} %copy-done.95, bf16[256,640]{1,0:T(8,128)(2,1)} %copy-done.98, bf16[256,640]{1,0:T(8,128)(2,1)} %copy-done.102, bf16[256,640]{1,0:T(8,128)(2,1)} %copy-done.96, ...), custom_call_target="tpu_custom_call" | custom-call | tf_op jit(solution)/shard_map/pallas_call | solution.py:528
  321.0 7.1 collective-permute-done.31.refs_2_
  328.3 6.7 collective-permute-done.6.refs_3_
  341.2 15.2 %shard_map.341 = (bf16[4,256,640]{2,1,0:T(8,128)(2,1)S(1)}, f32[4,256,640]{2,1,0:T(8,128)S(1)}, f32[4,256,640]{2,1,0:T(8,128)S(1)}, f32[4,256,640]{2,1,0:T(8,128)S(1)}) custom-call(s32[4,5]{1,0:T(4,128)S(1)} %pad_add_fusion.info, bf16[4,256,640]{2,1,0:T(8,128)(2,1)S(1)} %bitcast.384, bf16[4,16,640]{2,1,0:T(8,128)(2,1)S(1)} %bitcast.386, ...), custom_call_target="tpu_custom_call" | custom-call | flops 1677721600 | bytes 10485760 | tf_op jit(solution)/shard_map/pallas_call | solution.py:420
  363.7 81.2 %shard_map.339 = bf16[2048,640]{1,0:T(8,128)(2,1)} custom-call(s32[8]{0:T(128)} %concatenate.34.at, bf16[256,640]{1,0:T(8,128)(2,1)} %collective-permute-done.3.refs_0_, bf16[256,640]{1,0:T(8,128)(2,1)} %collective-permute-done.4.refs_1_, bf16[256,640]{1,0:T(8,128)(2,1)} %collective-permute-done.5.refs_2_, bf16[256,640]{1,0:T(8,128)(2,1)} %copy-done.100, ...), custom_call_target="tpu_custom_call" | custom-call | tf_op jit(solution)/shard_map/pallas_call | solution.py:528
  445.6 81.2 %shard_map.343 = bf16[2048,640]{1,0:T(8,128)(2,1)} custom-call(s32[8]{0:T(128)} %concatenate.34.at, bf16[256,640]{1,0:T(8,128)(2,1)} %copy-done.90, bf16[256,640]{1,0:T(8,128)(2,1)} %copy-done.91, bf16[256,640]{1,0:T(8,128)(2,1)} %collective-permute-done.31.refs_2_, bf16[256,640]{1,0:T(8,128)(2,1)} %collective-permute-done.32.refs_3_, ...), custom_call_target="tpu_custom_call" | custom-call | tf_op jit(solution)/shard_map/pallas_call | solution.py:528
  538.5 5.4 fusion.16
  546.0 9.4 collective-permute-done.52
  564.2 15.1 %collective-permute-done.45 = bf16[192,2048]{1,0:T(8,128)(2,1)S(1)} collective-permute-done((bf16[192,2048]{1,0:T(8,128)(2,1)S(1)}, bf16[192,2048]{1,0:T(8,128)(2,1)S(1)}, u32[]{:S(2)}, u32[]{:S(2)}) %collective-permute-start.45) | collective-permute-done | bytes 786464 | tf_op jit(solution)/shard_map/ppermute | solution.py:57
  586.6 9.6 collective-permute-done.59
  607.2 11.3 collective-permute-done.40
  618.6 10.8 fusion.134
  630.8 6.1 collective-permute-done.42
  637.5 8.7 fusion.133
  646.1 18.4 %fusion.6 = (bf16[1024,1536]{1,0:T(8,128)(2,1)}, bf16[1024,1536]{1,0:T(8,128)(2,1)}, bf16[1024,1536]{1,0:T(8,128)(2,1)}) fusion(f32[1024,1536]{1,0:T(8,128)} %fusion.134, f32[1024,1536]{1,0:T(8,128)} %fusion.133, bf16[1024,2048]{1,0:T(8,128)(2,1)S(1)} %bitcast.406, bf16[1536,2048]{1,0:T(8,128)(2,1)} %constant_dynamic-update-slice_fusion), kind=kOutput, calls=%fused_computation.12 | convolution fusion | flops 6483345408 | bytes 32505856 | tf_op jit(solution)/shard_map/dot_general | solution.py:30
  664.6 10.0 convolution_convert_fusion.1
  681.0 7.2 convolution_convert_fusion
  688.2 6.8 convolution_convert_fusion.4
  700.6 7.6 convolution_convert_fusion.2
  711.3 5.4 fusion.30
  716.8 4.7 fusion.32
  726.6 15.3 %collective-permute-done.71 = bf16[256,2048]{1,0:T(8,128)(2,1)S(1)} collective-permute-done((bf16[256,2048]{1,0:T(8,128)(2,1)S(1)}, bf16[256,2048]{1,0:T(8,128)(2,1)S(1)}, u32[]{:S(2)}, u32[]{:S(2)}) %collective-permute-start.71) | collective-permute-done | bytes 1048608 | tf_op jit(solution)/shard_map/ppermute | solution.py:57
  741.9 4.7 fusion.31
  748.4 4.6 convolution_convert_fusion.5
  758.8 5.6 fusion.29
  766.4 5.5 multiply_reduce_fusion.1
  775.6 11.8 collective-permute-done.64
  791.4 7.1 fusion.37
  798.6 11.5 collective-permute-done.73
  815.2 9.2 collective-permute-done.121
  827.1 13.5 %collective-permute-done.117 = bf16[192,2048]{1,0:T(8,128)(2,1)S(1)} collective-permute-done((bf16[192,2048]{1,0:T(8,128)(2,1)S(1)}, bf16[192,2048]{1,0:T(8,128)(2,1)S(1)}, u32[]{:S(2)}, u32[]{:S(2)}) %collective-permute-start.117) | collective-permute-done | bytes 786464 | tf_op jit(solution)/shard_map/ppermute | solution.py:57
  843.3 14.2 %collective-permute-done.113 = bf16[192,2048]{1,0:T(8,128)(2,1)S(1)} collective-permute-done((bf16[192,2048]{1,0:T(8,128)(2,1)S(1)}, bf16[192,2048]{1,0:T(8,128)(2,1)S(1)}, u32[]{:S(2)}, u32[]{:S(2)}) %collective-permute-start.113) | collective-permute-done | bytes 786464 | tf_op jit(solution)/shard_map/ppermute | solution.py:57
  866.0 5.7 convert_reduce_fusion.1
  874.7 19.1 %collective-permute-start.76 = (f32[4,2,640]{2,1,0:T(2,128)S(1)}, f32[4,2,640]{2,1,0:T(2,128)S(1)}, u32[]{:S(2)}, u32[]{:S(2)}) collective-permute-start(f32[4,2,640]{2,1,0:T(2,128)S(1)} %get-tuple-element.89), channel_id=1, source_target_pairs={{0,4},{1,5},{2,6},{3,7},{4,0},{5,1},{6,2},{7,3},{8,12},{9,13},{10,... | collective-permute-start | bytes 61448 | tf_op jit(solution)/shard_map/ppermute | solution.py:57
  921.5 25.9 %shard_map.346 = (bf16[4,256,1280]{2,1,0:T(8,128)(2,1)S(1)}, f32[4,256,640]{2,1,0:T(8,128)S(1)}, f32[4,8,640]{2,1,0:T(8,128)S(1)}, f32[8,640]{1,0:T(8,128)S(1)}) custom-call(s32[4,5]{1,0:T(4,128)S(1)} %copy-done.27, bf16[4,256,640]{2,1,0:T(8,128)(2,1)S(1)} %bitcast.385, bf16[4,16,640]{2,1,0:T(8,128)(2,1)S(1)} %bitcast.387, f32[16,640]{1,0:T(8,128)S(1)} %copy-done.23, ...), custom_call_target="tpu_custom_call" | custom-call | flops 3355443200 | bytes 20971520 | tf_op jit(solution)/shard_map/pallas_call | solution.py:484
  954.2 4.6 copy.57
  958.8 5.0 select_reduce_fusion
  965.1 7.4 bitcast_convert_fusion
  1012.5 25.8 %collective-permute-done.98 = bf16[320,640]{1,0:T(8,128)(2,1)S(1)} collective-permute-done((bf16[320,640]{1,0:T(8,128)(2,1)S(1)}, bf16[320,640]{1,0:T(8,128)(2,1)S(1)}, u32[]{:S(2)}, u32[]{:S(2)}) %collective-permute-start.98) | collective-permute-done | bytes 409632 | tf_op jit(solution)/shard_map/ppermute | solution.py:57
  1043.3 9.0 collective-permute-done.82
  1053.3 8.6 collective-permute-done.100
  1066.3 13.1 %collective-permute-done.119 = bf16[192,2048]{1,0:T(8,128)(2,1)S(1)} collective-permute-done((bf16[192,2048]{1,0:T(8,128)(2,1)S(1)}, bf16[192,2048]{1,0:T(8,128)(2,1)S(1)}, u32[]{:S(2)}, u32[]{:S(2)}) %collective-permute-start.119) | collective-permute-done | bytes 786464 | tf_op jit(solution)/shard_map/ppermute | solution.py:57
  1082.3 13.9 %collective-permute-done.115 = bf16[192,2048]{1,0:T(8,128)(2,1)S(1)} collective-permute-done((bf16[192,2048]{1,0:T(8,128)(2,1)S(1)}, bf16[192,2048]{1,0:T(8,128)(2,1)S(1)}, u32[]{:S(2)}, u32[]{:S(2)}) %collective-permute-start.115) | collective-permute-done | bytes 786464 | tf_op jit(solution)/shard_map/ppermute | solution.py:57
  1099.3 4.7 collective-permute-done.103
  1104.1 5.5 collective-permute-done.85
  1110.9 5.8 collective-permute-done.90
  1116.9 6.8 collective-permute-done.104
  1123.9 6.8 collective-permute-done.86
  1130.9 6.8 collective-permute-done.91
  1139.4 5.3 collective-permute-done.105
  1166.5 56.0 %collective-permute-done.88 = bf16[256,640]{1,0:T(8,128)(2,1)S(1)} collective-permute-done((bf16[256,640]{1,0:T(8,128)(2,1)S(1)}, bf16[256,640]{1,0:T(8,128)(2,1)S(1)}, u32[]{:S(2)}, u32[]{:S(2)}) %collective-permute-start.88) | collective-permute-done | bytes 327712 | tf_op jit(solution)/shard_map/ppermute | solution.py:57
  1224.2 5.3 collective-permute-done.93
  (662 shorter events, 293.8 us)
Async XLA Ops:
  0.7 93.8 %collective-permute-start.12 = (bf16[256,640]{1,0:T(8,128)(2,1)}, bf16[256,640]{1,0:T(8,128)(2,1)}, u32[]{:S(2)}, u32[]{:S(2)}) collective-permute-start(bf16[256,640]{1,0:T(8,128)(2,1)} %param.26), channel_id=1, source_target_pairs={{0,0},{1,8},{2,16},{3,24},{4,4},{5,12},{6,20},{7,28},{8,1},{9,9},{... | collective-permute-start | bytes 983048 | tf_op jit(solution)/shard_map/ppermute | solution.py:57
  8.9 66.2 %collective-permute-start.11 = (bf16[16,640]{1,0:T(8,128)(2,1)S(1)}, bf16[16,640]{1,0:T(8,128)(2,1)S(1)}, u32[]{:S(2)}, u32[]{:S(2)}) collective-permute-start(bf16[16,640]{1,0:T(8,128)(2,1)S(1)} %concatenate.35), channel_id=1, source_target_pairs={{0,0},{1,8},{2,16},{3,24},{4,4},{5,12},{6,20},{7,28},{8,1},{9,9},{... | collective-permute-start | bytes 61448 | tf_op jit(solution)/shard_map/ppermute | solution.py:57
  19.4 86.1 %collective-permute-start.24 = (bf16[320,640]{1,0:T(8,128)(2,1)}, bf16[320,640]{1,0:T(8,128)(2,1)S(1)}, u32[]{:S(2)}, u32[]{:S(2)}) collective-permute-start(bf16[320,640]{1,0:T(8,128)(2,1)} %pad_maximum_fusion.5), channel_id=1, source_target_pairs={{0,0},{1,8},{2,16},{3,24},{4,4},{5,12},{6,20},{7,28},{8,1},{9,9},{... | collective-permute-start | bytes 1228808 | tf_op jit(solution)/shard_map/ppermute | solution.py:57
  24.8 76.3 %collective-permute-start.3 = (bf16[256,640]{1,0:T(8,128)(2,1)}, bf16[256,640]{1,0:T(8,128)(2,1)}, u32[]{:S(2)}, u32[]{:S(2)}) collective-permute-start(bf16[256,640]{1,0:T(8,128)(2,1)} %param.25), channel_id=1, source_target_pairs={{0,0},{1,8},{2,16},{3,24},{4,4},{5,12},{6,20},{7,28},{8,1},{9,9},{... | collective-permute-start | bytes 983048 | tf_op jit(solution)/shard_map/ppermute | solution.py:57
  33.2 43.9 %collective-permute-start.21 = (bf16[16,2048]{1,0:T(8,128)(2,1)}, bf16[16,2048]{1,0:T(8,128)(2,1)}, u32[]{:S(2)}, u32[]{:S(2)}) collective-permute-start(bf16[16,2048]{1,0:T(8,128)(2,1)} %collective-permute-done.20), channel_id=1, source_target_pairs={{0,8},{1,9},{2,10},{3,11},{4,20},{5,21},{6,22},{7,23},{8,0},{9,1},... | collective-permute-start | bytes 196616 | tf_op jit(solution)/shard_map/ppermute | solution.py:57
  75.1 29.8 %collective-permute-start.29 = (bf16[256,640]{1,0:T(8,128)(2,1)}, bf16[256,640]{1,0:T(8,128)(2,1)S(1)}, u32[]{:S(2)}, u32[]{:S(2)}) collective-permute-start(bf16[256,640]{1,0:T(8,128)(2,1)} %bitcast.435), channel_id=1, source_target_pairs={{0,0},{1,8},{2,16},{3,24},{4,4},{5,12},{6,20},{7,28},{8,1},{9,9},{... | collective-permute-start | bytes 983048 | tf_op jit(solution)/shard_map/ppermute | solution.py:57
  94.5 36.4 %collective-permute-start.13 = (bf16[256,640]{1,0:T(8,128)(2,1)}, bf16[256,640]{1,0:T(8,128)(2,1)S(1)}, u32[]{:S(2)}, u32[]{:S(2)}) collective-permute-start(bf16[256,640]{1,0:T(8,128)(2,1)} %collective-permute-done.12.refs_0_), channel_id=1, source_target_pairs={{0,1},{1,2},{2,3},{3,0},{4,5},{5,6},{6,7},{7,4},{8,9},{9,10},{10,1... | collective-permute-start | bytes 983048 | tf_op jit(solution)/shard_map/ppermute | solution.py:57
  101.1 29.9 %collective-permute-start.16 = (bf16[256,640]{1,0:T(8,128)(2,1)}, bf16[256,640]{1,0:T(8,128)(2,1)S(1)}, u32[]{:S(2)}, u32[]{:S(2)}) collective-permute-start(bf16[256,640]{1,0:T(8,128)(2,1)} %collective-permute-done.12.refs_0_), channel_id=1, source_target_pairs={{0,4},{1,5},{2,6},{3,7},{4,0},{5,1},{6,2},{7,3},{8,12},{9,13},{10,... | collective-permute-start | bytes 983048 | tf_op jit(solution)/shard_map/ppermute | solution.py:57
  101.1 30.6 %collective-permute-start.4 = (bf16[256,640]{1,0:T(8,128)(2,1)}, bf16[256,640]{1,0:T(8,128)(2,1)}, u32[]{:S(2)}, u32[]{:S(2)}) collective-permute-start(bf16[256,640]{1,0:T(8,128)(2,1)} %collective-permute-done.3.refs_0_), channel_id=1, source_target_pairs={{0,1},{1,2},{2,3},{3,0},{4,5},{5,6},{6,7},{7,4},{8,9},{9,10},{10,1... | collective-permute-start | bytes 983048 | tf_op jit(solution)/shard_map/ppermute | solution.py:57
  105.0 38.8 %collective-permute-start.50 = (bf16[192,2048]{1,0:T(8,128)(2,1)S(1)}, bf16[192,2048]{1,0:T(8,128)(2,1)S(1)}, u32[]{:S(2)}, u32[]{:S(2)}) collective-permute-start(bf16[192,2048]{1,0:T(8,128)(2,1)S(1)} %bitcast.431), channel_id=1, source_target_pairs={{0,1},{1,2},{2,3},{3,0},{4,5},{5,6},{6,7},{7,4},{8,9},{9,10},{10,1... | collective-permute-start | bytes 2359304 | tf_op jit(solution)/shard_map/ppermute | solution.py:57
  105.6 26.8 %collective-permute-start.7 = (bf16[256,640]{1,0:T(8,128)(2,1)}, bf16[256,640]{1,0:T(8,128)(2,1)S(1)}, u32[]{:S(2)}, u32[]{:S(2)}) collective-permute-start(bf16[256,640]{1,0:T(8,128)(2,1)} %collective-permute-done.3.refs_0_), channel_id=1, source_target_pairs={{0,4},{1,5},{2,6},{3,7},{4,0},{5,1},{6,2},{7,3},{8,12},{9,13},{10,... | collective-permute-start | bytes 983048 | tf_op jit(solution)/shard_map/ppermute | solution.py:57
  131.1 30.9 %collective-permute-start.43 = (bf16[192,2048]{1,0:T(8,128)(2,1)}, bf16[192,2048]{1,0:T(8,128)(2,1)S(1)}, u32[]{:S(2)}, u32[]{:S(2)}) collective-permute-start(bf16[192,2048]{1,0:T(8,128)(2,1)} %bitcast.433), channel_id=1, source_target_pairs={{0,1},{1,2},{2,3},{3,0},{4,5},{5,6},{6,7},{7,4},{8,9},{9,10},{10,1... | collective-permute-start | bytes 2359304 | tf_op jit(solution)/shard_map/ppermute | solution.py:57
  132.4 70.1 %collective-permute-start = (bf16[256,2048]{1,0:T(8,128)(2,1)S(1)}, bf16[256,2048]{1,0:T(8,128)(2,1)}, u32[]{:S(2)}, u32[]{:S(2)}) collective-permute-start(bf16[256,2048]{1,0:T(8,128)(2,1)S(1)} %copy-done.74), channel_id=1, source_target_pairs={{0,8},{1,9},{2,10},{3,11},{4,20},{5,21},{6,22},{7,23},{8,0},{9,1},... | collective-permute-start | bytes 3145736 | tf_op jit(solution)/shard_map/ppermute | solution.py:57
  142.6 42.1 %collective-permute-start.57 = (bf16[192,2048]{1,0:T(8,128)(2,1)}, bf16[192,2048]{1,0:T(8,128)(2,1)S(1)}, u32[]{:S(2)}, u32[]{:S(2)}) collective-permute-start(bf16[192,2048]{1,0:T(8,128)(2,1)} %param.41), channel_id=1, source_target_pairs={{0,1},{1,2},{2,3},{3,0},{4,5},{5,6},{6,7},{7,4},{8,9},{9,10},{10,1... | collective-permute-start | bytes 2359304 | tf_op jit(solution)/shard_map/ppermute | solution.py:57
  142.6 40.7 %collective-permute-start.14 = (bf16[256,640]{1,0:T(8,128)(2,1)S(1)}, bf16[256,640]{1,0:T(8,128)(2,1)S(1)}, u32[]{:S(2)}, u32[]{:S(2)}) collective-permute-start(bf16[256,640]{1,0:T(8,128)(2,1)S(1)} %collective-permute-done.13.refs_1_), channel_id=1, source_target_pairs={{0,1},{1,2},{2,3},{3,0},{4,5},{5,6},{6,7},{7,4},{8,9},{9,10},{10,1... | collective-permute-start | bytes 983048 | tf_op jit(solution)/shard_map/ppermute | solution.py:57
  143.8 41.0 %collective-permute-start.17 = (bf16[256,640]{1,0:T(8,128)(2,1)S(1)}, bf16[256,640]{1,0:T(8,128)(2,1)S(1)}, u32[]{:S(2)}, u32[]{:S(2)}) collective-permute-start(bf16[256,640]{1,0:T(8,128)(2,1)S(1)} %collective-permute-done.13.refs_1_), channel_id=1, source_target_pairs={{0,4},{1,5},{2,6},{3,7},{4,0},{5,1},{6,2},{7,3},{8,12},{9,13},{10,... | collective-permute-start | bytes 983048 | tf_op jit(solution)/shard_map/ppermute | solution.py:57
  162.0 63.9 %collective-permute-start.51 = (bf16[192,2048]{1,0:T(8,128)(2,1)S(1)}, bf16[192,2048]{1,0:T(8,128)(2,1)}, u32[]{:S(2)}, u32[]{:S(2)}) collective-permute-start(bf16[192,2048]{1,0:T(8,128)(2,1)S(1)} %collective-permute-done.50), channel_id=1, source_target_pairs={{0,1},{1,2},{2,3},{3,0},{4,5},{5,6},{6,7},{7,4},{8,9},{9,10},{10,1... | collective-permute-start | bytes 2359304 | tf_op jit(solution)/shard_map/ppermute | solution.py:57
  184.7 45.0 %collective-permute-start.44 = (bf16[192,2048]{1,0:T(8,128)(2,1)S(1)}, bf16[192,2048]{1,0:T(8,128)(2,1)S(1)}, u32[]{:S(2)}, u32[]{:S(2)}) collective-permute-start(bf16[192,2048]{1,0:T(8,128)(2,1)S(1)} %collective-permute-done.43), channel_id=1, source_target_pairs={{0,1},{1,2},{2,3},{3,0},{4,5},{5,6},{6,7},{7,4},{8,9},{9,10},{10,1... | collective-permute-start | bytes 2359304 | tf_op jit(solution)/shard_map/ppermute | solution.py:57
  202.5 115.8 %collective-permute-start.1 = (bf16[256,2048]{1,0:T(8,128)(2,1)S(1)}, bf16[256,2048]{1,0:T(8,128)(2,1)}, u32[]{:S(2)}, u32[]{:S(2)}) collective-permute-start(bf16[256,2048]{1,0:T(8,128)(2,1)S(1)} %copy-done.74), channel_id=1, source_target_pairs={{0,16},{1,17},{2,18},{3,19},{4,12},{5,13},{6,14},{7,15},{8,24},{9,... | collective-permute-start | bytes 3145736 | tf_op jit(solution)/shard_map/ppermute | solution.py:57
  207.3 111.1 %collective-permute-start.2 = (bf16[256,2048]{1,0:T(8,128)(2,1)}, bf16[256,2048]{1,0:T(8,128)(2,1)}, u32[]{:S(2)}, u32[]{:S(2)}) collective-permute-start(bf16[256,2048]{1,0:T(8,128)(2,1)} %collective-permute-done), channel_id=1, source_target_pairs={{0,16},{1,17},{2,18},{3,19},{4,12},{5,13},{6,14},{7,15},{8,24},{9,... | collective-permute-start | bytes 3145736 | tf_op jit(solution)/shard_map/ppermute | solution.py:57
  225.9 102.4 %collective-permute-start.67 = (bf16[256,2048]{1,0:T(8,128)(2,1)}, bf16[256,2048]{1,0:T(8,128)(2,1)}, u32[]{:S(2)}, u32[]{:S(2)}) collective-permute-start(bf16[256,2048]{1,0:T(8,128)(2,1)} %param.23), channel_id=1, source_target_pairs={{0,8},{1,9},{2,10},{3,11},{4,20},{5,21},{6,22},{7,23},{8,0},{9,1},... | collective-permute-start | bytes 3145736 | tf_op jit(solution)/shard_map/ppermute | solution.py:57
  229.7 87.6 %collective-permute-start.5 = (bf16[256,640]{1,0:T(8,128)(2,1)}, bf16[256,640]{1,0:T(8,128)(2,1)}, u32[]{:S(2)}, u32[]{:S(2)}) collective-permute-start(bf16[256,640]{1,0:T(8,128)(2,1)} %collective-permute-done.4.refs_1_), channel_id=1, source_target_pairs={{0,1},{1,2},{2,3},{3,0},{4,5},{5,6},{6,7},{7,4},{8,9},{9,10},{10,1... | collective-permute-start | bytes 983048 | tf_op jit(solution)/shard_map/ppermute | solution.py:57
  229.8 87.6 %collective-permute-start.8 = (bf16[256,640]{1,0:T(8,128)(2,1)}, bf16[256,640]{1,0:T(8,128)(2,1)}, u32[]{:S(2)}, u32[]{:S(2)}) collective-permute-start(bf16[256,640]{1,0:T(8,128)(2,1)} %collective-permute-done.4.refs_1_), channel_id=1, source_target_pairs={{0,4},{1,5},{2,6},{3,7},{4,0},{5,1},{6,2},{7,3},{8,12},{9,13},{10,... | collective-permute-start | bytes 983048 | tf_op jit(solution)/shard_map/ppermute | solution.py:57
  328.1 199.2 %collective-permute-start.68 = (bf16[256,2048]{1,0:T(8,128)(2,1)}, bf16[256,2048]{1,0:T(8,128)(2,1)}, u32[]{:S(2)}, u32[]{:S(2)}) collective-permute-start(bf16[256,2048]{1,0:T(8,128)(2,1)} %param.23), channel_id=1, source_target_pairs={{0,16},{1,17},{2,18},{3,19},{4,12},{5,13},{6,14},{7,15},{8,24},{9,... | collective-permute-start | bytes 3145736 | tf_op jit(solution)/shard_map/ppermute | solution.py:57
  328.2 33.3 %collective-permute-start.58 = (bf16[192,2048]{1,0:T(8,128)(2,1)S(1)}, bf16[192,2048]{1,0:T(8,128)(2,1)S(1)}, u32[]{:S(2)}, u32[]{:S(2)}) collective-permute-start(bf16[192,2048]{1,0:T(8,128)(2,1)S(1)} %copy-done.79), channel_id=1, source_target_pairs={{0,1},{1,2},{2,3},{3,0},{4,5},{5,6},{6,7},{7,4},{8,9},{9,10},{10,1... | collective-permute-start | bytes 2359304 | tf_op jit(solution)/shard_map/ppermute | solution.py:57
  328.2 32.4 %collective-permute-start.32 = (bf16[256,640]{1,0:T(8,128)(2,1)}, bf16[256,640]{1,0:T(8,128)(2,1)}, u32[]{:S(2)}, u32[]{:S(2)}) collective-permute-start(bf16[256,640]{1,0:T(8,128)(2,1)} %collective-permute-done.31.refs_2_), channel_id=1, source_target_pairs={{0,1},{1,2},{2,3},{3,0},{4,5},{5,6},{6,7},{7,4},{8,9},{9,10},{10,1... | collective-permute-start | bytes 983048 | tf_op jit(solution)/shard_map/ppermute | solution.py:57
  335.1 194.1 %collective-permute-start.69 = (bf16[256,2048]{1,0:T(8,128)(2,1)}, bf16[256,2048]{1,0:T(8,128)(2,1)}, u32[]{:S(2)}, u32[]{:S(2)}) collective-permute-start(bf16[256,2048]{1,0:T(8,128)(2,1)} %collective-permute-done.67), channel_id=1, source_target_pairs={{0,16},{1,17},{2,18},{3,19},{4,12},{5,13},{6,14},{7,15},{8,24},{9,... | collective-permute-start | bytes 3145736 | tf_op jit(solution)/shard_map/ppermute | solution.py:57
  335.1 26.5 %collective-permute-start.10 = (bf16[256,640]{1,0:T(8,128)(2,1)S(1)}, bf16[256,640]{1,0:T(8,128)(2,1)S(1)}, u32[]{:S(2)}, u32[]{:S(2)}) collective-permute-start(bf16[256,640]{1,0:T(8,128)(2,1)S(1)} %collective-permute-done.6.refs_3_), channel_id=1, source_target_pairs={{0,4},{1,5},{2,6},{3,7},{4,0},{5,1},{6,2},{7,3},{8,12},{9,13},{10,... | collective-permute-start | bytes 983048 | tf_op jit(solution)/shard_map/ppermute | solution.py:57
  360.7 84.3 %collective-permute-start.35 = (bf16[256,640]{1,0:T(8,128)(2,1)}, bf16[256,640]{1,0:T(8,128)(2,1)}, u32[]{:S(2)}, u32[]{:S(2)}) collective-permute-start(bf16[256,640]{1,0:T(8,128)(2,1)} %collective-permute-done.31.refs_2_), channel_id=1, source_target_pairs={{0,4},{1,5},{2,6},{3,7},{4,0},{5,1},{6,2},{7,3},{8,12},{9,13},{10,... | collective-permute-start | bytes 983048 | tf_op jit(solution)/shard_map/ppermute | solution.py:57
  361.5 83.8 %collective-permute-start.36 = (bf16[256,640]{1,0:T(8,128)(2,1)}, bf16[256,640]{1,0:T(8,128)(2,1)}, u32[]{:S(2)}, u32[]{:S(2)}) collective-permute-start(bf16[256,640]{1,0:T(8,128)(2,1)} %collective-permute-done.32.refs_3_), channel_id=1, source_target_pairs={{0,4},{1,5},{2,6},{3,7},{4,0},{5,1},{6,2},{7,3},{8,12},{9,13},{10,... | collective-permute-start | bytes 983048 | tf_op jit(solution)/shard_map/ppermute | solution.py:57
  362.5 164.3 %collective-permute-start.25 = (f32[4,2,640]{2,1,0:T(2,128)S(1)}, f32[4,2,640]{2,1,0:T(2,128)S(1)}, u32[]{:S(2)}, u32[]{:S(2)}) collective-permute-start(f32[4,2,640]{2,1,0:T(2,128)S(1)} %get-tuple-element.91), channel_id=1, source_target_pairs={{0,4},{1,5},{2,6},{3,7},{4,0},{5,1},{6,2},{7,3},{8,12},{9,13},{10,... | collective-permute-start | bytes 61448 | tf_op jit(solution)/shard_map/ppermute | solution.py:57
  445.0 113.4 %collective-permute-start.53 = (bf16[192,2048]{1,0:T(8,128)(2,1)S(1)}, bf16[192,2048]{1,0:T(8,128)(2,1)}, u32[]{:S(2)}, u32[]{:S(2)}) collective-permute-start(bf16[192,2048]{1,0:T(8,128)(2,1)S(1)} %bitcast.432), channel_id=1, source_target_pairs={{0,4},{1,5},{2,6},{3,7},{4,0},{5,1},{6,2},{7,3},{8,12},{9,13},{10,... | collective-permute-start | bytes 2359304 | tf_op jit(solution)/shard_map/ppermute | solution.py:57
  445.3 137.6 %collective-permute-start.46 = (bf16[192,2048]{1,0:T(8,128)(2,1)}, bf16[192,2048]{1,0:T(8,128)(2,1)}, u32[]{:S(2)}, u32[]{:S(2)}) collective-permute-start(bf16[192,2048]{1,0:T(8,128)(2,1)} %bitcast.434), channel_id=1, source_target_pairs={{0,4},{1,5},{2,6},{3,7},{4,0},{5,1},{6,2},{7,3},{8,12},{9,13},{10,... | collective-permute-start | bytes 2359304 | tf_op jit(solution)/shard_map/ppermute | solution.py:57
  533.3 27.2 %collective-permute-start.54 = (bf16[192,2048]{1,0:T(8,128)(2,1)S(1)}, bf16[192,2048]{1,0:T(8,128)(2,1)}, u32[]{:S(2)}, u32[]{:S(2)}) collective-permute-start(bf16[192,2048]{1,0:T(8,128)(2,1)S(1)} %copy-done.84), channel_id=1, source_target_pairs={{0,4},{1,5},{2,6},{3,7},{4,0},{5,1},{6,2},{7,3},{8,12},{9,13},{10,... | collective-permute-start | bytes 2359304 | tf_op jit(solution)/shard_map/ppermute | solution.py:57
  560.5 24.7 %collective-permute-start.47 = (bf16[192,2048]{1,0:T(8,128)(2,1)S(1)}, bf16[192,2048]{1,0:T(8,128)(2,1)S(1)}, u32[]{:S(2)}, u32[]{:S(2)}) collective-permute-start(bf16[192,2048]{1,0:T(8,128)(2,1)S(1)} %copy-done.82), channel_id=1, source_target_pairs={{0,4},{1,5},{2,6},{3,7},{4,0},{5,1},{6,2},{7,3},{8,12},{9,13},{10,... | collective-permute-start | bytes 2359304 | tf_op jit(solution)/shard_map/ppermute | solution.py:57
  562.7 33.6 %collective-permute-start.59 = (bf16[192,2048]{1,0:T(8,128)(2,1)S(1)}, bf16[192,2048]{1,0:T(8,128)(2,1)S(1)}, u32[]{:S(2)}, u32[]{:S(2)}) collective-permute-start(bf16[192,2048]{1,0:T(8,128)(2,1)S(1)} %copy-done.88), channel_id=1, source_target_pairs={{0,1},{1,2},{2,3},{3,0},{4,5},{5,6},{6,7},{7,4},{8,9},{9,10},{10,1... | collective-permute-start | bytes 2359304 | tf_op jit(solution)/shard_map/ppermute | solution.py:57
  564.2 33.8 %collective-permute-start.37 = (bf16[256,2048]{1,0:T(8,128)(2,1)S(1)}, bf16[256,2048]{1,0:T(8,128)(2,1)S(1)}, u32[]{:S(2)}, u32[]{:S(2)}) collective-permute-start(bf16[256,2048]{1,0:T(8,128)(2,1)S(1)} %convolution_convert_fusion.7), channel_id=1, source_target_pairs={{0,16},{1,17},{2,18},{3,19},{4,12},{5,13},{6,14},{7,15},{8,24},{9,... | collective-permute-start | bytes 3145736 | tf_op jit(solution)/shard_map/ppermute | solution.py:57
  602.8 26.6 %collective-permute-start.56 = (bf16[192,2048]{1,0:T(8,128)(2,1)}, bf16[192,2048]{1,0:T(8,128)(2,1)S(1)}, u32[]{:S(2)}, u32[]{:S(2)}) collective-permute-start(bf16[192,2048]{1,0:T(8,128)(2,1)} %collective-permute-done.52), channel_id=1, source_target_pairs={{0,4},{1,5},{2,6},{3,7},{4,0},{5,1},{6,2},{7,3},{8,12},{9,13},{10,... | collective-permute-start | bytes 2359304 | tf_op jit(solution)/shard_map/ppermute | solution.py:57
  603.8 25.7 %collective-permute-start.49 = (bf16[192,2048]{1,0:T(8,128)(2,1)S(1)}, bf16[192,2048]{1,0:T(8,128)(2,1)S(1)}, u32[]{:S(2)}, u32[]{:S(2)}) collective-permute-start(bf16[192,2048]{1,0:T(8,128)(2,1)S(1)} %collective-permute-done.45), channel_id=1, source_target_pairs={{0,4},{1,5},{2,6},{3,7},{4,0},{5,1},{6,2},{7,3},{8,12},{9,13},{10,... | collective-permute-start | bytes 2359304 | tf_op jit(solution)/shard_map/ppermute | solution.py:57
  697.2 112.9 %collective-permute-start.120 = (bf16[4,192,2048]{2,1,0:T(8,128)(2,1)}, bf16[4,192,2048]{2,1,0:T(8,128)(2,1)}, u32[]{:S(2)}, u32[]{:S(2)}) collective-permute-start(bf16[4,192,2048]{2,1,0:T(8,128)(2,1)} %bitcast.135), channel_id=1, source_target_pairs={{0,4},{1,5},{2,6},{3,7},{4,0},{5,1},{6,2},{7,3},{8,12},{9,13},{10,... | collective-permute-start | bytes 9437192 | tf_op jit(solution)/shard_map/ppermute | solution.py:57
  699.6 112.2 %collective-permute-start.116 = (bf16[4,192,2048]{2,1,0:T(8,128)(2,1)}, bf16[4,192,2048]{2,1,0:T(8,128)(2,1)}, u32[]{:S(2)}, u32[]{:S(2)}) collective-permute-start(bf16[4,192,2048]{2,1,0:T(8,128)(2,1)} %bitcast.124), channel_id=1, source_target_pairs={{0,4},{1,5},{2,6},{3,7},{4,0},{5,1},{6,2},{7,3},{8,12},{9,13},{10,... | collective-permute-start | bytes 9437192 | tf_op jit(solution)/shard_map/ppermute | solution.py:57
  716.7 47.7 %collective-permute-start.70 = (bf16[256,2048]{1,0:T(8,128)(2,1)S(1)}, bf16[256,2048]{1,0:T(8,128)(2,1)S(1)}, u32[]{:S(2)}, u32[]{:S(2)}) collective-permute-start(bf16[256,2048]{1,0:T(8,128)(2,1)S(1)} %fusion.30), channel_id=1, source_target_pairs={{0,16},{1,17},{2,18},{3,19},{4,12},{5,13},{6,14},{7,15},{8,24},{9,... | collective-permute-start | bytes 3145736 | tf_op jit(solution)/shard_map/ppermute | solution.py:57
  722.9 32.2 %collective-permute-start.65 = (bf16[256,2048]{1,0:T(8,128)(2,1)S(1)}, bf16[256,2048]{1,0:T(8,128)(2,1)S(1)}, u32[]{:S(2)}, u32[]{:S(2)}) collective-permute-start(bf16[256,2048]{1,0:T(8,128)(2,1)S(1)} %convolution_convert_fusion.4), channel_id=1, source_target_pairs={{0,16},{1,17},{2,18},{3,19},{4,12},{5,13},{6,14},{7,15},{8,24},{9,... | collective-permute-start | bytes 3145736 | tf_op jit(solution)/shard_map/ppermute | solution.py:57
  755.1 58.4 %collective-permute-start.112 = (bf16[4,192,2048]{2,1,0:T(8,128)(2,1)}, bf16[4,192,2048]{2,1,0:T(8,128)(2,1)}, u32[]{:S(2)}, u32[]{:S(2)}) collective-permute-start(bf16[4,192,2048]{2,1,0:T(8,128)(2,1)} %bitcast.113), channel_id=1, source_target_pairs={{0,4},{1,5},{2,6},{3,7},{4,0},{5,1},{6,2},{7,3},{8,12},{9,13},{10,... | collective-permute-start | bytes 9437192 | tf_op jit(solution)/shard_map/ppermute | solution.py:57
  765.0 26.4 %collective-permute-start.66 = (bf16[256,2048]{1,0:T(8,128)(2,1)}, bf16[256,2048]{1,0:T(8,128)(2,1)}, u32[]{:S(2)}, u32[]{:S(2)}) collective-permute-start(bf16[256,2048]{1,0:T(8,128)(2,1)} %fusion.29), channel_id=1, source_target_pairs={{0,8},{1,9},{2,10},{3,11},{4,20},{5,21},{6,22},{7,23},{8,0},{9,1},... | collective-permute-start | bytes 3145736 | tf_op jit(solution)/shard_map/ppermute | solution.py:57
  791.4 68.7 %collective-permute-start.74 = (bf16[256,2048]{1,0:T(8,128)(2,1)}, bf16[256,2048]{1,0:T(8,128)(2,1)S(1)}, u32[]{:S(2)}, u32[]{:S(2)}) collective-permute-start(bf16[256,2048]{1,0:T(8,128)(2,1)} %fusion.129), channel_id=1, source_target_pairs={{0,16},{1,17},{2,18},{3,19},{4,12},{5,13},{6,14},{7,15},{8,24},{9,... | collective-permute-start | bytes 3145736 | tf_op jit(solution)/shard_map/ppermute | solution.py:57
  810.0 50.1 %collective-permute-start.75 = (bf16[256,2048]{1,0:T(8,128)(2,1)}, bf16[256,2048]{1,0:T(8,128)(2,1)S(1)}, u32[]{:S(2)}, u32[]{:S(2)}) collective-permute-start(bf16[256,2048]{1,0:T(8,128)(2,1)} %collective-permute-done.73), channel_id=1, source_target_pairs={{0,16},{1,17},{2,18},{3,19},{4,12},{5,13},{6,14},{7,15},{8,24},{9,... | collective-permute-start | bytes 3145736 | tf_op jit(solution)/shard_map/ppermute | solution.py:57
  813.4 27.2 %collective-permute-start.117 = (bf16[192,2048]{1,0:T(8,128)(2,1)S(1)}, bf16[192,2048]{1,0:T(8,128)(2,1)S(1)}, u32[]{:S(2)}, u32[]{:S(2)}) collective-permute-start(bf16[192,2048]{1,0:T(8,128)(2,1)S(1)} %fusion.51), channel_id=1, source_target_pairs={{0,1},{1,2},{2,3},{3,0},{4,5},{5,6},{6,7},{7,4},{8,9},{9,10},{10,1... | collective-permute-start | bytes 2359304 | tf_op jit(solution)/shard_map/ppermute | solution.py:57
  815.1 42.4 %collective-permute-start.113 = (bf16[192,2048]{1,0:T(8,128)(2,1)S(1)}, bf16[192,2048]{1,0:T(8,128)(2,1)S(1)}, u32[]{:S(2)}, u32[]{:S(2)}) collective-permute-start(bf16[192,2048]{1,0:T(8,128)(2,1)S(1)} %fusion.55), channel_id=1, source_target_pairs={{0,1},{1,2},{2,3},{3,0},{4,5},{5,6},{6,7},{7,4},{8,9},{9,10},{10,1... | collective-permute-start | bytes 2359304 | tf_op jit(solution)/shard_map/ppermute | solution.py:57
  827.1 180.1 %collective-permute-start.122 = (bf16[192,2048]{1,0:T(8,128)(2,1)}, bf16[192,2048]{1,0:T(8,128)(2,1)}, u32[]{:S(2)}, u32[]{:S(2)}) collective-permute-start(bf16[192,2048]{1,0:T(8,128)(2,1)} %fusion.46), channel_id=1, source_target_pairs={{0,1},{1,2},{2,3},{3,0},{4,5},{5,6},{6,7},{7,4},{8,9},{9,10},{10,1... | collective-permute-start | bytes 2359304 | tf_op jit(solution)/shard_map/ppermute | solution.py:57
  843.3 195.0 %collective-permute-start.118 = (bf16[192,2048]{1,0:T(8,128)(2,1)}, bf16[192,2048]{1,0:T(8,128)(2,1)}, u32[]{:S(2)}, u32[]{:S(2)}) collective-permute-start(bf16[192,2048]{1,0:T(8,128)(2,1)} %fusion.50), channel_id=1, source_target_pairs={{0,1},{1,2},{2,3},{3,0},{4,5},{5,6},{6,7},{7,4},{8,9},{9,10},{10,1... | collective-permute-start | bytes 2359304 | tf_op jit(solution)/shard_map/ppermute | solution.py:57
  874.7 25.7 %collective-permute-start.76 = (f32[4,2,640]{2,1,0:T(2,128)S(1)}, f32[4,2,640]{2,1,0:T(2,128)S(1)}, u32[]{:S(2)}, u32[]{:S(2)}) collective-permute-start(f32[4,2,640]{2,1,0:T(2,128)S(1)} %get-tuple-element.89), channel_id=1, source_target_pairs={{0,4},{1,5},{2,6},{3,7},{4,0},{5,1},{6,2},{7,3},{8,12},{9,13},{10,... | collective-permute-start | bytes 61448 | tf_op jit(solution)/shard_map/ppermute | solution.py:57
  913.6 127.2 %collective-permute-start.114 = (bf16[192,2048]{1,0:T(8,128)(2,1)}, bf16[192,2048]{1,0:T(8,128)(2,1)}, u32[]{:S(2)}, u32[]{:S(2)}) collective-permute-start(bf16[192,2048]{1,0:T(8,128)(2,1)} %fusion.54), channel_id=1, source_target_pairs={{0,1},{1,2},{2,3},{3,0},{4,5},{5,6},{6,7},{7,4},{8,9},{9,10},{10,1... | collective-permute-start | bytes 2359304 | tf_op jit(solution)/shard_map/ppermute | solution.py:57
  996.7 65.8 %collective-permute-start.102 = (bf16[1,4,256,640]{2,3,1,0:T(8,128)(2,1)S(1)}, bf16[1,4,256,640]{2,3,1,0:T(8,128)(2,1)S(1)}, u32[]{:S(2)}, u32[]{:S(2)}) collective-permute-start(bf16[1,4,256,640]{2,3,1,0:T(8,128)(2,1)S(1)} %bitcast.424), channel_id=1, source_target_pairs={{0,4},{1,5},{2,6},{3,7},{4,0},{5,1},{6,2},{7,3},{8,12},{9,13},{10,... | collective-permute-start | bytes 3932168 | tf_op jit(solution)/shard_map/ppermute | solution.py:57
  1003.0 59.3 %collective-permute-start.84 = (bf16[1,4,256,640]{3,2,1,0:T(8,128)(2,1)S(1)}, bf16[1,4,256,640]{3,2,1,0:T(8,128)(2,1)S(1)}, u32[]{:S(2)}, u32[]{:S(2)}) collective-permute-start(bf16[1,4,256,640]{3,2,1,0:T(8,128)(2,1)S(1)} %copy-done.67), channel_id=1, source_target_pairs={{0,4},{1,5},{2,6},{3,7},{4,0},{5,1},{6,2},{7,3},{8,12},{9,13},{10,... | collective-permute-start | bytes 3932168 | tf_op jit(solution)/shard_map/ppermute | solution.py:57
  1007.2 31.1 %collective-permute-start.98 = (bf16[320,640]{1,0:T(8,128)(2,1)S(1)}, bf16[320,640]{1,0:T(8,128)(2,1)S(1)}, u32[]{:S(2)}, u32[]{:S(2)}) collective-permute-start(bf16[320,640]{1,0:T(8,128)(2,1)S(1)} %bitcast.458), channel_id=1, source_target_pairs={{0,0},{1,8},{2,16},{3,24},{4,4},{5,12},{6,20},{7,28},{8,1},{9,9},{... | collective-permute-start | bytes 1228808 | tf_op jit(solution)/shard_map/ppermute | solution.py:57
  1043.0 56.2 %collective-permute-start.89 = (bf16[1,4,256,640]{3,2,1,0:T(8,128)(2,1)S(1)}, bf16[1,4,256,640]{3,2,1,0:T(8,128)(2,1)S(1)}, u32[]{:S(2)}, u32[]{:S(2)}) collective-permute-start(bf16[1,4,256,640]{3,2,1,0:T(8,128)(2,1)S(1)} %dynamic-slice_bitcast_fusion), channel_id=1, source_target_pairs={{0,4},{1,5},{2,6},{3,7},{4,0},{5,1},{6,2},{7,3},{8,12},{9,13},{10,... | collective-permute-start | bytes 3932168 | tf_op jit(solution)/shard_map/ppermute | solution.py:57
  1061.9 76.0 %collective-permute-start.81 = (bf16[256,2048]{1,0:T(8,128)(2,1)S(1)}, bf16[256,2048]{1,0:T(8,128)(2,1)S(1)}, u32[]{:S(2)}, u32[]{:S(2)}) collective-permute-start(bf16[256,2048]{1,0:T(8,128)(2,1)S(1)} %copy-done.75), channel_id=1, source_target_pairs={{0,16},{1,17},{2,18},{3,19},{4,12},{5,13},{6,14},{7,15},{8,24},{9,... | collective-permute-start | bytes 3145736 | tf_op jit(solution)/shard_map/ppermute | solution.py:57
  1062.5 33.8 %collective-permute-start.115 = (bf16[192,2048]{1,0:T(8,128)(2,1)S(1)}, bf16[192,2048]{1,0:T(8,128)(2,1)S(1)}, u32[]{:S(2)}, u32[]{:S(2)}) collective-permute-start(bf16[192,2048]{1,0:T(8,128)(2,1)S(1)} %fusion.53), channel_id=1, source_target_pairs={{0,1},{1,2},{2,3},{3,0},{4,5},{5,6},{6,7},{7,4},{8,9},{9,10},{10,1... | collective-permute-start | bytes 2359304 | tf_op jit(solution)/shard_map/ppermute | solution.py:57
  1062.7 75.3 %collective-permute-start.83 = (bf16[256,2048]{1,0:T(8,128)(2,1)S(1)}, bf16[256,2048]{1,0:T(8,128)(2,1)S(1)}, u32[]{:S(2)}, u32[]{:S(2)}) collective-permute-start(bf16[256,2048]{1,0:T(8,128)(2,1)S(1)} %fusion.33), channel_id=1, source_target_pairs={{0,8},{1,9},{2,10},{3,11},{4,20},{5,21},{6,22},{7,23},{8,0},{9,1},... | collective-permute-start | bytes 3145736 | tf_op jit(solution)/shard_map/ppermute | solution.py:57
  1079.4 30.4 %collective-permute-start.101 = (bf16[320,640]{1,0:T(8,128)(2,1)S(1)}, bf16[320,640]{1,0:T(8,128)(2,1)S(1)}, u32[]{:S(2)}, u32[]{:S(2)}) collective-permute-start(bf16[320,640]{1,0:T(8,128)(2,1)S(1)} %add.1080), channel_id=1, source_target_pairs={{0,16},{1,17},{2,18},{3,19},{4,20},{5,21},{6,22},{7,23},{8,24},{9,... | collective-permute-start | bytes 1228808 | tf_op jit(solution)/shard_map/ppermute | solution.py:57
  1144.9 78.5 %collective-permute-start.106 = (bf16[256,640]{0,1:T(8,128)(2,1)S(1)}, bf16[256,640]{0,1:T(8,128)(2,1)S(1)}, u32[]{:S(2)}, u32[]{:S(2)}) collective-permute-start(bf16[256,640]{0,1:T(8,128)(2,1)S(1)} %fusion.87), channel_id=1, source_target_pairs={{0,0},{1,8},{2,16},{3,24},{4,4},{5,12},{6,20},{7,28},{8,1},{9,9},{... | collective-permute-start | bytes 983048 | tf_op jit(solution)/shard_map/ppermute | solution.py:57
  1151.9 70.5 %collective-permute-start.88 = (bf16[256,640]{1,0:T(8,128)(2,1)S(1)}, bf16[256,640]{1,0:T(8,128)(2,1)S(1)}, u32[]{:S(2)}, u32[]{:S(2)}) collective-permute-start(bf16[256,640]{1,0:T(8,128)(2,1)S(1)} %fusion.85), channel_id=1, source_target_pairs={{0,0},{1,8},{2,16},{3,24},{4,4},{5,12},{6,20},{7,28},{8,1},{9,9},{... | collective-permute-start | bytes 983048 | tf_op jit(solution)/shard_map/ppermute | solution.py:57
  1159.0 70.5 %collective-permute-start.93 = (bf16[256,640]{1,0:T(8,128)(2,1)S(1)}, bf16[256,640]{1,0:T(8,128)(2,1)S(1)}, u32[]{:S(2)}, u32[]{:S(2)}) collective-permute-start(bf16[256,640]{1,0:T(8,128)(2,1)S(1)} %fusion.86), channel_id=1, source_target_pairs={{0,0},{1,8},{2,16},{3,24},{4,4},{5,12},{6,20},{7,28},{8,1},{9,9},{... | collective-permute-start | bytes 983048 | tf_op jit(solution)/shard_map/ppermute | solution.py:57
  (197 other events, 4799.9 us)

commit v2 on v1

--- a/solution.py
+++ b/solution.py
@@ -63,7 +63,7 @@
         return self.send(x, lambda h, p, c, z: (h, p ^ (2 - c), c, z))
 
     def flip_p(self, x, bit):
-        return self.send(x, lambda h, p, c, z: (h, p ^ bit, c, z))
+        return x if bit == 0 else self.send(x, lambda h, p, c, z: (h, p ^ bit, c, z))
 
     def flip_z(self, x, bit):
         return self.send(x, lambda h, p, c, z: (h, p, c, z ^ bit))
@@ -76,9 +76,6 @@
 
     def along_h(self, x):
         return self.send(x, lambda h, p, c, z: ((h + 1) % self.high, p, c, z))
-
-    def turn(self, x):
-        return self.send(x, lambda h, p, c, z: (h, z, c, p))
 
     def next_rows(self, x):
         def route(*at):
@@ -102,24 +99,40 @@
         second = self.two(x)
         return x, first, second, self.two(first)
 
+    def gather_rows_direct(self, x):
+        return x, self.one(x), self.two(x), self.flip_p(x, 3)
+
     def scatter_rows(self, parts):
-        far = self.two(parts[3]().astype(bf16))
-        side = self.two(parts[2]().astype(bf16))
-        near = self.one((parts[1]() + far.astype(f32)).astype(bf16))
-        return parts[0]() + side.astype(f32) + near.astype(f32)
-
-    def gather_high(self, x):
-        held = [x]
-        for _ in range(self.high - 1):
-            held.append(self.along_h(held[-1]))
-        return jnp.concatenate(held, axis=0) if len(held) > 1 else x
-
-    def gather_column(self, x):
-        x = self.gather_high(x)
-        held = [x]
-        for _ in range(3):
-            held.append(self.along_z(held[-1]))
-        return held, [self.core(a) for a in held]
+        far = self.two(parts[3].astype(bf16))
+        side = self.two(parts[2].astype(bf16))
+        joined = (parts[1] + far.astype(f32)).astype(bf16)
+        return parts[0] + side.astype(f32) + self.one(joined).astype(f32), joined
+
+    def spread(self, x, p):
+        groups = [
+            [self.join(h, q, c, z) for h in range(self.high) for z in range(4)]
+            for q in range(QUARTERS)
+            for c in range(2)
+        ]
+        every = lax.all_gather(x, AXES, axis_index_groups=groups, axis=0, tiled=True)
+        slab, width = x.shape
+
+        def pick(m):
+            if self.high == 1:
+                return lax.dynamic_slice_in_dim(every, (p ^ m) * slab, slab, 0)[None]
+            return lax.dynamic_index_in_dim(
+                every.reshape(self.high, 4, slab, width), p ^ m, 1, False
+            )
+
+        own = [self.flip_p(pick(m), m) for m in range(4)]
+        return every, [own, [self.core(a) for a in own]]
+
+    def gather_rest(self, x, axis=0):
+        groups = [
+            [self.join(h, p, c, z) for c in range(2) for z in range(4) for h in range(self.high)]
+            for p in range(QUARTERS)
+        ]
+        return lax.all_gather(x, AXES, axis_index_groups=groups, axis=axis, tiled=True)
 
     def scatter_high(self, x):
         if self.high == 1:
@@ -131,24 +144,10 @@
             total = self.along_h(total.astype(bf16)).astype(f32) + piece[(k + 1) % self.high]
         return total
 
-    def scatter_column(self, own, other):
-        came = self.core(other)
-        total = own(1).astype(f32) + came[1].astype(f32)
-        for k in (2, 3, 0):
-            total = (
-                self.along_z(total.astype(bf16)).astype(f32)
-                + own(k).astype(f32)
-                + came[k].astype(f32)
-            )
-        return total
-
-    def sum_plane(self, x):
+    def sum_all(self, x):
         x = x + self.core(x)
         x = x + self.flip_p(x, 1)
-        return x + self.flip_p(x, 2)
-
-    def sum_all(self, x):
-        x = self.sum_plane(x)
+        x = x + self.flip_p(x, 2)
         x = x + self.flip_z(x, 1)
         x = x + self.flip_z(x, 2)
         total = x
@@ -157,12 +156,9 @@
             total = total + x
         return total
 
-    def sum_high(self, x):
-        total = x
-        for _ in range(self.high - 1):
-            x = self.along_h(x)
-            total = total + x
-        return total
+
+def after(x, *others):
+    return lax.optimization_barrier((x, *others))[0]
 
 
 def swapped(offset):
@@ -430,7 +426,7 @@
         compiler_params=params(),
         cost_estimate=pl.CostEstimate(
             flops=4 * count * rows * width * width,
-            bytes_accessed=count * rows * width * 16,
+            bytes_accessed=count * rows * width * 84,
             transcendentals=count * rows * width * 5,
         ),
     )(info, chan, rim, vec, dense)
@@ -497,40 +493,45 @@
         compiler_params=params(),
         cost_estimate=pl.CostEstimate(
             flops=8 * count * rows * width * width,
-            bytes_accessed=count * rows * width * 32,
+            bytes_accessed=count * rows * width * 144,
             transcendentals=count * rows * width * 6,
         ),
     )(info, *cut)
 
 
-def laid_kernel(rows, at, *refs):
-    count = len(refs) - 2
-    pieces, out, sems = refs[:count], refs[count], refs[count + 1]
-    each = pieces[0].shape[0] // rows
-    copies = []
+def laid_kernel(cuts, at, *refs):
+    pieces, outs = refs[: -len(cuts)], refs[-len(cuts) :]
+    each = pieces[0].shape[0]
     for i, piece in enumerate(pieces):
         for k in range(each):
-            n = i * each + k
-            to = pl.ds(pl.multiple_of(at[n] * rows, rows), rows)
-            copies.append(
-                pltpu.make_async_copy(piece.at[pl.ds(k * rows, rows)], out.at[to], sems.at[n])
-            )
-    for copy in copies:
-        copy.start()
-    for copy in copies:
-        copy.wait()
-
-
-def lay(pieces, at, rows):
+            first = 0
+            for rows, out in zip(cuts, outs):
+                to = pl.multiple_of(at[i * each + k] * rows, TILE)
+
+                def move(t, _, piece=piece, k=k, to=to, first=first, out=out):
+                    step = pl.multiple_of(t * TILE, TILE)
+                    out[pl.ds(pl.multiple_of(to + step, TILE), TILE), :] = piece[
+                        k, pl.ds(pl.multiple_of(first + step, TILE), TILE), :
+                    ]
+                    return 0
+
+                lax.fori_loop(0, rows // TILE, move, 0)
+                first += rows
+
+
+def lay(pieces, at, cuts):
     count = at.shape[0]
-    width = pieces[0].shape[1]
-    anywhere = pl.BlockSpec(memory_space=pl.ANY)
+    width = pieces[0].shape[-1]
+    vmem = pl.BlockSpec(memory_space=pltpu.VMEM)
     return pl.pallas_call(
-        partial(laid_kernel, rows),
-        out_shape=jax.ShapeDtypeStruct((count * rows, width), pieces[0].dtype),
-        in_specs=[in_smem(), *[anywhere for _ in pieces]],
-        out_specs=anywhere,
-        scratch_shapes=[pltpu.SemaphoreType.DMA((count,))],
+        partial(laid_kernel, cuts),
+        out_shape=[jax.ShapeDtypeStruct((count * rows, width), pieces[0].dtype) for rows in cuts],
+        in_specs=[in_smem(), *[vmem for _ in pieces]],
+        out_specs=[vmem for _ in cuts],
+        compiler_params=params(),
+        cost_estimate=pl.CostEstimate(
+            flops=0, bytes_accessed=4 * count * sum(cuts) * width, transcendentals=0
+        ),
     )(at, *pieces)
 
 
@@ -592,33 +593,40 @@
     low_one = (xs_one * gain_one).astype(bf16)
     rim_rows = places.next_rows(low_one[rows - TILE :])
 
-    def quarter(piece):
-        own, other = places.gather_column(places.turn(piece))
-        back = jnp.arange(high, dtype=jnp.int32)
-        at = []
-        for core in (c, 1 - c):
-            for k in range(4):
-                at.append((((h - back + high) % high) * 4 + (z - k + 4) % 4) * 2 + core)
-        return lay([*own, *other], jnp.concatenate(at), slab)
-
-    packed = jnp.concatenate(
+    def quarter(x, cuts):
+        every, pieces = places.spread(x, p)
+        at = [
+            (jnp.arange(high) * 4 + (p ^ m)) * 2 + core for core in (c, 1 - c) for m in range(4)
+        ]
+        return every, lay([*pieces[0], *pieces[1]], jnp.concatenate(at).astype(jnp.int32), cuts)
+
+    small = jnp.concatenate(
         [
             jnp.stack([branch_bias, mixer_bias]),
             conv_taps.T,
             jnp.stack([conv_bias, decay_bias, input_bias, decay_param]),
-            jnp.zeros((6, width), bf16),
+            jnp.zeros((TILE - PARAM - 1, width), bf16),
+            decay_weight.T,
+            input_weight.T,
         ],
         axis=0,
     )
-    gate_flat = jnp.concatenate([decay_weight.T, input_weight.T], axis=0)
-    mixer_own = quarter(mixer_weight)
-    vectors = places.turn(packed).astype(f32)
-    low_rows = jnp.stack(places.gather_rows(low_one)).reshape(QUARTERS * rows, features)
-    rim_low = jnp.stack(places.gather_rows(rim_rows)).reshape(QUARTERS * TILE, features)
-    gate_turned = places.turn(gate_flat)
-    branch_own = quarter(branch_weight)
-    output_own = quarter(output_weight.T)
-
+    total_dp = 8 * high
+    share = -(-small.shape[0] // (total_dp * TILE)) * TILE
+    small = jnp.pad(small, ((0, share * total_dp - small.shape[0]), (0, 0)))
+    small = lax.dynamic_slice_in_dim(small, dp_at * share, share, 0)
+    early, (mixer_own, small) = quarter(
+        jnp.concatenate([mixer_weight, small], axis=0), (slab, share)
+    )
+    vectors = small[:TILE].astype(f32)
+    gate_turned = small[TILE : TILE + 2 * block_width]
+    held = places.gather_rows(jnp.concatenate([rim_rows, low_one], axis=0))
+    low_rows = jnp.concatenate([a[TILE:] for a in held], axis=0)
+    rim_low = jnp.concatenate([a[:TILE] for a in held], axis=0)
+    middle, (branch_own, output_own) = quarter(
+        after(jnp.concatenate([branch_weight, output_weight.T], axis=0), early, held[3]),
+        (slab, slab),
+    )
     param = vectors[PARAM]
     vec = jnp.concatenate(
         [vectors[:SLOPE], -DECAY * jax.nn.softplus(-param)[None], vectors[SLOPE + 1 :]], axis=0
@@ -633,25 +641,21 @@
         axis=0,
     ).astype(bf16)
 
-    gate_col = places.gather_column(gate_weight.T)
-    up_col = places.gather_column(up_weight.T)
-    down_col = places.gather_column(down_weight)
-    gate_use, up_use, down_use = (
-        jnp.concatenate([*own, *other], axis=0) for own, other in (gate_col, up_col, down_col)
-    )
-    feed_grad = jnp.stack(places.gather_rows(cotangent)).reshape(QUARTERS * rows, features)
-
     channels = (plain(low_rows, mixer_own) + vec[MIXER_BIAS]).astype(bf16)
     rim = (plain(rim_low, mixer_own) + vec[MIXER_BIAS]).astype(bf16)
+    feed_held = places.gather_rows_direct(after(cotangent, mixer_own))
+    feed_grad = jnp.concatenate(feed_held, axis=0)
     channels = channels.reshape(QUARTERS, rows, width)
     rim = rim.reshape(QUARTERS, TILE, width)
     conv_low, decays, state_local, reach = run_forward(info, channels, rim, vec, dense)
+    gate_use = places.gather_rest(after(gate_weight.T, mixer_own))
+    up_use = places.gather_rest(after(up_weight.T, conv_low))
     branch_pre = plain(low_rows, branch_own) + vec[BRANCH_BIAS]
 
-    def entering(parts, back):
+    def entering(parts, back, others=()):
         pair = jnp.stack([parts, places.core(parts)])
         every = jnp.stack([pair] + [places.along_z(pair, k) for k in (1, 2, 3)])
-        own, total = run_chain(spot, every, back)
+        own, total = run_chain(spot, after(every, *others), back)
         if high == 1:
             return own[:, 1:2]
         held = [total]
@@ -666,7 +670,8 @@
             state = jnp.where(ahead, picked[0:1] * state + picked[1:2], state)
         return own[:, 1:2] + own[:, 0:1] * state[None]
 
-    enter = entering(jnp.stack([reach[:, -1], state_local[:, -1]], axis=1), False)
+    enter = entering(jnp.stack([reach[:, -1], state_local[:, -1]], axis=1), False, feed_held)
+    down_use = places.gather_rest(after(down_weight, enter))
     branch_act, gelu_back_one = jax.vjp(jax.nn.gelu, branch_pre)
     state_low = (state_local + reach * enter).astype(bf16).reshape(QUARTERS * rows, width)
     mixed_low = (branch_act * state_low.astype(f32)).astype(bf16)
@@ -674,48 +679,129 @@
     def rows_of(array, k):
         return array[k * rows : (k + 1) * rows]
 
-    resid = inputs + places.scatter_rows(
-        [lambda k=k: trailing(rows_of(mixed_low, k), output_own) for k in range(QUARTERS)]
-    )
+    resid_sum, _ = places.scatter_rows(
+        [trailing(rows_of(mixed_low, k), output_own) for k in range(QUARTERS)]
+    )
+    resid = inputs + resid_sum
 
     rs_two, xs_two = normed(resid)
     low_two = (xs_two * gain_two).astype(bf16)
-    feed_rows = jnp.stack(places.gather_rows(low_two)).reshape(QUARTERS * rows, features)
+    feed_rows = jnp.concatenate(places.gather_rows(low_two), axis=0)
     gate_pre = trailing(feed_rows, gate_use)
     up_pre = trailing(feed_rows, up_use)
     gate_act, gelu_back_two = jax.vjp(jax.nn.gelu, gate_pre)
     hidden = (gate_act * up_pre).astype(bf16)
-    hidden_grad = trailing(feed_grad, down_use)
+    half = hidden.shape[1] // 2
+
+    def columns(array, core):
+        return lax.dynamic_slice_in_dim(array, core * half, half, 1)
+
+    def column_far(grad, rows_in):
+        return leading(columns(grad, 1 - c), rows_in).astype(bf16)
+
+    def column_own(grad, rows_in, far):
+        total = leading(columns(grad, c), rows_in) + places.core(far).astype(f32)
+        return total.astype(bf16)
+
+    def column_scatter(total):
+        return lax.psum_scatter(total, "blk", scatter_dimension=0, tiled=True)
+
+    def column_sum(total):
+        if high > 1:
+            total = total.reshape(high, -1, features)
+            total = jnp.take(total, (h - jnp.arange(high)) % high, axis=0)
+            total = places.scatter_high(total.reshape(-1, features))
+        return total.astype(f32)
+
+    down_far = column_far(hidden, feed_grad)
+    down_own = column_own(hidden, feed_grad, down_far)
+    down_scattered = column_scatter(down_own)
+    hidden_grad = trailing(feed_grad, after(down_use, down_own))
     gate_grad = gelu_back_two(hidden_grad * up_pre)[0].astype(bf16)
     up_grad = (hidden_grad * gate_act).astype(bf16)
-    norm_grad = places.scatter_rows(
-        [
-            lambda k=k: plain(rows_of(gate_grad, k), gate_use) + plain(rows_of(up_grad, k), up_use)
-            for k in range(QUARTERS)
-        ]
-    )
-
-    def column_sum(term):
-        term = term.astype(bf16).reshape(2, 4, -1, features)
-        return places.scatter_high(places.scatter_column(lambda k: term[0, k], term[1]))
-
-    down_sum = column_sum(leading(hidden, feed_grad))
-    gate_sum = column_sum(leading(gate_grad, feed_rows)).T
-    up_sum = column_sum(leading(up_grad, feed_rows)).T
+    def norm_part(k, gate_in, up_in):
+        return plain(rows_of(gate_in, k), gate_use) + plain(rows_of(up_in, k), up_use)
+
+    norm_parts = [norm_part(k, gate_grad, up_grad) for k in range(QUARTERS)]
+    norm_grad, _ = places.scatter_rows(norm_parts)
+    gate_late, *_ = lax.optimization_barrier((gate_grad, *norm_parts))
+    gate_far = column_far(gate_late, feed_rows)
+    norm_grad = after(norm_grad, gate_far)
     second_term = jnp.sum(norm_grad * xs_two, axis=0)
     resid_grad = cotangent.astype(f32) + norm_back(rs_two, xs_two, gain_two, norm_grad)
 
-    resid_rows = jnp.stack(places.gather_rows(resid_grad.astype(bf16)))
-    resid_rows = resid_rows.reshape(QUARTERS * rows, features)
+    resid_low = resid_grad.astype(bf16)
+    resid_rows = jnp.concatenate(places.gather_rows(resid_low), axis=0)
+    gate_last, up_late, hidden_last, _ = lax.optimization_barrier(
+        (gate_late, up_grad, hidden, resid_low)
+    )
+    gate_own = column_own(gate_last, feed_rows, gate_far)
+    gate_scattered = column_scatter(gate_own)
+    up_far = column_far(up_late, feed_rows)
+    output_terms = [plain(rows_of(hidden_last, k), down_use) for k in range(QUARTERS)]
+    resid_rows, *output_terms = lax.optimization_barrier(
+        (resid_rows, *output_terms, up_far, gate_own, down_scattered)
+    )[:-3]
+    output, output_joined = places.scatter_rows(output_terms)
+    output = (resid + output).astype(bf16)
     mixed_grad = plain(resid_rows, output_own)
     state_grad = (mixed_grad * branch_act).astype(bf16).reshape(QUARTERS, rows, width)
     branch_grad = gelu_back_one(mixed_grad * state_low.astype(f32))[0].astype(bf16)
     moved, span_back = run_reverse(decays, state_grad)
+    resid_late, mixed_late, low_late, branch_late, up_last, _ = lax.optimization_barrier(
+        (resid_rows, mixed_low, low_rows, branch_grad, up_late, moved)
+    )
     leave = entering(jnp.stack([span_back[:, 0], moved[:, 0]], axis=1), True)
+    def quarter_half(term):
+        slab_in = term.shape[0] // total_dp
+        term = term.astype(bf16).reshape(high * 4, 2 * slab_in, width)
+        own = lax.dynamic_slice_in_dim(term, c * slab_in, slab_in, 1)
+        came = places.core(lax.dynamic_slice_in_dim(term, (1 - c) * slab_in, slab_in, 1))
+        return (own + came).reshape(high, 4, slab_in, width), came
+
+    def quarter_rows(half):
+        return [
+            places.flip_p(lax.dynamic_index_in_dim(half, p ^ m, 1, False), m) for m in range(4)
+        ]
+
+    def quarter_high(total):
+        if high > 1:
+            total = jnp.take(total, (h - jnp.arange(high)) % high, axis=0)
+            return places.scatter_high(total.reshape(-1, width))
+        return total[0].astype(f32)
+
+    def quarter_near(parts):
+        stacked = jnp.stack(parts)
+
+        def by(k):
+            return lax.dynamic_index_in_dim(stacked, p ^ ((z + k) % 4), 0, False)
+
+        total = by(0).astype(f32)
+        for k in (1, 2, 3):
+            total = total + places.along_z(by(k), k).astype(f32)
+        return quarter_high(total)
+
+    def quarter_far(parts, gates):
+        *parts, _ = lax.optimization_barrier((*parts, gates))
+        stacked = jnp.take(jnp.stack(parts), p ^ straight, axis=0)
+        return quarter_high(lax.psum_scatter(stacked, "blk", scatter_dimension=0, tiled=True)[0])
+
+    output_term = leading(resid_late, mixed_late)
+    branch_term = leading(low_late, branch_late)
+    up_own = column_own(up_last, feed_rows, up_far)
+    up_scattered = column_scatter(up_own)
+    output_half, output_came = quarter_half(output_term)
+    branch_half, branch_came = quarter_half(branch_term)
+    leave = after(leave, output_came, branch_came, output_joined, up_own, gate_scattered)
+    output_parts = quarter_rows(output_half)
+    branch_parts = quarter_rows(branch_half)
     gates, chan_grad, rim_grad, sums = run_backward(
         info, channels, rim, vec, dense, conv_low, state_local, reach, enter, state_grad, moved,
         span_back, leave,
     )
+
+    output_sum = quarter_far(output_parts, gates).T
+    branch_sum = quarter_far(branch_parts, gates)
 
     came = places.back_rows(rim_grad)
     last = (c == 1) & (z == 3)
@@ -733,46 +819,19 @@
     if high > 1:
         returned = returned + picked(pick * (1.0 - here), places.back_high(came))
     chan_grad = chan_grad + jnp.pad(returned, ((0, 0), (rows - 8, 0), (0, 0)))
-    mixer_grad = chan_grad.astype(bf16).reshape(QUARTERS * rows, width)
-
-    branch_term = leading(low_rows, branch_grad)
-    mixer_term = leading(low_rows, mixer_grad)
-    output_term = leading(resid_rows, mixed_low)
-
-    def quarter_sum(term):
-        term = term.astype(bf16).reshape(high, 4, 2, slab, width)
-        own = lax.dynamic_index_in_dim(term, c, 2, False)
-        other = lax.dynamic_index_in_dim(term, 1 - c, 2, False)
-
-        def by(array, k):
-            return lax.dynamic_index_in_dim(array, (z - k + 4) % 4, 1, False)
-
-        came_over = places.core(other)
-        total = by(own, 1).astype(f32) + by(came_over, 1).astype(f32)
-        for k in (2, 3, 0):
-            total = (
-                places.along_z(total.astype(bf16)).astype(f32)
-                + by(own, k).astype(f32)
-                + by(came_over, k).astype(f32)
-            )
-        if high > 1:
-            back = (h - jnp.arange(high)) % high
-            total = places.scatter_high(
-                jnp.take(total, back, axis=0).reshape(high * slab, width)
-            )
-        return places.turn(total.astype(bf16).reshape(slab, width)).astype(f32)
-
-    output_sum = quarter_sum(output_term).T
-    branch_sum = quarter_sum(branch_term)
-    mixer_sum = quarter_sum(mixer_term)
-
-    low_grad = places.scatter_rows(
-        [
-            lambda k=k: trailing(rows_of(branch_grad, k), branch_own)
-            + trailing(rows_of(mixer_grad, k), mixer_own)
-            for k in range(QUARTERS)
-        ]
-    )
+    mixer_grad = after(chan_grad, *output_parts, *branch_parts, up_scattered).astype(bf16)
+    mixer_grad = mixer_grad.reshape(QUARTERS * rows, width)
+
+    low_parts = [
+        trailing(rows_of(branch_grad, k), branch_own) + trailing(rows_of(mixer_grad, k), mixer_own)
+        for k in range(QUARTERS)
+    ]
+    low_grad, _ = places.scatter_rows(low_parts)
+    mixer_late, *_ = lax.optimization_barrier((mixer_grad, *low_parts))
+    mixer_term = leading(low_rows, mixer_late)
+    mixer_half, mixer_came = quarter_half(mixer_term)
+    mixer_sum = quarter_near(quarter_rows(mixer_half))
+    gates, mixer_term, _ = lax.optimization_barrier((gates, mixer_term, mixer_came))
     token_grad = (resid_grad + norm_back(rs_one, xs_one, gain_one, low_grad)).astype(bf16)
 
     first_term = (
@@ -786,7 +845,7 @@
     gate_terms = jnp.sum(
         jnp.where(picked_blocks[None, :, None, :], crossed.reshape(2, heads, block_width, width), 0),
         axis=1,
-    ).astype(bf16)
+    )
     vector_terms = jnp.concatenate(
         [
             sums,
@@ -798,12 +857,34 @@
     )
     slope_back = DECAY * jax.nn.sigmoid(-param)
     vector_terms = vector_terms.at[2].multiply(slope_back)
-    gate_total = places.sum_high(
-        places.sum_plane(places.turn(gate_terms.reshape(2 * block_width, width)))
-    ).astype(f32)
-    vector_total = places.sum_high(places.sum_plane(places.turn(vector_terms)))
+    small_terms = jnp.concatenate(
+        [vector_terms, gate_terms.reshape(2 * block_width, width)], axis=0
+    )
+    small_terms = jnp.pad(small_terms, ((0, share * total_dp - small_terms.shape[0]), (0, 0)))
+    small_sum = quarter_near(quarter_rows(quarter_half(small_terms)[0]))
+    small_held = [small_sum]
+    for _ in range(high - 1):
+        small_held.append(places.along_h(small_held[-1]))
+    small_held = jnp.stack(small_held)
+    small_held = jnp.stack(places.gather_rows(small_held))
+    small_held = jnp.stack([small_held, places.core(small_held)])
+    where = []
+    for hh in range(high):
+        for a in range(4):
+            for core in range(2):
+                offset = p ^ a
+                crossed_at = (offset & 1) * 2 + offset // 2
+                slot = offset if core == 0 else crossed_at
+                where.append((((c ^ core) * 4 + slot) * high) + (h - hh + high) % high)
+    small_total = jnp.take(
+        small_held.reshape(-1, share, width), jnp.stack(where), axis=0
+    ).reshape(-1, width)
+    vector_total = small_total[:TILE]
+    gate_total = small_total[TILE : TILE + 2 * block_width]
+    gate_sum, up_sum = column_sum(gate_scattered).T, column_sum(up_scattered).T
+    down_sum = column_sum(down_scattered)
     return (
-        (resid + feed_part(places, hidden, down_use, rows)).astype(bf16),
+        output,
         token_grad,
         branch_sum,
         mixer_sum,
@@ -825,15 +906,6 @@
     )
 
 
-def feed_part(places, hidden, down_use, rows):
-    return places.scatter_rows(
-        [
-            lambda k=k: plain(hidden[k * rows : (k + 1) * rows], down_use)
-            for k in range(QUARTERS)
-        ]
-    )
-
-
 def solution(mesh):
     places = Places(mesh.shape["dp"], mesh.shape["blk"])
     return jax.shard_map(

time: 1240 us -> 776 us (0.63)
  Pallas kernels: 290 us -> 51.3 us
  waiting for transfers between devices: 422 us -> 266 us
  starting transfers between devices: 193 us -> 112 us
  matrix products: 172 us -> 186 us
  local copies, waits for them, and re-layouts: 88.7 us -> 75.5 us
  between operations: 3.51 us -> 16.6 us
    pallas_call x3 -> x2, Pallas kernels: 244 us -> 5.35 us  [lay(): pl.pallas_call(partial(laid_kernel, cuts), out_shape=[jax.ShapeDtypeStruc...]
    ppermute x124 -> x82, waiting for transfers between devices: 422 us -> 263 us  [send(): return jax.tree.map(lambda a: lax.ppermute(a, AXES, pairs), x)]
    ppermute x124 -> x82, starting transfers between devices: 193 us -> 111 us  [send(): return jax.tree.map(lambda a: lax.ppermute(a, AXES, pairs), x)]
    dot_general x7 -> x10, matrix products: 44.9 us -> 66.7 us  [leading(): lax.dot_general(former, latter, (((0,), (0,)), ((), ())), preferred_eleme...]
    unnamed x301 -> x252, local copies, waits for them, and re-layouts: 59 us -> 38.6 us
    convert_element_type x23 -> x6, other arithmetic: 25.6 us -> 7.7 us  [the longest x2 2.85 us: scatter_rows(): joined = (parts[1] + far.astype(f32)).astype(bf16)]
  transfers between devices with their start and end apart: 124 -> 92, of which waited for: 42 -> 36; matrix products, arithmetic and copies ran while one was open for 19% -> 36% of each run, Pallas kernels for 24% -> 7%
where the time goes in v2:
time: 776 us; the launch traced here: 761 us
  waiting for transfers between devices  266 us (34%)
  matrix products  186 us (24%)
  starting transfers between devices  112 us (14%)
  local copies, waits for them, and re-layouts  75.5 us (10%)
  other arithmetic  53.7 us (7%)
  Pallas kernels  51.3 us (7%)
  between operations  16.6 us (2%)
    ppermute x82, waiting for transfers between devices, send(): return jax.tree.map(lambda a: lax.ppermute(a, AXES, pairs), x)  263 us
    ppermute x82, starting transfers between devices, send(): return jax.tree.map(lambda a: lax.ppermute(a, AXES, pairs), x)  111 us
    dot_general x10, matrix products, leading(): lax.dot_general(former, latter, (((0,), (0,)), ((), ())), preferred_eleme...  66.7 us
    dot_general x15, matrix products, trailing(): lax.dot_general(former, latter, (((1,), (1,)), ((), ())), preferred_eleme...  60.4 us
    dot_general x16, matrix products, plain(): return jnp.dot(former, latter, preferred_element_type=f32)  58.8 us
    unnamed x252, local copies, waits for them, and re-layouts  38.6 us
    pallas_call x1, Pallas kernels, run_backward(): pl.pallas_call(backward_kernel, grid=(count,), out_shape=outs, in_specs=[...  25.5 us
  transfers between devices with their start and end apart: 92, of which 36 were waited for; matrix products, arithmetic and copies ran while one was open for 36% of the time, Pallas kernels for 7%

profile of v2, /device:TPU:3, one launch (start us, length us, event | category | flops | bytes accessed | tf_op | source)
XLA Modules:
  0.0 760.9 jit_solution(17403151906055864690)
XLA Ops:
  11.3 3.3 collective-permute-start
  16.1 3.6 collective-permute-done
  20.9 13.7 %collective-permute-done.1 = bf16[272,2048]{1,0:T(8,128)(2,1)} collective-permute-done((bf16[272,2048]{1,0:T(8,128)(2,1)S(1)}, bf16[272,2048]{1,0:T(8,128)(2,1)}, u32[]{:S(2)}, u32[]{:S(2)}) %collective-permute-start.1) | collective-permute-done | bytes 1114144 | tf_op jit(solution)/shard_map/ppermute | solution.py:57
  35.7 13.9 %collective-permute-done.3 = bf16[272,2048]{1,0:T(8,128)(2,1)S(1)} collective-permute-done((bf16[272,2048]{1,0:T(8,128)(2,1)}, bf16[272,2048]{1,0:T(8,128)(2,1)S(1)}, u32[]{:S(2)}, u32[]{:S(2)}) %collective-permute-start.3) | collective-permute-done | bytes 1114144 | tf_op jit(solution)/shard_map/ppermute | solution.py:57
  49.6 3.1 all-gather.6.cloned.1.call-done
  59.3 4.1 collective-permute-done.11.refs_1_
  63.4 4.4 collective-permute-start.15
  67.8 5.6 collective-permute-start.16
  91.7 10.6 %collective-permute-done.2 = bf16[272,2048]{1,0:T(8,128)(2,1)} collective-permute-done((bf16[272,2048]{1,0:T(8,128)(2,1)}, bf16[272,2048]{1,0:T(8,128)(2,1)}, u32[]{:S(2)}, u32[]{:S(2)}) %collective-permute-start.2) | collective-permute-done | bytes 1114144 | tf_op jit(solution)/shard_map/ppermute | solution.py:57
  108.1 3.4 add_convert_fusion.4
  111.6 15.2 %shard_map.341 = (bf16[4,256,640]{2,1,0:T(8,128)(2,1)S(1)}, f32[4,256,640]{2,1,0:T(8,128)S(1)}, f32[4,256,640]{2,1,0:T(8,128)S(1)}, f32[4,256,640]{2,1,0:T(8,128)S(1)}) custom-call(s32[4,5]{1,0:T(4,128)S(1)} %pad_add_fusion.1.info, bf16[4,256,640]{2,1,0:T(8,128)(2,1)S(1)} %bitcast.237, bf16[4,16,640]{2,1,0:T(8,128)(2,1)S(1)} %bitcast.239, ...), custom_call_target="tpu_custom_call" | custom-call | flops 1677721600 | bytes 55050240 | tf_op jit(solution)/shard_map/pallas_call | solution.py:416
  144.2 3.0 constant_dynamic-slice_fusion.18
  157.9 5.0 collective-permute-start.7
  162.9 31.5 %collective-permute-done.4.refs_1_ = bf16[1,512,640]{2,1,0:T(8,128)(2,1)} collective-permute-done((bf16[1,512,640]{2,1,0:T(8,128)(2,1)}, bf16[1,512,640]{2,1,0:T(8,128)(2,1)}, u32[]{:S(2)}, u32[]{:S(2)}) %collective-permute-start.4) | collective-permute-done | bytes 655392 | tf_op jit(solution)/shard_map/ppermute | solution.py:57
  195.0 12.0 %collective-permute-done.6.refs_3_ = bf16[1,512,640]{2,1,0:T(8,128)(2,1)} collective-permute-done((bf16[1,512,640]{2,1,0:T(8,128)(2,1)}, bf16[1,512,640]{2,1,0:T(8,128)(2,1)}, u32[]{:S(2)}, u32[]{:S(2)}) %collective-permute-start.6) | collective-permute-done | bytes 655392 | tf_op jit(solution)/shard_map/ppermute | solution.py:57
  212.6 3.8 shard_map.339
  216.4 5.4 fusion.11
  225.4 11.5 %collective-permute-done.26 = bf16[256,2048]{1,0:T(8,128)(2,1)S(1)} collective-permute-done((bf16[256,2048]{1,0:T(8,128)(2,1)S(1)}, bf16[256,2048]{1,0:T(8,128)(2,1)S(1)}, u32[]{:S(2)}, u32[]{:S(2)}) %collective-permute-start.26) | collective-permute-done | bytes 1048608 | tf_op jit(solution)/shard_map/ppermute | solution.py:57
  239.3 14.8 %collective-permute-done.25 = bf16[256,2048]{1,0:T(8,128)(2,1)S(1)} collective-permute-done((bf16[256,2048]{1,0:T(8,128)(2,1)S(1)}, bf16[256,2048]{1,0:T(8,128)(2,1)S(1)}, u32[]{:S(2)}, u32[]{:S(2)}) %collective-permute-start.25) | collective-permute-done | bytes 1048608 | tf_op jit(solution)/shard_map/ppermute | solution.py:57
  254.1 5.4 collective-permute-done.27
  264.9 19.9 %collective-permute-done.28 = bf16[256,2048]{1,0:T(8,128)(2,1)} collective-permute-done((bf16[256,2048]{1,0:T(8,128)(2,1)}, bf16[256,2048]{1,0:T(8,128)(2,1)}, u32[]{:S(2)}, u32[]{:S(2)}) %collective-permute-start.28) | collective-permute-done | bytes 1048608 | tf_op jit(solution)/shard_map/ppermute | solution.py:57
  295.4 4.7 collective-permute-done.30
  300.1 13.2 %fusion.121 = f32[1024,1536]{1,0:T(8,128)} fusion(bf16[1536,2048]{1,0:T(8,128)(2,1)} %all-gather.12.cloned.1.call-done, bf16[256,2048]{1,0:T(8,128)(2,1)} %collective-permute-done.30, bf16[256,2048]{1,0:T(8,128)(2,1)} %collective-permute-done.29, bf16[256,2048]{1,0:T(8,128)(2,1)} %collective-permute-done.28, bf16[256,2048]{1,0:T(8,128)(2,1)} %multiply_convert_fusion.3), kind=kOutput, calls=%fused_computation.329 | convolution fusion | flops 6459228160 | bytes 16777216 | tf_op jit(solution)/shard_map/dot_general | solution.py:30
  313.4 15.2 %multiply_convert_fusion.1 = (bf16[1024,1536]{1,0:T(8,128)(2,1)S(1)}, f32[1024,1536]{1,0:T(8,128)}) fusion(f32[1024,1536]{1,0:T(8,128)} %fusion.121, bf16[1536,2048]{1,0:T(8,128)(2,1)} %all-gather.14.cloned.1.call-done, bf16[256,2048]{1,0:T(8,128)(2,1)} %collective-permute-done.30, bf16[256,2048]{1,0:T(8,128)(2,1)} %collective-permute-done.29, ...), kind=kOutput, calls=%fused_computation.17 | convolution fusion | flops 6474956800 | bytes 26214400 | tf_op jit(solution)/shard_map/dot_general | solution.py:30
  328.5 8.6 %convolution_convert_fusion.2 = bf16[768,2048]{1,0:T(8,128)(2,1)} fusion(bf16[1024,2048]{1,0:T(8,128)(2,1)} %constant_dynamic-update-slice_fusion, bf16[1024,1536]{1,0:T(8,128)(2,1)S(1)} %get-tuple-element.100, s32[]{:T(128)S(6)} %select_n.400), kind=kOutput, calls=%fused_computation.28 | convolution fusion | flops 3222798336 | bytes 8912900 | tf_op jit(solution)/shard_map/dot_general | solution.py:34
  337.2 3.0 collective-permute-start.31
  340.1 5.6 collective-permute-done.31
  345.8 8.7 %add_convert_fusion.2 = bf16[768,2048]{1,0:T(8,128)(2,1)} fusion(bf16[768,2048]{1,0:T(8,128)(2,1)} %collective-permute-done.31, bf16[1024,2048]{1,0:T(8,128)(2,1)} %constant_dynamic-update-slice_fusion, bf16[1024,1536]{1,0:T(8,128)(2,1)} %copy-done.84, s32[]{:T(128)S(6)} %select_n.399), kind=kOutput, calls=%fused_computation.16 | convolution fusion | flops 3225944064 | bytes 12058628 | tf_op jit(solution)/shard_map/dot_general | solution.py:34
  354.6 16.8 %multiply_convert_fusion = (bf16[1024,1536]{1,0:T(8,128)(2,1)S(1)}, bf16[1024,1536]{1,0:T(8,128)(2,1)S(1)}) fusion(f32[1024,1536]{1,0:T(8,128)} %fusion.121, f32[1024,1536]{1,0:T(8,128)} %get-tuple-element.245, bf16[1024,2048]{1,0:T(8,128)(2,1)} %constant_dynamic-update-slice_fusion, bf16[1536,2048]{1,0:T(8,128)(2,1)} %all-gather.10.cloned.1.call-done), kind=kOutput, calls=%fused_computation.15 | convolution fusion | flops 6480199680 | bytes 29360128 | tf_op jit(solution)/shard_map/dot_general | solution.py:30
  371.4 5.8 fusion.37
  377.2 4.8 convolution_add_fusion.6
  392.4 3.7 collective-permute-done.33
  397.9 5.9 convolution_convert_fusion.1
  408.5 19.6 %collective-permute-done.32 = bf16[256,2048]{1,0:T(8,128)(2,1)S(1)} collective-permute-done((bf16[256,2048]{1,0:T(8,128)(2,1)S(1)}, bf16[256,2048]{1,0:T(8,128)(2,1)S(1)}, u32[]{:S(2)}, u32[]{:S(2)}) %collective-permute-start.32) | collective-permute-done | bytes 1048608 | tf_op jit(solution)/shard_map/ppermute | solution.py:57
  436.1 7.6 add_convert_fusion.1
  444.2 8.1 %convolution_convert_fusion = bf16[768,2048]{1,0:T(8,128)(2,1)} fusion(bf16[1024,1536]{1,0:T(8,128)(2,1)} %copy-done.115, s32[]{:T(128)S(6)} %select_n.400, bf16[256,2048]{1,0:T(8,128)(2,1)} %collective-permute-done.30, bf16[256,2048]{1,0:T(8,128)(2,1)} %collective-permute-done.29, bf16[256,2048]{1,0:T(8,128)(2,1)} %collective-permute-done.28, ...), kind=kOutput, calls=%fused_computation.26 | convolution fusion | flops 3239575552 | bytes 8912900 | tf_op jit(solution)/shard_map/dot_general | solution.py:34
  453.6 6.2 fusion.54
  459.8 6.3 fusion.52
  466.1 2.8 fusion.50
  468.9 2.8 fusion.48
  471.7 8.7 %collective-permute-done.37 = bf16[256,2048]{1,0:T(8,128)(2,1)S(1)} collective-permute-done((bf16[256,2048]{1,0:T(8,128)(2,1)}, bf16[256,2048]{1,0:T(8,128)(2,1)S(1)}, u32[]{:S(2)}, u32[]{:S(2)}) %collective-permute-start.37) | collective-permute-done | bytes 1048608 | tf_op jit(solution)/shard_map/ppermute | solution.py:57
  480.4 3.8 pad_maximum_fusion.2
  484.2 10.2 %convert_reduce_fusion.1 = (bf16[640]{0:T(1024)(128)(2,1)}, bf16[1024,640]{1,0:T(8,128)(2,1)}, bf16[1024,640]{1,0:T(8,128)(2,1)S(1)}) fusion(f32[1024,640]{1,0:T(8,128)} %get-tuple-element.241, f32[640]{0:T(1024)S(1)} %copy-done.106, bf16[4,256,640]{2,1,0:T(8,128)(2,1)} %copy-done.82, bf16[1024,2048]{1,0:T(8,128)(2,1)} %pad_maximum_fusion.2, ...), kind=kOutput, calls=%fused_computation.55 | convolution fusion | flops 2702704128 | bytes 13373184 | tf_op jit(solution)/shard_map/dot_general | solution.py:26
  494.4 2.8 shard_map.343
  499.8 9.3 %add_convert_fusion = bf16[768,2048]{1,0:T(8,128)(2,1)} fusion(bf16[768,2048]{1,0:T(8,128)(2,1)} %collective-permute-done.48, bf16[1024,1536]{1,0:T(8,128)(2,1)S(1)} %copy-done.116, s32[]{:T(128)S(6)} %select_n.399, bf16[256,2048]{1,0:T(8,128)(2,1)} %collective-permute-done.30, bf16[256,2048]{1,0:T(8,128)(2,1)} %collective-permute-done.29, ...), kind=kOutput, calls=%fused_computation.13 | convolution fusion | flops 3242721280 | bytes 12058628 | tf_op jit(solution)/shard_map/dot_general | solution.py:34
  511.0 6.2 convolution_convert_fusion.3
  519.5 4.8 multiply_reduce_fusion.1
  528.8 3.1 collective-permute-done.45
  533.6 2.7 collective-permute-done.44
  552.8 25.5 %shard_map.345 = (bf16[4,256,1280]{2,1,0:T(8,128)(2,1)S(1)}, f32[4,256,640]{2,1,0:T(8,128)S(1)}, f32[4,8,640]{2,1,0:T(8,128)S(1)}, f32[8,640]{1,0:T(8,128)S(1)}) custom-call(s32[4,5]{1,0:T(4,128)S(1)} %copy-done.48, bf16[4,256,640]{2,1,0:T(8,128)(2,1)S(1)} %bitcast.238, bf16[4,16,640]{2,1,0:T(8,128)(2,1)S(1)} %bitcast.240, f32[16,640]{1,0:T(8,128)S(1)} %copy-done.44, ...), custom_call_target="tpu_custom_call" | custom-call | flops 3355443200 | bytes 94371840 | tf_op jit(solution)/shard_map/pallas_call | solution.py:480
  594.5 11.4 %collective-permute-start.49 = (f32[4,8,640]{2,1,0:T(8,128)S(1)}, f32[4,8,640]{2,1,0:T(8,128)S(1)}, u32[]{:S(2)}, u32[]{:S(2)}) collective-permute-start(f32[4,8,640]{2,1,0:T(8,128)S(1)} %get-tuple-element.119), channel_id=1, source_target_pairs={{0,7},{1,0},{2,1},{3,2},{4,3},{5,4},{6,5},{7,6},{8,15},{9,8},{10,9... | collective-permute-start | bytes 245768 | tf_op jit(solution)/shard_map/ppermute | solution.py:57
  609.6 3.0 pad_add_fusion
  622.5 16.8 %collective-permute-done.57 = bf16[256,2048]{1,0:T(8,128)(2,1)S(1)} collective-permute-done((bf16[256,2048]{1,0:T(8,128)(2,1)S(1)}, bf16[256,2048]{1,0:T(8,128)(2,1)S(1)}, u32[]{:S(2)}, u32[]{:S(2)}) %collective-permute-start.57) | collective-permute-done | bytes 1048608 | tf_op jit(solution)/shard_map/ppermute | solution.py:57
  644.1 12.0 %collective-permute-done.56 = bf16[256,2048]{1,0:T(8,128)(2,1)S(1)} collective-permute-done((bf16[256,2048]{1,0:T(8,128)(2,1)S(1)}, bf16[256,2048]{1,0:T(8,128)(2,1)S(1)}, u32[]{:S(2)}, u32[]{:S(2)}) %collective-permute-start.56) | collective-permute-done | bytes 1048608 | tf_op jit(solution)/shard_map/ppermute | solution.py:57
  656.1 6.6 collective-permute-done.58
  662.8 2.6 fusion.21
  665.4 5.3 fusion.125
  679.4 4.5 copy.60
  683.9 3.3 multiply_reduce_fusion
  700.1 3.4 collective-permute-start.81
  708.5 4.7 fusion.25
  714.8 5.2 collective-permute-done.61
  726.9 4.7 collective-permute-start.76
  732.2 17.6 %collective-permute-done.64 = bf16[1,256,640]{2,1,0:T(8,128)(2,1)S(1)} collective-permute-done((bf16[1,256,640]{2,1,0:T(8,128)(2,1)S(1)}, bf16[1,256,640]{2,1,0:T(8,128)(2,1)S(1)}, u32[]{:S(2)}, u32[]{:S(2)}) %collective-permute-start.64) | collective-permute-done | bytes 327712 | tf_op jit(solution)/shard_map/ppermute | solution.py:57
  (579 shorter events, 223.8 us)
Async XLA Ops:
  7.3 45.4 %all-gather.6.cloned.1.call-start = ((), (), s32[]{:S(2)}) async-start(), calls=%async_computation.5 | async-start | bytes 1945600 | tf_op jit(solution)/shard_map/all_gather | solution.py:117
  16.0 128.2 %all-gather.8.cloned.1.call-start = ((), (), s32[]{:S(2)}) async-start(), calls=%async_computation.6 | async-start | bytes 3276800 | tf_op jit(solution)/shard_map/all_gather | solution.py:117
  19.8 14.8 %collective-permute-start.1 = (bf16[272,2048]{1,0:T(8,128)(2,1)S(1)}, bf16[272,2048]{1,0:T(8,128)(2,1)}, u32[]{:S(2)}, u32[]{:S(2)}) collective-permute-start(bf16[272,2048]{1,0:T(8,128)(2,1)S(1)} %pad_maximum_fusion.5), channel_id=1, source_target_pairs={{0,8},{1,9},{2,10},{3,11},{4,20},{5,21},{6,22},{7,23},{8,0},{9,1},... | collective-permute-start | bytes 3342344 | tf_op jit(solution)/shard_map/ppermute | solution.py:57
  34.6 15.0 %collective-permute-start.3 = (bf16[272,2048]{1,0:T(8,128)(2,1)}, bf16[272,2048]{1,0:T(8,128)(2,1)S(1)}, u32[]{:S(2)}, u32[]{:S(2)}) collective-permute-start(bf16[272,2048]{1,0:T(8,128)(2,1)} %collective-permute-done.1), channel_id=1, source_target_pairs={{0,16},{1,17},{2,18},{3,19},{4,12},{5,13},{6,14},{7,15},{8,24},{9,... | collective-permute-start | bytes 3342344 | tf_op jit(solution)/shard_map/ppermute | solution.py:57
  52.7 247.4 %all-gather.12.cloned.1.call-start = ((), (), s32[]{:S(2)}) async-start(), calls=%async_computation.8 | async-start | bytes 7077888 | tf_op jit(solution)/shard_map/all_gather | solution.py:135
  54.6 13.2 %collective-permute-start.12 = (bf16[1,304,640]{2,1,0:T(8,128)(2,1)S(1)}, bf16[1,304,640]{2,1,0:T(8,128)(2,1)S(1)}, u32[]{:S(2)}, u32[]{:S(2)}) collective-permute-start(bf16[1,304,640]{2,1,0:T(8,128)(2,1)S(1)} %get-tuple-element.196), channel_id=1, source_target_pairs={{0,16},{1,17},{2,18},{3,19},{4,20},{5,21},{6,22},{7,23},{8,24},{9,... | collective-permute-start | bytes 1167368 | tf_op jit(solution)/shard_map/ppermute | solution.py:57
  55.8 18.4 %collective-permute-start.13 = (bf16[1,304,640]{2,1,0:T(8,128)(2,1)S(1)}, bf16[1,304,640]{2,1,0:T(8,128)(2,1)S(1)}, u32[]{:S(2)}, u32[]{:S(2)}) collective-permute-start(bf16[1,304,640]{2,1,0:T(8,128)(2,1)S(1)} %get-tuple-element.195), channel_id=1, source_target_pairs={{0,24},{1,25},{2,26},{3,27},{4,28},{5,29},{6,30},{7,31},{8,16},{9,... | collective-permute-start | bytes 1167368 | tf_op jit(solution)/shard_map/ppermute | solution.py:57
  57.0 18.9 %collective-permute-start.14 = (bf16[1,304,640]{2,1,0:T(8,128)(2,1)S(1)}, bf16[1,304,640]{2,1,0:T(8,128)(2,1)S(1)}, u32[]{:S(2)}, u32[]{:S(2)}) collective-permute-start(bf16[1,304,640]{2,1,0:T(8,128)(2,1)S(1)} %get-tuple-element.198.refs_0_), channel_id=1, source_target_pairs={{0,4},{1,5},{2,6},{3,7},{4,0},{5,1},{6,2},{7,3},{8,12},{9,13},{10,... | collective-permute-start | bytes 1167368 | tf_op jit(solution)/shard_map/ppermute | solution.py:57
  63.4 13.2 %collective-permute-start.15 = (bf16[1,304,640]{2,1,0:T(8,128)(2,1)S(1)}, bf16[1,304,640]{2,1,0:T(8,128)(2,1)S(1)}, u32[]{:S(2)}, u32[]{:S(2)}) collective-permute-start(bf16[1,304,640]{2,1,0:T(8,128)(2,1)S(1)} %collective-permute-done.11.refs_1_), channel_id=1, source_target_pairs={{0,4},{1,5},{2,6},{3,7},{4,0},{5,1},{6,2},{7,3},{8,12},{9,13},{10,... | collective-permute-start | bytes 1167368 | tf_op jit(solution)/shard_map/ppermute | solution.py:57
  67.8 9.6 %collective-permute-start.16 = (bf16[1,304,640]{2,1,0:T(8,128)(2,1)S(1)}, bf16[1,304,640]{2,1,0:T(8,128)(2,1)S(1)}, u32[]{:S(2)}, u32[]{:S(2)}) collective-permute-start(bf16[1,304,640]{2,1,0:T(8,128)(2,1)S(1)} %collective-permute-done.12.refs_2_), channel_id=1, source_target_pairs={{0,4},{1,5},{2,6},{3,7},{4,0},{5,1},{6,2},{7,3},{8,12},{9,13},{10,... | collective-permute-start | bytes 1167368 | tf_op jit(solution)/shard_map/ppermute | solution.py:57
  87.3 226.1 %all-gather.14.cloned.1.call-start = ((), (), s32[]{:S(2)}) async-start(), calls=%async_computation.9 | async-start | bytes 7077888 | tf_op jit(solution)/shard_map/all_gather | solution.py:135
  87.3 15.0 %collective-permute-start.2 = (bf16[272,2048]{1,0:T(8,128)(2,1)}, bf16[272,2048]{1,0:T(8,128)(2,1)}, u32[]{:S(2)}, u32[]{:S(2)}) collective-permute-start(bf16[272,2048]{1,0:T(8,128)(2,1)} %copy-done.83), channel_id=1, source_target_pairs={{0,16},{1,17},{2,18},{3,19},{4,12},{5,13},{6,14},{7,15},{8,24},{9,... | collective-permute-start | bytes 3342344 | tf_op jit(solution)/shard_map/ppermute | solution.py:57
  131.0 223.6 %all-gather.10.cloned.1.call-start = ((), (), s32[]{:S(2)}) async-start(), calls=%async_computation.7 | async-start | bytes 7077888 | tf_op jit(solution)/shard_map/all_gather | solution.py:135
  131.1 22.9 %collective-permute-start.22 = (bf16[256,2048]{1,0:T(8,128)(2,1)}, bf16[256,2048]{1,0:T(8,128)(2,1)}, u32[]{:S(2)}, u32[]{:S(2)}) collective-permute-start(bf16[256,2048]{1,0:T(8,128)(2,1)} %param.25), channel_id=1, source_target_pairs={{0,8},{1,9},{2,10},{3,11},{4,20},{5,21},{6,22},{7,23},{8,0},{9,1},... | collective-permute-start | bytes 3145736 | tf_op jit(solution)/shard_map/ppermute | solution.py:57
  132.5 25.4 %collective-permute-start.23 = (bf16[256,2048]{1,0:T(8,128)(2,1)}, bf16[256,2048]{1,0:T(8,128)(2,1)}, u32[]{:S(2)}, u32[]{:S(2)}) collective-permute-start(bf16[256,2048]{1,0:T(8,128)(2,1)} %param.25), channel_id=1, source_target_pairs={{0,16},{1,17},{2,18},{3,19},{4,12},{5,13},{6,14},{7,15},{8,24},{9,... | collective-permute-start | bytes 3145736 | tf_op jit(solution)/shard_map/ppermute | solution.py:57
  139.5 69.5 %collective-permute-start.24 = (bf16[256,2048]{1,0:T(8,128)(2,1)}, bf16[256,2048]{1,0:T(8,128)(2,1)}, u32[]{:S(2)}, u32[]{:S(2)}) collective-permute-start(bf16[256,2048]{1,0:T(8,128)(2,1)} %param.25), channel_id=1, source_target_pairs={{0,24},{1,25},{2,26},{3,27},{4,28},{5,29},{6,30},{7,31},{8,16},{9,... | collective-permute-start | bytes 3145736 | tf_op jit(solution)/shard_map/ppermute | solution.py:57
  139.5 13.1 %collective-permute-start.20 = (f32[2,4,2,640]{3,2,1,0:T(2,128)S(1)}, f32[2,4,2,640]{3,2,1,0:T(2,128)S(1)}, u32[]{:S(2)}, u32[]{:S(2)}) collective-permute-start(f32[2,4,2,640]{3,2,1,0:T(2,128)S(1)} %get-tuple-element.230), channel_id=1, source_target_pairs={{0,2},{1,3},{2,0},{3,1},{4,6},{5,7},{6,4},{7,5},{8,10},{9,11},{10,... | collective-permute-start | bytes 122888 | tf_op jit(solution)/shard_map/ppermute | solution.py:57
  141.8 11.1 %collective-permute-start.19 = (f32[2,4,2,640]{3,2,1,0:T(2,128)S(1)}, f32[2,4,2,640]{3,2,1,0:T(2,128)S(1)}, u32[]{:S(2)}, u32[]{:S(2)}) collective-permute-start(f32[2,4,2,640]{3,2,1,0:T(2,128)S(1)} %get-tuple-element.230), channel_id=1, source_target_pairs={{0,1},{1,2},{2,3},{3,0},{4,5},{5,6},{6,7},{7,4},{8,9},{9,10},{10,1... | collective-permute-start | bytes 122888 | tf_op jit(solution)/shard_map/ppermute | solution.py:57
  152.6 41.8 %collective-permute-start.4 = (bf16[1,512,640]{2,1,0:T(8,128)(2,1)}, bf16[1,512,640]{2,1,0:T(8,128)(2,1)}, u32[]{:S(2)}, u32[]{:S(2)}) collective-permute-start(bf16[1,512,640]{2,1,0:T(8,128)(2,1)} %bitcast.258), channel_id=1, source_target_pairs={{0,8},{1,9},{2,10},{3,11},{4,12},{5,13},{6,14},{7,15},{8,0},{9,1},... | collective-permute-start | bytes 1966088 | tf_op jit(solution)/shard_map/ppermute | solution.py:57
  152.8 42.2 %collective-permute-start.5 = (bf16[1,512,640]{2,1,0:T(8,128)(2,1)}, bf16[1,512,640]{2,1,0:T(8,128)(2,1)}, u32[]{:S(2)}, u32[]{:S(2)}) collective-permute-start(bf16[1,512,640]{2,1,0:T(8,128)(2,1)} %bitcast.257), channel_id=1, source_target_pairs={{0,16},{1,17},{2,18},{3,19},{4,20},{5,21},{6,22},{7,23},{8,24},{9,... | collective-permute-start | bytes 1966088 | tf_op jit(solution)/shard_map/ppermute | solution.py:57
  154.0 53.0 %collective-permute-start.6 = (bf16[1,512,640]{2,1,0:T(8,128)(2,1)}, bf16[1,512,640]{2,1,0:T(8,128)(2,1)}, u32[]{:S(2)}, u32[]{:S(2)}) collective-permute-start(bf16[1,512,640]{2,1,0:T(8,128)(2,1)} %bitcast.256), channel_id=1, source_target_pairs={{0,24},{1,25},{2,26},{3,27},{4,28},{5,29},{6,30},{7,31},{8,16},{9,... | collective-permute-start | bytes 1966088 | tf_op jit(solution)/shard_map/ppermute | solution.py:57
  157.9 54.7 %collective-permute-start.7 = (bf16[1,512,640]{2,1,0:T(8,128)(2,1)S(1)}, bf16[1,512,640]{2,1,0:T(8,128)(2,1)S(1)}, u32[]{:S(2)}, u32[]{:S(2)}) collective-permute-start(bf16[1,512,640]{2,1,0:T(8,128)(2,1)S(1)} %bitcast.234), channel_id=1, source_target_pairs={{0,4},{1,5},{2,6},{3,7},{4,0},{5,1},{6,2},{7,3},{8,12},{9,13},{10,... | collective-permute-start | bytes 1966088 | tf_op jit(solution)/shard_map/ppermute | solution.py:57
  194.4 18.1 %collective-permute-start.8 = (bf16[1,512,640]{2,1,0:T(8,128)(2,1)}, bf16[1,512,640]{2,1,0:T(8,128)(2,1)S(1)}, u32[]{:S(2)}, u32[]{:S(2)}) collective-permute-start(bf16[1,512,640]{2,1,0:T(8,128)(2,1)} %collective-permute-done.4.refs_1_), channel_id=1, source_target_pairs={{0,4},{1,5},{2,6},{3,7},{4,0},{5,1},{6,2},{7,3},{8,12},{9,13},{10,... | collective-permute-start | bytes 1966088 | tf_op jit(solution)/shard_map/ppermute | solution.py:57
  195.0 17.5 %collective-permute-start.9 = (bf16[1,512,640]{2,1,0:T(8,128)(2,1)}, bf16[1,512,640]{2,1,0:T(8,128)(2,1)S(1)}, u32[]{:S(2)}, u32[]{:S(2)}) collective-permute-start(bf16[1,512,640]{2,1,0:T(8,128)(2,1)} %collective-permute-done.5.refs_2_), channel_id=1, source_target_pairs={{0,4},{1,5},{2,6},{3,7},{4,0},{5,1},{6,2},{7,3},{8,12},{9,13},{10,... | collective-permute-start | bytes 1966088 | tf_op jit(solution)/shard_map/ppermute | solution.py:57
  222.8 14.1 %collective-permute-start.26 = (bf16[256,2048]{1,0:T(8,128)(2,1)S(1)}, bf16[256,2048]{1,0:T(8,128)(2,1)S(1)}, u32[]{:S(2)}, u32[]{:S(2)}) collective-permute-start(bf16[256,2048]{1,0:T(8,128)(2,1)S(1)} %convolution_convert_fusion.4), channel_id=1, source_target_pairs={{0,16},{1,17},{2,18},{3,19},{4,12},{5,13},{6,14},{7,15},{8,24},{9,... | collective-permute-start | bytes 3145736 | tf_op jit(solution)/shard_map/ppermute | solution.py:57
  225.2 28.8 %collective-permute-start.25 = (bf16[256,2048]{1,0:T(8,128)(2,1)S(1)}, bf16[256,2048]{1,0:T(8,128)(2,1)S(1)}, u32[]{:S(2)}, u32[]{:S(2)}) collective-permute-start(bf16[256,2048]{1,0:T(8,128)(2,1)S(1)} %convolution_convert_fusion.5), channel_id=1, source_target_pairs={{0,16},{1,17},{2,18},{3,19},{4,12},{5,13},{6,14},{7,15},{8,24},{9,... | collective-permute-start | bytes 3145736 | tf_op jit(solution)/shard_map/ppermute | solution.py:57
  237.9 21.5 %collective-permute-start.27 = (bf16[256,2048]{1,0:T(8,128)(2,1)S(1)}, bf16[256,2048]{1,0:T(8,128)(2,1)S(1)}, u32[]{:S(2)}, u32[]{:S(2)}) collective-permute-start(bf16[256,2048]{1,0:T(8,128)(2,1)S(1)} %fusion.19), channel_id=1, source_target_pairs={{0,8},{1,9},{2,10},{3,11},{4,20},{5,21},{6,22},{7,23},{8,0},{9,1},... | collective-permute-start | bytes 3145736 | tf_op jit(solution)/shard_map/ppermute | solution.py:57
  262.1 22.8 %collective-permute-start.28 = (bf16[256,2048]{1,0:T(8,128)(2,1)}, bf16[256,2048]{1,0:T(8,128)(2,1)}, u32[]{:S(2)}, u32[]{:S(2)}) collective-permute-start(bf16[256,2048]{1,0:T(8,128)(2,1)} %multiply_convert_fusion.3), channel_id=1, source_target_pairs={{0,8},{1,9},{2,10},{3,11},{4,20},{5,21},{6,22},{7,23},{8,0},{9,1},... | collective-permute-start | bytes 3145736 | tf_op jit(solution)/shard_map/ppermute | solution.py:57
  263.5 220.7 %reduce-scatter.6.cloned.1.call-start = ((), (), s32[]{:S(2)}) async-start(), calls=%async_computation.10 | async-start | bytes 3932160 | tf_op jit(solution)/shard_map/reduce_scatter | solution.py:707
  263.7 31.7 %collective-permute-start.29 = (bf16[256,2048]{1,0:T(8,128)(2,1)}, bf16[256,2048]{1,0:T(8,128)(2,1)}, u32[]{:S(2)}, u32[]{:S(2)}) collective-permute-start(bf16[256,2048]{1,0:T(8,128)(2,1)} %multiply_convert_fusion.3), channel_id=1, source_target_pairs={{0,16},{1,17},{2,18},{3,19},{4,12},{5,13},{6,14},{7,15},{8,24},{9,... | collective-permute-start | bytes 3145736 | tf_op jit(solution)/shard_map/ppermute | solution.py:57
  284.9 15.3 %collective-permute-start.30 = (bf16[256,2048]{1,0:T(8,128)(2,1)}, bf16[256,2048]{1,0:T(8,128)(2,1)}, u32[]{:S(2)}, u32[]{:S(2)}) collective-permute-start(bf16[256,2048]{1,0:T(8,128)(2,1)} %collective-permute-done.28), channel_id=1, source_target_pairs={{0,16},{1,17},{2,18},{3,19},{4,12},{5,13},{6,14},{7,15},{8,24},{9,... | collective-permute-start | bytes 3145736 | tf_op jit(solution)/shard_map/ppermute | solution.py:57
  354.5 192.8 %reduce-scatter.8.cloned.1.call-start = ((), (), s32[]{:S(2)}) async-start(), calls=%async_computation.11 | async-start | bytes 3932160 | tf_op jit(solution)/shard_map/reduce_scatter | solution.py:707
  381.9 14.1 %collective-permute-start.33 = (bf16[256,2048]{1,0:T(8,128)(2,1)S(1)}, bf16[256,2048]{1,0:T(8,128)(2,1)S(1)}, u32[]{:S(2)}, u32[]{:S(2)}) collective-permute-start(bf16[256,2048]{1,0:T(8,128)(2,1)S(1)} %convolution_add_fusion.6), channel_id=1, source_target_pairs={{0,16},{1,17},{2,18},{3,19},{4,12},{5,13},{6,14},{7,15},{8,24},{9,... | collective-permute-start | bytes 3145736 | tf_op jit(solution)/shard_map/ppermute | solution.py:57
  403.8 32.4 %collective-permute-start.38 = (bf16[768,2048]{1,0:T(8,128)(2,1)S(1)}, bf16[768,2048]{1,0:T(8,128)(2,1)S(1)}, u32[]{:S(2)}, u32[]{:S(2)}) collective-permute-start(bf16[768,2048]{1,0:T(8,128)(2,1)S(1)} %convolution_convert_fusion.1), channel_id=1, source_target_pairs={{0,4},{1,5},{2,6},{3,7},{4,0},{5,1},{6,2},{7,3},{8,12},{9,13},{10,... | collective-permute-start | bytes 9437192 | tf_op jit(solution)/shard_map/ppermute | solution.py:57
  405.0 23.1 %collective-permute-start.32 = (bf16[256,2048]{1,0:T(8,128)(2,1)S(1)}, bf16[256,2048]{1,0:T(8,128)(2,1)S(1)}, u32[]{:S(2)}, u32[]{:S(2)}) collective-permute-start(bf16[256,2048]{1,0:T(8,128)(2,1)S(1)} %convolution_add_fusion.8), channel_id=1, source_target_pairs={{0,16},{1,17},{2,18},{3,19},{4,12},{5,13},{6,14},{7,15},{8,24},{9,... | collective-permute-start | bytes 3145736 | tf_op jit(solution)/shard_map/ppermute | solution.py:57
  406.8 23.7 %collective-permute-start.34 = (bf16[256,2048]{1,0:T(8,128)(2,1)S(1)}, bf16[256,2048]{1,0:T(8,128)(2,1)S(1)}, u32[]{:S(2)}, u32[]{:S(2)}) collective-permute-start(bf16[256,2048]{1,0:T(8,128)(2,1)S(1)} %add_convert_fusion.8), channel_id=1, source_target_pairs={{0,8},{1,9},{2,10},{3,11},{4,20},{5,21},{6,22},{7,23},{8,0},{9,1},... | collective-permute-start | bytes 3145736 | tf_op jit(solution)/shard_map/ppermute | solution.py:57
  433.4 32.7 %collective-permute-start.35 = (bf16[256,2048]{1,0:T(8,128)(2,1)}, bf16[256,2048]{1,0:T(8,128)(2,1)}, u32[]{:S(2)}, u32[]{:S(2)}) collective-permute-start(bf16[256,2048]{1,0:T(8,128)(2,1)} %fusion.119), channel_id=1, source_target_pairs={{0,8},{1,9},{2,10},{3,11},{4,20},{5,21},{6,22},{7,23},{8,0},{9,1},... | collective-permute-start | bytes 3145736 | tf_op jit(solution)/shard_map/ppermute | solution.py:57
  435.1 36.6 %collective-permute-start.36 = (bf16[256,2048]{1,0:T(8,128)(2,1)}, bf16[256,2048]{1,0:T(8,128)(2,1)}, u32[]{:S(2)}, u32[]{:S(2)}) collective-permute-start(bf16[256,2048]{1,0:T(8,128)(2,1)} %fusion.119), channel_id=1, source_target_pairs={{0,16},{1,17},{2,18},{3,19},{4,12},{5,13},{6,14},{7,15},{8,24},{9,... | collective-permute-start | bytes 3145736 | tf_op jit(solution)/shard_map/ppermute | solution.py:57
  443.7 168.8 %reduce-scatter.10.cloned.1.call-start = ((), (), s32[]{:S(2)}) async-start(), calls=%async_computation.12 | async-start | bytes 3932160 | tf_op jit(solution)/shard_map/reduce_scatter | solution.py:707
  452.3 47.5 %collective-permute-start.48 = (bf16[768,2048]{1,0:T(8,128)(2,1)}, bf16[768,2048]{1,0:T(8,128)(2,1)}, u32[]{:S(2)}, u32[]{:S(2)}) collective-permute-start(bf16[768,2048]{1,0:T(8,128)(2,1)} %convolution_convert_fusion), channel_id=1, source_target_pairs={{0,4},{1,5},{2,6},{3,7},{4,0},{5,1},{6,2},{7,3},{8,12},{9,13},{10,... | collective-permute-start | bytes 9437192 | tf_op jit(solution)/shard_map/ppermute | solution.py:57
  466.1 14.3 %collective-permute-start.37 = (bf16[256,2048]{1,0:T(8,128)(2,1)}, bf16[256,2048]{1,0:T(8,128)(2,1)S(1)}, u32[]{:S(2)}, u32[]{:S(2)}) collective-permute-start(bf16[256,2048]{1,0:T(8,128)(2,1)} %collective-permute-done.35), channel_id=1, source_target_pairs={{0,16},{1,17},{2,18},{3,19},{4,12},{5,13},{6,14},{7,15},{8,24},{9,... | collective-permute-start | bytes 3145736 | tf_op jit(solution)/shard_map/ppermute | solution.py:57
  509.1 166.3 %reduce-scatter.14.cloned.1.call-start = ((), (), s32[]{:S(2)}) async-start(), calls=%async_computation.14 | async-start | bytes 1638400 | tf_op jit(solution)/shard_map/reduce_scatter | solution.py:787
  510.1 16.8 %collective-permute-start.42 = (f32[4,2,640]{2,1,0:T(2,128)S(1)}, f32[4,2,640]{2,1,0:T(2,128)S(1)}, u32[]{:S(2)}, u32[]{:S(2)}) collective-permute-start(f32[4,2,640]{2,1,0:T(2,128)S(1)} %get-tuple-element.233), channel_id=1, source_target_pairs={{0,4},{1,5},{2,6},{3,7},{4,0},{5,1},{6,2},{7,3},{8,12},{9,13},{10,... | collective-permute-start | bytes 61448 | tf_op jit(solution)/shard_map/ppermute | solution.py:57
  518.5 20.7 %collective-permute-start.46 = (bf16[4,256,640]{2,1,0:T(8,128)(2,1)}, bf16[4,256,640]{2,1,0:T(8,128)(2,1)}, u32[]{:S(2)}, u32[]{:S(2)}) collective-permute-start(bf16[4,256,640]{2,1,0:T(8,128)(2,1)} %constant_dynamic-slice_fusion.17), channel_id=1, source_target_pairs={{0,4},{1,5},{2,6},{3,7},{4,0},{5,1},{6,2},{7,3},{8,12},{9,13},{10,... | collective-permute-start | bytes 3932168 | tf_op jit(solution)/shard_map/ppermute | solution.py:57
  518.5 26.3 %collective-permute-start.40 = (bf16[256,2048]{1,0:T(8,128)(2,1)}, bf16[256,2048]{1,0:T(8,128)(2,1)}, u32[]{:S(2)}, u32[]{:S(2)}) collective-permute-start(bf16[256,2048]{1,0:T(8,128)(2,1)} %fusion.48), channel_id=1, source_target_pairs={{0,16},{1,17},{2,18},{3,19},{4,12},{5,13},{6,14},{7,15},{8,24},{9,... | collective-permute-start | bytes 3145736 | tf_op jit(solution)/shard_map/ppermute | solution.py:57
  527.0 20.4 %collective-permute-start.47 = (bf16[4,256,640]{2,1,0:T(8,128)(2,1)}, bf16[4,256,640]{2,1,0:T(8,128)(2,1)}, u32[]{:S(2)}, u32[]{:S(2)}) collective-permute-start(bf16[4,256,640]{2,1,0:T(8,128)(2,1)} %constant_dynamic-slice_fusion.16), channel_id=1, source_target_pairs={{0,4},{1,5},{2,6},{3,7},{4,0},{5,1},{6,2},{7,3},{8,12},{9,13},{10,... | collective-permute-start | bytes 3932168 | tf_op jit(solution)/shard_map/ppermute | solution.py:57
  542.0 39.3 %collective-permute-start.50 = (bf16[1,256,640]{2,1,0:T(8,128)(2,1)}, bf16[1,256,640]{2,1,0:T(8,128)(2,1)}, u32[]{:S(2)}, u32[]{:S(2)}) collective-permute-start(bf16[1,256,640]{2,1,0:T(8,128)(2,1)} %get-tuple-element.212), channel_id=1, source_target_pairs={{0,8},{1,9},{2,10},{3,11},{4,12},{5,13},{6,14},{7,15},{8,0},{9,1},... | collective-permute-start | bytes 983048 | tf_op jit(solution)/shard_map/ppermute | solution.py:57
  543.3 38.0 %collective-permute-start.51 = (bf16[1,256,640]{2,1,0:T(8,128)(2,1)}, bf16[1,256,640]{2,1,0:T(8,128)(2,1)}, u32[]{:S(2)}, u32[]{:S(2)}) collective-permute-start(bf16[1,256,640]{2,1,0:T(8,128)(2,1)} %get-tuple-element.211), channel_id=1, source_target_pairs={{0,16},{1,17},{2,18},{3,19},{4,20},{5,21},{6,22},{7,23},{8,24},{9,... | collective-permute-start | bytes 983048 | tf_op jit(solution)/shard_map/ppermute | solution.py:57
  543.7 37.6 %collective-permute-start.52 = (bf16[1,256,640]{2,1,0:T(8,128)(2,1)S(1)}, bf16[1,256,640]{2,1,0:T(8,128)(2,1)}, u32[]{:S(2)}, u32[]{:S(2)}) collective-permute-start(bf16[1,256,640]{2,1,0:T(8,128)(2,1)S(1)} %get-tuple-element.210), channel_id=1, source_target_pairs={{0,24},{1,25},{2,26},{3,27},{4,28},{5,29},{6,30},{7,31},{8,16},{9,... | collective-permute-start | bytes 983048 | tf_op jit(solution)/shard_map/ppermute | solution.py:57
  584.9 92.7 %reduce-scatter.12.cloned.1.call-start = ((), (), s32[]{:S(2)}) async-start(), calls=%async_computation.13 | async-start | bytes 1638400 | tf_op jit(solution)/shard_map/reduce_scatter | solution.py:787
  589.8 16.2 %collective-permute-start.54 = (bf16[1,256,640]{2,1,0:T(8,128)(2,1)S(1)}, bf16[1,256,640]{2,1,0:T(8,128)(2,1)S(1)}, u32[]{:S(2)}, u32[]{:S(2)}) collective-permute-start(bf16[1,256,640]{2,1,0:T(8,128)(2,1)S(1)} %get-tuple-element.207), channel_id=1, source_target_pairs={{0,16},{1,17},{2,18},{3,19},{4,20},{5,21},{6,22},{7,23},{8,24},{9,... | collective-permute-start | bytes 983048 | tf_op jit(solution)/shard_map/ppermute | solution.py:57
  590.1 15.8 %collective-permute-start.55 = (bf16[1,256,640]{2,1,0:T(8,128)(2,1)S(1)}, bf16[1,256,640]{2,1,0:T(8,128)(2,1)S(1)}, u32[]{:S(2)}, u32[]{:S(2)}) collective-permute-start(bf16[1,256,640]{2,1,0:T(8,128)(2,1)S(1)} %get-tuple-element.206), channel_id=1, source_target_pairs={{0,24},{1,25},{2,26},{3,27},{4,28},{5,29},{6,30},{7,31},{8,16},{9,... | collective-permute-start | bytes 983048 | tf_op jit(solution)/shard_map/ppermute | solution.py:57
  591.3 115.3 %collective-permute-start.39 = (bf16[256,2048]{1,0:T(8,128)(2,1)}, bf16[256,2048]{1,0:T(8,128)(2,1)}, u32[]{:S(2)}, u32[]{:S(2)}) collective-permute-start(bf16[256,2048]{1,0:T(8,128)(2,1)} %fusion.50), channel_id=1, source_target_pairs={{0,16},{1,17},{2,18},{3,19},{4,12},{5,13},{6,14},{7,15},{8,24},{9,... | collective-permute-start | bytes 3145736 | tf_op jit(solution)/shard_map/ppermute | solution.py:57
  593.9 112.8 %collective-permute-start.41 = (bf16[256,2048]{1,0:T(8,128)(2,1)}, bf16[256,2048]{1,0:T(8,128)(2,1)}, u32[]{:S(2)}, u32[]{:S(2)}) collective-permute-start(bf16[256,2048]{1,0:T(8,128)(2,1)} %add_convert_fusion.7), channel_id=1, source_target_pairs={{0,8},{1,9},{2,10},{3,11},{4,20},{5,21},{6,22},{7,23},{8,0},{9,1},... | collective-permute-start | bytes 3145736 | tf_op jit(solution)/shard_map/ppermute | solution.py:57
  594.5 14.9 %collective-permute-start.49 = (f32[4,8,640]{2,1,0:T(8,128)S(1)}, f32[4,8,640]{2,1,0:T(8,128)S(1)}, u32[]{:S(2)}, u32[]{:S(2)}) collective-permute-start(f32[4,8,640]{2,1,0:T(8,128)S(1)} %get-tuple-element.119), channel_id=1, source_target_pairs={{0,7},{1,0},{2,1},{3,2},{4,3},{5,4},{6,5},{7,6},{8,15},{9,8},{10,9... | collective-permute-start | bytes 245768 | tf_op jit(solution)/shard_map/ppermute | solution.py:57
  617.8 21.4 %collective-permute-start.57 = (bf16[256,2048]{1,0:T(8,128)(2,1)S(1)}, bf16[256,2048]{1,0:T(8,128)(2,1)S(1)}, u32[]{:S(2)}, u32[]{:S(2)}) collective-permute-start(bf16[256,2048]{1,0:T(8,128)(2,1)S(1)} %convolution_add_fusion), channel_id=1, source_target_pairs={{0,16},{1,17},{2,18},{3,19},{4,12},{5,13},{6,14},{7,15},{8,24},{9,... | collective-permute-start | bytes 3145736 | tf_op jit(solution)/shard_map/ppermute | solution.py:57
  619.2 36.9 %collective-permute-start.56 = (bf16[256,2048]{1,0:T(8,128)(2,1)S(1)}, bf16[256,2048]{1,0:T(8,128)(2,1)S(1)}, u32[]{:S(2)}, u32[]{:S(2)}) collective-permute-start(bf16[256,2048]{1,0:T(8,128)(2,1)S(1)} %convolution_add_fusion.2), channel_id=1, source_target_pairs={{0,16},{1,17},{2,18},{3,19},{4,12},{5,13},{6,14},{7,15},{8,24},{9,... | collective-permute-start | bytes 3145736 | tf_op jit(solution)/shard_map/ppermute | solution.py:57
  639.6 23.2 %collective-permute-start.58 = (bf16[256,2048]{1,0:T(8,128)(2,1)S(1)}, bf16[256,2048]{1,0:T(8,128)(2,1)S(1)}, u32[]{:S(2)}, u32[]{:S(2)}) collective-permute-start(bf16[256,2048]{1,0:T(8,128)(2,1)S(1)} %add_convert_fusion.5), channel_id=1, source_target_pairs={{0,8},{1,9},{2,10},{3,11},{4,20},{5,21},{6,22},{7,23},{8,0},{9,1},... | collective-permute-start | bytes 3145736 | tf_op jit(solution)/shard_map/ppermute | solution.py:57
  704.9 9.9 %collective-permute-start.62 = (bf16[1,256,640]{2,1,0:T(8,128)(2,1)S(1)}, bf16[1,256,640]{2,1,0:T(8,128)(2,1)S(1)}, u32[]{:S(2)}, u32[]{:S(2)}) collective-permute-start(bf16[1,256,640]{2,1,0:T(8,128)(2,1)S(1)} %get-tuple-element.203), channel_id=1, source_target_pairs={{0,24},{1,25},{2,26},{3,27},{4,28},{5,29},{6,30},{7,31},{8,16},{9,... | collective-permute-start | bytes 983048 | tf_op jit(solution)/shard_map/ppermute | solution.py:57
  706.6 13.5 %collective-permute-start.61 = (bf16[1,256,640]{2,1,0:T(8,128)(2,1)S(1)}, bf16[1,256,640]{2,1,0:T(8,128)(2,1)S(1)}, u32[]{:S(2)}, u32[]{:S(2)}) collective-permute-start(bf16[1,256,640]{2,1,0:T(8,128)(2,1)S(1)} %get-tuple-element.204), channel_id=1, source_target_pairs={{0,16},{1,17},{2,18},{3,19},{4,20},{5,21},{6,22},{7,23},{8,24},{9,... | collective-permute-start | bytes 983048 | tf_op jit(solution)/shard_map/ppermute | solution.py:57
  706.7 13.4 %collective-permute-start.60 = (bf16[1,256,640]{2,1,0:T(8,128)(2,1)S(1)}, bf16[1,256,640]{2,1,0:T(8,128)(2,1)S(1)}, u32[]{:S(2)}, u32[]{:S(2)}) collective-permute-start(bf16[1,256,640]{2,1,0:T(8,128)(2,1)S(1)} %get-tuple-element.205), channel_id=1, source_target_pairs={{0,8},{1,9},{2,10},{3,11},{4,12},{5,13},{6,14},{7,15},{8,0},{9,1},... | collective-permute-start | bytes 983048 | tf_op jit(solution)/shard_map/ppermute | solution.py:57
  725.2 24.7 %collective-permute-start.64 = (bf16[1,256,640]{2,1,0:T(8,128)(2,1)S(1)}, bf16[1,256,640]{2,1,0:T(8,128)(2,1)S(1)}, u32[]{:S(2)}, u32[]{:S(2)}) collective-permute-start(bf16[1,256,640]{2,1,0:T(8,128)(2,1)S(1)} %get-tuple-element.201), channel_id=1, source_target_pairs={{0,2},{1,3},{2,0},{3,1},{4,6},{5,7},{6,4},{7,5},{8,10},{9,11},{10,... | collective-permute-start | bytes 983048 | tf_op jit(solution)/shard_map/ppermute | solution.py:57
  725.5 24.3 %collective-permute-start.63 = (bf16[1,256,640]{2,1,0:T(8,128)(2,1)S(1)}, bf16[1,256,640]{2,1,0:T(8,128)(2,1)S(1)}, u32[]{:S(2)}, u32[]{:S(2)}) collective-permute-start(bf16[1,256,640]{2,1,0:T(8,128)(2,1)S(1)} %get-tuple-element.199), channel_id=1, source_target_pairs={{0,1},{1,2},{2,3},{3,0},{4,5},{5,6},{6,7},{7,4},{8,9},{9,10},{10,1... | collective-permute-start | bytes 983048 | tf_op jit(solution)/shard_map/ppermute | solution.py:57
  726.9 23.9 %collective-permute-start.76 = (f32[4,1,48,640]{3,2,1,0:T(8,128)S(1)}, f32[4,1,48,640]{3,2,1,0:T(8,128)S(1)}, u32[]{:S(2)}, u32[]{:S(2)}) collective-permute-start(f32[4,1,48,640]{3,2,1,0:T(8,128)S(1)} %get-tuple-element.217), channel_id=1, source_target_pairs={{0,4},{1,5},{2,6},{3,7},{4,0},{5,1},{6,2},{7,3},{8,12},{9,13},{10,... | collective-permute-start | bytes 1474568 | tf_op jit(solution)/shard_map/ppermute | solution.py:57
  (153 other events, 1599.5 us)
Sparse Core Ops, SparseCore 0:
  16.1 36.4 all-gather.5
  54.8 54.4 all-gather.7
  110.9 67.3 all-gather.11
  179.7 63.3 all-gather.13
  263.6 64.7 all-gather.9
  354.6 60.3 reduce-scatter.5
  443.8 59.4 reduce-scatter.7
  509.3 61.3 reduce-scatter.9
  585.0 36.0 reduce-scatter.13
  623.3 29.9 reduce-scatter.11

commit v3 on v2

--- a/solution.py
+++ b/solution.py
@@ -96,19 +96,27 @@
 
     def gather_rows(self, x):
         first = self.one(x)
+        second = self.two(jnp.concatenate([x, first], axis=0))
+        return x, first, second
+
+    def gather_rows_early(self, x):
+        first = self.one(x)
         second = self.two(x)
         return x, first, second, self.two(first)
 
-    def gather_rows_direct(self, x):
-        return x, self.one(x), self.two(x), self.flip_p(x, 3)
-
-    def scatter_rows(self, parts):
+    def scatter_rows(self, far, near):
+        rows = near.shape[0] // 2
+        came = self.two(far.astype(bf16)).astype(f32)
+        joined = (near[rows:] + came[rows:]).astype(bf16)
+        return near[:rows] + came[:rows] + self.one(joined).astype(f32), joined
+
+    def scatter_rows_early(self, parts):
         far = self.two(parts[3].astype(bf16))
         side = self.two(parts[2].astype(bf16))
-        joined = (parts[1] + far.astype(f32)).astype(bf16)
-        return parts[0] + side.astype(f32) + self.one(joined).astype(f32), joined
-
-    def spread(self, x, p):
+        near = self.one((parts[1] + far.astype(f32)).astype(bf16))
+        return parts[0] + side.astype(f32) + near.astype(f32)
+
+    def spread(self, x, p, *others):
         groups = [
             [self.join(h, q, c, z) for h in range(self.high) for z in range(4)]
             for q in range(QUARTERS)
@@ -125,7 +133,7 @@
             )
 
         own = [self.flip_p(pick(m), m) for m in range(4)]
-        return every, [own, [self.core(a) for a in own]]
+        return every, [own, [self.core(after(a, *others)) for a in own]]
 
     def gather_rest(self, x, axis=0):
         groups = [
@@ -165,7 +173,16 @@
     return (offset & 1) * 2 + offset // 2
 
 
-def place_rows(info, chunk, first, shape):
+LANES = 128
+
+
+def wide(mask, width):
+    mask = jnp.where(mask, 1.0, 0.0)
+    return jnp.concatenate([mask] * (width // LANES), axis=1)
+
+
+def place_rows(info, chunk, first, count):
+    shape = (count, LANES)
     spot = info[chunk, 0] + first + lax.broadcasted_iota(jnp.int32, shape, 0)
     begin = jnp.zeros(shape, jnp.int32)
     for border in (1, 2, 3):
@@ -206,12 +223,13 @@
     def conv(t, _):
         base = pl.multiple_of(t * TILE, TILE)
         near = ext[pl.ds(base, 2 * TILE), :]
-        seg, _filled = place_rows(info, chunk, base, (TILE, width))
+        seg, _filled = place_rows(info, chunk, base, TILE)
         total = jnp.broadcast_to(vec[CONV_BIAS : CONV_BIAS + 1, :], (TILE, width))
         for lag in range(TAPS):
             moved = near[TILE - lag : 2 * TILE - lag]
             tap = vec[TAP_ROW + lag : TAP_ROW + lag + 1, :]
-            total = total + jnp.where(seg >= lag, tap * moved, 0.0)
+            moved = tap * moved
+            total = total + (wide(seg >= lag, width) * moved if lag else moved)
         low[0, pl.ds(base, TILE), :] = total.astype(bf16)
         return 0
 
@@ -221,13 +239,15 @@
     def tile(t, held):
         base = pl.multiple_of(t * TILE, TILE)
         span = pl.ds(base, TILE)
-        seg, filled = place_rows(info, chunk, base, (TILE, width))
+        seg, filled = place_rows(info, chunk, base, TILE)
         open_decay = sigmoid(pre[span, :width] + vec[DECAY_BIAS : DECAY_BIAS + 1, :])
         open_input = sigmoid(pre[span, width:] + vec[INPUT_BIAS : INPUT_BIAS + 1, :])
         log_decay = open_decay * vec[SLOPE : SLOPE + 1, :]
-        decay = jnp.where((seg != 0) & filled, jnp.exp(log_decay), 0.0)
-        factor = jnp.where(seg == 0, 1.0, jnp.sqrt(less_one(2.0 * log_decay)))
-        drive = jnp.where(filled, factor * open_input * low[0, span, :].astype(f32), 0.0)
+        decay = wide((seg != 0) & filled, width) * jnp.exp(log_decay)
+        factor = wide((seg == 0) & filled, width) + wide((seg != 0) & filled, width) * jnp.sqrt(
+            less_one(2.0 * log_decay)
+        )
+        drive = factor * open_input * low[0, span, :].astype(f32)
         dec[0, span, :] = decay
         entered, passed = held
         for half in range(TILE // 8):
@@ -294,8 +314,8 @@
 
 def backward_kernel(
     info, chan, rim, vec, dense, low, state, reach, enter, grad, moved, span_back, leave,
-    gates, chan_grad, rim_grad, sums,
-    ext, pre, past, later, conv_grad,
+    crossed, chan_grad, rim_grad, sums,
+    ext, pre, past, later, conv_grad, gates,
 ):
     chunk = pl.program_id(0)
     rows, width = chan.shape[1:]
@@ -310,6 +330,7 @@
     @pl.when(chunk == 0)
     def _():
         sums[...] = jnp.zeros_like(sums)
+        crossed[...] = jnp.zeros_like(crossed)
 
     def fill(t, _):
         base = pl.multiple_of(t * TILE, TILE)
@@ -328,8 +349,9 @@
     def tile(t, _):
         base = pl.multiple_of(t * TILE, TILE)
         span = pl.ds(base, TILE)
-        seg, filled = place_rows(info, chunk, base, (TILE, width))
-        restart = seg == 0
+        seg, filled = place_rows(info, chunk, base, TILE)
+        restart = wide((seg == 0) & filled, width)
+        going = wide((seg != 0) & filled, width)
         before = past[pl.ds(base, 2 * TILE), :][TILE - 1 : 2 * TILE - 1]
         adjoint = grad[0, span, :].astype(f32) + later[pl.ds(base, 2 * TILE), :][1 : TILE + 1]
         open_decay = sigmoid(pre[span, :width] + vec[DECAY_BIAS : DECAY_BIAS + 1, :])
@@ -340,19 +362,16 @@
         square = less_one(2.0 * log_decay)
         value = low[0, span, :].astype(f32)
         root = lax.rsqrt(square)
-        factor = jnp.where(restart, 1.0, square * root)
-        factor = jnp.where(square == 0.0, jnp.where(restart, 1.0, 0.0), factor)
-        opened = jnp.where(filled, open_input * adjoint, 0.0)
-        direct = factor * opened
+        root = jnp.where(going > 0.0, root, 0.0)
+        opened = open_input * adjoint
+        direct = (restart + square * root) * opened
         input_grad = direct * value * (1.0 - open_input)
-        log_grad = jnp.where(restart | ~filled, 0.0, adjoint * before * decay) - jnp.where(
-            restart, 0.0, opened * value * decay * decay * root
-        )
+        log_grad = going * decay * (adjoint * before - opened * value * decay * root)
         decay_grad = log_grad * slope * open_decay * (1.0 - open_decay)
         decay_low = decay_grad.astype(bf16)
         input_low = input_grad.astype(bf16)
-        gates[0, span, :width] = decay_low
-        gates[0, span, width:] = input_low
+        gates[span, :width] = decay_low
+        gates[span, width:] = input_low
         conv_grad[pl.ds(pl.multiple_of(base + TILE, TILE), TILE), :] = direct
         add(0, decay_low.astype(f32))
         add(1, input_low.astype(f32))
@@ -360,16 +379,17 @@
         return 0
 
     lax.fori_loop(0, rows // TILE, tile, 0)
-    conv_grad[TILE : rows + TILE] += plain(gates[0], dense[...])
+    conv_grad[TILE : rows + TILE] += plain(gates[...], dense[...])
+    crossed[...] += leading(gates[...], low[0])
 
     def taps(t, _):
         base = pl.multiple_of(t * TILE, TILE)
         near = conv_grad[pl.ds(base, 2 * TILE), :]
         back = jnp.zeros((TILE, width), f32)
         for lag in range(TAPS):
-            seg, _filled = place_rows(info, chunk, base - TILE + lag, (TILE, width))
-            tap = vec[TAP_ROW + lag : TAP_ROW + lag + 1, :]
-            back = back + jnp.where(seg >= lag, tap * near[lag : TILE + lag], 0.0)
+            seg, _filled = place_rows(info, chunk, base - TILE + lag, TILE)
+            tap = vec[TAP_ROW + lag : TAP_ROW + lag + 1, :] * near[lag : TILE + lag]
+            back = back + (wide(seg >= lag, width) * tap if lag else tap)
 
         @pl.when(t == 0)
         def _():
@@ -380,12 +400,13 @@
             at = pl.multiple_of(base - TILE, TILE)
             chan_grad[0, pl.ds(at, TILE), :] = back
             around = ext[pl.ds(at, 2 * TILE), :]
-            seg, _filled = place_rows(info, chunk, at, (TILE, width))
+            seg, _filled = place_rows(info, chunk, at, TILE)
             own = near[:TILE]
             add(3, own)
             for lag in range(TAPS):
                 moved_in = around[TILE - lag : 2 * TILE - lag]
-                add(4 + lag, jnp.where(seg >= lag, own * moved_in, 0.0))
+                moved_in = own * moved_in
+                add(4 + lag, wide(seg >= lag, width) * moved_in if lag else moved_in)
 
         return 0
 
@@ -470,7 +491,7 @@
     count, rows, width = chan.shape
     shape = jax.ShapeDtypeStruct
     outs = [
-        shape((count, rows, 2 * width), bf16),
+        shape((2 * width, width), f32),
         shape((count, rows, width), f32),
         shape((count, 8, width), f32),
         shape((8, width), f32),
@@ -482,13 +503,14 @@
         grid=(count,),
         out_shape=outs,
         in_specs=[in_smem(), *specs],
-        out_specs=[per_chunk(o) for o in outs[:3]] + [whole(outs[3])],
+        out_specs=[whole(outs[0]), per_chunk(outs[1]), per_chunk(outs[2]), whole(outs[3])],
         scratch_shapes=[
             pltpu.VMEM((rows + TILE, width), f32),
             pltpu.VMEM((rows, 2 * width), f32),
             pltpu.VMEM((rows + TILE, width), f32),
             pltpu.VMEM((rows + TILE, width), f32),
             pltpu.VMEM((rows + 2 * TILE, width), f32),
+            pltpu.VMEM((rows, 2 * width), bf16),
         ],
         compiler_params=params(),
         cost_estimate=pl.CostEstimate(
@@ -593,8 +615,8 @@
     low_one = (xs_one * gain_one).astype(bf16)
     rim_rows = places.next_rows(low_one[rows - TILE :])
 
-    def quarter(x, cuts):
-        every, pieces = places.spread(x, p)
+    def quarter(x, cuts, *others):
+        every, pieces = places.spread(x, p, *others)
         at = [
             (jnp.arange(high) * 4 + (p ^ m)) * 2 + core for core in (c, 1 - c) for m in range(4)
         ]
@@ -615,14 +637,14 @@
     share = -(-small.shape[0] // (total_dp * TILE)) * TILE
     small = jnp.pad(small, ((0, share * total_dp - small.shape[0]), (0, 0)))
     small = lax.dynamic_slice_in_dim(small, dp_at * share, share, 0)
+    held = places.gather_rows_early(jnp.concatenate([rim_rows, low_one], axis=0))
+    low_rows = jnp.concatenate([a[TILE:] for a in held], axis=0)
+    rim_low = jnp.concatenate([a[:TILE] for a in held], axis=0)
     early, (mixer_own, small) = quarter(
-        jnp.concatenate([mixer_weight, small], axis=0), (slab, share)
+        jnp.concatenate([mixer_weight, small], axis=0), (slab, share), held[2]
     )
     vectors = small[:TILE].astype(f32)
     gate_turned = small[TILE : TILE + 2 * block_width]
-    held = places.gather_rows(jnp.concatenate([rim_rows, low_one], axis=0))
-    low_rows = jnp.concatenate([a[TILE:] for a in held], axis=0)
-    rim_low = jnp.concatenate([a[:TILE] for a in held], axis=0)
     middle, (branch_own, output_own) = quarter(
         after(jnp.concatenate([branch_weight, output_weight.T], axis=0), early, held[3]),
         (slab, slab),
@@ -643,21 +665,25 @@
 
     channels = (plain(low_rows, mixer_own) + vec[MIXER_BIAS]).astype(bf16)
     rim = (plain(rim_low, mixer_own) + vec[MIXER_BIAS]).astype(bf16)
-    feed_held = places.gather_rows_direct(after(cotangent, mixer_own))
-    feed_grad = jnp.concatenate(feed_held, axis=0)
-    channels = channels.reshape(QUARTERS, rows, width)
+    grad_near = places.one(after(cotangent, mixer_own))
+    channels = after(channels, grad_near).reshape(QUARTERS, rows, width)
     rim = rim.reshape(QUARTERS, TILE, width)
     conv_low, decays, state_local, reach = run_forward(info, channels, rim, vec, dense)
+    grad_late = after(cotangent, conv_low)
+    grad_held = (cotangent, grad_near, places.two(grad_late), places.flip_p(grad_late, 3))
+    feed_grad = jnp.concatenate(grad_held, axis=0)
     gate_use = places.gather_rest(after(gate_weight.T, mixer_own))
-    up_use = places.gather_rest(after(up_weight.T, conv_low))
+    up_use = places.gather_rest(after(up_weight.T, mixer_own))
+    down_use = places.gather_rest(after(down_weight, conv_low))
     branch_pre = plain(low_rows, branch_own) + vec[BRANCH_BIAS]
 
-    def entering(parts, back, others=()):
-        pair = jnp.stack([parts, places.core(parts)])
+    def entering(parts, back):
+        other = places.core(parts)
+        pair = jnp.stack([parts, other])
         every = jnp.stack([pair] + [places.along_z(pair, k) for k in (1, 2, 3)])
-        own, total = run_chain(spot, after(every, *others), back)
+        own, total = run_chain(spot, every, back)
         if high == 1:
-            return own[:, 1:2]
+            return own[:, 1:2], other
         held = [total]
         for _ in range(high - 1):
             held.append(places.along_h(held[-1]))
@@ -668,29 +694,38 @@
             picked = lax.dynamic_index_in_dim(jnp.stack(held), far, 0, False)
             ahead = source > h if back else source < h
             state = jnp.where(ahead, picked[0:1] * state + picked[1:2], state)
-        return own[:, 1:2] + own[:, 0:1] * state[None]
-
-    enter = entering(jnp.stack([reach[:, -1], state_local[:, -1]], axis=1), False, feed_held)
-    down_use = places.gather_rest(after(down_weight, enter))
-    branch_act, gelu_back_one = jax.vjp(jax.nn.gelu, branch_pre)
+        return own[:, 1:2] + own[:, 0:1] * state[None], other
+
+    enter, _ = entering(jnp.stack([reach[:, -1], state_local[:, -1]], axis=1), False)
     state_low = (state_local + reach * enter).astype(bf16).reshape(QUARTERS * rows, width)
-    mixed_low = (branch_act * state_low.astype(f32)).astype(bf16)
-
-    def rows_of(array, k):
-        return array[k * rows : (k + 1) * rows]
-
-    resid_sum, _ = places.scatter_rows(
-        [trailing(rows_of(mixed_low, k), output_own) for k in range(QUARTERS)]
+    mixed_low = (jax.nn.gelu(branch_pre) * state_low.astype(f32)).astype(bf16)
+
+    two_rows = 2 * rows
+    mixed_low = after(mixed_low, grad_held[2], grad_held[3])
+    resid_sum = places.scatter_rows_early(
+        [trailing(mixed_low[k * rows : (k + 1) * rows], output_own) for k in range(QUARTERS)]
+    )
+    both_own = jnp.concatenate(
+        [after(branch_own, mixed_low), after(mixer_own, mixed_low)], axis=1
+    )
+    pre_late = after(branch_pre, mixed_low)
+    branch_act, gelu_back_one = jax.vjp(jax.nn.gelu, pre_late)
+    branch_slope = gelu_back_one(state_low.astype(f32))[0]
+    resid_sum, branch_act, branch_slope, both_own = lax.optimization_barrier(
+        (resid_sum, branch_act, branch_slope, both_own)
     )
     resid = inputs + resid_sum
 
     rs_two, xs_two = normed(resid)
     low_two = (xs_two * gain_two).astype(bf16)
-    feed_rows = jnp.concatenate(places.gather_rows(low_two), axis=0)
+    feed_held = places.gather_rows(low_two)
+    feed_rows = jnp.concatenate(feed_held, axis=0)
     gate_pre = trailing(feed_rows, gate_use)
     up_pre = trailing(feed_rows, up_use)
     gate_act, gelu_back_two = jax.vjp(jax.nn.gelu, gate_pre)
-    hidden = (gate_act * up_pre).astype(bf16)
+    hidden, gate_act, gate_slope = lax.optimization_barrier(
+        ((gate_act * up_pre).astype(bf16), gate_act, gelu_back_two(up_pre)[0])
+    )
     half = hidden.shape[1] // 2
 
     def columns(array, core):
@@ -717,14 +752,14 @@
     down_own = column_own(hidden, feed_grad, down_far)
     down_scattered = column_scatter(down_own)
     hidden_grad = trailing(feed_grad, after(down_use, down_own))
-    gate_grad = gelu_back_two(hidden_grad * up_pre)[0].astype(bf16)
+    gate_grad = (hidden_grad * gate_slope).astype(bf16)
     up_grad = (hidden_grad * gate_act).astype(bf16)
-    def norm_part(k, gate_in, up_in):
-        return plain(rows_of(gate_in, k), gate_use) + plain(rows_of(up_in, k), up_use)
-
-    norm_parts = [norm_part(k, gate_grad, up_grad) for k in range(QUARTERS)]
-    norm_grad, _ = places.scatter_rows(norm_parts)
-    gate_late, *_ = lax.optimization_barrier((gate_grad, *norm_parts))
+    def norm_part(span):
+        return plain(gate_grad[span], gate_use) + plain(up_grad[span], up_use)
+
+    norm_far, norm_near = norm_part(slice(two_rows, None)), norm_part(slice(two_rows))
+    norm_grad, _ = places.scatter_rows(norm_far, norm_near)
+    gate_late, *_ = lax.optimization_barrier((gate_grad, norm_far, norm_near))
     gate_far = column_far(gate_late, feed_rows)
     norm_grad = after(norm_grad, gate_far)
     second_term = jnp.sum(norm_grad * xs_two, axis=0)
@@ -738,26 +773,29 @@
     gate_own = column_own(gate_last, feed_rows, gate_far)
     gate_scattered = column_scatter(gate_own)
     up_far = column_far(up_late, feed_rows)
-    output_terms = [plain(rows_of(hidden_last, k), down_use) for k in range(QUARTERS)]
-    resid_rows, *output_terms = lax.optimization_barrier(
-        (resid_rows, *output_terms, up_far, gate_own, down_scattered)
-    )[:-3]
-    output, output_joined = places.scatter_rows(output_terms)
+    output_far = plain(hidden_last[two_rows:], down_use)
+    output_near = plain(hidden_last[:two_rows], down_use)
+    resid_rows, output_far, output_near, *_ = lax.optimization_barrier(
+        (resid_rows, output_far, output_near, up_far, gate_own, down_scattered)
+    )
+    output, output_joined = places.scatter_rows(output_far, output_near)
     output = (resid + output).astype(bf16)
     mixed_grad = plain(resid_rows, output_own)
     state_grad = (mixed_grad * branch_act).astype(bf16).reshape(QUARTERS, rows, width)
-    branch_grad = gelu_back_one(mixed_grad * state_low.astype(f32))[0].astype(bf16)
+    branch_grad = (mixed_grad * branch_slope).astype(bf16)
     moved, span_back = run_reverse(decays, state_grad)
-    resid_late, mixed_late, low_late, branch_late, up_last, _ = lax.optimization_barrier(
-        (resid_rows, mixed_low, low_rows, branch_grad, up_late, moved)
-    )
-    leave = entering(jnp.stack([span_back[:, 0], moved[:, 0]], axis=1), True)
-    def quarter_half(term):
+    leave, other = entering(jnp.stack([span_back[:, 0], moved[:, 0]], axis=1), True)
+    up_last = after(up_late, other)
+    resid_late, mixed_late, _ = lax.optimization_barrier((resid_rows, mixed_low, other))
+
+    def quarter_half(term, *others):
         slab_in = term.shape[0] // total_dp
         term = term.astype(bf16).reshape(high * 4, 2 * slab_in, width)
         own = lax.dynamic_slice_in_dim(term, c * slab_in, slab_in, 1)
-        came = places.core(lax.dynamic_slice_in_dim(term, (1 - c) * slab_in, slab_in, 1))
-        return (own + came).reshape(high, 4, slab_in, width), came
+        other = lax.dynamic_slice_in_dim(term, (1 - c) * slab_in, slab_in, 1)
+        came = places.core(other)
+        half = own + after(came, *others)
+        return half.reshape(high, 4, slab_in, width), other, came
 
     def quarter_rows(half):
         return [
@@ -781,27 +819,26 @@
             total = total + places.along_z(by(k), k).astype(f32)
         return quarter_high(total)
 
-    def quarter_far(parts, gates):
-        *parts, _ = lax.optimization_barrier((*parts, gates))
+    def quarter_far(parts, other):
+        *parts, _ = lax.optimization_barrier((*parts, other))
         stacked = jnp.take(jnp.stack(parts), p ^ straight, axis=0)
         return quarter_high(lax.psum_scatter(stacked, "blk", scatter_dimension=0, tiled=True)[0])
 
     output_term = leading(resid_late, mixed_late)
-    branch_term = leading(low_late, branch_late)
     up_own = column_own(up_last, feed_rows, up_far)
     up_scattered = column_scatter(up_own)
-    output_half, output_came = quarter_half(output_term)
-    branch_half, branch_came = quarter_half(branch_term)
-    leave = after(leave, output_came, branch_came, output_joined, up_own, gate_scattered)
+    output_half, _, _ = quarter_half(output_term)
+    leave, output_half, *_ = lax.optimization_barrier(
+        (leave, output_half, output_joined, up_own, gate_scattered)
+    )
     output_parts = quarter_rows(output_half)
-    branch_parts = quarter_rows(branch_half)
-    gates, chan_grad, rim_grad, sums = run_backward(
+    crossed, chan_grad, rim_grad, sums = run_backward(
         info, channels, rim, vec, dense, conv_low, state_local, reach, enter, state_grad, moved,
         span_back, leave,
     )
 
-    output_sum = quarter_far(output_parts, gates).T
-    branch_sum = quarter_far(branch_parts, gates)
+    low_late, branch_late, _ = lax.optimization_barrier((low_rows, branch_grad, rim_grad))
+    branch_term = leading(low_late, branch_late)
 
     came = places.back_rows(rim_grad)
     last = (c == 1) & (z == 3)
@@ -818,29 +855,10 @@
     returned = picked(pick * here, came)
     if high > 1:
         returned = returned + picked(pick * (1.0 - here), places.back_high(came))
+    output_sum = quarter_far(output_parts, came).T
     chan_grad = chan_grad + jnp.pad(returned, ((0, 0), (rows - 8, 0), (0, 0)))
-    mixer_grad = after(chan_grad, *output_parts, *branch_parts, up_scattered).astype(bf16)
-    mixer_grad = mixer_grad.reshape(QUARTERS * rows, width)
-
-    low_parts = [
-        trailing(rows_of(branch_grad, k), branch_own) + trailing(rows_of(mixer_grad, k), mixer_own)
-        for k in range(QUARTERS)
-    ]
-    low_grad, _ = places.scatter_rows(low_parts)
-    mixer_late, *_ = lax.optimization_barrier((mixer_grad, *low_parts))
-    mixer_term = leading(low_rows, mixer_late)
-    mixer_half, mixer_came = quarter_half(mixer_term)
-    mixer_sum = quarter_near(quarter_rows(mixer_half))
-    gates, mixer_term, _ = lax.optimization_barrier((gates, mixer_term, mixer_came))
-    token_grad = (resid_grad + norm_back(rs_one, xs_one, gain_one, low_grad)).astype(bf16)
-
-    first_term = (
-        jnp.sum(branch_term * branch_own.astype(f32), axis=1)
-        + jnp.sum(mixer_term * mixer_own.astype(f32), axis=1)
-    ) / gain_one
-    gain_sums = places.sum_all(jnp.stack([first_term, second_term]))
-
-    crossed = leading(gates.reshape(QUARTERS * rows, 2 * width), conv_low.reshape(-1, width))
+    mixer_grad = chan_grad.astype(bf16).reshape(QUARTERS * rows, width)
+
     picked_blocks = block_of[None, :] == jnp.arange(heads)[:, None]
     gate_terms = jnp.sum(
         jnp.where(picked_blocks[None, :, None, :], crossed.reshape(2, heads, block_width, width), 0),
@@ -859,14 +877,43 @@
     vector_terms = vector_terms.at[2].multiply(slope_back)
     small_terms = jnp.concatenate(
         [vector_terms, gate_terms.reshape(2 * block_width, width)], axis=0
-    )
+    ).astype(bf16)
     small_terms = jnp.pad(small_terms, ((0, share * total_dp - small_terms.shape[0]), (0, 0)))
-    small_sum = quarter_near(quarter_rows(quarter_half(small_terms)[0]))
+    branch_term, branch_both = lax.optimization_barrier((branch_term, branch_term.astype(bf16)))
+    branch_both = jnp.concatenate(
+        [branch_both.reshape(total_dp, slab, width), small_terms.reshape(total_dp, share, width)],
+        axis=1,
+    ).reshape(-1, width)
+    mixer_term = leading(low_rows, mixer_grad)
+    mixer_half, mixer_other, mixer_came = quarter_half(mixer_term)
+    both_grads = jnp.concatenate([branch_grad, mixer_grad], axis=1)
+    both_grads = after(both_grads, mixer_other)
+    low_far = trailing(both_grads[two_rows:], both_own).astype(bf16)
+    both_near, low_far, mixer_half, _ = lax.optimization_barrier(
+        (both_grads[:two_rows], low_far, mixer_half, mixer_came)
+    )
+    branch_half, _, _ = quarter_half(after(branch_both, low_far))
+    branch_parts = quarter_rows(branch_half)
+    mixer_parts = quarter_rows(mixer_half)
+    low_near = trailing(both_near, both_own)
+    low_grad, low_joined = places.scatter_rows(low_far, low_near)
+    branch_sum = quarter_far(branch_parts, low_near)
+    mixer_sum = quarter_near(mixer_parts)
+    mixer_term, second_term, _ = lax.optimization_barrier((mixer_term, second_term, low_grad))
+    token_grad = (resid_grad + norm_back(rs_one, xs_one, gain_one, low_grad)).astype(bf16)
+
+    first_term = (
+        jnp.sum(branch_term * branch_own.astype(f32), axis=1)
+        + jnp.sum(mixer_term * mixer_own.astype(f32), axis=1)
+    ) / gain_one
+    gain_sums = places.sum_all(jnp.stack([first_term, second_term]))
+
+    branch_sum, small_sum = branch_sum[:slab], branch_sum[slab:]
     small_held = [small_sum]
     for _ in range(high - 1):
         small_held.append(places.along_h(small_held[-1]))
     small_held = jnp.stack(small_held)
-    small_held = jnp.stack(places.gather_rows(small_held))
+    small_held = jnp.concatenate(places.gather_rows(small_held), axis=0)
     small_held = jnp.stack([small_held, places.core(small_held)])
     where = []
     for hh in range(high):

time: 776 us -> 740 us (0.954)
  waiting for transfers between devices: 266 us -> 226 us
  other arithmetic: 53.7 us -> 82 us
  starting transfers between devices: 112 us -> 98.1 us
  matrix products: 186 us -> 174 us
    ppermute x82 -> x69, waiting for transfers between devices: 263 us -> 218 us  [send(): return jax.tree.map(lambda a: lax.ppermute(a, AXES, pairs), x)]
    ppermute x82 -> x69, starting transfers between devices: 111 us -> 97.6 us  [send(): return jax.tree.map(lambda a: lax.ppermute(a, AXES, pairs), x)]
    dot_general x16 -> x10, matrix products: 58.8 us -> 48.1 us  [plain(): return jnp.dot(former, latter, preferred_element_type=f32)]
    concatenate x1 -> x7, other arithmetic: 0.07 us -> 8.68 us  [the longest x3 3.57 us: gather_rows(): second = self.two(jnp.concatenate([x, first], axis=0))]
    unnamed x252 -> x250, local copies, waits for them, and re-layouts: 38.6 us -> 46.5 us
    dot_general x10 -> x9, matrix products: 66.7 us -> 65.1 us  [leading(): lax.dot_general(former, latter, (((0,), (0,)), ((), ())), preferred_eleme...]
    dot_general x15 -> x9, matrix products: 60.4 us -> 60.7 us  [trailing(): lax.dot_general(former, latter, (((1,), (1,)), ((), ())), preferred_eleme...]
  transfers between devices with their start and end apart: 92 -> 79, of which waited for: 36 -> 32; matrix products, arithmetic and copies ran while one was open for 36% -> 39% of each run, Pallas kernels for 7% -> 7%
where the time goes in v3:
time: 740 us; the launch traced here: 730 us
  waiting for transfers between devices  226 us (31%)
  matrix products  174 us (24%)
  starting transfers between devices  98.1 us (13%)
  other arithmetic  82 us (11%)
  local copies, waits for them, and re-layouts  78.8 us (11%)
  Pallas kernels  54.2 us (7%)
  between operations  16.4 us (2%)
    ppermute x69, waiting for transfers between devices, send(): return jax.tree.map(lambda a: lax.ppermute(a, AXES, pairs), x)  218 us
    ppermute x69, starting transfers between devices, send(): return jax.tree.map(lambda a: lax.ppermute(a, AXES, pairs), x)  97.6 us
    dot_general x9, matrix products, leading(): lax.dot_general(former, latter, (((0,), (0,)), ((), ())), preferred_eleme...  65.1 us
    dot_general x9, matrix products, trailing(): lax.dot_general(former, latter, (((1,), (1,)), ((), ())), preferred_eleme...  60.7 us
    dot_general x10, matrix products, plain(): return jnp.dot(former, latter, preferred_element_type=f32)  48.1 us
    unnamed x250, local copies, waits for them, and re-layouts  46.5 us
    pallas_call x1, Pallas kernels, run_backward(): pl.pallas_call(backward_kernel, grid=(count,), out_shape=outs, in_specs=[...  28.8 us
    pallas_call x1, Pallas kernels, run_forward(): pl.pallas_call(forward_kernel, grid=(count,), out_shape=outs, in_specs=[i...  15.1 us
  transfers between devices with their start and end apart: 79, of which 32 were waited for; matrix products, arithmetic and copies ran while one was open for 39% of the time, Pallas kernels for 7%

profile of v3, /device:TPU:3, one launch (start us, length us, event | category | flops | bytes accessed | tf_op | source)
XLA Modules:
  0.0 729.7 jit_solution(9997298024558121592)
XLA Ops:
  11.3 3.3 collective-permute-start
  16.1 3.6 collective-permute-done
  20.9 13.7 %collective-permute-done.1 = bf16[272,2048]{1,0:T(8,128)(2,1)} collective-permute-done((bf16[272,2048]{1,0:T(8,128)(2,1)S(1)}, bf16[272,2048]{1,0:T(8,128)(2,1)}, u32[]{:S(2)}, u32[]{:S(2)}) %collective-permute-start.1) | collective-permute-done | bytes 1114144 | tf_op jit(solution)/shard_map/ppermute | solution.py:57
  35.7 13.9 %collective-permute-done.3 = bf16[272,2048]{1,0:T(8,128)(2,1)S(1)} collective-permute-done((bf16[272,2048]{1,0:T(8,128)(2,1)}, bf16[272,2048]{1,0:T(8,128)(2,1)S(1)}, u32[]{:S(2)}, u32[]{:S(2)}) %collective-permute-start.3) | collective-permute-done | bytes 1114144 | tf_op jit(solution)/shard_map/ppermute | solution.py:57
  49.6 3.1 all-gather.6.cloned.1.call-done
  57.3 17.6 %collective-permute-done.2 = bf16[272,2048]{1,0:T(8,128)(2,1)S(1)} collective-permute-done((bf16[272,2048]{1,0:T(8,128)(2,1)}, bf16[272,2048]{1,0:T(8,128)(2,1)S(1)}, u32[]{:S(2)}, u32[]{:S(2)}) %collective-permute-start.2) | collective-permute-done | bytes 1114144 | tf_op jit(solution)/shard_map/ppermute | solution.py:57
  75.9 3.5 collective-permute-start.14
  80.3 6.4 collective-permute-start.16
  111.6 4.5 add_convert_fusion.5
  116.0 3.2 constant_dynamic-slice_fusion.8
  135.2 15.1 %shard_map.341 = (bf16[4,256,640]{2,1,0:T(8,128)(2,1)S(1)}, f32[4,256,640]{2,1,0:T(8,128)S(1)}, f32[4,256,640]{2,1,0:T(8,128)S(1)}, f32[4,256,640]{2,1,0:T(8,128)S(1)}) custom-call(s32[4,5]{1,0:T(4,128)S(1)} %pad_add_fusion.info, bf16[4,256,640]{2,1,0:T(8,128)(2,1)S(1)} %bitcast.196, bf16[4,16,640]{2,1,0:T(8,128)(2,1)S(1)} %bitcast.198, ...), custom_call_target="tpu_custom_call" | custom-call | flops 1677721600 | bytes 55050240 | tf_op jit(solution)/shard_map/pallas_call | solution.py:437
  154.6 4.7 collective-permute-done.20
  162.4 3.6 collective-permute-start.22
  172.8 3.4 shard_map.339
  176.2 4.0 fusion.23
  180.2 9.5 %collective-permute-done.23 = bf16[256,2048]{1,0:T(8,128)(2,1)} collective-permute-done((bf16[256,2048]{1,0:T(8,128)(2,1)S(1)}, bf16[256,2048]{1,0:T(8,128)(2,1)}, u32[]{:S(2)}, u32[]{:S(2)}) %collective-permute-start.23) | collective-permute-done | bytes 1048608 | tf_op jit(solution)/shard_map/ppermute | solution.py:57
  189.8 16.3 %collective-permute-done.24 = bf16[256,2048]{1,0:T(8,128)(2,1)} collective-permute-done((bf16[256,2048]{1,0:T(8,128)(2,1)S(1)}, bf16[256,2048]{1,0:T(8,128)(2,1)}, u32[]{:S(2)}, u32[]{:S(2)}) %collective-permute-start.24) | collective-permute-done | bytes 1048608 | tf_op jit(solution)/shard_map/ppermute | solution.py:57
  209.7 11.5 %collective-permute-done.26 = bf16[256,2048]{1,0:T(8,128)(2,1)S(1)} collective-permute-done((bf16[256,2048]{1,0:T(8,128)(2,1)S(1)}, bf16[256,2048]{1,0:T(8,128)(2,1)S(1)}, u32[]{:S(2)}, u32[]{:S(2)}) %collective-permute-start.26) | collective-permute-done | bytes 1048608 | tf_op jit(solution)/shard_map/ppermute | solution.py:57
  225.2 3.6 fusion.15
  228.8 9.1 %collective-permute-done.25 = bf16[256,2048]{1,0:T(8,128)(2,1)S(1)} collective-permute-done((bf16[256,2048]{1,0:T(8,128)(2,1)S(1)}, bf16[256,2048]{1,0:T(8,128)(2,1)S(1)}, u32[]{:S(2)}, u32[]{:S(2)}) %collective-permute-start.25) | collective-permute-done | bytes 1048608 | tf_op jit(solution)/shard_map/ppermute | solution.py:57
  237.9 6.4 collective-permute-done.27
  248.2 12.8 %collective-permute-done.28 = bf16[256,2048]{1,0:T(8,128)(2,1)S(1)} collective-permute-done((bf16[256,2048]{1,0:T(8,128)(2,1)S(1)}, bf16[256,2048]{1,0:T(8,128)(2,1)S(1)}, u32[]{:S(2)}, u32[]{:S(2)}) %collective-permute-start.28) | collective-permute-done | bytes 1048608 | tf_op jit(solution)/shard_map/ppermute | solution.py:57
  271.3 16.8 %collective-permute-done.29 = bf16[512,2048]{1,0:T(8,128)(2,1)} collective-permute-done((bf16[512,2048]{1,0:T(8,128)(2,1)}, bf16[512,2048]{1,0:T(8,128)(2,1)}, u32[]{:S(2)}, u32[]{:S(2)}) %collective-permute-start.29) | collective-permute-done | bytes 2097184 | tf_op jit(solution)/shard_map/ppermute | solution.py:57
  288.1 11.7 %fusion.118 = f32[1024,1536]{1,0:T(8,128)} fusion(bf16[1536,2048]{1,0:T(8,128)(2,1)} %all-gather.14.cloned.1.call-done, bf16[512,2048]{1,0:T(8,128)(2,1)} %collective-permute-done.29, bf16[256,2048]{1,0:T(8,128)(2,1)} %copy-done.81, bf16[256,2048]{1,0:T(8,128)(2,1)} %copy-done.67), kind=kOutput, calls=%fused_computation.319 | convolution fusion | flops 6455033856 | bytes 16777216 | tf_op jit(solution)/shard_map/dot_general | solution.py:30
  299.9 19.3 %fusion.5 = (f32[1024,1536]{1,0:T(8,128)}, bf16[1024,1536]{1,0:T(8,128)(2,1)}, f32[1024,1536]{1,0:T(8,128)}) fusion(f32[1024,1536]{1,0:T(8,128)} %fusion.118, bf16[1536,2048]{1,0:T(8,128)(2,1)} %all-gather.12.cloned.1.call-done, bf16[512,2048]{1,0:T(8,128)(2,1)} %collective-permute-done.29, bf16[256,2048]{1,0:T(8,128)(2,1)} %copy-done.81, ...), kind=kOutput, calls=%fused_computation.11 | convolution fusion | flops 6489636864 | bytes 32505856 | tf_op jit(solution)/shard_map/dot_general | solution.py:30
  319.2 7.8 %convolution_convert_fusion.2 = bf16[768,2048]{1,0:T(8,128)(2,1)} fusion(bf16[1024,2048]{1,0:T(8,128)(2,1)} %constant_dynamic-update-slice_fusion, bf16[1024,1536]{1,0:T(8,128)(2,1)} %get-tuple-element.132, s32[]{:T(128)S(6)} %select_n.408), kind=kOutput, calls=%fused_computation.33 | convolution fusion | flops 3222798336 | bytes 8912900 | tf_op jit(solution)/shard_map/dot_general | solution.py:34
  328.5 5.6 collective-permute-done.30
  334.1 8.7 %add_convert_fusion.2 = bf16[768,2048]{1,0:T(8,128)(2,1)} fusion(bf16[768,2048]{1,0:T(8,128)(2,1)} %collective-permute-done.30, bf16[1024,2048]{1,0:T(8,128)(2,1)} %constant_dynamic-update-slice_fusion, bf16[1024,1536]{1,0:T(8,128)(2,1)} %get-tuple-element.132, s32[]{:T(128)S(6)} %select_n.407), kind=kOutput, calls=%fused_computation.16 | convolution fusion | flops 3225944064 | bytes 12058628 | tf_op jit(solution)/shard_map/dot_general | solution.py:34
  342.9 12.8 %multiply_convert_fusion = (bf16[1024,1536]{1,0:T(8,128)(2,1)S(1)}, bf16[1024,1536]{1,0:T(8,128)(2,1)S(1)}) fusion(f32[1024,1536]{1,0:T(8,128)} %get-tuple-element.129, f32[1024,1536]{1,0:T(8,128)} %get-tuple-element.128, bf16[1024,2048]{1,0:T(8,128)(2,1)} %constant_dynamic-update-slice_fusion, bf16[1536,2048]{1,0:T(8,128)(2,1)} %all-gather.10.cloned.1.call-done), kind=kOutput, calls=%fused_computation.14 | convolution fusion | flops 6448742400 | bytes 29360128 | tf_op jit(solution)/shard_map/dot_general | solution.py:30
  355.8 6.8 fusion.44
  362.6 7.3 %convolution_add_fusion = bf16[512,2048]{1,0:T(8,128)(2,1)S(1)} fusion(f32[512,2048]{1,0:T(8,128)S(1)} %fusion.44, bf16[1536,2048]{1,0:T(8,128)(2,1)} %all-gather.14.cloned.1.call-done, bf16[1024,1536]{1,0:T(8,128)(2,1)S(1)} %get-tuple-element.146), kind=kOutput, calls=%fused_computation.40 | convolution fusion | flops 3223322624 | bytes 14155776 | tf_op jit(solution)/shard_map/dot_general | solution.py:26
  370.4 3.5 fusion.47
  374.0 3.4 convolution_add_fusion.1
  377.4 5.1 convolution_convert_fusion.1
  383.1 12.2 %collective-permute-done.31 = bf16[512,2048]{1,0:T(8,128)(2,1)S(1)} collective-permute-done((bf16[512,2048]{1,0:T(8,128)(2,1)S(1)}, bf16[512,2048]{1,0:T(8,128)(2,1)S(1)}, u32[]{:S(2)}, u32[]{:S(2)}) %collective-permute-start.31) | collective-permute-done | bytes 2097184 | tf_op jit(solution)/shard_map/ppermute | solution.py:57
  396.4 13.8 %collective-permute-done.32 = bf16[256,2048]{1,0:T(8,128)(2,1)S(1)} collective-permute-done((bf16[256,2048]{1,0:T(8,128)(2,1)S(1)}, bf16[256,2048]{1,0:T(8,128)(2,1)S(1)}, u32[]{:S(2)}, u32[]{:S(2)}) %collective-permute-start.32) | collective-permute-done | bytes 1048608 | tf_op jit(solution)/shard_map/ppermute | solution.py:57
  413.3 7.1 add_convert_fusion.1
  420.5 6.8 collective-permute-done.33
  429.7 8.1 %convolution_convert_fusion = bf16[768,2048]{1,0:T(8,128)(2,1)} fusion(bf16[1024,1536]{1,0:T(8,128)(2,1)} %copy-done.112, s32[]{:T(128)S(6)} %select_n.408, bf16[512,2048]{1,0:T(8,128)(2,1)} %collective-permute-done.29, bf16[256,2048]{1,0:T(8,128)(2,1)S(1)} %copy-done.83, bf16[256,2048]{1,0:T(8,128)(2,1)S(1)} %copy-done.69), kind=kOutput, calls=%fused_computation.31 | convolution fusion | flops 3235381248 | bytes 8912900 | tf_op jit(solution)/shard_map/dot_general | solution.py:34
  440.3 5.0 fusion.52
  445.3 4.6 fusion.54
  449.9 4.6 collective-permute-done.34
  454.6 3.3 pad_maximum_fusion.3
  457.9 8.4 %convert_reduce_fusion.1 = (bf16[640]{0:T(1024)(128)(2,1)S(1)}, bf16[1024,640]{1,0:T(8,128)(2,1)}, bf16[1024,640]{1,0:T(8,128)(2,1)S(1)}) fusion(f32[1024,640]{1,0:T(8,128)} %get-tuple-element.138, f32[1024,640]{1,0:T(8,128)} %get-tuple-element.139, bf16[1024,2048]{1,0:T(8,128)(2,1)} %pad_maximum_fusion.3, bf16[2048,640]{1,0:T(8,128)(2,1)S(1)} %copy-done.3), kind=kOutput, calls=%fused_computation.68 | convolution fusion | flops 2688286208 | bytes 14681344 | tf_op jit(solution)/shard_map/dot_general | solution.py:26
  472.7 3.7 collective-permute-start.38
  477.3 6.2 convolution_convert_fusion.3
  490.0 7.7 %add_convert_fusion = bf16[768,2048]{1,0:T(8,128)(2,1)} fusion(bf16[768,2048]{1,0:T(8,128)(2,1)} %collective-permute-done.43, bf16[1024,1536]{1,0:T(8,128)(2,1)S(1)} %copy-done.113, s32[]{:T(128)S(6)} %select_n.407, bf16[512,2048]{1,0:T(8,128)(2,1)} %collective-permute-done.29, bf16[256,2048]{1,0:T(8,128)(2,1)S(1)} %copy-done.84, ...), kind=kOutput, calls=%fused_computation.12 | convolution fusion | flops 3238526976 | bytes 12058628 | tf_op jit(solution)/shard_map/dot_general | solution.py:34
  518.8 28.8 %shard_map.345 = (f32[1280,640]{1,0:T(8,128)}, f32[4,256,640]{2,1,0:T(8,128)S(1)}, f32[4,8,640]{2,1,0:T(8,128)S(1)}, f32[8,640]{1,0:T(8,128)S(1)}) custom-call(s32[4,5]{1,0:T(4,128)S(1)} %copy-done.43, bf16[4,256,640]{2,1,0:T(8,128)(2,1)S(1)} %bitcast.197, bf16[4,16,640]{2,1,0:T(8,128)(2,1)S(1)} %bitcast.199, f32[16,640]{1,0:T(8,128)S(1)} %pad_maximum_fusion.18.vec, ...), custom_call_target="tpu_custom_call" | custom-call | flops 3355443200 | bytes 94371840 | tf_op jit(solution)/shard_map/pallas_call | solution.py:501
  549.2 4.8 collective-permute-start.44
  559.1 9.1 %fusion.124 = (bf16[2048,640]{1,0:T(8,128)(2,1)}, f32[2048,640]{1,0:T(8,128)}) fusion(bf16[1024,2048]{1,0:T(8,128)(2,1)} %pad_maximum_fusion.1, bf16[1024,640]{1,0:T(8,128)(2,1)S(1)} %copy-done.79), kind=kOutput, calls=%fused_computation.324 | convolution fusion | flops 2685665280 | bytes 13369344 | tf_op jit(solution)/shard_map/dot_general | solution.py:34
  571.5 5.3 fusion.123
  583.1 6.8 convolution_convert_fusion.4
  602.9 4.9 fusion.125
  611.9 17.5 %collective-permute-done.46 = bf16[512,2048]{1,0:T(8,128)(2,1)} collective-permute-done((bf16[512,2048]{1,0:T(8,128)(2,1)}, bf16[512,2048]{1,0:T(8,128)(2,1)}, u32[]{:S(2)}, u32[]{:S(2)}) %collective-permute-start.46) | collective-permute-done | bytes 2097184 | tf_op jit(solution)/shard_map/ppermute | solution.py:57
  640.7 4.8 collective-permute-done.49
  646.3 3.1 collective-permute-start.56
  649.4 5.8 collective-permute-done.51
  655.2 3.4 collective-permute-start.57
  663.6 4.7 fusion.29
  668.3 3.1 multiply_reduce_fusion
  684.0 15.3 %collective-permute-start.67 = (f32[2,2048]{1,0:T(2,128)S(1)}, f32[2,2048]{1,0:T(2,128)S(1)}, u32[]{:S(2)}, u32[]{:S(2)}) collective-permute-start(f32[2,2048]{1,0:T(2,128)S(1)} %add.821), channel_id=1, source_target_pairs={{0,1},{1,0},{2,3},{3,2},{4,5},{5,4},{6,7},{7,6},{8,9},{9,8},{10,11... | collective-permute-start | bytes 49160 | tf_op jit(solution)/shard_map/ppermute | solution.py:57
  699.3 4.7 reduce-scatter.10.cloned.1.call-done
  709.4 5.5 fusion.33
  715.1 3.1 collective-permute-start.60
  (551 shorter events, 209.2 us)
Async XLA Ops:
  7.3 45.4 %all-gather.6.cloned.1.call-start = ((), (), s32[]{:S(2)}) async-start(), calls=%async_computation.5 | async-start | bytes 1945600 | tf_op jit(solution)/shard_map/all_gather | solution.py:125
  16.0 100.0 %all-gather.8.cloned.1.call-start = ((), (), s32[]{:S(2)}) async-start(), calls=%async_computation.6 | async-start | bytes 3276800 | tf_op jit(solution)/shard_map/all_gather | solution.py:125
  19.8 14.8 %collective-permute-start.1 = (bf16[272,2048]{1,0:T(8,128)(2,1)S(1)}, bf16[272,2048]{1,0:T(8,128)(2,1)}, u32[]{:S(2)}, u32[]{:S(2)}) collective-permute-start(bf16[272,2048]{1,0:T(8,128)(2,1)S(1)} %pad_maximum_fusion.10), channel_id=1, source_target_pairs={{0,8},{1,9},{2,10},{3,11},{4,20},{5,21},{6,22},{7,23},{8,0},{9,1},... | collective-permute-start | bytes 3342344 | tf_op jit(solution)/shard_map/ppermute | solution.py:57
  34.6 15.0 %collective-permute-start.3 = (bf16[272,2048]{1,0:T(8,128)(2,1)}, bf16[272,2048]{1,0:T(8,128)(2,1)S(1)}, u32[]{:S(2)}, u32[]{:S(2)}) collective-permute-start(bf16[272,2048]{1,0:T(8,128)(2,1)} %collective-permute-done.1), channel_id=1, source_target_pairs={{0,16},{1,17},{2,18},{3,19},{4,12},{5,13},{6,14},{7,15},{8,24},{9,... | collective-permute-start | bytes 3342344 | tf_op jit(solution)/shard_map/ppermute | solution.py:57
  52.7 235.4 %all-gather.14.cloned.1.call-start = ((), (), s32[]{:S(2)}) async-start(), calls=%async_computation.9 | async-start | bytes 7077888 | tf_op jit(solution)/shard_map/all_gather | solution.py:143
  52.8 22.1 %collective-permute-start.2 = (bf16[272,2048]{1,0:T(8,128)(2,1)}, bf16[272,2048]{1,0:T(8,128)(2,1)S(1)}, u32[]{:S(2)}, u32[]{:S(2)}) collective-permute-start(bf16[272,2048]{1,0:T(8,128)(2,1)} %copy-done.80), channel_id=1, source_target_pairs={{0,16},{1,17},{2,18},{3,19},{4,12},{5,13},{6,14},{7,15},{8,24},{9,... | collective-permute-start | bytes 3342344 | tf_op jit(solution)/shard_map/ppermute | solution.py:57
  54.6 25.7 %collective-permute-start.11 = (bf16[1,304,640]{2,1,0:T(8,128)(2,1)S(1)}, bf16[1,304,640]{2,1,0:T(8,128)(2,1)S(1)}, u32[]{:S(2)}, u32[]{:S(2)}) collective-permute-start(bf16[1,304,640]{2,1,0:T(8,128)(2,1)S(1)} %get-tuple-element.249), channel_id=1, source_target_pairs={{0,8},{1,9},{2,10},{3,11},{4,12},{5,13},{6,14},{7,15},{8,0},{9,1},... | collective-permute-start | bytes 1167368 | tf_op jit(solution)/shard_map/ppermute | solution.py:57
  55.8 24.5 %collective-permute-start.12 = (bf16[1,304,640]{2,1,0:T(8,128)(2,1)S(1)}, bf16[1,304,640]{2,1,0:T(8,128)(2,1)S(1)}, u32[]{:S(2)}, u32[]{:S(2)}) collective-permute-start(bf16[1,304,640]{2,1,0:T(8,128)(2,1)S(1)} %get-tuple-element.248), channel_id=1, source_target_pairs={{0,16},{1,17},{2,18},{3,19},{4,20},{5,21},{6,22},{7,23},{8,24},{9,... | collective-permute-start | bytes 1167368 | tf_op jit(solution)/shard_map/ppermute | solution.py:57
  57.0 30.4 %collective-permute-start.13 = (bf16[1,304,640]{2,1,0:T(8,128)(2,1)S(1)}, bf16[1,304,640]{2,1,0:T(8,128)(2,1)S(1)}, u32[]{:S(2)}, u32[]{:S(2)}) collective-permute-start(bf16[1,304,640]{2,1,0:T(8,128)(2,1)S(1)} %get-tuple-element.247), channel_id=1, source_target_pairs={{0,24},{1,25},{2,26},{3,27},{4,28},{5,29},{6,30},{7,31},{8,16},{9,... | collective-permute-start | bytes 1167368 | tf_op jit(solution)/shard_map/ppermute | solution.py:57
  75.9 12.4 %collective-permute-start.14 = (bf16[1,304,640]{2,1,0:T(8,128)(2,1)S(1)}, bf16[1,304,640]{2,1,0:T(8,128)(2,1)S(1)}, u32[]{:S(2)}, u32[]{:S(2)}) collective-permute-start(bf16[1,304,640]{2,1,0:T(8,128)(2,1)S(1)} %get-tuple-element.104.refs_0_), channel_id=1, source_target_pairs={{0,4},{1,5},{2,6},{3,7},{4,0},{5,1},{6,2},{7,3},{8,12},{9,13},{10,... | collective-permute-start | bytes 1167368 | tf_op jit(solution)/shard_map/ppermute | solution.py:57
  80.3 8.7 %collective-permute-start.15 = (bf16[1,304,640]{2,1,0:T(8,128)(2,1)S(1)}, bf16[1,304,640]{2,1,0:T(8,128)(2,1)S(1)}, u32[]{:S(2)}, u32[]{:S(2)}) collective-permute-start(bf16[1,304,640]{2,1,0:T(8,128)(2,1)S(1)} %collective-permute-done.11.refs_1_), channel_id=1, source_target_pairs={{0,4},{1,5},{2,6},{3,7},{4,0},{5,1},{6,2},{7,3},{8,12},{9,13},{10,... | collective-permute-start | bytes 1167368 | tf_op jit(solution)/shard_map/ppermute | solution.py:57
  80.3 9.5 %collective-permute-start.16 = (bf16[1,304,640]{2,1,0:T(8,128)(2,1)S(1)}, bf16[1,304,640]{2,1,0:T(8,128)(2,1)S(1)}, u32[]{:S(2)}, u32[]{:S(2)}) collective-permute-start(bf16[1,304,640]{2,1,0:T(8,128)(2,1)S(1)} %collective-permute-done.12.refs_2_), channel_id=1, source_target_pairs={{0,4},{1,5},{2,6},{3,7},{4,0},{5,1},{6,2},{7,3},{8,12},{9,13},{10,... | collective-permute-start | bytes 1167368 | tf_op jit(solution)/shard_map/ppermute | solution.py:57
  99.7 200.2 %all-gather.12.cloned.1.call-start = ((), (), s32[]{:S(2)}) async-start(), calls=%async_computation.8 | async-start | bytes 7077888 | tf_op jit(solution)/shard_map/all_gather | solution.py:143
  107.4 235.5 %all-gather.10.cloned.1.call-start = ((), (), s32[]{:S(2)}) async-start(), calls=%async_computation.7 | async-start | bytes 7077888 | tf_op jit(solution)/shard_map/all_gather | solution.py:143
  107.5 22.7 %collective-permute-start.18 = (bf16[256,2048]{1,0:T(8,128)(2,1)}, bf16[256,2048]{1,0:T(8,128)(2,1)}, u32[]{:S(2)}, u32[]{:S(2)}) collective-permute-start(bf16[256,2048]{1,0:T(8,128)(2,1)} %param.23), channel_id=1, source_target_pairs={{0,8},{1,9},{2,10},{3,11},{4,20},{5,21},{6,22},{7,23},{8,0},{9,1},... | collective-permute-start | bytes 3145736 | tf_op jit(solution)/shard_map/ppermute | solution.py:57
  121.5 31.8 %collective-permute-start.6 = (bf16[1,512,640]{2,1,0:T(8,128)(2,1)}, bf16[1,512,640]{2,1,0:T(8,128)(2,1)}, u32[]{:S(2)}, u32[]{:S(2)}) collective-permute-start(bf16[1,512,640]{2,1,0:T(8,128)(2,1)} %bitcast.221), channel_id=1, source_target_pairs={{0,24},{1,25},{2,26},{3,27},{4,28},{5,29},{6,30},{7,31},{8,16},{9,... | collective-permute-start | bytes 1966088 | tf_op jit(solution)/shard_map/ppermute | solution.py:57
  123.7 30.3 %collective-permute-start.4 = (bf16[1,512,640]{2,1,0:T(8,128)(2,1)}, bf16[1,512,640]{2,1,0:T(8,128)(2,1)}, u32[]{:S(2)}, u32[]{:S(2)}) collective-permute-start(bf16[1,512,640]{2,1,0:T(8,128)(2,1)} %bitcast.220), channel_id=1, source_target_pairs={{0,8},{1,9},{2,10},{3,11},{4,12},{5,13},{6,14},{7,15},{8,0},{9,1},... | collective-permute-start | bytes 1966088 | tf_op jit(solution)/shard_map/ppermute | solution.py:57
  126.0 28.5 %collective-permute-start.5 = (bf16[1,512,640]{2,1,0:T(8,128)(2,1)}, bf16[1,512,640]{2,1,0:T(8,128)(2,1)}, u32[]{:S(2)}, u32[]{:S(2)}) collective-permute-start(bf16[1,512,640]{2,1,0:T(8,128)(2,1)} %bitcast.219), channel_id=1, source_target_pairs={{0,16},{1,17},{2,18},{3,19},{4,20},{5,21},{6,22},{7,23},{8,24},{9,... | collective-permute-start | bytes 1966088 | tf_op jit(solution)/shard_map/ppermute | solution.py:57
  131.5 38.7 %collective-permute-start.7 = (bf16[1,512,640]{2,1,0:T(8,128)(2,1)S(1)}, bf16[1,512,640]{2,1,0:T(8,128)(2,1)S(1)}, u32[]{:S(2)}, u32[]{:S(2)}) collective-permute-start(bf16[1,512,640]{2,1,0:T(8,128)(2,1)S(1)} %bitcast.194), channel_id=1, source_target_pairs={{0,4},{1,5},{2,6},{3,7},{4,0},{5,1},{6,2},{7,3},{8,12},{9,13},{10,... | collective-permute-start | bytes 1966088 | tf_op jit(solution)/shard_map/ppermute | solution.py:57
  153.2 9.1 %collective-permute-start.21 = (f32[2,4,2,640]{3,2,1,0:T(2,128)S(1)}, f32[2,4,2,640]{3,2,1,0:T(2,128)S(1)}, u32[]{:S(2)}, u32[]{:S(2)}) collective-permute-start(f32[2,4,2,640]{3,2,1,0:T(2,128)S(1)} %get-tuple-element.271), channel_id=1, source_target_pairs={{0,2},{1,3},{2,0},{3,1},{4,6},{5,7},{6,4},{7,5},{8,10},{9,11},{10,... | collective-permute-start | bytes 122888 | tf_op jit(solution)/shard_map/ppermute | solution.py:57
  154.1 18.7 %collective-permute-start.10 = (bf16[1,512,640]{2,1,0:T(8,128)(2,1)}, bf16[1,512,640]{2,1,0:T(8,128)(2,1)S(1)}, u32[]{:S(2)}, u32[]{:S(2)}) collective-permute-start(bf16[1,512,640]{2,1,0:T(8,128)(2,1)} %collective-permute-done.6.refs_3_), channel_id=1, source_target_pairs={{0,4},{1,5},{2,6},{3,7},{4,0},{5,1},{6,2},{7,3},{8,12},{9,13},{10,... | collective-permute-start | bytes 1966088 | tf_op jit(solution)/shard_map/ppermute | solution.py:57
  154.5 18.2 %collective-permute-start.8 = (bf16[1,512,640]{2,1,0:T(8,128)(2,1)}, bf16[1,512,640]{2,1,0:T(8,128)(2,1)S(1)}, u32[]{:S(2)}, u32[]{:S(2)}) collective-permute-start(bf16[1,512,640]{2,1,0:T(8,128)(2,1)} %collective-permute-done.4.refs_1_), channel_id=1, source_target_pairs={{0,4},{1,5},{2,6},{3,7},{4,0},{5,1},{6,2},{7,3},{8,12},{9,13},{10,... | collective-permute-start | bytes 1966088 | tf_op jit(solution)/shard_map/ppermute | solution.py:57
  159.3 13.5 %collective-permute-start.9 = (bf16[1,512,640]{2,1,0:T(8,128)(2,1)}, bf16[1,512,640]{2,1,0:T(8,128)(2,1)S(1)}, u32[]{:S(2)}, u32[]{:S(2)}) collective-permute-start(bf16[1,512,640]{2,1,0:T(8,128)(2,1)} %collective-permute-done.5.refs_2_), channel_id=1, source_target_pairs={{0,4},{1,5},{2,6},{3,7},{4,0},{5,1},{6,2},{7,3},{8,12},{9,13},{10,... | collective-permute-start | bytes 1966088 | tf_op jit(solution)/shard_map/ppermute | solution.py:57
  168.6 21.2 %collective-permute-start.23 = (bf16[256,2048]{1,0:T(8,128)(2,1)S(1)}, bf16[256,2048]{1,0:T(8,128)(2,1)}, u32[]{:S(2)}, u32[]{:S(2)}) collective-permute-start(bf16[256,2048]{1,0:T(8,128)(2,1)S(1)} %copy-done.55), channel_id=1, source_target_pairs={{0,16},{1,17},{2,18},{3,19},{4,12},{5,13},{6,14},{7,15},{8,24},{9,... | collective-permute-start | bytes 3145736 | tf_op jit(solution)/shard_map/ppermute | solution.py:57
  170.3 35.7 %collective-permute-start.24 = (bf16[256,2048]{1,0:T(8,128)(2,1)S(1)}, bf16[256,2048]{1,0:T(8,128)(2,1)}, u32[]{:S(2)}, u32[]{:S(2)}) collective-permute-start(bf16[256,2048]{1,0:T(8,128)(2,1)S(1)} %copy-done.55), channel_id=1, source_target_pairs={{0,24},{1,25},{2,26},{3,27},{4,28},{5,29},{6,30},{7,31},{8,16},{9,... | collective-permute-start | bytes 3145736 | tf_op jit(solution)/shard_map/ppermute | solution.py:57
  207.1 14.1 %collective-permute-start.26 = (bf16[256,2048]{1,0:T(8,128)(2,1)S(1)}, bf16[256,2048]{1,0:T(8,128)(2,1)S(1)}, u32[]{:S(2)}, u32[]{:S(2)}) collective-permute-start(bf16[256,2048]{1,0:T(8,128)(2,1)S(1)} %convolution_convert_fusion.5), channel_id=1, source_target_pairs={{0,16},{1,17},{2,18},{3,19},{4,12},{5,13},{6,14},{7,15},{8,24},{9,... | collective-permute-start | bytes 3145736 | tf_op jit(solution)/shard_map/ppermute | solution.py:57
  208.5 29.4 %collective-permute-start.25 = (bf16[256,2048]{1,0:T(8,128)(2,1)S(1)}, bf16[256,2048]{1,0:T(8,128)(2,1)S(1)}, u32[]{:S(2)}, u32[]{:S(2)}) collective-permute-start(bf16[256,2048]{1,0:T(8,128)(2,1)S(1)} %convolution_convert_fusion.6), channel_id=1, source_target_pairs={{0,16},{1,17},{2,18},{3,19},{4,12},{5,13},{6,14},{7,15},{8,24},{9,... | collective-permute-start | bytes 3145736 | tf_op jit(solution)/shard_map/ppermute | solution.py:57
  222.2 22.1 %collective-permute-start.27 = (bf16[256,2048]{1,0:T(8,128)(2,1)S(1)}, bf16[256,2048]{1,0:T(8,128)(2,1)S(1)}, u32[]{:S(2)}, u32[]{:S(2)}) collective-permute-start(bf16[256,2048]{1,0:T(8,128)(2,1)S(1)} %fusion.27), channel_id=1, source_target_pairs={{0,8},{1,9},{2,10},{3,11},{4,20},{5,21},{6,22},{7,23},{8,0},{9,1},... | collective-permute-start | bytes 3145736 | tf_op jit(solution)/shard_map/ppermute | solution.py:57
  247.0 14.0 %collective-permute-start.28 = (bf16[256,2048]{1,0:T(8,128)(2,1)S(1)}, bf16[256,2048]{1,0:T(8,128)(2,1)S(1)}, u32[]{:S(2)}, u32[]{:S(2)}) collective-permute-start(bf16[256,2048]{1,0:T(8,128)(2,1)S(1)} %multiply_convert_fusion.5), channel_id=1, source_target_pairs={{0,8},{1,9},{2,10},{3,11},{4,20},{5,21},{6,22},{7,23},{8,0},{9,1},... | collective-permute-start | bytes 3145736 | tf_op jit(solution)/shard_map/ppermute | solution.py:57
  262.6 25.5 %collective-permute-start.29 = (bf16[512,2048]{1,0:T(8,128)(2,1)}, bf16[512,2048]{1,0:T(8,128)(2,1)}, u32[]{:S(2)}, u32[]{:S(2)}) collective-permute-start(bf16[512,2048]{1,0:T(8,128)(2,1)} %pad_maximum_fusion.6), channel_id=1, source_target_pairs={{0,16},{1,17},{2,18},{3,19},{4,12},{5,13},{6,14},{7,15},{8,24},{9,... | collective-permute-start | bytes 6291464 | tf_op jit(solution)/shard_map/ppermute | solution.py:57
  263.1 194.8 %reduce-scatter.6.cloned.1.call-start = ((), (), s32[]{:S(2)}) async-start(), calls=%async_computation.10 | async-start | bytes 3932160 | tf_op jit(solution)/shard_map/reduce_scatter | solution.py:742
  342.8 164.6 %reduce-scatter.8.cloned.1.call-start = ((), (), s32[]{:S(2)}) async-start(), calls=%async_computation.11 | async-start | bytes 3932160 | tf_op jit(solution)/shard_map/reduce_scatter | solution.py:742
  369.9 25.4 %collective-permute-start.31 = (bf16[512,2048]{1,0:T(8,128)(2,1)S(1)}, bf16[512,2048]{1,0:T(8,128)(2,1)S(1)}, u32[]{:S(2)}, u32[]{:S(2)}) collective-permute-start(bf16[512,2048]{1,0:T(8,128)(2,1)S(1)} %convolution_add_fusion), channel_id=1, source_target_pairs={{0,16},{1,17},{2,18},{3,19},{4,12},{5,13},{6,14},{7,15},{8,24},{9,... | collective-permute-start | bytes 6291464 | tf_op jit(solution)/shard_map/ppermute | solution.py:57
  382.5 30.8 %collective-permute-start.35 = (bf16[768,2048]{1,0:T(8,128)(2,1)S(1)}, bf16[768,2048]{1,0:T(8,128)(2,1)S(1)}, u32[]{:S(2)}, u32[]{:S(2)}) collective-permute-start(bf16[768,2048]{1,0:T(8,128)(2,1)S(1)} %convolution_convert_fusion.1), channel_id=1, source_target_pairs={{0,4},{1,5},{2,6},{3,7},{4,0},{5,1},{6,2},{7,3},{8,12},{9,13},{10,... | collective-permute-start | bytes 9437192 | tf_op jit(solution)/shard_map/ppermute | solution.py:57
  396.2 14.0 %collective-permute-start.32 = (bf16[256,2048]{1,0:T(8,128)(2,1)S(1)}, bf16[256,2048]{1,0:T(8,128)(2,1)S(1)}, u32[]{:S(2)}, u32[]{:S(2)}) collective-permute-start(bf16[256,2048]{1,0:T(8,128)(2,1)S(1)} %fusion.41), channel_id=1, source_target_pairs={{0,8},{1,9},{2,10},{3,11},{4,20},{5,21},{6,22},{7,23},{8,0},{9,1},... | collective-permute-start | bytes 3145736 | tf_op jit(solution)/shard_map/ppermute | solution.py:57
  413.1 14.2 %collective-permute-start.33 = (bf16[256,2048]{1,0:T(8,128)(2,1)}, bf16[256,2048]{1,0:T(8,128)(2,1)S(1)}, u32[]{:S(2)}, u32[]{:S(2)}) collective-permute-start(bf16[256,2048]{1,0:T(8,128)(2,1)} %fusion.117), channel_id=1, source_target_pairs={{0,8},{1,9},{2,10},{3,11},{4,20},{5,21},{6,22},{7,23},{8,0},{9,1},... | collective-permute-start | bytes 3145736 | tf_op jit(solution)/shard_map/ppermute | solution.py:57
  420.4 255.6 %reduce-scatter.12.cloned.1.call-start = ((), (), s32[]{:S(2)}) async-start(), calls=%async_computation.13 | async-start | bytes 1638400 | tf_op jit(solution)/shard_map/reduce_scatter | solution.py:825
  429.2 25.4 %collective-permute-start.34 = (bf16[512,2048]{1,0:T(8,128)(2,1)S(1)}, bf16[512,2048]{1,0:T(8,128)(2,1)S(1)}, u32[]{:S(2)}, u32[]{:S(2)}) collective-permute-start(bf16[512,2048]{1,0:T(8,128)(2,1)S(1)} %pad_maximum_fusion.7), channel_id=1, source_target_pairs={{0,16},{1,17},{2,18},{3,19},{4,12},{5,13},{6,14},{7,15},{8,24},{9,... | collective-permute-start | bytes 6291464 | tf_op jit(solution)/shard_map/ppermute | solution.py:57
  437.8 51.8 %collective-permute-start.43 = (bf16[768,2048]{1,0:T(8,128)(2,1)}, bf16[768,2048]{1,0:T(8,128)(2,1)}, u32[]{:S(2)}, u32[]{:S(2)}) collective-permute-start(bf16[768,2048]{1,0:T(8,128)(2,1)} %convolution_convert_fusion), channel_id=1, source_target_pairs={{0,4},{1,5},{2,6},{3,7},{4,0},{5,1},{6,2},{7,3},{8,12},{9,13},{10,... | collective-permute-start | bytes 9437192 | tf_op jit(solution)/shard_map/ppermute | solution.py:57
  476.5 25.5 %collective-permute-start.36 = (bf16[512,2048]{1,0:T(8,128)(2,1)}, bf16[512,2048]{1,0:T(8,128)(2,1)}, u32[]{:S(2)}, u32[]{:S(2)}) collective-permute-start(bf16[512,2048]{1,0:T(8,128)(2,1)} %fusion.54), channel_id=1, source_target_pairs={{0,16},{1,17},{2,18},{3,19},{4,12},{5,13},{6,14},{7,15},{8,24},{9,... | collective-permute-start | bytes 6291464 | tf_op jit(solution)/shard_map/ppermute | solution.py:57
  484.7 14.3 %collective-permute-start.42 = (bf16[4,256,640]{2,1,0:T(8,128)(2,1)}, bf16[4,256,640]{2,1,0:T(8,128)(2,1)}, u32[]{:S(2)}, u32[]{:S(2)}) collective-permute-start(bf16[4,256,640]{2,1,0:T(8,128)(2,1)} %constant_dynamic-slice_fusion.7), channel_id=1, source_target_pairs={{0,4},{1,5},{2,6},{3,7},{4,0},{5,1},{6,2},{7,3},{8,12},{9,13},{10,... | collective-permute-start | bytes 3932168 | tf_op jit(solution)/shard_map/ppermute | solution.py:57
  485.1 12.5 %collective-permute-start.39 = (f32[2,4,2,640]{3,2,1,0:T(2,128)S(1)}, f32[2,4,2,640]{3,2,1,0:T(2,128)S(1)}, u32[]{:S(2)}, u32[]{:S(2)}) collective-permute-start(f32[2,4,2,640]{3,2,1,0:T(2,128)S(1)} %get-tuple-element.269), channel_id=1, source_target_pairs={{0,1},{1,2},{2,3},{3,0},{4,5},{5,6},{6,7},{7,4},{8,9},{9,10},{10,1... | collective-permute-start | bytes 122888 | tf_op jit(solution)/shard_map/ppermute | solution.py:57
  486.8 10.8 %collective-permute-start.40 = (f32[2,4,2,640]{3,2,1,0:T(2,128)S(1)}, f32[2,4,2,640]{3,2,1,0:T(2,128)S(1)}, u32[]{:S(2)}, u32[]{:S(2)}) collective-permute-start(f32[2,4,2,640]{3,2,1,0:T(2,128)S(1)} %get-tuple-element.269), channel_id=1, source_target_pairs={{0,2},{1,3},{2,0},{3,1},{4,6},{5,7},{6,4},{7,5},{8,10},{9,11},{10,... | collective-permute-start | bytes 122888 | tf_op jit(solution)/shard_map/ppermute | solution.py:57
  509.0 46.5 %collective-permute-start.61 = (bf16[1,256,640]{2,1,0:T(8,128)(2,1)S(1)}, bf16[1,256,640]{2,1,0:T(8,128)(2,1)S(1)}, u32[]{:S(2)}, u32[]{:S(2)}) collective-permute-start(bf16[1,256,640]{2,1,0:T(8,128)(2,1)S(1)} %get-tuple-element.253), channel_id=1, source_target_pairs={{0,8},{1,9},{2,10},{3,11},{4,12},{5,13},{6,14},{7,15},{8,0},{9,1},... | collective-permute-start | bytes 983048 | tf_op jit(solution)/shard_map/ppermute | solution.py:57
  509.9 45.6 %collective-permute-start.62 = (bf16[1,256,640]{2,1,0:T(8,128)(2,1)S(1)}, bf16[1,256,640]{2,1,0:T(8,128)(2,1)S(1)}, u32[]{:S(2)}, u32[]{:S(2)}) collective-permute-start(bf16[1,256,640]{2,1,0:T(8,128)(2,1)S(1)} %get-tuple-element.252), channel_id=1, source_target_pairs={{0,16},{1,17},{2,18},{3,19},{4,20},{5,21},{6,22},{7,23},{8,24},{9,... | collective-permute-start | bytes 983048 | tf_op jit(solution)/shard_map/ppermute | solution.py:57
  510.6 44.9 %collective-permute-start.63 = (bf16[1,256,640]{2,1,0:T(8,128)(2,1)S(1)}, bf16[1,256,640]{2,1,0:T(8,128)(2,1)S(1)}, u32[]{:S(2)}, u32[]{:S(2)}) collective-permute-start(bf16[1,256,640]{2,1,0:T(8,128)(2,1)S(1)} %get-tuple-element.251), channel_id=1, source_target_pairs={{0,24},{1,25},{2,26},{3,27},{4,28},{5,29},{6,30},{7,31},{8,16},{9,... | collective-permute-start | bytes 983048 | tf_op jit(solution)/shard_map/ppermute | solution.py:57
  557.8 123.7 %reduce-scatter.14.cloned.1.call-start = ((), (), s32[]{:S(2)}) async-start(), calls=%async_computation.14 | async-start | bytes 3932160 | tf_op jit(solution)/shard_map/reduce_scatter | solution.py:742
  558.5 145.5 %reduce-scatter.10.cloned.1.call-start = ((), (), s32[]{:S(2)}) async-start(), calls=%async_computation.12 | async-start | bytes 1945600 | tf_op jit(solution)/shard_map/reduce_scatter | solution.py:825
  578.1 11.9 %collective-permute-start.45 = (bf16[4,256,640]{2,1,0:T(8,128)(2,1)}, bf16[4,256,640]{2,1,0:T(8,128)(2,1)}, u32[]{:S(2)}, u32[]{:S(2)}) collective-permute-start(bf16[4,256,640]{2,1,0:T(8,128)(2,1)} %constant_dynamic-slice_fusion.6), channel_id=1, source_target_pairs={{0,4},{1,5},{2,6},{3,7},{4,0},{5,1},{6,2},{7,3},{8,12},{9,13},{10,... | collective-permute-start | bytes 3932168 | tf_op jit(solution)/shard_map/ppermute | solution.py:57
  592.7 36.7 %collective-permute-start.46 = (bf16[512,2048]{1,0:T(8,128)(2,1)}, bf16[512,2048]{1,0:T(8,128)(2,1)}, u32[]{:S(2)}, u32[]{:S(2)}) collective-permute-start(bf16[512,2048]{1,0:T(8,128)(2,1)} %convolution_convert_fusion.4), channel_id=1, source_target_pairs={{0,16},{1,17},{2,18},{3,19},{4,12},{5,13},{6,14},{7,15},{8,24},{9,... | collective-permute-start | bytes 6291464 | tf_op jit(solution)/shard_map/ppermute | solution.py:57
  594.8 13.0 %collective-permute-start.48 = (bf16[4,304,640]{2,1,0:T(8,128)(2,1)}, bf16[4,304,640]{2,1,0:T(8,128)(2,1)}, u32[]{:S(2)}, u32[]{:S(2)}) collective-permute-start(bf16[4,304,640]{2,1,0:T(8,128)(2,1)} %constant_dynamic-slice_fusion.5), channel_id=1, source_target_pairs={{0,4},{1,5},{2,6},{3,7},{4,0},{5,1},{6,2},{7,3},{8,12},{9,13},{10,... | collective-permute-start | bytes 4669448 | tf_op jit(solution)/shard_map/ppermute | solution.py:57
  600.1 34.2 %collective-permute-start.52 = (bf16[1,256,640]{2,1,0:T(8,128)(2,1)S(1)}, bf16[1,256,640]{2,1,0:T(8,128)(2,1)S(1)}, u32[]{:S(2)}, u32[]{:S(2)}) collective-permute-start(bf16[1,256,640]{2,1,0:T(8,128)(2,1)S(1)} %get-tuple-element.261), channel_id=1, source_target_pairs={{0,8},{1,9},{2,10},{3,11},{4,12},{5,13},{6,14},{7,15},{8,0},{9,1},... | collective-permute-start | bytes 983048 | tf_op jit(solution)/shard_map/ppermute | solution.py:57
  601.1 35.3 %collective-permute-start.53 = (bf16[1,256,640]{2,1,0:T(8,128)(2,1)S(1)}, bf16[1,256,640]{2,1,0:T(8,128)(2,1)S(1)}, u32[]{:S(2)}, u32[]{:S(2)}) collective-permute-start(bf16[1,256,640]{2,1,0:T(8,128)(2,1)S(1)} %get-tuple-element.260), channel_id=1, source_target_pairs={{0,16},{1,17},{2,18},{3,19},{4,20},{5,21},{6,22},{7,23},{8,24},{9,... | collective-permute-start | bytes 983048 | tf_op jit(solution)/shard_map/ppermute | solution.py:57
  601.4 37.1 %collective-permute-start.54 = (bf16[1,256,640]{2,1,0:T(8,128)(2,1)S(1)}, bf16[1,256,640]{2,1,0:T(8,128)(2,1)S(1)}, u32[]{:S(2)}, u32[]{:S(2)}) collective-permute-start(bf16[1,256,640]{2,1,0:T(8,128)(2,1)S(1)} %get-tuple-element.259), channel_id=1, source_target_pairs={{0,24},{1,25},{2,26},{3,27},{4,28},{5,29},{6,30},{7,31},{8,16},{9,... | collective-permute-start | bytes 983048 | tf_op jit(solution)/shard_map/ppermute | solution.py:57
  611.0 34.5 %collective-permute-start.49 = (bf16[1,304,640]{2,1,0:T(8,128)(2,1)S(1)}, bf16[1,304,640]{2,1,0:T(8,128)(2,1)S(1)}, u32[]{:S(2)}, u32[]{:S(2)}) collective-permute-start(bf16[1,304,640]{2,1,0:T(8,128)(2,1)S(1)} %get-tuple-element.245), channel_id=1, source_target_pairs={{0,8},{1,9},{2,10},{3,11},{4,12},{5,13},{6,14},{7,15},{8,0},{9,1},... | collective-permute-start | bytes 1167368 | tf_op jit(solution)/shard_map/ppermute | solution.py:57
  629.4 16.9 %collective-permute-start.50 = (bf16[1,304,640]{2,1,0:T(8,128)(2,1)S(1)}, bf16[1,304,640]{2,1,0:T(8,128)(2,1)S(1)}, u32[]{:S(2)}, u32[]{:S(2)}) collective-permute-start(bf16[1,304,640]{2,1,0:T(8,128)(2,1)S(1)} %get-tuple-element.244), channel_id=1, source_target_pairs={{0,16},{1,17},{2,18},{3,19},{4,20},{5,21},{6,22},{7,23},{8,24},{9,... | collective-permute-start | bytes 1167368 | tf_op jit(solution)/shard_map/ppermute | solution.py:57
  635.7 19.5 %collective-permute-start.51 = (bf16[1,304,640]{2,1,0:T(8,128)(2,1)S(1)}, bf16[1,304,640]{2,1,0:T(8,128)(2,1)S(1)}, u32[]{:S(2)}, u32[]{:S(2)}) collective-permute-start(bf16[1,304,640]{2,1,0:T(8,128)(2,1)S(1)} %get-tuple-element.243), channel_id=1, source_target_pairs={{0,24},{1,25},{2,26},{3,27},{4,28},{5,29},{6,30},{7,31},{8,16},{9,... | collective-permute-start | bytes 1167368 | tf_op jit(solution)/shard_map/ppermute | solution.py:57
  636.4 27.2 %collective-permute-start.47 = (bf16[256,2048]{1,0:T(8,128)(2,1)}, bf16[256,2048]{1,0:T(8,128)(2,1)}, u32[]{:S(2)}, u32[]{:S(2)}) collective-permute-start(bf16[256,2048]{1,0:T(8,128)(2,1)} %fusion.35), channel_id=1, source_target_pairs={{0,8},{1,9},{2,10},{3,11},{4,20},{5,21},{6,22},{7,23},{8,0},{9,1},... | collective-permute-start | bytes 3145736 | tf_op jit(solution)/shard_map/ppermute | solution.py:57
  638.5 70.9 %collective-permute-start.37 = (bf16[256,2048]{1,0:T(8,128)(2,1)}, bf16[256,2048]{1,0:T(8,128)(2,1)}, u32[]{:S(2)}, u32[]{:S(2)}) collective-permute-start(bf16[256,2048]{1,0:T(8,128)(2,1)} %fusion.37), channel_id=1, source_target_pairs={{0,8},{1,9},{2,10},{3,11},{4,20},{5,21},{6,22},{7,23},{8,0},{9,1},... | collective-permute-start | bytes 3145736 | tf_op jit(solution)/shard_map/ppermute | solution.py:57
  645.5 26.1 %collective-permute-start.55 = (bf16[1,256,640]{2,1,0:T(8,128)(2,1)}, bf16[1,256,640]{2,1,0:T(8,128)(2,1)}, u32[]{:S(2)}, u32[]{:S(2)}) collective-permute-start(bf16[1,256,640]{2,1,0:T(8,128)(2,1)} %get-tuple-element.255), channel_id=1, source_target_pairs={{0,1},{1,2},{2,3},{3,0},{4,5},{5,6},{6,7},{7,4},{8,9},{9,10},{10,1... | collective-permute-start | bytes 983048 | tf_op jit(solution)/shard_map/ppermute | solution.py:57
  646.3 27.0 %collective-permute-start.56 = (bf16[1,256,640]{2,1,0:T(8,128)(2,1)S(1)}, bf16[1,256,640]{2,1,0:T(8,128)(2,1)}, u32[]{:S(2)}, u32[]{:S(2)}) collective-permute-start(bf16[1,256,640]{2,1,0:T(8,128)(2,1)S(1)} %get-tuple-element.257), channel_id=1, source_target_pairs={{0,2},{1,3},{2,0},{3,1},{4,6},{5,7},{6,4},{7,5},{8,10},{9,11},{10,... | collective-permute-start | bytes 983048 | tf_op jit(solution)/shard_map/ppermute | solution.py:57
  655.2 18.2 %collective-permute-start.57 = (bf16[1,256,640]{2,1,0:T(8,128)(2,1)S(1)}, bf16[1,256,640]{2,1,0:T(8,128)(2,1)}, u32[]{:S(2)}, u32[]{:S(2)}) collective-permute-start(bf16[1,256,640]{2,1,0:T(8,128)(2,1)S(1)} %get-tuple-element.256), channel_id=1, source_target_pairs={{0,3},{1,0},{2,1},{3,2},{4,7},{5,4},{6,5},{7,6},{8,11},{9,8},{10,9... | collective-permute-start | bytes 983048 | tf_op jit(solution)/shard_map/ppermute | solution.py:57
  684.0 22.2 %collective-permute-start.67 = (f32[2,2048]{1,0:T(2,128)S(1)}, f32[2,2048]{1,0:T(2,128)S(1)}, u32[]{:S(2)}, u32[]{:S(2)}) collective-permute-start(f32[2,2048]{1,0:T(2,128)S(1)} %add.821), channel_id=1, source_target_pairs={{0,1},{1,0},{2,3},{3,2},{4,5},{5,4},{6,7},{7,6},{8,9},{9,8},{10,11... | collective-permute-start | bytes 49160 | tf_op jit(solution)/shard_map/ppermute | solution.py:57
  706.2 8.7 %collective-permute-start.68 = (f32[2,2048]{1,0:T(2,128)S(1)}, f32[2,2048]{1,0:T(2,128)S(1)}, u32[]{:S(2)}, u32[]{:S(2)}) collective-permute-start(f32[2,2048]{1,0:T(2,128)S(1)} %add.822), channel_id=1, source_target_pairs={{0,2},{1,3},{2,0},{3,1},{4,6},{5,7},{6,4},{7,5},{8,10},{9,11},{10,... | collective-permute-start | bytes 49160 | tf_op jit(solution)/shard_map/ppermute | solution.py:57
  (142 other events, 1482.5 us)
Sparse Core Ops, SparseCore 0:
  16.1 36.4 all-gather.5
  54.8 54.4 all-gather.7
  110.9 67.3 all-gather.13
  179.7 63.3 all-gather.11
  263.2 70.6 all-gather.9
  343.0 61.1 reduce-scatter.5
  420.5 63.8 reduce-scatter.7
  557.9 32.8 reduce-scatter.11
  593.1 66.0 reduce-scatter.13
  663.7 40.2 reduce-scatter.9

commit v4 on v3

--- a/solution.py
+++ b/solution.py
@@ -106,9 +106,9 @@
 
     def scatter_rows(self, far, near):
         rows = near.shape[0] // 2
-        came = self.two(far.astype(bf16)).astype(f32)
-        joined = (near[rows:] + came[rows:]).astype(bf16)
-        return near[:rows] + came[:rows] + self.one(joined).astype(f32), joined
+        came = self.two(far.astype(bf16))
+        joined = (near[rows:] + came[rows:].astype(f32)).astype(bf16)
+        return near[:rows] + came[:rows].astype(f32) + self.one(joined).astype(f32), joined
 
     def scatter_rows_early(self, parts):
         far = self.two(parts[3].astype(bf16))
@@ -233,7 +233,7 @@
         low[0, pl.ds(base, TILE), :] = total.astype(bf16)
         return 0
 
-    lax.fori_loop(0, rows // TILE, conv, 0)
+    lax.fori_loop(0, rows // TILE, conv, 0, unroll=2)
     pre[...] = trailing(low[0], dense[...])
 
     def tile(t, held):
@@ -262,7 +262,11 @@
         return entered, passed
 
     lax.fori_loop(
-        0, rows // TILE, tile, (jnp.zeros((1, width), f32), jnp.ones((1, width), f32))
+        0,
+        rows // TILE,
+        tile,
+        (jnp.zeros((1, width), f32), jnp.ones((1, width), f32)),
+        unroll=2,
     )
 
 
@@ -287,7 +291,11 @@
         return entered, passed
 
     lax.fori_loop(
-        0, rows // TILE, tile, (jnp.zeros((1, width), f32), jnp.ones((1, width), f32))
+        0,
+        rows // TILE,
+        tile,
+        (jnp.zeros((1, width), f32), jnp.ones((1, width), f32)),
+        unroll=2,
     )
 
 
@@ -344,7 +352,9 @@
     lax.fori_loop(0, rows // TILE, fill, 0)
 
     def add(row, value):
-        sums[row : row + 1, :] += jnp.sum(value, axis=0, keepdims=True)
+        span = slice(row * 8, row * 8 + 8)
+        for half in range(0, TILE, 8):
+            sums[span, :] += value[half : half + 8]
 
     def tile(t, _):
         base = pl.multiple_of(t * TILE, TILE)
@@ -494,7 +504,7 @@
         shape((2 * width, width), f32),
         shape((count, rows, width), f32),
         shape((count, 8, width), f32),
-        shape((8, width), f32),
+        shape((64, width), f32),
     ]
     cut = [chan, rim, vec, dense, low, state, reach, enter, grad, moved, span, leave]
     specs = [whole(a) if a is vec or a is dense else per_chunk(a) for a in cut]
@@ -724,7 +734,11 @@
     up_pre = trailing(feed_rows, up_use)
     gate_act, gelu_back_two = jax.vjp(jax.nn.gelu, gate_pre)
     hidden, gate_act, gate_slope = lax.optimization_barrier(
-        ((gate_act * up_pre).astype(bf16), gate_act, gelu_back_two(up_pre)[0])
+        (
+            (gate_act * up_pre).astype(bf16),
+            gate_act.astype(bf16),
+            gelu_back_two(up_pre)[0].astype(bf16),
+        )
     )
     half = hidden.shape[1] // 2
 
@@ -749,17 +763,21 @@
         return total.astype(f32)
 
     down_far = column_far(hidden, feed_grad)
-    down_own = column_own(hidden, feed_grad, down_far)
-    down_scattered = column_scatter(down_own)
-    hidden_grad = trailing(feed_grad, after(down_use, down_own))
-    gate_grad = (hidden_grad * gate_slope).astype(bf16)
-    up_grad = (hidden_grad * gate_act).astype(bf16)
+    hidden_grad = trailing(feed_grad, after(down_use, down_far))
+    gate_grad = (hidden_grad * gate_slope.astype(f32)).astype(bf16)
+    up_grad = (hidden_grad * gate_act.astype(f32)).astype(bf16)
     def norm_part(span):
         return plain(gate_grad[span], gate_use) + plain(up_grad[span], up_use)
 
-    norm_far, norm_near = norm_part(slice(two_rows, None)), norm_part(slice(two_rows))
+    norm_far = norm_part(slice(two_rows, None)).astype(bf16)
+    gate_grad, up_grad, hidden_late, norm_far = lax.optimization_barrier(
+        (gate_grad, up_grad, hidden, norm_far)
+    )
+    down_own = column_own(hidden_late, feed_grad, down_far)
+    down_scattered = column_scatter(down_own)
+    norm_near = norm_part(slice(two_rows))
     norm_grad, _ = places.scatter_rows(norm_far, norm_near)
-    gate_late, *_ = lax.optimization_barrier((gate_grad, norm_far, norm_near))
+    gate_late, *_ = lax.optimization_barrier((gate_grad, norm_near, down_own))
     gate_far = column_far(gate_late, feed_rows)
     norm_grad = after(norm_grad, gate_far)
     second_term = jnp.sum(norm_grad * xs_two, axis=0)
@@ -814,10 +832,11 @@
         def by(k):
             return lax.dynamic_index_in_dim(stacked, p ^ ((z + k) % 4), 0, False)
 
+        came = [places.along_z(by(k), k) for k in (1, 2, 3)]
         total = by(0).astype(f32)
-        for k in (1, 2, 3):
-            total = total + places.along_z(by(k), k).astype(f32)
-        return quarter_high(total)
+        for a in came:
+            total = total + a.astype(f32)
+        return quarter_high(total), came
 
     def quarter_far(parts, other):
         *parts, _ = lax.optimization_barrier((*parts, other))
@@ -832,7 +851,7 @@
         (leave, output_half, output_joined, up_own, gate_scattered)
     )
     output_parts = quarter_rows(output_half)
-    crossed, chan_grad, rim_grad, sums = run_backward(
+    crossed, chan_grad, rim_grad, sums8 = run_backward(
         info, channels, rim, vec, dense, conv_low, state_local, reach, enter, state_grad, moved,
         span_back, leave,
     )
@@ -866,7 +885,7 @@
     )
     vector_terms = jnp.concatenate(
         [
-            sums,
+            jnp.sum(sums8.reshape(8, 8, width), axis=1),
             jnp.sum(branch_grad.astype(f32), axis=0)[None],
             jnp.sum(mixer_grad.astype(f32), axis=0)[None],
             jnp.zeros((6, width), f32),
@@ -892,14 +911,15 @@
     both_near, low_far, mixer_half, _ = lax.optimization_barrier(
         (both_grads[:two_rows], low_far, mixer_half, mixer_came)
     )
-    branch_half, _, _ = quarter_half(after(branch_both, low_far))
+    branch_half, _, _ = quarter_half(after(branch_both, low_far, up_scattered))
     branch_parts = quarter_rows(branch_half)
     mixer_parts = quarter_rows(mixer_half)
     low_near = trailing(both_near, both_own)
     low_grad, low_joined = places.scatter_rows(low_far, low_near)
     branch_sum = quarter_far(branch_parts, low_near)
-    mixer_sum = quarter_near(mixer_parts)
+    mixer_sum, mixer_last = quarter_near(mixer_parts)
     mixer_term, second_term, _ = lax.optimization_barrier((mixer_term, second_term, low_grad))
+    low_grad = after(low_grad, *mixer_last)
     token_grad = (resid_grad + norm_back(rs_one, xs_one, gain_one, low_grad)).astype(bf16)
 
     first_term = (

time: 740 us -> 709 us (0.958)
  local copies, waits for them, and re-layouts: 78.8 us -> 68.3 us
  starting transfers between devices: 98.1 us -> 89.1 us
  other arithmetic: 82 us -> 74.2 us
    ppermute x69, waiting for transfers between devices: 218 us -> 199 us  [send(): return jax.tree.map(lambda a: lax.ppermute(a, AXES, pairs), x)]
    reduce_scatter x2, waiting for transfers between devices: 4.73 us -> 18.8 us  [quarter_far(): lax.psum_scatter(stacked, 'blk', scatter_dimension=0, tiled=True)[0]]
    ppermute x69, starting transfers between devices: 97.6 us -> 88.2 us  [send(): return jax.tree.map(lambda a: lax.ppermute(a, AXES, pairs), x)]
    dot_general x10, matrix products: 48.1 us -> 57.3 us  [plain(): return jnp.dot(former, latter, preferred_element_type=f32)]
    unnamed x250 -> x262, local copies, waits for them, and re-layouts: 46.5 us -> 39.9 us
  transfers between devices with their start and end apart: 79 -> 79, of which waited for: 32 -> 31; matrix products, arithmetic and copies ran while one was open for 39% -> 40% of each run, Pallas kernels for 7% -> 7%
where the time goes in v4:
time: 709 us; the launch traced here: 699 us
  waiting for transfers between devices  221 us (31%)
  matrix products  179 us (25%)
  starting transfers between devices  89.1 us (13%)
  other arithmetic  74.2 us (10%)
  local copies, waits for them, and re-layouts  68.3 us (10%)
  Pallas kernels  50 us (7%)
  between operations  16.3 us (2%)
    ppermute x69, waiting for transfers between devices, send(): return jax.tree.map(lambda a: lax.ppermute(a, AXES, pairs), x)  199 us
    ppermute x69, starting transfers between devices, send(): return jax.tree.map(lambda a: lax.ppermute(a, AXES, pairs), x)  88.2 us
    dot_general x9, matrix products, leading(): lax.dot_general(former, latter, (((0,), (0,)), ((), ())), preferred_eleme...  64.8 us
    dot_general x10, matrix products, plain(): return jnp.dot(former, latter, preferred_element_type=f32)  57.3 us
    dot_general x9, matrix products, trailing(): lax.dot_general(former, latter, (((1,), (1,)), ((), ())), preferred_eleme...  57.1 us
    unnamed x262, local copies, waits for them, and re-layouts  39.9 us
    pallas_call x1, Pallas kernels, run_backward(): pl.pallas_call(backward_kernel, grid=(count,), out_shape=outs, in_specs=[...  26.5 us
    reduce_scatter x2, waiting for transfers between devices, quarter_far(): lax.psum_scatter(stacked, 'blk', scatter_dimension=0, tiled=True)[0]  18.8 us
  transfers between devices with their start and end apart: 79, of which 31 were waited for; matrix products, arithmetic and copies ran while one was open for 40% of the time, Pallas kernels for 7%

profile of v4, /device:TPU:3, one launch (start us, length us, event | category | flops | bytes accessed | tf_op | source)
XLA Modules:
  0.0 698.6 jit_solution(11543918763628751645)
XLA Ops:
  11.3 3.3 collective-permute-start
  16.1 3.6 collective-permute-done
  20.9 13.7 %collective-permute-done.1 = bf16[272,2048]{1,0:T(8,128)(2,1)} collective-permute-done((bf16[272,2048]{1,0:T(8,128)(2,1)S(1)}, bf16[272,2048]{1,0:T(8,128)(2,1)}, u32[]{:S(2)}, u32[]{:S(2)}) %collective-permute-start.1) | collective-permute-done | bytes 1114144 | tf_op jit(solution)/shard_map/ppermute | solution.py:57
  35.7 13.9 %collective-permute-done.3 = bf16[272,2048]{1,0:T(8,128)(2,1)S(1)} collective-permute-done((bf16[272,2048]{1,0:T(8,128)(2,1)}, bf16[272,2048]{1,0:T(8,128)(2,1)S(1)}, u32[]{:S(2)}, u32[]{:S(2)}) %collective-permute-start.3) | collective-permute-done | bytes 1114144 | tf_op jit(solution)/shard_map/ppermute | solution.py:57
  49.6 3.1 all-gather.6.cloned.1.call-done
  57.3 17.6 %collective-permute-done.2 = bf16[272,2048]{1,0:T(8,128)(2,1)S(1)} collective-permute-done((bf16[272,2048]{1,0:T(8,128)(2,1)}, bf16[272,2048]{1,0:T(8,128)(2,1)S(1)}, u32[]{:S(2)}, u32[]{:S(2)}) %collective-permute-start.2) | collective-permute-done | bytes 1114144 | tf_op jit(solution)/shard_map/ppermute | solution.py:57
  75.9 3.5 collective-permute-start.14
  80.3 6.4 collective-permute-start.16
  109.5 4.5 add_convert_fusion.6
  114.0 2.7 constant_dynamic-slice_fusion.8
  128.0 13.8 %shard_map.341 = (bf16[4,256,640]{2,1,0:T(8,128)(2,1)S(1)}, f32[4,256,640]{2,1,0:T(8,128)S(1)}, f32[4,256,640]{2,1,0:T(8,128)S(1)}, f32[4,256,640]{2,1,0:T(8,128)S(1)}) custom-call(s32[4,5]{1,0:T(4,128)S(1)} %pad_add_fusion.info, bf16[4,256,640]{2,1,0:T(8,128)(2,1)S(1)} %bitcast.198, bf16[4,16,640]{2,1,0:T(8,128)(2,1)S(1)} %bitcast.200, ...), custom_call_target="tpu_custom_call" | custom-call | flops 1677721600 | bytes 55050240 | tf_op jit(solution)/shard_map/pallas_call | solution.py:447
  145.8 2.9 collective-permute-done.4.refs_1_
  153.9 3.6 collective-permute-start.22
  166.2 3.0 shard_map.339
  169.3 5.4 fusion.25
  174.7 6.7 collective-permute-done.23
  181.5 16.4 %collective-permute-done.24 = bf16[256,2048]{1,0:T(8,128)(2,1)S(1)} collective-permute-done((bf16[256,2048]{1,0:T(8,128)(2,1)}, bf16[256,2048]{1,0:T(8,128)(2,1)S(1)}, u32[]{:S(2)}, u32[]{:S(2)}) %collective-permute-start.24) | collective-permute-done | bytes 1048608 | tf_op jit(solution)/shard_map/ppermute | solution.py:57
  203.6 10.5 %collective-permute-done.26 = bf16[256,2048]{1,0:T(8,128)(2,1)} collective-permute-done((bf16[256,2048]{1,0:T(8,128)(2,1)}, bf16[256,2048]{1,0:T(8,128)(2,1)}, u32[]{:S(2)}, u32[]{:S(2)}) %collective-permute-start.26) | collective-permute-done | bytes 1048608 | tf_op jit(solution)/shard_map/ppermute | solution.py:57
  216.7 3.7 fusion.17
  223.1 6.4 collective-permute-done.25
  229.5 7.9 %collective-permute-done.27 = bf16[256,2048]{1,0:T(8,128)(2,1)S(1)} collective-permute-done((bf16[256,2048]{1,0:T(8,128)(2,1)S(1)}, bf16[256,2048]{1,0:T(8,128)(2,1)S(1)}, u32[]{:S(2)}, u32[]{:S(2)}) %collective-permute-start.27) | collective-permute-done | bytes 1048608 | tf_op jit(solution)/shard_map/ppermute | solution.py:57
  240.4 12.6 %collective-permute-done.28 = bf16[256,2048]{1,0:T(8,128)(2,1)S(1)} collective-permute-done((bf16[256,2048]{1,0:T(8,128)(2,1)S(1)}, bf16[256,2048]{1,0:T(8,128)(2,1)S(1)}, u32[]{:S(2)}, u32[]{:S(2)}) %collective-permute-start.28) | collective-permute-done | bytes 1048608 | tf_op jit(solution)/shard_map/ppermute | solution.py:57
  262.8 18.2 %collective-permute-done.29 = bf16[512,2048]{1,0:T(8,128)(2,1)} collective-permute-done((bf16[512,2048]{1,0:T(8,128)(2,1)}, bf16[512,2048]{1,0:T(8,128)(2,1)}, u32[]{:S(2)}, u32[]{:S(2)}) %collective-permute-start.29) | collective-permute-done | bytes 2097184 | tf_op jit(solution)/shard_map/ppermute | solution.py:57
  281.0 11.6 %fusion.116 = f32[1024,1536]{1,0:T(8,128)} fusion(bf16[1536,2048]{1,0:T(8,128)(2,1)} %all-gather.14.cloned.1.call-done, bf16[512,2048]{1,0:T(8,128)(2,1)} %collective-permute-done.29, bf16[256,2048]{1,0:T(8,128)(2,1)} %copy-done.84, bf16[256,2048]{1,0:T(8,128)(2,1)S(1)} %multiply_convert_fusion.5), kind=kOutput, calls=%fused_computation.318 | convolution fusion | flops 6455033856 | bytes 16777216 | tf_op jit(solution)/shard_map/dot_general | solution.py:30
  292.6 17.6 %fusion.6 = (bf16[1024,1536]{1,0:T(8,128)(2,1)}, bf16[1024,1536]{1,0:T(8,128)(2,1)S(1)}, bf16[1024,1536]{1,0:T(8,128)(2,1)}) fusion(f32[1024,1536]{1,0:T(8,128)} %fusion.116, bf16[1536,2048]{1,0:T(8,128)(2,1)} %all-gather.12.cloned.1.call-done, bf16[512,2048]{1,0:T(8,128)(2,1)} %collective-permute-done.29, bf16[256,2048]{1,0:T(8,128)(2,1)} %copy-done.84, ...), kind=kOutput, calls=%fused_computation.12 | convolution fusion | flops 6492782592 | bytes 26214400 | tf_op jit(solution)/shard_map/dot_general | solution.py:30
  310.1 8.2 %convolution_convert_fusion.2 = bf16[768,2048]{1,0:T(8,128)(2,1)} fusion(bf16[1024,2048]{1,0:T(8,128)(2,1)} %constant_dynamic-update-slice_fusion, bf16[1024,1536]{1,0:T(8,128)(2,1)S(1)} %get-tuple-element.141, s32[]{:T(128)S(6)} %select_n.407), kind=kOutput, calls=%fused_computation.35 | convolution fusion | flops 3222798336 | bytes 8912900 | tf_op jit(solution)/shard_map/dot_general | solution.py:34
  319.6 11.6 %multiply_convert_fusion = (bf16[1024,1536]{1,0:T(8,128)(2,1)S(1)}, bf16[1024,1536]{1,0:T(8,128)(2,1)S(1)}) fusion(bf16[1024,1536]{1,0:T(8,128)(2,1)} %get-tuple-element.134, bf16[1024,1536]{1,0:T(8,128)(2,1)} %get-tuple-element.133, bf16[1024,2048]{1,0:T(8,128)(2,1)} %constant_dynamic-update-slice_fusion, bf16[1536,2048]{1,0:T(8,128)(2,1)} %all-gather.10.cloned.1.call-done), kind=kOutput, calls=%fused_computation.16 | convolution fusion | flops 6451888128 | bytes 23068672 | tf_op jit(solution)/shard_map/dot_general | solution.py:30
  331.3 7.9 %fusion.42 = f32[512,2048]{1,0:T(8,128)S(1)} fusion(bf16[1536,2048]{1,0:T(8,128)(2,1)} %all-gather.12.cloned.1.call-done, bf16[1024,1536]{1,0:T(8,128)(2,1)S(1)} %get-tuple-element.143), kind=kOutput, calls=%fused_computation.109 | convolution fusion | flops 3221225472 | bytes 12058624 | tf_op jit(solution)/shard_map/dot_general | solution.py:26
  339.2 7.9 %add_convert_fusion.3 = bf16[512,2048]{1,0:T(8,128)(2,1)} fusion(f32[512,2048]{1,0:T(8,128)S(1)} %fusion.42, bf16[1536,2048]{1,0:T(8,128)(2,1)} %all-gather.14.cloned.1.call-done, bf16[1024,1536]{1,0:T(8,128)(2,1)S(1)} %get-tuple-element.155), kind=kOutput, calls=%fused_computation.26 | convolution fusion | flops 3223322624 | bytes 14155776 | tf_op jit(solution)/shard_map/dot_general | solution.py:26
  347.3 5.0 fusion.54
  352.3 7.6 %add_convert_fusion.2 = bf16[768,2048]{1,0:T(8,128)(2,1)} fusion(bf16[768,2048]{1,0:T(8,128)(2,1)} %collective-permute-done.32, bf16[1024,2048]{1,0:T(8,128)(2,1)} %constant_dynamic-update-slice_fusion, bf16[1024,1536]{1,0:T(8,128)(2,1)S(1)} %copy-done.90, s32[]{:T(128)S(6)} %select_n.408), kind=kOutput, calls=%fused_computation.15 | convolution fusion | flops 3225944064 | bytes 12058628 | tf_op jit(solution)/shard_map/dot_general | solution.py:34
  360.4 8.0 %convolution_add_fusion = f32[512,2048]{1,0:T(8,128)S(1)} fusion(f32[512,2048]{1,0:T(8,128)} %fusion.54, bf16[1536,2048]{1,0:T(8,128)(2,1)} %all-gather.14.cloned.1.call-done, bf16[1024,1536]{1,0:T(8,128)(2,1)} %copy-done.115), kind=kOutput, calls=%fused_computation.42 | convolution fusion | flops 3222274048 | bytes 16252928 | tf_op jit(solution)/shard_map/dot_general | solution.py:26
  368.4 8.3 %convolution_convert_fusion.1 = bf16[768,2048]{1,0:T(8,128)(2,1)} fusion(bf16[1024,1536]{1,0:T(8,128)(2,1)S(1)} %copy-done.118, s32[]{:T(128)S(6)} %select_n.407, bf16[512,2048]{1,0:T(8,128)(2,1)} %collective-permute-done.29, bf16[256,2048]{1,0:T(8,128)(2,1)S(1)} %copy-done.85, bf16[256,2048]{1,0:T(8,128)(2,1)S(1)} %multiply_convert_fusion.5), kind=kOutput, calls=%fused_computation.34 | convolution fusion | flops 3235381248 | bytes 8912900 | tf_op jit(solution)/shard_map/dot_general | solution.py:34
  381.3 12.7 %collective-permute-done.31 = bf16[256,2048]{1,0:T(8,128)(2,1)S(1)} collective-permute-done((bf16[256,2048]{1,0:T(8,128)(2,1)}, bf16[256,2048]{1,0:T(8,128)(2,1)S(1)}, u32[]{:S(2)}, u32[]{:S(2)}) %collective-permute-start.31) | collective-permute-done | bytes 1048608 | tf_op jit(solution)/shard_map/ppermute | solution.py:57
  400.4 7.8 %add_convert_fusion.1 = bf16[768,2048]{1,0:T(8,128)(2,1)} fusion(bf16[768,2048]{1,0:T(8,128)(2,1)} %collective-permute-done.35, bf16[1024,1536]{1,0:T(8,128)(2,1)S(1)} %copy-done.119, s32[]{:T(128)S(6)} %select_n.408, bf16[512,2048]{1,0:T(8,128)(2,1)} %collective-permute-done.29, bf16[256,2048]{1,0:T(8,128)(2,1)S(1)} %copy-done.86, ...), kind=kOutput, calls=%fused_computation.14 | convolution fusion | flops 3238526976 | bytes 12058628 | tf_op jit(solution)/shard_map/dot_general | solution.py:34
  408.5 4.8 collective-permute-done.33
  414.3 8.0 %convolution_convert_fusion = bf16[768,2048]{1,0:T(8,128)(2,1)} fusion(bf16[1024,1536]{1,0:T(8,128)(2,1)} %copy-done.115, s32[]{:T(128)S(6)} %select_n.407, bf16[512,2048]{1,0:T(8,128)(2,1)} %collective-permute-done.29, bf16[256,2048]{1,0:T(8,128)(2,1)S(1)} %copy-done.87, bf16[256,2048]{1,0:T(8,128)(2,1)S(1)} %copy-done.67), kind=kOutput, calls=%fused_computation.33 | convolution fusion | flops 3235381248 | bytes 8912900 | tf_op jit(solution)/shard_map/dot_general | solution.py:34
  424.5 5.0 fusion.47
  429.5 4.6 fusion.49
  434.1 4.7 collective-permute-done.34
  441.1 8.4 %convert_reduce_fusion.1 = (bf16[640]{0:T(1024)(128)(2,1)S(1)}, bf16[1024,640]{1,0:T(8,128)(2,1)}, bf16[1024,640]{1,0:T(8,128)(2,1)S(1)}) fusion(f32[1024,640]{1,0:T(8,128)} %get-tuple-element.147, f32[1024,640]{1,0:T(8,128)} %get-tuple-element.148, bf16[1024,2048]{1,0:T(8,128)(2,1)} %pad_maximum_fusion.3, bf16[2048,640]{1,0:T(8,128)(2,1)S(1)} %copy-done.3), kind=kOutput, calls=%fused_computation.70 | convolution fusion | flops 2688286208 | bytes 14681344 | tf_op jit(solution)/shard_map/dot_general | solution.py:26
  449.4 2.7 shard_map.343
  460.8 6.2 convolution_convert_fusion.3
  473.7 7.8 %add_convert_fusion = bf16[768,2048]{1,0:T(8,128)(2,1)} fusion(bf16[768,2048]{1,0:T(8,128)(2,1)} %collective-permute-done.43, bf16[1024,1536]{1,0:T(8,128)(2,1)S(1)} %copy-done.116, s32[]{:T(128)S(6)} %select_n.408, bf16[512,2048]{1,0:T(8,128)(2,1)} %collective-permute-done.29, bf16[256,2048]{1,0:T(8,128)(2,1)S(1)} %copy-done.88, ...), kind=kOutput, calls=%fused_computation.13 | convolution fusion | flops 3238526976 | bytes 12058628 | tf_op jit(solution)/shard_map/dot_general | solution.py:34
  483.4 2.7 add_bitcast_fusion.1
  496.1 26.5 %shard_map.345 = (f32[1280,640]{1,0:T(8,128)}, f32[4,256,640]{2,1,0:T(8,128)S(1)}, f32[4,8,640]{2,1,0:T(8,128)S(1)}, f32[64,640]{1,0:T(8,128)S(1)}) custom-call(s32[4,5]{1,0:T(4,128)S(1)} %pad_add_fusion.info, bf16[4,256,640]{2,1,0:T(8,128)(2,1)S(1)} %bitcast.199, bf16[4,16,640]{2,1,0:T(8,128)(2,1)S(1)} %bitcast.201, f32[16,640]{1,0:T(8,128)S(1)} %pad_maximum_fusion.18.vec, ...), custom_call_target="tpu_custom_call" | custom-call | flops 3355443200 | bytes 94371840 | tf_op jit(solution)/shard_map/pallas_call | solution.py:511
  522.5 3.2 collective-permute-start.44
  530.8 5.7 fusion.121
  537.7 5.3 fusion.120
  544.2 2.7 slice-done.1
  547.3 4.1 convolution_convert_fusion.4
  557.9 3.1 gather_fusion.3
  570.0 4.9 fusion.122
  574.9 14.0 %collective-permute-done.48 = bf16[1,256,640]{2,1,0:T(8,128)(2,1)} collective-permute-done((bf16[1,256,640]{2,1,0:T(8,128)(2,1)}, bf16[1,256,640]{2,1,0:T(8,128)(2,1)}, u32[]{:S(2)}, u32[]{:S(2)}) %collective-permute-start.48) | collective-permute-done | bytes 327712 | tf_op jit(solution)/shard_map/ppermute | solution.py:57
  588.9 3.2 collective-permute-done.50
  606.5 11.1 %collective-permute-done.52 = bf16[1,256,640]{2,1,0:T(8,128)(2,1)S(1)} collective-permute-done((bf16[1,256,640]{2,1,0:T(8,128)(2,1)S(1)}, bf16[1,256,640]{2,1,0:T(8,128)(2,1)S(1)}, u32[]{:S(2)}, u32[]{:S(2)}) %collective-permute-start.52) | collective-permute-done | bytes 327712 | tf_op jit(solution)/shard_map/ppermute | solution.py:57
  623.2 6.5 collective-permute-done.57
  632.3 4.1 fusion.38
  636.4 3.2 multiply_reduce_fusion
  639.7 3.2 collective-permute-start.64
  651.6 2.7 collective-permute-start.67
  654.4 18.8 %reduce-scatter.12.cloned.1.call-done = bf16[1,1,304,640]{3,2,1,0:T(8,128)(2,1)} async-done(((bf16[4,1,304,640]{3,2,1,0:T(8,128)(2,1)}), bf16[1,1,304,640]{3,2,1,0:T(8,128)(2,1)}) %reduce-scatter.12.cloned.1.call-update) | async-done | bytes 389136 | tf_op jit(solution)/shard_map/reduce_scatter | solution.py:844
  678.7 5.3 fusion.35
  684.1 3.0 collective-permute-start.60
  (562 shorter events, 199.2 us)
Async XLA Ops:
  7.3 45.4 %all-gather.6.cloned.1.call-start = ((), (), s32[]{:S(2)}) async-start(), calls=%async_computation.5 | async-start | bytes 1945600 | tf_op jit(solution)/shard_map/all_gather | solution.py:125
  16.0 98.0 %all-gather.8.cloned.1.call-start = ((), (), s32[]{:S(2)}) async-start(), calls=%async_computation.6 | async-start | bytes 3276800 | tf_op jit(solution)/shard_map/all_gather | solution.py:125
  19.8 14.8 %collective-permute-start.1 = (bf16[272,2048]{1,0:T(8,128)(2,1)S(1)}, bf16[272,2048]{1,0:T(8,128)(2,1)}, u32[]{:S(2)}, u32[]{:S(2)}) collective-permute-start(bf16[272,2048]{1,0:T(8,128)(2,1)S(1)} %pad_maximum_fusion.10), channel_id=1, source_target_pairs={{0,8},{1,9},{2,10},{3,11},{4,20},{5,21},{6,22},{7,23},{8,0},{9,1},... | collective-permute-start | bytes 3342344 | tf_op jit(solution)/shard_map/ppermute | solution.py:57
  34.6 15.0 %collective-permute-start.3 = (bf16[272,2048]{1,0:T(8,128)(2,1)}, bf16[272,2048]{1,0:T(8,128)(2,1)S(1)}, u32[]{:S(2)}, u32[]{:S(2)}) collective-permute-start(bf16[272,2048]{1,0:T(8,128)(2,1)} %collective-permute-done.1), channel_id=1, source_target_pairs={{0,16},{1,17},{2,18},{3,19},{4,12},{5,13},{6,14},{7,15},{8,24},{9,... | collective-permute-start | bytes 3342344 | tf_op jit(solution)/shard_map/ppermute | solution.py:57
  52.7 228.3 %all-gather.14.cloned.1.call-start = ((), (), s32[]{:S(2)}) async-start(), calls=%async_computation.9 | async-start | bytes 7077888 | tf_op jit(solution)/shard_map/all_gather | solution.py:143
  52.8 22.1 %collective-permute-start.2 = (bf16[272,2048]{1,0:T(8,128)(2,1)}, bf16[272,2048]{1,0:T(8,128)(2,1)S(1)}, u32[]{:S(2)}, u32[]{:S(2)}) collective-permute-start(bf16[272,2048]{1,0:T(8,128)(2,1)} %copy-done.79), channel_id=1, source_target_pairs={{0,16},{1,17},{2,18},{3,19},{4,12},{5,13},{6,14},{7,15},{8,24},{9,... | collective-permute-start | bytes 3342344 | tf_op jit(solution)/shard_map/ppermute | solution.py:57
  54.6 25.7 %collective-permute-start.11 = (bf16[1,304,640]{2,1,0:T(8,128)(2,1)S(1)}, bf16[1,304,640]{2,1,0:T(8,128)(2,1)S(1)}, u32[]{:S(2)}, u32[]{:S(2)}) collective-permute-start(bf16[1,304,640]{2,1,0:T(8,128)(2,1)S(1)} %get-tuple-element.257), channel_id=1, source_target_pairs={{0,8},{1,9},{2,10},{3,11},{4,12},{5,13},{6,14},{7,15},{8,0},{9,1},... | collective-permute-start | bytes 1167368 | tf_op jit(solution)/shard_map/ppermute | solution.py:57
  55.8 24.5 %collective-permute-start.12 = (bf16[1,304,640]{2,1,0:T(8,128)(2,1)S(1)}, bf16[1,304,640]{2,1,0:T(8,128)(2,1)S(1)}, u32[]{:S(2)}, u32[]{:S(2)}) collective-permute-start(bf16[1,304,640]{2,1,0:T(8,128)(2,1)S(1)} %get-tuple-element.256), channel_id=1, source_target_pairs={{0,16},{1,17},{2,18},{3,19},{4,20},{5,21},{6,22},{7,23},{8,24},{9,... | collective-permute-start | bytes 1167368 | tf_op jit(solution)/shard_map/ppermute | solution.py:57
  57.0 30.4 %collective-permute-start.13 = (bf16[1,304,640]{2,1,0:T(8,128)(2,1)S(1)}, bf16[1,304,640]{2,1,0:T(8,128)(2,1)S(1)}, u32[]{:S(2)}, u32[]{:S(2)}) collective-permute-start(bf16[1,304,640]{2,1,0:T(8,128)(2,1)S(1)} %get-tuple-element.255), channel_id=1, source_target_pairs={{0,24},{1,25},{2,26},{3,27},{4,28},{5,29},{6,30},{7,31},{8,16},{9,... | collective-permute-start | bytes 1167368 | tf_op jit(solution)/shard_map/ppermute | solution.py:57
  75.9 12.4 %collective-permute-start.14 = (bf16[1,304,640]{2,1,0:T(8,128)(2,1)S(1)}, bf16[1,304,640]{2,1,0:T(8,128)(2,1)S(1)}, u32[]{:S(2)}, u32[]{:S(2)}) collective-permute-start(bf16[1,304,640]{2,1,0:T(8,128)(2,1)S(1)} %get-tuple-element.109.refs_0_), channel_id=1, source_target_pairs={{0,4},{1,5},{2,6},{3,7},{4,0},{5,1},{6,2},{7,3},{8,12},{9,13},{10,... | collective-permute-start | bytes 1167368 | tf_op jit(solution)/shard_map/ppermute | solution.py:57
  80.3 9.5 %collective-permute-start.16 = (bf16[1,304,640]{2,1,0:T(8,128)(2,1)S(1)}, bf16[1,304,640]{2,1,0:T(8,128)(2,1)S(1)}, u32[]{:S(2)}, u32[]{:S(2)}) collective-permute-start(bf16[1,304,640]{2,1,0:T(8,128)(2,1)S(1)} %collective-permute-done.12.refs_2_), channel_id=1, source_target_pairs={{0,4},{1,5},{2,6},{3,7},{4,0},{5,1},{6,2},{7,3},{8,12},{9,13},{10,... | collective-permute-start | bytes 1167368 | tf_op jit(solution)/shard_map/ppermute | solution.py:57
  99.7 192.9 %all-gather.12.cloned.1.call-start = ((), (), s32[]{:S(2)}) async-start(), calls=%async_computation.8 | async-start | bytes 7077888 | tf_op jit(solution)/shard_map/all_gather | solution.py:143
  100.2 219.4 %all-gather.10.cloned.1.call-start = ((), (), s32[]{:S(2)}) async-start(), calls=%async_computation.7 | async-start | bytes 7077888 | tf_op jit(solution)/shard_map/all_gather | solution.py:143
  106.0 17.9 %collective-permute-start.18 = (bf16[256,2048]{1,0:T(8,128)(2,1)}, bf16[256,2048]{1,0:T(8,128)(2,1)}, u32[]{:S(2)}, u32[]{:S(2)}) collective-permute-start(bf16[256,2048]{1,0:T(8,128)(2,1)} %param.23), channel_id=1, source_target_pairs={{0,8},{1,9},{2,10},{3,11},{4,20},{5,21},{6,22},{7,23},{8,0},{9,1},... | collective-permute-start | bytes 3145736 | tf_op jit(solution)/shard_map/ppermute | solution.py:57
  117.8 27.1 %collective-permute-start.6 = (bf16[1,512,640]{2,1,0:T(8,128)(2,1)}, bf16[1,512,640]{2,1,0:T(8,128)(2,1)S(1)}, u32[]{:S(2)}, u32[]{:S(2)}) collective-permute-start(bf16[1,512,640]{2,1,0:T(8,128)(2,1)} %bitcast.224), channel_id=1, source_target_pairs={{0,24},{1,25},{2,26},{3,27},{4,28},{5,29},{6,30},{7,31},{8,16},{9,... | collective-permute-start | bytes 1966088 | tf_op jit(solution)/shard_map/ppermute | solution.py:57
  119.4 29.3 %collective-permute-start.4 = (bf16[1,512,640]{2,1,0:T(8,128)(2,1)}, bf16[1,512,640]{2,1,0:T(8,128)(2,1)}, u32[]{:S(2)}, u32[]{:S(2)}) collective-permute-start(bf16[1,512,640]{2,1,0:T(8,128)(2,1)} %bitcast.223), channel_id=1, source_target_pairs={{0,8},{1,9},{2,10},{3,11},{4,12},{5,13},{6,14},{7,15},{8,0},{9,1},... | collective-permute-start | bytes 1966088 | tf_op jit(solution)/shard_map/ppermute | solution.py:57
  121.7 28.6 %collective-permute-start.5 = (bf16[1,512,640]{2,1,0:T(8,128)(2,1)}, bf16[1,512,640]{2,1,0:T(8,128)(2,1)}, u32[]{:S(2)}, u32[]{:S(2)}) collective-permute-start(bf16[1,512,640]{2,1,0:T(8,128)(2,1)} %bitcast.12), channel_id=1, source_target_pairs={{0,16},{1,17},{2,18},{3,19},{4,20},{5,21},{6,22},{7,23},{8,24},{9,... | collective-permute-start | bytes 1966088 | tf_op jit(solution)/shard_map/ppermute | solution.py:57
  125.8 35.8 %collective-permute-start.7 = (bf16[1,512,640]{2,1,0:T(8,128)(2,1)S(1)}, bf16[1,512,640]{2,1,0:T(8,128)(2,1)S(1)}, u32[]{:S(2)}, u32[]{:S(2)}) collective-permute-start(bf16[1,512,640]{2,1,0:T(8,128)(2,1)S(1)} %bitcast.196), channel_id=1, source_target_pairs={{0,4},{1,5},{2,6},{3,7},{4,0},{5,1},{6,2},{7,3},{8,12},{9,13},{10,... | collective-permute-start | bytes 1966088 | tf_op jit(solution)/shard_map/ppermute | solution.py:57
  144.9 9.0 %collective-permute-start.21 = (f32[2,4,2,640]{3,2,1,0:T(2,128)S(1)}, f32[2,4,2,640]{3,2,1,0:T(2,128)S(1)}, u32[]{:S(2)}, u32[]{:S(2)}) collective-permute-start(f32[2,4,2,640]{3,2,1,0:T(2,128)S(1)} %get-tuple-element.279), channel_id=1, source_target_pairs={{0,2},{1,3},{2,0},{3,1},{4,6},{5,7},{6,4},{7,5},{8,10},{9,11},{10,... | collective-permute-start | bytes 122888 | tf_op jit(solution)/shard_map/ppermute | solution.py:57
  148.7 15.7 %collective-permute-start.10 = (bf16[1,512,640]{2,1,0:T(8,128)(2,1)S(1)}, bf16[1,512,640]{2,1,0:T(8,128)(2,1)S(1)}, u32[]{:S(2)}, u32[]{:S(2)}) collective-permute-start(bf16[1,512,640]{2,1,0:T(8,128)(2,1)S(1)} %collective-permute-done.6.refs_3_), channel_id=1, source_target_pairs={{0,4},{1,5},{2,6},{3,7},{4,0},{5,1},{6,2},{7,3},{8,12},{9,13},{10,... | collective-permute-start | bytes 1966088 | tf_op jit(solution)/shard_map/ppermute | solution.py:57
  150.2 14.1 %collective-permute-start.8 = (bf16[1,512,640]{2,1,0:T(8,128)(2,1)}, bf16[1,512,640]{2,1,0:T(8,128)(2,1)S(1)}, u32[]{:S(2)}, u32[]{:S(2)}) collective-permute-start(bf16[1,512,640]{2,1,0:T(8,128)(2,1)} %collective-permute-done.4.refs_1_), channel_id=1, source_target_pairs={{0,4},{1,5},{2,6},{3,7},{4,0},{5,1},{6,2},{7,3},{8,12},{9,13},{10,... | collective-permute-start | bytes 1966088 | tf_op jit(solution)/shard_map/ppermute | solution.py:57
  150.8 13.6 %collective-permute-start.9 = (bf16[1,512,640]{2,1,0:T(8,128)(2,1)}, bf16[1,512,640]{2,1,0:T(8,128)(2,1)S(1)}, u32[]{:S(2)}, u32[]{:S(2)}) collective-permute-start(bf16[1,512,640]{2,1,0:T(8,128)(2,1)} %collective-permute-done.5.refs_2_), channel_id=1, source_target_pairs={{0,4},{1,5},{2,6},{3,7},{4,0},{5,1},{6,2},{7,3},{8,12},{9,13},{10,... | collective-permute-start | bytes 1966088 | tf_op jit(solution)/shard_map/ppermute | solution.py:57
  160.1 21.3 %collective-permute-start.23 = (bf16[256,2048]{1,0:T(8,128)(2,1)}, bf16[256,2048]{1,0:T(8,128)(2,1)S(1)}, u32[]{:S(2)}, u32[]{:S(2)}) collective-permute-start(bf16[256,2048]{1,0:T(8,128)(2,1)} %param.23), channel_id=1, source_target_pairs={{0,16},{1,17},{2,18},{3,19},{4,12},{5,13},{6,14},{7,15},{8,24},{9,... | collective-permute-start | bytes 3145736 | tf_op jit(solution)/shard_map/ppermute | solution.py:57
  161.7 36.1 %collective-permute-start.24 = (bf16[256,2048]{1,0:T(8,128)(2,1)}, bf16[256,2048]{1,0:T(8,128)(2,1)S(1)}, u32[]{:S(2)}, u32[]{:S(2)}) collective-permute-start(bf16[256,2048]{1,0:T(8,128)(2,1)} %param.23), channel_id=1, source_target_pairs={{0,24},{1,25},{2,26},{3,27},{4,28},{5,29},{6,30},{7,31},{8,16},{9,... | collective-permute-start | bytes 3145736 | tf_op jit(solution)/shard_map/ppermute | solution.py:57
  199.8 14.3 %collective-permute-start.26 = (bf16[256,2048]{1,0:T(8,128)(2,1)}, bf16[256,2048]{1,0:T(8,128)(2,1)}, u32[]{:S(2)}, u32[]{:S(2)}) collective-permute-start(bf16[256,2048]{1,0:T(8,128)(2,1)} %convolution_convert_fusion.5), channel_id=1, source_target_pairs={{0,16},{1,17},{2,18},{3,19},{4,12},{5,13},{6,14},{7,15},{8,24},{9,... | collective-permute-start | bytes 3145736 | tf_op jit(solution)/shard_map/ppermute | solution.py:57
  200.0 241.1 %reduce-scatter.6.cloned.1.call-start = ((), (), s32[]{:S(2)}) async-start(), calls=%async_computation.10 | async-start | bytes 3932160 | tf_op jit(solution)/shard_map/reduce_scatter | solution.py:756
  202.2 27.3 %collective-permute-start.25 = (bf16[256,2048]{1,0:T(8,128)(2,1)S(1)}, bf16[256,2048]{1,0:T(8,128)(2,1)S(1)}, u32[]{:S(2)}, u32[]{:S(2)}) collective-permute-start(bf16[256,2048]{1,0:T(8,128)(2,1)S(1)} %convolution_convert_fusion.6), channel_id=1, source_target_pairs={{0,16},{1,17},{2,18},{3,19},{4,12},{5,13},{6,14},{7,15},{8,24},{9,... | collective-permute-start | bytes 3145736 | tf_op jit(solution)/shard_map/ppermute | solution.py:57
  216.4 21.1 %collective-permute-start.27 = (bf16[256,2048]{1,0:T(8,128)(2,1)S(1)}, bf16[256,2048]{1,0:T(8,128)(2,1)S(1)}, u32[]{:S(2)}, u32[]{:S(2)}) collective-permute-start(bf16[256,2048]{1,0:T(8,128)(2,1)S(1)} %fusion.29), channel_id=1, source_target_pairs={{0,8},{1,9},{2,10},{3,11},{4,20},{5,21},{6,22},{7,23},{8,0},{9,1},... | collective-permute-start | bytes 3145736 | tf_op jit(solution)/shard_map/ppermute | solution.py:57
  239.1 13.8 %collective-permute-start.28 = (bf16[256,2048]{1,0:T(8,128)(2,1)S(1)}, bf16[256,2048]{1,0:T(8,128)(2,1)S(1)}, u32[]{:S(2)}, u32[]{:S(2)}) collective-permute-start(bf16[256,2048]{1,0:T(8,128)(2,1)S(1)} %multiply_convert_fusion.5), channel_id=1, source_target_pairs={{0,8},{1,9},{2,10},{3,11},{4,20},{5,21},{6,22},{7,23},{8,0},{9,1},... | collective-permute-start | bytes 3145736 | tf_op jit(solution)/shard_map/ppermute | solution.py:57
  255.5 25.5 %collective-permute-start.29 = (bf16[512,2048]{1,0:T(8,128)(2,1)}, bf16[512,2048]{1,0:T(8,128)(2,1)}, u32[]{:S(2)}, u32[]{:S(2)}) collective-permute-start(bf16[512,2048]{1,0:T(8,128)(2,1)} %pad_maximum_fusion.6), channel_id=1, source_target_pairs={{0,16},{1,17},{2,18},{3,19},{4,12},{5,13},{6,14},{7,15},{8,24},{9,... | collective-permute-start | bytes 6291464 | tf_op jit(solution)/shard_map/ppermute | solution.py:57
  318.4 33.9 %collective-permute-start.32 = (bf16[768,2048]{1,0:T(8,128)(2,1)}, bf16[768,2048]{1,0:T(8,128)(2,1)}, u32[]{:S(2)}, u32[]{:S(2)}) collective-permute-start(bf16[768,2048]{1,0:T(8,128)(2,1)} %convolution_convert_fusion.2), channel_id=1, source_target_pairs={{0,4},{1,5},{2,6},{3,7},{4,0},{5,1},{6,2},{7,3},{8,12},{9,13},{10,... | collective-permute-start | bytes 9437192 | tf_op jit(solution)/shard_map/ppermute | solution.py:57
  347.1 30.1 %collective-permute-start.30 = (bf16[512,2048]{1,0:T(8,128)(2,1)}, bf16[512,2048]{1,0:T(8,128)(2,1)}, u32[]{:S(2)}, u32[]{:S(2)}) collective-permute-start(bf16[512,2048]{1,0:T(8,128)(2,1)} %add_convert_fusion.3), channel_id=1, source_target_pairs={{0,16},{1,17},{2,18},{3,19},{4,12},{5,13},{6,14},{7,15},{8,24},{9,... | collective-permute-start | bytes 6291464 | tf_op jit(solution)/shard_map/ppermute | solution.py:57
  359.9 128.8 %reduce-scatter.8.cloned.1.call-start = ((), (), s32[]{:S(2)}) async-start(), calls=%async_computation.11 | async-start | bytes 3932160 | tf_op jit(solution)/shard_map/reduce_scatter | solution.py:756
  376.7 23.7 %collective-permute-start.35 = (bf16[768,2048]{1,0:T(8,128)(2,1)}, bf16[768,2048]{1,0:T(8,128)(2,1)}, u32[]{:S(2)}, u32[]{:S(2)}) collective-permute-start(bf16[768,2048]{1,0:T(8,128)(2,1)} %convolution_convert_fusion.1), channel_id=1, source_target_pairs={{0,4},{1,5},{2,6},{3,7},{4,0},{5,1},{6,2},{7,3},{8,12},{9,13},{10,... | collective-permute-start | bytes 9437192 | tf_op jit(solution)/shard_map/ppermute | solution.py:57
  379.8 14.3 %collective-permute-start.31 = (bf16[256,2048]{1,0:T(8,128)(2,1)}, bf16[256,2048]{1,0:T(8,128)(2,1)S(1)}, u32[]{:S(2)}, u32[]{:S(2)}) collective-permute-start(bf16[256,2048]{1,0:T(8,128)(2,1)} %fusion.39), channel_id=1, source_target_pairs={{0,8},{1,9},{2,10},{3,11},{4,20},{5,21},{6,22},{7,23},{8,0},{9,1},... | collective-permute-start | bytes 3145736 | tf_op jit(solution)/shard_map/ppermute | solution.py:57
  399.2 14.1 %collective-permute-start.33 = (bf16[256,2048]{1,0:T(8,128)(2,1)S(1)}, bf16[256,2048]{1,0:T(8,128)(2,1)S(1)}, u32[]{:S(2)}, u32[]{:S(2)}) collective-permute-start(bf16[256,2048]{1,0:T(8,128)(2,1)S(1)} %fusion.115), channel_id=1, source_target_pairs={{0,8},{1,9},{2,10},{3,11},{4,20},{5,21},{6,22},{7,23},{8,0},{9,1},... | collective-permute-start | bytes 3145736 | tf_op jit(solution)/shard_map/ppermute | solution.py:57
  408.3 160.4 %reduce-scatter.10.cloned.1.call-start = ((), (), s32[]{:S(2)}) async-start(), calls=%async_computation.12 | async-start | bytes 3932160 | tf_op jit(solution)/shard_map/reduce_scatter | solution.py:756
  413.4 25.4 %collective-permute-start.34 = (bf16[512,2048]{1,0:T(8,128)(2,1)S(1)}, bf16[512,2048]{1,0:T(8,128)(2,1)S(1)}, u32[]{:S(2)}, u32[]{:S(2)}) collective-permute-start(bf16[512,2048]{1,0:T(8,128)(2,1)S(1)} %pad_maximum_fusion.7), channel_id=1, source_target_pairs={{0,16},{1,17},{2,18},{3,19},{4,12},{5,13},{6,14},{7,15},{8,24},{9,... | collective-permute-start | bytes 6291464 | tf_op jit(solution)/shard_map/ppermute | solution.py:57
  422.3 50.1 %collective-permute-start.43 = (bf16[768,2048]{1,0:T(8,128)(2,1)}, bf16[768,2048]{1,0:T(8,128)(2,1)}, u32[]{:S(2)}, u32[]{:S(2)}) collective-permute-start(bf16[768,2048]{1,0:T(8,128)(2,1)} %convolution_convert_fusion), channel_id=1, source_target_pairs={{0,4},{1,5},{2,6},{3,7},{4,0},{5,1},{6,2},{7,3},{8,12},{9,13},{10,... | collective-permute-start | bytes 9437192 | tf_op jit(solution)/shard_map/ppermute | solution.py:57
  458.3 27.8 %collective-permute-start.36 = (bf16[512,2048]{1,0:T(8,128)(2,1)}, bf16[512,2048]{1,0:T(8,128)(2,1)}, u32[]{:S(2)}, u32[]{:S(2)}) collective-permute-start(bf16[512,2048]{1,0:T(8,128)(2,1)} %fusion.49), channel_id=1, source_target_pairs={{0,16},{1,17},{2,18},{3,19},{4,12},{5,13},{6,14},{7,15},{8,24},{9,... | collective-permute-start | bytes 6291464 | tf_op jit(solution)/shard_map/ppermute | solution.py:57
  468.2 15.1 %collective-permute-start.42 = (bf16[4,256,640]{2,1,0:T(8,128)(2,1)}, bf16[4,256,640]{2,1,0:T(8,128)(2,1)}, u32[]{:S(2)}, u32[]{:S(2)}) collective-permute-start(bf16[4,256,640]{2,1,0:T(8,128)(2,1)} %constant_dynamic-slice_fusion.7), channel_id=1, source_target_pairs={{0,4},{1,5},{2,6},{3,7},{4,0},{5,1},{6,2},{7,3},{8,12},{9,13},{10,... | collective-permute-start | bytes 3932168 | tf_op jit(solution)/shard_map/ppermute | solution.py:57
  468.6 12.9 %collective-permute-start.39 = (f32[2,4,2,640]{3,2,1,0:T(2,128)S(1)}, f32[2,4,2,640]{3,2,1,0:T(2,128)S(1)}, u32[]{:S(2)}, u32[]{:S(2)}) collective-permute-start(f32[2,4,2,640]{3,2,1,0:T(2,128)S(1)} %get-tuple-element.277), channel_id=1, source_target_pairs={{0,1},{1,2},{2,3},{3,0},{4,5},{5,6},{6,7},{7,4},{8,9},{9,10},{10,1... | collective-permute-start | bytes 122888 | tf_op jit(solution)/shard_map/ppermute | solution.py:57
  471.3 10.2 %collective-permute-start.40 = (f32[2,4,2,640]{3,2,1,0:T(2,128)S(1)}, f32[2,4,2,640]{3,2,1,0:T(2,128)S(1)}, u32[]{:S(2)}, u32[]{:S(2)}) collective-permute-start(f32[2,4,2,640]{3,2,1,0:T(2,128)S(1)} %get-tuple-element.277), channel_id=1, source_target_pairs={{0,2},{1,3},{2,0},{3,1},{4,6},{5,7},{6,4},{7,5},{8,10},{9,11},{10,... | collective-permute-start | bytes 122888 | tf_op jit(solution)/shard_map/ppermute | solution.py:57
  472.4 9.2 %collective-permute-start.41 = (f32[2,4,2,640]{3,2,1,0:T(2,128)S(1)}, f32[2,4,2,640]{3,2,1,0:T(2,128)S(1)}, u32[]{:S(2)}, u32[]{:S(2)}) collective-permute-start(f32[2,4,2,640]{3,2,1,0:T(2,128)S(1)} %get-tuple-element.277), channel_id=1, source_target_pairs={{0,3},{1,0},{2,1},{3,2},{4,7},{5,4},{6,5},{7,6},{8,11},{9,8},{10,9... | collective-permute-start | bytes 122888 | tf_op jit(solution)/shard_map/ppermute | solution.py:57
  481.5 161.4 %reduce-scatter.14.cloned.1.call-start = ((), (), s32[]{:S(2)}) async-start(), calls=%async_computation.14 | async-start | bytes 1638400 | tf_op jit(solution)/shard_map/reduce_scatter | solution.py:844
  522.5 14.7 %collective-permute-start.44 = (f32[4,8,640]{2,1,0:T(8,128)S(1)}, f32[4,8,640]{2,1,0:T(8,128)S(1)}, u32[]{:S(2)}, u32[]{:S(2)}) collective-permute-start(f32[4,8,640]{2,1,0:T(8,128)S(1)} %get-tuple-element.158), channel_id=1, source_target_pairs={{0,7},{1,0},{2,1},{3,2},{4,3},{5,4},{6,5},{7,6},{8,15},{9,8},{10,9... | collective-permute-start | bytes 245768 | tf_op jit(solution)/shard_map/ppermute | solution.py:57
  526.7 28.6 %collective-permute-start.61 = (bf16[1,256,640]{2,1,0:T(8,128)(2,1)}, bf16[1,256,640]{2,1,0:T(8,128)(2,1)}, u32[]{:S(2)}, u32[]{:S(2)}) collective-permute-start(bf16[1,256,640]{2,1,0:T(8,128)(2,1)} %get-tuple-element.261), channel_id=1, source_target_pairs={{0,8},{1,9},{2,10},{3,11},{4,12},{5,13},{6,14},{7,15},{8,0},{9,1},... | collective-permute-start | bytes 983048 | tf_op jit(solution)/shard_map/ppermute | solution.py:57
  527.0 28.4 %collective-permute-start.62 = (bf16[1,256,640]{2,1,0:T(8,128)(2,1)}, bf16[1,256,640]{2,1,0:T(8,128)(2,1)}, u32[]{:S(2)}, u32[]{:S(2)}) collective-permute-start(bf16[1,256,640]{2,1,0:T(8,128)(2,1)} %get-tuple-element.260), channel_id=1, source_target_pairs={{0,16},{1,17},{2,18},{3,19},{4,20},{5,21},{6,22},{7,23},{8,24},{9,... | collective-permute-start | bytes 983048 | tf_op jit(solution)/shard_map/ppermute | solution.py:57
  528.0 27.4 %collective-permute-start.63 = (bf16[1,256,640]{2,1,0:T(8,128)(2,1)}, bf16[1,256,640]{2,1,0:T(8,128)(2,1)}, u32[]{:S(2)}, u32[]{:S(2)}) collective-permute-start(bf16[1,256,640]{2,1,0:T(8,128)(2,1)} %get-tuple-element.259), channel_id=1, source_target_pairs={{0,24},{1,25},{2,26},{3,27},{4,28},{5,29},{6,30},{7,31},{8,16},{9,... | collective-permute-start | bytes 983048 | tf_op jit(solution)/shard_map/ppermute | solution.py:57
  552.9 44.4 %collective-permute-start.46 = (bf16[512,2048]{1,0:T(8,128)(2,1)}, bf16[512,2048]{1,0:T(8,128)(2,1)}, u32[]{:S(2)}, u32[]{:S(2)}) collective-permute-start(bf16[512,2048]{1,0:T(8,128)(2,1)} %convolution_convert_fusion.4), channel_id=1, source_target_pairs={{0,16},{1,17},{2,18},{3,19},{4,12},{5,13},{6,14},{7,15},{8,24},{9,... | collective-permute-start | bytes 6291464 | tf_op jit(solution)/shard_map/ppermute | solution.py:57
  563.8 109.4 %reduce-scatter.12.cloned.1.call-start = ((), (), s32[]{:S(2)}) async-start(), calls=%async_computation.13 | async-start | bytes 1945600 | tf_op jit(solution)/shard_map/reduce_scatter | solution.py:844
  566.1 22.8 %collective-permute-start.48 = (bf16[1,256,640]{2,1,0:T(8,128)(2,1)}, bf16[1,256,640]{2,1,0:T(8,128)(2,1)}, u32[]{:S(2)}, u32[]{:S(2)}) collective-permute-start(bf16[1,256,640]{2,1,0:T(8,128)(2,1)} %get-tuple-element.269), channel_id=1, source_target_pairs={{0,8},{1,9},{2,10},{3,11},{4,12},{5,13},{6,14},{7,15},{8,0},{9,1},... | collective-permute-start | bytes 983048 | tf_op jit(solution)/shard_map/ppermute | solution.py:57
  567.2 21.7 %collective-permute-start.49 = (bf16[1,256,640]{2,1,0:T(8,128)(2,1)}, bf16[1,256,640]{2,1,0:T(8,128)(2,1)}, u32[]{:S(2)}, u32[]{:S(2)}) collective-permute-start(bf16[1,256,640]{2,1,0:T(8,128)(2,1)} %get-tuple-element.268), channel_id=1, source_target_pairs={{0,16},{1,17},{2,18},{3,19},{4,20},{5,21},{6,22},{7,23},{8,24},{9,... | collective-permute-start | bytes 983048 | tf_op jit(solution)/shard_map/ppermute | solution.py:57
  567.2 24.9 %collective-permute-start.50 = (bf16[1,256,640]{2,1,0:T(8,128)(2,1)}, bf16[1,256,640]{2,1,0:T(8,128)(2,1)}, u32[]{:S(2)}, u32[]{:S(2)}) collective-permute-start(bf16[1,256,640]{2,1,0:T(8,128)(2,1)} %get-tuple-element.267), channel_id=1, source_target_pairs={{0,24},{1,25},{2,26},{3,27},{4,28},{5,29},{6,30},{7,31},{8,16},{9,... | collective-permute-start | bytes 983048 | tf_op jit(solution)/shard_map/ppermute | solution.py:57
  568.8 32.3 %collective-permute-start.54 = (bf16[4,304,640]{2,1,0:T(8,128)(2,1)S(1)}, bf16[4,304,640]{2,1,0:T(8,128)(2,1)S(1)}, u32[]{:S(2)}, u32[]{:S(2)}) collective-permute-start(bf16[4,304,640]{2,1,0:T(8,128)(2,1)S(1)} %constant_dynamic-slice_fusion.4), channel_id=1, source_target_pairs={{0,4},{1,5},{2,6},{3,7},{4,0},{5,1},{6,2},{7,3},{8,12},{9,13},{10,... | collective-permute-start | bytes 4669448 | tf_op jit(solution)/shard_map/ppermute | solution.py:57
  593.8 10.1 %collective-permute-start.51 = (bf16[1,256,640]{2,1,0:T(8,128)(2,1)S(1)}, bf16[1,256,640]{2,1,0:T(8,128)(2,1)S(1)}, u32[]{:S(2)}, u32[]{:S(2)}) collective-permute-start(bf16[1,256,640]{2,1,0:T(8,128)(2,1)S(1)} %get-tuple-element.265), channel_id=1, source_target_pairs={{0,1},{1,2},{2,3},{3,0},{4,5},{5,6},{6,7},{7,4},{8,9},{9,10},{10,1... | collective-permute-start | bytes 983048 | tf_op jit(solution)/shard_map/ppermute | solution.py:57
  593.8 23.8 %collective-permute-start.52 = (bf16[1,256,640]{2,1,0:T(8,128)(2,1)S(1)}, bf16[1,256,640]{2,1,0:T(8,128)(2,1)S(1)}, u32[]{:S(2)}, u32[]{:S(2)}) collective-permute-start(bf16[1,256,640]{2,1,0:T(8,128)(2,1)S(1)} %get-tuple-element.264), channel_id=1, source_target_pairs={{0,2},{1,3},{2,0},{3,1},{4,6},{5,7},{6,4},{7,5},{8,10},{9,11},{10,... | collective-permute-start | bytes 983048 | tf_op jit(solution)/shard_map/ppermute | solution.py:57
  594.8 24.8 %collective-permute-start.53 = (bf16[1,256,640]{2,1,0:T(8,128)(2,1)S(1)}, bf16[1,256,640]{2,1,0:T(8,128)(2,1)S(1)}, u32[]{:S(2)}, u32[]{:S(2)}) collective-permute-start(bf16[1,256,640]{2,1,0:T(8,128)(2,1)S(1)} %get-tuple-element.263), channel_id=1, source_target_pairs={{0,3},{1,0},{2,1},{3,2},{4,7},{5,4},{6,5},{7,6},{8,11},{9,8},{10,9... | collective-permute-start | bytes 983048 | tf_op jit(solution)/shard_map/ppermute | solution.py:57
  599.8 32.5 %collective-permute-start.47 = (bf16[256,2048]{1,0:T(8,128)(2,1)}, bf16[256,2048]{1,0:T(8,128)(2,1)}, u32[]{:S(2)}, u32[]{:S(2)}) collective-permute-start(bf16[256,2048]{1,0:T(8,128)(2,1)} %fusion.37), channel_id=1, source_target_pairs={{0,8},{1,9},{2,10},{3,11},{4,20},{5,21},{6,22},{7,23},{8,0},{9,1},... | collective-permute-start | bytes 3145736 | tf_op jit(solution)/shard_map/ppermute | solution.py:57
  601.8 20.5 %collective-permute-start.55 = (bf16[1,304,640]{2,1,0:T(8,128)(2,1)S(1)}, bf16[1,304,640]{2,1,0:T(8,128)(2,1)S(1)}, u32[]{:S(2)}, u32[]{:S(2)}) collective-permute-start(bf16[1,304,640]{2,1,0:T(8,128)(2,1)S(1)} %get-tuple-element.253), channel_id=1, source_target_pairs={{0,8},{1,9},{2,10},{3,11},{4,12},{5,13},{6,14},{7,15},{8,0},{9,1},... | collective-permute-start | bytes 1167368 | tf_op jit(solution)/shard_map/ppermute | solution.py:57
  603.9 19.3 %collective-permute-start.56 = (bf16[1,304,640]{2,1,0:T(8,128)(2,1)S(1)}, bf16[1,304,640]{2,1,0:T(8,128)(2,1)S(1)}, u32[]{:S(2)}, u32[]{:S(2)}) collective-permute-start(bf16[1,304,640]{2,1,0:T(8,128)(2,1)S(1)} %get-tuple-element.252), channel_id=1, source_target_pairs={{0,16},{1,17},{2,18},{3,19},{4,20},{5,21},{6,22},{7,23},{8,24},{9,... | collective-permute-start | bytes 1167368 | tf_op jit(solution)/shard_map/ppermute | solution.py:57
  617.6 12.1 %collective-permute-start.57 = (bf16[1,304,640]{2,1,0:T(8,128)(2,1)S(1)}, bf16[1,304,640]{2,1,0:T(8,128)(2,1)S(1)}, u32[]{:S(2)}, u32[]{:S(2)}) collective-permute-start(bf16[1,304,640]{2,1,0:T(8,128)(2,1)S(1)} %get-tuple-element.251), channel_id=1, source_target_pairs={{0,24},{1,25},{2,26},{3,27},{4,28},{5,29},{6,30},{7,31},{8,16},{9,... | collective-permute-start | bytes 1167368 | tf_op jit(solution)/shard_map/ppermute | solution.py:57
  619.6 59.0 %collective-permute-start.37 = (bf16[256,2048]{1,0:T(8,128)(2,1)}, bf16[256,2048]{1,0:T(8,128)(2,1)}, u32[]{:S(2)}, u32[]{:S(2)}) collective-permute-start(bf16[256,2048]{1,0:T(8,128)(2,1)} %add_convert_fusion.8), channel_id=1, source_target_pairs={{0,8},{1,9},{2,10},{3,11},{4,20},{5,21},{6,22},{7,23},{8,0},{9,1},... | collective-permute-start | bytes 3145736 | tf_op jit(solution)/shard_map/ppermute | solution.py:57
  651.6 23.8 %collective-permute-start.67 = (f32[2,2048]{1,0:T(2,128)S(1)}, f32[2,2048]{1,0:T(2,128)S(1)}, u32[]{:S(2)}, u32[]{:S(2)}) collective-permute-start(f32[2,2048]{1,0:T(2,128)S(1)} %add.821), channel_id=1, source_target_pairs={{0,1},{1,0},{2,3},{3,2},{4,5},{5,4},{6,7},{7,6},{8,9},{9,8},{10,11... | collective-permute-start | bytes 49160 | tf_op jit(solution)/shard_map/ppermute | solution.py:57
  (148 other events, 1590.7 us)
Sparse Core Ops, SparseCore 0:
  16.1 36.4 all-gather.5
  54.8 54.4 all-gather.7
  110.9 67.2 all-gather.13
  179.7 63.4 all-gather.11
  244.6 63.3 all-gather.9
  360.0 61.1 reduce-scatter.5
  423.5 62.9 reduce-scatter.7
  488.8 62.0 reduce-scatter.9
  563.9 28.8 reduce-scatter.13
  632.4 40.7 reduce-scatter.11

commit v5 on v4

--- a/solution.py
+++ b/solution.py
@@ -372,7 +372,7 @@
         square = less_one(2.0 * log_decay)
         value = low[0, span, :].astype(f32)
         root = lax.rsqrt(square)
-        root = jnp.where(going > 0.0, root, 0.0)
+        root = jnp.where(going * square > 0.0, root, 0.0)
         opened = open_input * adjoint
         direct = (restart + square * root) * opened
         input_grad = direct * value * (1.0 - open_input)

time: 709 us -> 710 us (level)
  no operation moved by 1% of the time
where the time goes in v5:
time: 710 us; the launch traced here: 699 us
  waiting for transfers between devices  222 us (31%)
  matrix products  179 us (25%)
  starting transfers between devices  88.8 us (13%)
  other arithmetic  74.2 us (10%)
  local copies, waits for them, and re-layouts  68.3 us (10%)
  Pallas kernels  50.3 us (7%)
  between operations  16.3 us (2%)
    ppermute x69, waiting for transfers between devices, send(): return jax.tree.map(lambda a: lax.ppermute(a, AXES, pairs), x)  199 us
    ppermute x69, starting transfers between devices, send(): return jax.tree.map(lambda a: lax.ppermute(a, AXES, pairs), x)  87.8 us
    dot_general x9, matrix products, leading(): lax.dot_general(former, latter, (((0,), (0,)), ((), ())), preferred_eleme...  64.8 us
    dot_general x10, matrix products, plain(): return jnp.dot(former, latter, preferred_element_type=f32)  57.3 us
    dot_general x9, matrix products, trailing(): lax.dot_general(former, latter, (((1,), (1,)), ((), ())), preferred_eleme...  57.2 us
    unnamed x262, local copies, waits for them, and re-layouts  39.9 us
    pallas_call x1, Pallas kernels, run_backward(): pl.pallas_call(backward_kernel, grid=(count,), out_shape=outs, in_specs=[...  26.7 us
    reduce_scatter x2, waiting for transfers between devices, quarter_far(): lax.psum_scatter(stacked, 'blk', scatter_dimension=0, tiled=True)[0]  18.7 us
  transfers between devices with their start and end apart: 79, of which 31 were waited for; matrix products, arithmetic and copies ran while one was open for 40% of the time, Pallas kernels for 7%

profile of v5, /device:TPU:3, one launch (start us, length us, event | category | flops | bytes accessed | tf_op | source)
XLA Modules:
  0.0 698.8 jit_solution(17594430675161016671)
XLA Ops:
  11.3 3.3 collective-permute-start
  16.1 3.6 collective-permute-done
  20.9 13.7 %collective-permute-done.1 = bf16[272,2048]{1,0:T(8,128)(2,1)} collective-permute-done((bf16[272,2048]{1,0:T(8,128)(2,1)S(1)}, bf16[272,2048]{1,0:T(8,128)(2,1)}, u32[]{:S(2)}, u32[]{:S(2)}) %collective-permute-start.1) | collective-permute-done | bytes 1114144 | tf_op jit(solution)/shard_map/ppermute | solution.py:57
  35.7 13.9 %collective-permute-done.3 = bf16[272,2048]{1,0:T(8,128)(2,1)S(1)} collective-permute-done((bf16[272,2048]{1,0:T(8,128)(2,1)}, bf16[272,2048]{1,0:T(8,128)(2,1)S(1)}, u32[]{:S(2)}, u32[]{:S(2)}) %collective-permute-start.3) | collective-permute-done | bytes 1114144 | tf_op jit(solution)/shard_map/ppermute | solution.py:57
  49.6 3.1 all-gather.6.cloned.1.call-done
  57.3 17.6 %collective-permute-done.2 = bf16[272,2048]{1,0:T(8,128)(2,1)S(1)} collective-permute-done((bf16[272,2048]{1,0:T(8,128)(2,1)}, bf16[272,2048]{1,0:T(8,128)(2,1)S(1)}, u32[]{:S(2)}, u32[]{:S(2)}) %collective-permute-start.2) | collective-permute-done | bytes 1114144 | tf_op jit(solution)/shard_map/ppermute | solution.py:57
  75.9 3.5 collective-permute-start.14
  80.3 6.4 collective-permute-start.16
  109.5 4.5 add_convert_fusion.6
  114.0 2.7 constant_dynamic-slice_fusion.8
  128.0 13.8 %shard_map.341 = (bf16[4,256,640]{2,1,0:T(8,128)(2,1)S(1)}, f32[4,256,640]{2,1,0:T(8,128)S(1)}, f32[4,256,640]{2,1,0:T(8,128)S(1)}, f32[4,256,640]{2,1,0:T(8,128)S(1)}) custom-call(s32[4,5]{1,0:T(4,128)S(1)} %pad_add_fusion.info, bf16[4,256,640]{2,1,0:T(8,128)(2,1)S(1)} %bitcast.198, bf16[4,16,640]{2,1,0:T(8,128)(2,1)S(1)} %bitcast.200, ...), custom_call_target="tpu_custom_call" | custom-call | flops 1677721600 | bytes 55050240 | tf_op jit(solution)/shard_map/pallas_call | solution.py:447
  145.8 2.9 collective-permute-done.4.refs_1_
  153.9 3.6 collective-permute-start.22
  166.2 3.0 shard_map.339
  169.3 5.4 fusion.25
  174.7 6.7 collective-permute-done.23
  181.5 16.4 %collective-permute-done.24 = bf16[256,2048]{1,0:T(8,128)(2,1)S(1)} collective-permute-done((bf16[256,2048]{1,0:T(8,128)(2,1)}, bf16[256,2048]{1,0:T(8,128)(2,1)S(1)}, u32[]{:S(2)}, u32[]{:S(2)}) %collective-permute-start.24) | collective-permute-done | bytes 1048608 | tf_op jit(solution)/shard_map/ppermute | solution.py:57
  203.6 10.5 %collective-permute-done.26 = bf16[256,2048]{1,0:T(8,128)(2,1)} collective-permute-done((bf16[256,2048]{1,0:T(8,128)(2,1)}, bf16[256,2048]{1,0:T(8,128)(2,1)}, u32[]{:S(2)}, u32[]{:S(2)}) %collective-permute-start.26) | collective-permute-done | bytes 1048608 | tf_op jit(solution)/shard_map/ppermute | solution.py:57
  216.7 3.7 fusion.17
  223.1 6.4 collective-permute-done.25
  229.5 7.9 %collective-permute-done.27 = bf16[256,2048]{1,0:T(8,128)(2,1)S(1)} collective-permute-done((bf16[256,2048]{1,0:T(8,128)(2,1)S(1)}, bf16[256,2048]{1,0:T(8,128)(2,1)S(1)}, u32[]{:S(2)}, u32[]{:S(2)}) %collective-permute-start.27) | collective-permute-done | bytes 1048608 | tf_op jit(solution)/shard_map/ppermute | solution.py:57
  240.4 12.6 %collective-permute-done.28 = bf16[256,2048]{1,0:T(8,128)(2,1)S(1)} collective-permute-done((bf16[256,2048]{1,0:T(8,128)(2,1)S(1)}, bf16[256,2048]{1,0:T(8,128)(2,1)S(1)}, u32[]{:S(2)}, u32[]{:S(2)}) %collective-permute-start.28) | collective-permute-done | bytes 1048608 | tf_op jit(solution)/shard_map/ppermute | solution.py:57
  262.8 18.2 %collective-permute-done.29 = bf16[512,2048]{1,0:T(8,128)(2,1)} collective-permute-done((bf16[512,2048]{1,0:T(8,128)(2,1)}, bf16[512,2048]{1,0:T(8,128)(2,1)}, u32[]{:S(2)}, u32[]{:S(2)}) %collective-permute-start.29) | collective-permute-done | bytes 2097184 | tf_op jit(solution)/shard_map/ppermute | solution.py:57
  281.0 11.6 %fusion.116 = f32[1024,1536]{1,0:T(8,128)} fusion(bf16[1536,2048]{1,0:T(8,128)(2,1)} %all-gather.14.cloned.1.call-done, bf16[512,2048]{1,0:T(8,128)(2,1)} %collective-permute-done.29, bf16[256,2048]{1,0:T(8,128)(2,1)} %copy-done.84, bf16[256,2048]{1,0:T(8,128)(2,1)S(1)} %multiply_convert_fusion.5), kind=kOutput, calls=%fused_computation.318 | convolution fusion | flops 6455033856 | bytes 16777216 | tf_op jit(solution)/shard_map/dot_general | solution.py:30
  292.6 17.6 %fusion.6 = (bf16[1024,1536]{1,0:T(8,128)(2,1)}, bf16[1024,1536]{1,0:T(8,128)(2,1)S(1)}, bf16[1024,1536]{1,0:T(8,128)(2,1)}) fusion(f32[1024,1536]{1,0:T(8,128)} %fusion.116, bf16[1536,2048]{1,0:T(8,128)(2,1)} %all-gather.12.cloned.1.call-done, bf16[512,2048]{1,0:T(8,128)(2,1)} %collective-permute-done.29, bf16[256,2048]{1,0:T(8,128)(2,1)} %copy-done.84, ...), kind=kOutput, calls=%fused_computation.12 | convolution fusion | flops 6492782592 | bytes 26214400 | tf_op jit(solution)/shard_map/dot_general | solution.py:30
  310.1 8.2 %convolution_convert_fusion.2 = bf16[768,2048]{1,0:T(8,128)(2,1)} fusion(bf16[1024,2048]{1,0:T(8,128)(2,1)} %constant_dynamic-update-slice_fusion, bf16[1024,1536]{1,0:T(8,128)(2,1)S(1)} %get-tuple-element.141, s32[]{:T(128)S(6)} %select_n.407), kind=kOutput, calls=%fused_computation.35 | convolution fusion | flops 3222798336 | bytes 8912900 | tf_op jit(solution)/shard_map/dot_general | solution.py:34
  319.6 11.6 %multiply_convert_fusion = (bf16[1024,1536]{1,0:T(8,128)(2,1)S(1)}, bf16[1024,1536]{1,0:T(8,128)(2,1)S(1)}) fusion(bf16[1024,1536]{1,0:T(8,128)(2,1)} %get-tuple-element.134, bf16[1024,1536]{1,0:T(8,128)(2,1)} %get-tuple-element.133, bf16[1024,2048]{1,0:T(8,128)(2,1)} %constant_dynamic-update-slice_fusion, bf16[1536,2048]{1,0:T(8,128)(2,1)} %all-gather.10.cloned.1.call-done), kind=kOutput, calls=%fused_computation.16 | convolution fusion | flops 6451888128 | bytes 23068672 | tf_op jit(solution)/shard_map/dot_general | solution.py:30
  331.3 7.9 %fusion.42 = f32[512,2048]{1,0:T(8,128)S(1)} fusion(bf16[1536,2048]{1,0:T(8,128)(2,1)} %all-gather.12.cloned.1.call-done, bf16[1024,1536]{1,0:T(8,128)(2,1)S(1)} %get-tuple-element.143), kind=kOutput, calls=%fused_computation.109 | convolution fusion | flops 3221225472 | bytes 12058624 | tf_op jit(solution)/shard_map/dot_general | solution.py:26
  339.2 7.9 %add_convert_fusion.3 = bf16[512,2048]{1,0:T(8,128)(2,1)} fusion(f32[512,2048]{1,0:T(8,128)S(1)} %fusion.42, bf16[1536,2048]{1,0:T(8,128)(2,1)} %all-gather.14.cloned.1.call-done, bf16[1024,1536]{1,0:T(8,128)(2,1)S(1)} %get-tuple-element.155), kind=kOutput, calls=%fused_computation.26 | convolution fusion | flops 3223322624 | bytes 14155776 | tf_op jit(solution)/shard_map/dot_general | solution.py:26
  347.3 5.0 fusion.54
  352.3 7.6 %add_convert_fusion.2 = bf16[768,2048]{1,0:T(8,128)(2,1)} fusion(bf16[768,2048]{1,0:T(8,128)(2,1)} %collective-permute-done.32, bf16[1024,2048]{1,0:T(8,128)(2,1)} %constant_dynamic-update-slice_fusion, bf16[1024,1536]{1,0:T(8,128)(2,1)S(1)} %copy-done.90, s32[]{:T(128)S(6)} %select_n.408), kind=kOutput, calls=%fused_computation.15 | convolution fusion | flops 3225944064 | bytes 12058628 | tf_op jit(solution)/shard_map/dot_general | solution.py:34
  360.4 8.0 %convolution_add_fusion = f32[512,2048]{1,0:T(8,128)S(1)} fusion(f32[512,2048]{1,0:T(8,128)} %fusion.54, bf16[1536,2048]{1,0:T(8,128)(2,1)} %all-gather.14.cloned.1.call-done, bf16[1024,1536]{1,0:T(8,128)(2,1)} %copy-done.115), kind=kOutput, calls=%fused_computation.42 | convolution fusion | flops 3222274048 | bytes 16252928 | tf_op jit(solution)/shard_map/dot_general | solution.py:26
  368.4 8.3 %convolution_convert_fusion.1 = bf16[768,2048]{1,0:T(8,128)(2,1)} fusion(bf16[1024,1536]{1,0:T(8,128)(2,1)S(1)} %copy-done.118, s32[]{:T(128)S(6)} %select_n.407, bf16[512,2048]{1,0:T(8,128)(2,1)} %collective-permute-done.29, bf16[256,2048]{1,0:T(8,128)(2,1)S(1)} %copy-done.85, bf16[256,2048]{1,0:T(8,128)(2,1)S(1)} %multiply_convert_fusion.5), kind=kOutput, calls=%fused_computation.34 | convolution fusion | flops 3235381248 | bytes 8912900 | tf_op jit(solution)/shard_map/dot_general | solution.py:34
  381.3 12.7 %collective-permute-done.31 = bf16[256,2048]{1,0:T(8,128)(2,1)S(1)} collective-permute-done((bf16[256,2048]{1,0:T(8,128)(2,1)}, bf16[256,2048]{1,0:T(8,128)(2,1)S(1)}, u32[]{:S(2)}, u32[]{:S(2)}) %collective-permute-start.31) | collective-permute-done | bytes 1048608 | tf_op jit(solution)/shard_map/ppermute | solution.py:57
  400.4 7.8 %add_convert_fusion.1 = bf16[768,2048]{1,0:T(8,128)(2,1)} fusion(bf16[768,2048]{1,0:T(8,128)(2,1)} %collective-permute-done.35, bf16[1024,1536]{1,0:T(8,128)(2,1)S(1)} %copy-done.119, s32[]{:T(128)S(6)} %select_n.408, bf16[512,2048]{1,0:T(8,128)(2,1)} %collective-permute-done.29, bf16[256,2048]{1,0:T(8,128)(2,1)S(1)} %copy-done.86, ...), kind=kOutput, calls=%fused_computation.14 | convolution fusion | flops 3238526976 | bytes 12058628 | tf_op jit(solution)/shard_map/dot_general | solution.py:34
  408.5 4.8 collective-permute-done.33
  414.3 8.0 %convolution_convert_fusion = bf16[768,2048]{1,0:T(8,128)(2,1)} fusion(bf16[1024,1536]{1,0:T(8,128)(2,1)} %copy-done.115, s32[]{:T(128)S(6)} %select_n.407, bf16[512,2048]{1,0:T(8,128)(2,1)} %collective-permute-done.29, bf16[256,2048]{1,0:T(8,128)(2,1)S(1)} %copy-done.87, bf16[256,2048]{1,0:T(8,128)(2,1)S(1)} %copy-done.67), kind=kOutput, calls=%fused_computation.33 | convolution fusion | flops 3235381248 | bytes 8912900 | tf_op jit(solution)/shard_map/dot_general | solution.py:34
  424.5 5.0 fusion.47
  429.5 4.6 fusion.49
  434.1 4.7 collective-permute-done.34
  441.1 8.4 %convert_reduce_fusion.1 = (bf16[640]{0:T(1024)(128)(2,1)S(1)}, bf16[1024,640]{1,0:T(8,128)(2,1)}, bf16[1024,640]{1,0:T(8,128)(2,1)S(1)}) fusion(f32[1024,640]{1,0:T(8,128)} %get-tuple-element.147, f32[1024,640]{1,0:T(8,128)} %get-tuple-element.148, bf16[1024,2048]{1,0:T(8,128)(2,1)} %pad_maximum_fusion.3, bf16[2048,640]{1,0:T(8,128)(2,1)S(1)} %copy-done.3), kind=kOutput, calls=%fused_computation.70 | convolution fusion | flops 2688286208 | bytes 14681344 | tf_op jit(solution)/shard_map/dot_general | solution.py:26
  449.4 2.7 shard_map.343
  460.8 6.2 convolution_convert_fusion.3
  473.7 7.8 %add_convert_fusion = bf16[768,2048]{1,0:T(8,128)(2,1)} fusion(bf16[768,2048]{1,0:T(8,128)(2,1)} %collective-permute-done.43, bf16[1024,1536]{1,0:T(8,128)(2,1)S(1)} %copy-done.116, s32[]{:T(128)S(6)} %select_n.408, bf16[512,2048]{1,0:T(8,128)(2,1)} %collective-permute-done.29, bf16[256,2048]{1,0:T(8,128)(2,1)S(1)} %copy-done.88, ...), kind=kOutput, calls=%fused_computation.13 | convolution fusion | flops 3238526976 | bytes 12058628 | tf_op jit(solution)/shard_map/dot_general | solution.py:34
  483.4 2.7 add_bitcast_fusion.1
  496.1 26.7 %shard_map.345 = (f32[1280,640]{1,0:T(8,128)}, f32[4,256,640]{2,1,0:T(8,128)S(1)}, f32[4,8,640]{2,1,0:T(8,128)S(1)}, f32[64,640]{1,0:T(8,128)S(1)}) custom-call(s32[4,5]{1,0:T(4,128)S(1)} %pad_add_fusion.info, bf16[4,256,640]{2,1,0:T(8,128)(2,1)S(1)} %bitcast.199, bf16[4,16,640]{2,1,0:T(8,128)(2,1)S(1)} %bitcast.201, f32[16,640]{1,0:T(8,128)S(1)} %pad_maximum_fusion.18.vec, ...), custom_call_target="tpu_custom_call" | custom-call | flops 3355443200 | bytes 94371840 | tf_op jit(solution)/shard_map/pallas_call | solution.py:511
  522.7 3.2 collective-permute-start.44
  531.0 5.7 fusion.121
  537.9 5.3 fusion.120
  544.5 2.7 slice-done.1
  547.5 4.1 convolution_convert_fusion.4
  558.1 3.1 gather_fusion.3
  570.2 4.9 fusion.122
  575.1 14.0 %collective-permute-done.48 = bf16[1,256,640]{2,1,0:T(8,128)(2,1)} collective-permute-done((bf16[1,256,640]{2,1,0:T(8,128)(2,1)}, bf16[1,256,640]{2,1,0:T(8,128)(2,1)}, u32[]{:S(2)}, u32[]{:S(2)}) %collective-permute-start.48) | collective-permute-done | bytes 327712 | tf_op jit(solution)/shard_map/ppermute | solution.py:57
  589.1 3.2 collective-permute-done.50
  606.7 11.2 %collective-permute-done.52 = bf16[1,256,640]{2,1,0:T(8,128)(2,1)S(1)} collective-permute-done((bf16[1,256,640]{2,1,0:T(8,128)(2,1)S(1)}, bf16[1,256,640]{2,1,0:T(8,128)(2,1)S(1)}, u32[]{:S(2)}, u32[]{:S(2)}) %collective-permute-start.52) | collective-permute-done | bytes 327712 | tf_op jit(solution)/shard_map/ppermute | solution.py:57
  623.4 6.5 collective-permute-done.57
  632.5 4.1 fusion.38
  636.6 3.2 multiply_reduce_fusion
  639.9 3.2 collective-permute-start.64
  651.8 2.7 collective-permute-start.67
  654.6 18.7 %reduce-scatter.12.cloned.1.call-done = bf16[1,1,304,640]{3,2,1,0:T(8,128)(2,1)} async-done(((bf16[4,1,304,640]{3,2,1,0:T(8,128)(2,1)}), bf16[1,1,304,640]{3,2,1,0:T(8,128)(2,1)}) %reduce-scatter.12.cloned.1.call-update) | async-done | bytes 389136 | tf_op jit(solution)/shard_map/reduce_scatter | solution.py:844
  678.8 5.3 fusion.35
  684.3 3.0 collective-permute-start.60
  (562 shorter events, 199.1 us)
Async XLA Ops:
  7.3 45.4 %all-gather.6.cloned.1.call-start = ((), (), s32[]{:S(2)}) async-start(), calls=%async_computation.5 | async-start | bytes 1945600 | tf_op jit(solution)/shard_map/all_gather | solution.py:125
  16.0 98.0 %all-gather.8.cloned.1.call-start = ((), (), s32[]{:S(2)}) async-start(), calls=%async_computation.6 | async-start | bytes 3276800 | tf_op jit(solution)/shard_map/all_gather | solution.py:125
  19.8 14.8 %collective-permute-start.1 = (bf16[272,2048]{1,0:T(8,128)(2,1)S(1)}, bf16[272,2048]{1,0:T(8,128)(2,1)}, u32[]{:S(2)}, u32[]{:S(2)}) collective-permute-start(bf16[272,2048]{1,0:T(8,128)(2,1)S(1)} %pad_maximum_fusion.10), channel_id=1, source_target_pairs={{0,8},{1,9},{2,10},{3,11},{4,20},{5,21},{6,22},{7,23},{8,0},{9,1},... | collective-permute-start | bytes 3342344 | tf_op jit(solution)/shard_map/ppermute | solution.py:57
  34.6 15.0 %collective-permute-start.3 = (bf16[272,2048]{1,0:T(8,128)(2,1)}, bf16[272,2048]{1,0:T(8,128)(2,1)S(1)}, u32[]{:S(2)}, u32[]{:S(2)}) collective-permute-start(bf16[272,2048]{1,0:T(8,128)(2,1)} %collective-permute-done.1), channel_id=1, source_target_pairs={{0,16},{1,17},{2,18},{3,19},{4,12},{5,13},{6,14},{7,15},{8,24},{9,... | collective-permute-start | bytes 3342344 | tf_op jit(solution)/shard_map/ppermute | solution.py:57
  52.7 228.3 %all-gather.14.cloned.1.call-start = ((), (), s32[]{:S(2)}) async-start(), calls=%async_computation.9 | async-start | bytes 7077888 | tf_op jit(solution)/shard_map/all_gather | solution.py:143
  52.8 22.1 %collective-permute-start.2 = (bf16[272,2048]{1,0:T(8,128)(2,1)}, bf16[272,2048]{1,0:T(8,128)(2,1)S(1)}, u32[]{:S(2)}, u32[]{:S(2)}) collective-permute-start(bf16[272,2048]{1,0:T(8,128)(2,1)} %copy-done.79), channel_id=1, source_target_pairs={{0,16},{1,17},{2,18},{3,19},{4,12},{5,13},{6,14},{7,15},{8,24},{9,... | collective-permute-start | bytes 3342344 | tf_op jit(solution)/shard_map/ppermute | solution.py:57
  54.6 25.7 %collective-permute-start.11 = (bf16[1,304,640]{2,1,0:T(8,128)(2,1)S(1)}, bf16[1,304,640]{2,1,0:T(8,128)(2,1)S(1)}, u32[]{:S(2)}, u32[]{:S(2)}) collective-permute-start(bf16[1,304,640]{2,1,0:T(8,128)(2,1)S(1)} %get-tuple-element.257), channel_id=1, source_target_pairs={{0,8},{1,9},{2,10},{3,11},{4,12},{5,13},{6,14},{7,15},{8,0},{9,1},... | collective-permute-start | bytes 1167368 | tf_op jit(solution)/shard_map/ppermute | solution.py:57
  55.8 24.5 %collective-permute-start.12 = (bf16[1,304,640]{2,1,0:T(8,128)(2,1)S(1)}, bf16[1,304,640]{2,1,0:T(8,128)(2,1)S(1)}, u32[]{:S(2)}, u32[]{:S(2)}) collective-permute-start(bf16[1,304,640]{2,1,0:T(8,128)(2,1)S(1)} %get-tuple-element.256), channel_id=1, source_target_pairs={{0,16},{1,17},{2,18},{3,19},{4,20},{5,21},{6,22},{7,23},{8,24},{9,... | collective-permute-start | bytes 1167368 | tf_op jit(solution)/shard_map/ppermute | solution.py:57
  57.0 30.4 %collective-permute-start.13 = (bf16[1,304,640]{2,1,0:T(8,128)(2,1)S(1)}, bf16[1,304,640]{2,1,0:T(8,128)(2,1)S(1)}, u32[]{:S(2)}, u32[]{:S(2)}) collective-permute-start(bf16[1,304,640]{2,1,0:T(8,128)(2,1)S(1)} %get-tuple-element.255), channel_id=1, source_target_pairs={{0,24},{1,25},{2,26},{3,27},{4,28},{5,29},{6,30},{7,31},{8,16},{9,... | collective-permute-start | bytes 1167368 | tf_op jit(solution)/shard_map/ppermute | solution.py:57
  75.9 12.4 %collective-permute-start.14 = (bf16[1,304,640]{2,1,0:T(8,128)(2,1)S(1)}, bf16[1,304,640]{2,1,0:T(8,128)(2,1)S(1)}, u32[]{:S(2)}, u32[]{:S(2)}) collective-permute-start(bf16[1,304,640]{2,1,0:T(8,128)(2,1)S(1)} %get-tuple-element.109.refs_0_), channel_id=1, source_target_pairs={{0,4},{1,5},{2,6},{3,7},{4,0},{5,1},{6,2},{7,3},{8,12},{9,13},{10,... | collective-permute-start | bytes 1167368 | tf_op jit(solution)/shard_map/ppermute | solution.py:57
  80.3 9.5 %collective-permute-start.16 = (bf16[1,304,640]{2,1,0:T(8,128)(2,1)S(1)}, bf16[1,304,640]{2,1,0:T(8,128)(2,1)S(1)}, u32[]{:S(2)}, u32[]{:S(2)}) collective-permute-start(bf16[1,304,640]{2,1,0:T(8,128)(2,1)S(1)} %collective-permute-done.12.refs_2_), channel_id=1, source_target_pairs={{0,4},{1,5},{2,6},{3,7},{4,0},{5,1},{6,2},{7,3},{8,12},{9,13},{10,... | collective-permute-start | bytes 1167368 | tf_op jit(solution)/shard_map/ppermute | solution.py:57
  99.7 192.9 %all-gather.12.cloned.1.call-start = ((), (), s32[]{:S(2)}) async-start(), calls=%async_computation.8 | async-start | bytes 7077888 | tf_op jit(solution)/shard_map/all_gather | solution.py:143
  100.2 219.4 %all-gather.10.cloned.1.call-start = ((), (), s32[]{:S(2)}) async-start(), calls=%async_computation.7 | async-start | bytes 7077888 | tf_op jit(solution)/shard_map/all_gather | solution.py:143
  106.0 17.9 %collective-permute-start.18 = (bf16[256,2048]{1,0:T(8,128)(2,1)}, bf16[256,2048]{1,0:T(8,128)(2,1)}, u32[]{:S(2)}, u32[]{:S(2)}) collective-permute-start(bf16[256,2048]{1,0:T(8,128)(2,1)} %param.23), channel_id=1, source_target_pairs={{0,8},{1,9},{2,10},{3,11},{4,20},{5,21},{6,22},{7,23},{8,0},{9,1},... | collective-permute-start | bytes 3145736 | tf_op jit(solution)/shard_map/ppermute | solution.py:57
  117.8 27.1 %collective-permute-start.6 = (bf16[1,512,640]{2,1,0:T(8,128)(2,1)}, bf16[1,512,640]{2,1,0:T(8,128)(2,1)S(1)}, u32[]{:S(2)}, u32[]{:S(2)}) collective-permute-start(bf16[1,512,640]{2,1,0:T(8,128)(2,1)} %bitcast.224), channel_id=1, source_target_pairs={{0,24},{1,25},{2,26},{3,27},{4,28},{5,29},{6,30},{7,31},{8,16},{9,... | collective-permute-start | bytes 1966088 | tf_op jit(solution)/shard_map/ppermute | solution.py:57
  119.4 29.3 %collective-permute-start.4 = (bf16[1,512,640]{2,1,0:T(8,128)(2,1)}, bf16[1,512,640]{2,1,0:T(8,128)(2,1)}, u32[]{:S(2)}, u32[]{:S(2)}) collective-permute-start(bf16[1,512,640]{2,1,0:T(8,128)(2,1)} %bitcast.223), channel_id=1, source_target_pairs={{0,8},{1,9},{2,10},{3,11},{4,12},{5,13},{6,14},{7,15},{8,0},{9,1},... | collective-permute-start | bytes 1966088 | tf_op jit(solution)/shard_map/ppermute | solution.py:57
  121.7 28.6 %collective-permute-start.5 = (bf16[1,512,640]{2,1,0:T(8,128)(2,1)}, bf16[1,512,640]{2,1,0:T(8,128)(2,1)}, u32[]{:S(2)}, u32[]{:S(2)}) collective-permute-start(bf16[1,512,640]{2,1,0:T(8,128)(2,1)} %bitcast.12), channel_id=1, source_target_pairs={{0,16},{1,17},{2,18},{3,19},{4,20},{5,21},{6,22},{7,23},{8,24},{9,... | collective-permute-start | bytes 1966088 | tf_op jit(solution)/shard_map/ppermute | solution.py:57
  125.8 35.8 %collective-permute-start.7 = (bf16[1,512,640]{2,1,0:T(8,128)(2,1)S(1)}, bf16[1,512,640]{2,1,0:T(8,128)(2,1)S(1)}, u32[]{:S(2)}, u32[]{:S(2)}) collective-permute-start(bf16[1,512,640]{2,1,0:T(8,128)(2,1)S(1)} %bitcast.196), channel_id=1, source_target_pairs={{0,4},{1,5},{2,6},{3,7},{4,0},{5,1},{6,2},{7,3},{8,12},{9,13},{10,... | collective-permute-start | bytes 1966088 | tf_op jit(solution)/shard_map/ppermute | solution.py:57
  144.9 9.0 %collective-permute-start.21 = (f32[2,4,2,640]{3,2,1,0:T(2,128)S(1)}, f32[2,4,2,640]{3,2,1,0:T(2,128)S(1)}, u32[]{:S(2)}, u32[]{:S(2)}) collective-permute-start(f32[2,4,2,640]{3,2,1,0:T(2,128)S(1)} %get-tuple-element.279), channel_id=1, source_target_pairs={{0,2},{1,3},{2,0},{3,1},{4,6},{5,7},{6,4},{7,5},{8,10},{9,11},{10,... | collective-permute-start | bytes 122888 | tf_op jit(solution)/shard_map/ppermute | solution.py:57
  148.7 15.7 %collective-permute-start.10 = (bf16[1,512,640]{2,1,0:T(8,128)(2,1)S(1)}, bf16[1,512,640]{2,1,0:T(8,128)(2,1)S(1)}, u32[]{:S(2)}, u32[]{:S(2)}) collective-permute-start(bf16[1,512,640]{2,1,0:T(8,128)(2,1)S(1)} %collective-permute-done.6.refs_3_), channel_id=1, source_target_pairs={{0,4},{1,5},{2,6},{3,7},{4,0},{5,1},{6,2},{7,3},{8,12},{9,13},{10,... | collective-permute-start | bytes 1966088 | tf_op jit(solution)/shard_map/ppermute | solution.py:57
  150.2 14.1 %collective-permute-start.8 = (bf16[1,512,640]{2,1,0:T(8,128)(2,1)}, bf16[1,512,640]{2,1,0:T(8,128)(2,1)S(1)}, u32[]{:S(2)}, u32[]{:S(2)}) collective-permute-start(bf16[1,512,640]{2,1,0:T(8,128)(2,1)} %collective-permute-done.4.refs_1_), channel_id=1, source_target_pairs={{0,4},{1,5},{2,6},{3,7},{4,0},{5,1},{6,2},{7,3},{8,12},{9,13},{10,... | collective-permute-start | bytes 1966088 | tf_op jit(solution)/shard_map/ppermute | solution.py:57
  150.8 13.6 %collective-permute-start.9 = (bf16[1,512,640]{2,1,0:T(8,128)(2,1)}, bf16[1,512,640]{2,1,0:T(8,128)(2,1)S(1)}, u32[]{:S(2)}, u32[]{:S(2)}) collective-permute-start(bf16[1,512,640]{2,1,0:T(8,128)(2,1)} %collective-permute-done.5.refs_2_), channel_id=1, source_target_pairs={{0,4},{1,5},{2,6},{3,7},{4,0},{5,1},{6,2},{7,3},{8,12},{9,13},{10,... | collective-permute-start | bytes 1966088 | tf_op jit(solution)/shard_map/ppermute | solution.py:57
  160.1 21.3 %collective-permute-start.23 = (bf16[256,2048]{1,0:T(8,128)(2,1)}, bf16[256,2048]{1,0:T(8,128)(2,1)S(1)}, u32[]{:S(2)}, u32[]{:S(2)}) collective-permute-start(bf16[256,2048]{1,0:T(8,128)(2,1)} %param.23), channel_id=1, source_target_pairs={{0,16},{1,17},{2,18},{3,19},{4,12},{5,13},{6,14},{7,15},{8,24},{9,... | collective-permute-start | bytes 3145736 | tf_op jit(solution)/shard_map/ppermute | solution.py:57
  161.7 36.1 %collective-permute-start.24 = (bf16[256,2048]{1,0:T(8,128)(2,1)}, bf16[256,2048]{1,0:T(8,128)(2,1)S(1)}, u32[]{:S(2)}, u32[]{:S(2)}) collective-permute-start(bf16[256,2048]{1,0:T(8,128)(2,1)} %param.23), channel_id=1, source_target_pairs={{0,24},{1,25},{2,26},{3,27},{4,28},{5,29},{6,30},{7,31},{8,16},{9,... | collective-permute-start | bytes 3145736 | tf_op jit(solution)/shard_map/ppermute | solution.py:57
  199.8 14.3 %collective-permute-start.26 = (bf16[256,2048]{1,0:T(8,128)(2,1)}, bf16[256,2048]{1,0:T(8,128)(2,1)}, u32[]{:S(2)}, u32[]{:S(2)}) collective-permute-start(bf16[256,2048]{1,0:T(8,128)(2,1)} %convolution_convert_fusion.5), channel_id=1, source_target_pairs={{0,16},{1,17},{2,18},{3,19},{4,12},{5,13},{6,14},{7,15},{8,24},{9,... | collective-permute-start | bytes 3145736 | tf_op jit(solution)/shard_map/ppermute | solution.py:57
  200.0 241.1 %reduce-scatter.6.cloned.1.call-start = ((), (), s32[]{:S(2)}) async-start(), calls=%async_computation.10 | async-start | bytes 3932160 | tf_op jit(solution)/shard_map/reduce_scatter | solution.py:756
  202.2 27.3 %collective-permute-start.25 = (bf16[256,2048]{1,0:T(8,128)(2,1)S(1)}, bf16[256,2048]{1,0:T(8,128)(2,1)S(1)}, u32[]{:S(2)}, u32[]{:S(2)}) collective-permute-start(bf16[256,2048]{1,0:T(8,128)(2,1)S(1)} %convolution_convert_fusion.6), channel_id=1, source_target_pairs={{0,16},{1,17},{2,18},{3,19},{4,12},{5,13},{6,14},{7,15},{8,24},{9,... | collective-permute-start | bytes 3145736 | tf_op jit(solution)/shard_map/ppermute | solution.py:57
  216.4 21.1 %collective-permute-start.27 = (bf16[256,2048]{1,0:T(8,128)(2,1)S(1)}, bf16[256,2048]{1,0:T(8,128)(2,1)S(1)}, u32[]{:S(2)}, u32[]{:S(2)}) collective-permute-start(bf16[256,2048]{1,0:T(8,128)(2,1)S(1)} %fusion.29), channel_id=1, source_target_pairs={{0,8},{1,9},{2,10},{3,11},{4,20},{5,21},{6,22},{7,23},{8,0},{9,1},... | collective-permute-start | bytes 3145736 | tf_op jit(solution)/shard_map/ppermute | solution.py:57
  239.1 13.8 %collective-permute-start.28 = (bf16[256,2048]{1,0:T(8,128)(2,1)S(1)}, bf16[256,2048]{1,0:T(8,128)(2,1)S(1)}, u32[]{:S(2)}, u32[]{:S(2)}) collective-permute-start(bf16[256,2048]{1,0:T(8,128)(2,1)S(1)} %multiply_convert_fusion.5), channel_id=1, source_target_pairs={{0,8},{1,9},{2,10},{3,11},{4,20},{5,21},{6,22},{7,23},{8,0},{9,1},... | collective-permute-start | bytes 3145736 | tf_op jit(solution)/shard_map/ppermute | solution.py:57
  255.5 25.5 %collective-permute-start.29 = (bf16[512,2048]{1,0:T(8,128)(2,1)}, bf16[512,2048]{1,0:T(8,128)(2,1)}, u32[]{:S(2)}, u32[]{:S(2)}) collective-permute-start(bf16[512,2048]{1,0:T(8,128)(2,1)} %pad_maximum_fusion.6), channel_id=1, source_target_pairs={{0,16},{1,17},{2,18},{3,19},{4,12},{5,13},{6,14},{7,15},{8,24},{9,... | collective-permute-start | bytes 6291464 | tf_op jit(solution)/shard_map/ppermute | solution.py:57
  318.4 33.9 %collective-permute-start.32 = (bf16[768,2048]{1,0:T(8,128)(2,1)}, bf16[768,2048]{1,0:T(8,128)(2,1)}, u32[]{:S(2)}, u32[]{:S(2)}) collective-permute-start(bf16[768,2048]{1,0:T(8,128)(2,1)} %convolution_convert_fusion.2), channel_id=1, source_target_pairs={{0,4},{1,5},{2,6},{3,7},{4,0},{5,1},{6,2},{7,3},{8,12},{9,13},{10,... | collective-permute-start | bytes 9437192 | tf_op jit(solution)/shard_map/ppermute | solution.py:57
  347.1 30.1 %collective-permute-start.30 = (bf16[512,2048]{1,0:T(8,128)(2,1)}, bf16[512,2048]{1,0:T(8,128)(2,1)}, u32[]{:S(2)}, u32[]{:S(2)}) collective-permute-start(bf16[512,2048]{1,0:T(8,128)(2,1)} %add_convert_fusion.3), channel_id=1, source_target_pairs={{0,16},{1,17},{2,18},{3,19},{4,12},{5,13},{6,14},{7,15},{8,24},{9,... | collective-permute-start | bytes 6291464 | tf_op jit(solution)/shard_map/ppermute | solution.py:57
  359.9 128.8 %reduce-scatter.8.cloned.1.call-start = ((), (), s32[]{:S(2)}) async-start(), calls=%async_computation.11 | async-start | bytes 3932160 | tf_op jit(solution)/shard_map/reduce_scatter | solution.py:756
  376.7 23.7 %collective-permute-start.35 = (bf16[768,2048]{1,0:T(8,128)(2,1)}, bf16[768,2048]{1,0:T(8,128)(2,1)}, u32[]{:S(2)}, u32[]{:S(2)}) collective-permute-start(bf16[768,2048]{1,0:T(8,128)(2,1)} %convolution_convert_fusion.1), channel_id=1, source_target_pairs={{0,4},{1,5},{2,6},{3,7},{4,0},{5,1},{6,2},{7,3},{8,12},{9,13},{10,... | collective-permute-start | bytes 9437192 | tf_op jit(solution)/shard_map/ppermute | solution.py:57
  379.8 14.3 %collective-permute-start.31 = (bf16[256,2048]{1,0:T(8,128)(2,1)}, bf16[256,2048]{1,0:T(8,128)(2,1)S(1)}, u32[]{:S(2)}, u32[]{:S(2)}) collective-permute-start(bf16[256,2048]{1,0:T(8,128)(2,1)} %fusion.39), channel_id=1, source_target_pairs={{0,8},{1,9},{2,10},{3,11},{4,20},{5,21},{6,22},{7,23},{8,0},{9,1},... | collective-permute-start | bytes 3145736 | tf_op jit(solution)/shard_map/ppermute | solution.py:57
  399.2 14.1 %collective-permute-start.33 = (bf16[256,2048]{1,0:T(8,128)(2,1)S(1)}, bf16[256,2048]{1,0:T(8,128)(2,1)S(1)}, u32[]{:S(2)}, u32[]{:S(2)}) collective-permute-start(bf16[256,2048]{1,0:T(8,128)(2,1)S(1)} %fusion.115), channel_id=1, source_target_pairs={{0,8},{1,9},{2,10},{3,11},{4,20},{5,21},{6,22},{7,23},{8,0},{9,1},... | collective-permute-start | bytes 3145736 | tf_op jit(solution)/shard_map/ppermute | solution.py:57
  408.3 160.6 %reduce-scatter.10.cloned.1.call-start = ((), (), s32[]{:S(2)}) async-start(), calls=%async_computation.12 | async-start | bytes 3932160 | tf_op jit(solution)/shard_map/reduce_scatter | solution.py:756
  413.4 25.4 %collective-permute-start.34 = (bf16[512,2048]{1,0:T(8,128)(2,1)S(1)}, bf16[512,2048]{1,0:T(8,128)(2,1)S(1)}, u32[]{:S(2)}, u32[]{:S(2)}) collective-permute-start(bf16[512,2048]{1,0:T(8,128)(2,1)S(1)} %pad_maximum_fusion.7), channel_id=1, source_target_pairs={{0,16},{1,17},{2,18},{3,19},{4,12},{5,13},{6,14},{7,15},{8,24},{9,... | collective-permute-start | bytes 6291464 | tf_op jit(solution)/shard_map/ppermute | solution.py:57
  422.3 50.1 %collective-permute-start.43 = (bf16[768,2048]{1,0:T(8,128)(2,1)}, bf16[768,2048]{1,0:T(8,128)(2,1)}, u32[]{:S(2)}, u32[]{:S(2)}) collective-permute-start(bf16[768,2048]{1,0:T(8,128)(2,1)} %convolution_convert_fusion), channel_id=1, source_target_pairs={{0,4},{1,5},{2,6},{3,7},{4,0},{5,1},{6,2},{7,3},{8,12},{9,13},{10,... | collective-permute-start | bytes 9437192 | tf_op jit(solution)/shard_map/ppermute | solution.py:57
  458.3 27.8 %collective-permute-start.36 = (bf16[512,2048]{1,0:T(8,128)(2,1)}, bf16[512,2048]{1,0:T(8,128)(2,1)}, u32[]{:S(2)}, u32[]{:S(2)}) collective-permute-start(bf16[512,2048]{1,0:T(8,128)(2,1)} %fusion.49), channel_id=1, source_target_pairs={{0,16},{1,17},{2,18},{3,19},{4,12},{5,13},{6,14},{7,15},{8,24},{9,... | collective-permute-start | bytes 6291464 | tf_op jit(solution)/shard_map/ppermute | solution.py:57
  468.2 15.1 %collective-permute-start.42 = (bf16[4,256,640]{2,1,0:T(8,128)(2,1)}, bf16[4,256,640]{2,1,0:T(8,128)(2,1)}, u32[]{:S(2)}, u32[]{:S(2)}) collective-permute-start(bf16[4,256,640]{2,1,0:T(8,128)(2,1)} %constant_dynamic-slice_fusion.7), channel_id=1, source_target_pairs={{0,4},{1,5},{2,6},{3,7},{4,0},{5,1},{6,2},{7,3},{8,12},{9,13},{10,... | collective-permute-start | bytes 3932168 | tf_op jit(solution)/shard_map/ppermute | solution.py:57
  468.6 12.9 %collective-permute-start.39 = (f32[2,4,2,640]{3,2,1,0:T(2,128)S(1)}, f32[2,4,2,640]{3,2,1,0:T(2,128)S(1)}, u32[]{:S(2)}, u32[]{:S(2)}) collective-permute-start(f32[2,4,2,640]{3,2,1,0:T(2,128)S(1)} %get-tuple-element.277), channel_id=1, source_target_pairs={{0,1},{1,2},{2,3},{3,0},{4,5},{5,6},{6,7},{7,4},{8,9},{9,10},{10,1... | collective-permute-start | bytes 122888 | tf_op jit(solution)/shard_map/ppermute | solution.py:57
  471.3 10.2 %collective-permute-start.40 = (f32[2,4,2,640]{3,2,1,0:T(2,128)S(1)}, f32[2,4,2,640]{3,2,1,0:T(2,128)S(1)}, u32[]{:S(2)}, u32[]{:S(2)}) collective-permute-start(f32[2,4,2,640]{3,2,1,0:T(2,128)S(1)} %get-tuple-element.277), channel_id=1, source_target_pairs={{0,2},{1,3},{2,0},{3,1},{4,6},{5,7},{6,4},{7,5},{8,10},{9,11},{10,... | collective-permute-start | bytes 122888 | tf_op jit(solution)/shard_map/ppermute | solution.py:57
  472.4 9.2 %collective-permute-start.41 = (f32[2,4,2,640]{3,2,1,0:T(2,128)S(1)}, f32[2,4,2,640]{3,2,1,0:T(2,128)S(1)}, u32[]{:S(2)}, u32[]{:S(2)}) collective-permute-start(f32[2,4,2,640]{3,2,1,0:T(2,128)S(1)} %get-tuple-element.277), channel_id=1, source_target_pairs={{0,3},{1,0},{2,1},{3,2},{4,7},{5,4},{6,5},{7,6},{8,11},{9,8},{10,9... | collective-permute-start | bytes 122888 | tf_op jit(solution)/shard_map/ppermute | solution.py:57
  481.5 161.6 %reduce-scatter.14.cloned.1.call-start = ((), (), s32[]{:S(2)}) async-start(), calls=%async_computation.14 | async-start | bytes 1638400 | tf_op jit(solution)/shard_map/reduce_scatter | solution.py:844
  522.7 14.7 %collective-permute-start.44 = (f32[4,8,640]{2,1,0:T(8,128)S(1)}, f32[4,8,640]{2,1,0:T(8,128)S(1)}, u32[]{:S(2)}, u32[]{:S(2)}) collective-permute-start(f32[4,8,640]{2,1,0:T(8,128)S(1)} %get-tuple-element.158), channel_id=1, source_target_pairs={{0,7},{1,0},{2,1},{3,2},{4,3},{5,4},{6,5},{7,6},{8,15},{9,8},{10,9... | collective-permute-start | bytes 245768 | tf_op jit(solution)/shard_map/ppermute | solution.py:57
  526.9 28.6 %collective-permute-start.61 = (bf16[1,256,640]{2,1,0:T(8,128)(2,1)}, bf16[1,256,640]{2,1,0:T(8,128)(2,1)}, u32[]{:S(2)}, u32[]{:S(2)}) collective-permute-start(bf16[1,256,640]{2,1,0:T(8,128)(2,1)} %get-tuple-element.261), channel_id=1, source_target_pairs={{0,8},{1,9},{2,10},{3,11},{4,12},{5,13},{6,14},{7,15},{8,0},{9,1},... | collective-permute-start | bytes 983048 | tf_op jit(solution)/shard_map/ppermute | solution.py:57
  527.2 28.4 %collective-permute-start.62 = (bf16[1,256,640]{2,1,0:T(8,128)(2,1)}, bf16[1,256,640]{2,1,0:T(8,128)(2,1)}, u32[]{:S(2)}, u32[]{:S(2)}) collective-permute-start(bf16[1,256,640]{2,1,0:T(8,128)(2,1)} %get-tuple-element.260), channel_id=1, source_target_pairs={{0,16},{1,17},{2,18},{3,19},{4,20},{5,21},{6,22},{7,23},{8,24},{9,... | collective-permute-start | bytes 983048 | tf_op jit(solution)/shard_map/ppermute | solution.py:57
  528.2 27.4 %collective-permute-start.63 = (bf16[1,256,640]{2,1,0:T(8,128)(2,1)}, bf16[1,256,640]{2,1,0:T(8,128)(2,1)}, u32[]{:S(2)}, u32[]{:S(2)}) collective-permute-start(bf16[1,256,640]{2,1,0:T(8,128)(2,1)} %get-tuple-element.259), channel_id=1, source_target_pairs={{0,24},{1,25},{2,26},{3,27},{4,28},{5,29},{6,30},{7,31},{8,16},{9,... | collective-permute-start | bytes 983048 | tf_op jit(solution)/shard_map/ppermute | solution.py:57
  553.1 44.4 %collective-permute-start.46 = (bf16[512,2048]{1,0:T(8,128)(2,1)}, bf16[512,2048]{1,0:T(8,128)(2,1)}, u32[]{:S(2)}, u32[]{:S(2)}) collective-permute-start(bf16[512,2048]{1,0:T(8,128)(2,1)} %convolution_convert_fusion.4), channel_id=1, source_target_pairs={{0,16},{1,17},{2,18},{3,19},{4,12},{5,13},{6,14},{7,15},{8,24},{9,... | collective-permute-start | bytes 6291464 | tf_op jit(solution)/shard_map/ppermute | solution.py:57
  563.9 109.3 %reduce-scatter.12.cloned.1.call-start = ((), (), s32[]{:S(2)}) async-start(), calls=%async_computation.13 | async-start | bytes 1945600 | tf_op jit(solution)/shard_map/reduce_scatter | solution.py:844
  566.2 22.8 %collective-permute-start.48 = (bf16[1,256,640]{2,1,0:T(8,128)(2,1)}, bf16[1,256,640]{2,1,0:T(8,128)(2,1)}, u32[]{:S(2)}, u32[]{:S(2)}) collective-permute-start(bf16[1,256,640]{2,1,0:T(8,128)(2,1)} %get-tuple-element.269), channel_id=1, source_target_pairs={{0,8},{1,9},{2,10},{3,11},{4,12},{5,13},{6,14},{7,15},{8,0},{9,1},... | collective-permute-start | bytes 983048 | tf_op jit(solution)/shard_map/ppermute | solution.py:57
  567.4 21.7 %collective-permute-start.49 = (bf16[1,256,640]{2,1,0:T(8,128)(2,1)}, bf16[1,256,640]{2,1,0:T(8,128)(2,1)}, u32[]{:S(2)}, u32[]{:S(2)}) collective-permute-start(bf16[1,256,640]{2,1,0:T(8,128)(2,1)} %get-tuple-element.268), channel_id=1, source_target_pairs={{0,16},{1,17},{2,18},{3,19},{4,20},{5,21},{6,22},{7,23},{8,24},{9,... | collective-permute-start | bytes 983048 | tf_op jit(solution)/shard_map/ppermute | solution.py:57
  567.4 24.9 %collective-permute-start.50 = (bf16[1,256,640]{2,1,0:T(8,128)(2,1)}, bf16[1,256,640]{2,1,0:T(8,128)(2,1)}, u32[]{:S(2)}, u32[]{:S(2)}) collective-permute-start(bf16[1,256,640]{2,1,0:T(8,128)(2,1)} %get-tuple-element.267), channel_id=1, source_target_pairs={{0,24},{1,25},{2,26},{3,27},{4,28},{5,29},{6,30},{7,31},{8,16},{9,... | collective-permute-start | bytes 983048 | tf_op jit(solution)/shard_map/ppermute | solution.py:57
  569.0 32.3 %collective-permute-start.54 = (bf16[4,304,640]{2,1,0:T(8,128)(2,1)S(1)}, bf16[4,304,640]{2,1,0:T(8,128)(2,1)S(1)}, u32[]{:S(2)}, u32[]{:S(2)}) collective-permute-start(bf16[4,304,640]{2,1,0:T(8,128)(2,1)S(1)} %constant_dynamic-slice_fusion.4), channel_id=1, source_target_pairs={{0,4},{1,5},{2,6},{3,7},{4,0},{5,1},{6,2},{7,3},{8,12},{9,13},{10,... | collective-permute-start | bytes 4669448 | tf_op jit(solution)/shard_map/ppermute | solution.py:57
  594.0 10.1 %collective-permute-start.51 = (bf16[1,256,640]{2,1,0:T(8,128)(2,1)S(1)}, bf16[1,256,640]{2,1,0:T(8,128)(2,1)S(1)}, u32[]{:S(2)}, u32[]{:S(2)}) collective-permute-start(bf16[1,256,640]{2,1,0:T(8,128)(2,1)S(1)} %get-tuple-element.265), channel_id=1, source_target_pairs={{0,1},{1,2},{2,3},{3,0},{4,5},{5,6},{6,7},{7,4},{8,9},{9,10},{10,1... | collective-permute-start | bytes 983048 | tf_op jit(solution)/shard_map/ppermute | solution.py:57
  594.1 23.8 %collective-permute-start.52 = (bf16[1,256,640]{2,1,0:T(8,128)(2,1)S(1)}, bf16[1,256,640]{2,1,0:T(8,128)(2,1)S(1)}, u32[]{:S(2)}, u32[]{:S(2)}) collective-permute-start(bf16[1,256,640]{2,1,0:T(8,128)(2,1)S(1)} %get-tuple-element.264), channel_id=1, source_target_pairs={{0,2},{1,3},{2,0},{3,1},{4,6},{5,7},{6,4},{7,5},{8,10},{9,11},{10,... | collective-permute-start | bytes 983048 | tf_op jit(solution)/shard_map/ppermute | solution.py:57
  595.0 24.8 %collective-permute-start.53 = (bf16[1,256,640]{2,1,0:T(8,128)(2,1)S(1)}, bf16[1,256,640]{2,1,0:T(8,128)(2,1)S(1)}, u32[]{:S(2)}, u32[]{:S(2)}) collective-permute-start(bf16[1,256,640]{2,1,0:T(8,128)(2,1)S(1)} %get-tuple-element.263), channel_id=1, source_target_pairs={{0,3},{1,0},{2,1},{3,2},{4,7},{5,4},{6,5},{7,6},{8,11},{9,8},{10,9... | collective-permute-start | bytes 983048 | tf_op jit(solution)/shard_map/ppermute | solution.py:57
  600.0 32.5 %collective-permute-start.47 = (bf16[256,2048]{1,0:T(8,128)(2,1)}, bf16[256,2048]{1,0:T(8,128)(2,1)}, u32[]{:S(2)}, u32[]{:S(2)}) collective-permute-start(bf16[256,2048]{1,0:T(8,128)(2,1)} %fusion.37), channel_id=1, source_target_pairs={{0,8},{1,9},{2,10},{3,11},{4,20},{5,21},{6,22},{7,23},{8,0},{9,1},... | collective-permute-start | bytes 3145736 | tf_op jit(solution)/shard_map/ppermute | solution.py:57
  602.0 20.5 %collective-permute-start.55 = (bf16[1,304,640]{2,1,0:T(8,128)(2,1)S(1)}, bf16[1,304,640]{2,1,0:T(8,128)(2,1)S(1)}, u32[]{:S(2)}, u32[]{:S(2)}) collective-permute-start(bf16[1,304,640]{2,1,0:T(8,128)(2,1)S(1)} %get-tuple-element.253), channel_id=1, source_target_pairs={{0,8},{1,9},{2,10},{3,11},{4,12},{5,13},{6,14},{7,15},{8,0},{9,1},... | collective-permute-start | bytes 1167368 | tf_op jit(solution)/shard_map/ppermute | solution.py:57
  604.1 19.3 %collective-permute-start.56 = (bf16[1,304,640]{2,1,0:T(8,128)(2,1)S(1)}, bf16[1,304,640]{2,1,0:T(8,128)(2,1)S(1)}, u32[]{:S(2)}, u32[]{:S(2)}) collective-permute-start(bf16[1,304,640]{2,1,0:T(8,128)(2,1)S(1)} %get-tuple-element.252), channel_id=1, source_target_pairs={{0,16},{1,17},{2,18},{3,19},{4,20},{5,21},{6,22},{7,23},{8,24},{9,... | collective-permute-start | bytes 1167368 | tf_op jit(solution)/shard_map/ppermute | solution.py:57
  617.8 12.1 %collective-permute-start.57 = (bf16[1,304,640]{2,1,0:T(8,128)(2,1)S(1)}, bf16[1,304,640]{2,1,0:T(8,128)(2,1)S(1)}, u32[]{:S(2)}, u32[]{:S(2)}) collective-permute-start(bf16[1,304,640]{2,1,0:T(8,128)(2,1)S(1)} %get-tuple-element.251), channel_id=1, source_target_pairs={{0,24},{1,25},{2,26},{3,27},{4,28},{5,29},{6,30},{7,31},{8,16},{9,... | collective-permute-start | bytes 1167368 | tf_op jit(solution)/shard_map/ppermute | solution.py:57
  619.8 59.0 %collective-permute-start.37 = (bf16[256,2048]{1,0:T(8,128)(2,1)}, bf16[256,2048]{1,0:T(8,128)(2,1)}, u32[]{:S(2)}, u32[]{:S(2)}) collective-permute-start(bf16[256,2048]{1,0:T(8,128)(2,1)} %add_convert_fusion.8), channel_id=1, source_target_pairs={{0,8},{1,9},{2,10},{3,11},{4,20},{5,21},{6,22},{7,23},{8,0},{9,1},... | collective-permute-start | bytes 3145736 | tf_op jit(solution)/shard_map/ppermute | solution.py:57
  651.8 23.8 %collective-permute-start.67 = (f32[2,2048]{1,0:T(2,128)S(1)}, f32[2,2048]{1,0:T(2,128)S(1)}, u32[]{:S(2)}, u32[]{:S(2)}) collective-permute-start(f32[2,2048]{1,0:T(2,128)S(1)} %add.821), channel_id=1, source_target_pairs={{0,1},{1,0},{2,3},{3,2},{4,5},{5,4},{6,7},{7,6},{8,9},{9,8},{10,11... | collective-permute-start | bytes 49160 | tf_op jit(solution)/shard_map/ppermute | solution.py:57
  (148 other events, 1591.2 us)
Sparse Core Ops, SparseCore 0:
  16.1 36.4 all-gather.5
  54.8 54.4 all-gather.7
  110.9 67.2 all-gather.13
  179.7 63.4 all-gather.11
  244.6 63.3 all-gather.9
  360.0 61.1 reduce-scatter.5
  423.5 62.9 reduce-scatter.7
  488.8 62.0 reduce-scatter.9
  564.1 28.8 reduce-scatter.13
  632.6 40.6 reduce-scatter.11
